TPU v7x, 32 devices: a whole 2x2x4 slice. The times are simulated.
32 devices in a mesh: ctx: 8 (over y, x, core), fsdp: 4 (over z).
Axes of the slice: x: 2, y: 2, z: 4, core: 2. Of those that a mesh axis runs over, the one named last changes fastest.
Arguments:
- tokens: bfloat16 [4, 3072, 1536], P('fsdp', 'ctx'), may hold values from -6 to 6
- order: int32 [4, 3072], P('fsdp'), may hold values from 0 to 3071, as said below
- lengths: int32 [4, 4], P('fsdp'), may hold values from 1 to 2688, 3072 in all within a row
- norm_attn: bfloat16 [1536], P('fsdp'), may hold values from 0.099609375 to 1.8984375
- w_attn_in: bfloat16 [1536, 1792], P('fsdp'), may hold values from -0.15625 to 0.15625
- w_attn_out: bfloat16 [1536, 1536], P('fsdp'), may hold values from -2.5 to 2.5
- norm_mlp: bfloat16 [1536], P('fsdp'), may hold values from 0.099609375 to 1.8984375
- w_mlp_in: bfloat16 [1536, 9216], P('fsdp'), may hold values from -0.15625 to 0.15625
- w_mlp_out: bfloat16 [4608, 1536], P('fsdp'), may hold values from -0.09375 to 0.09375
- cotangent: bfloat16 [4, 3072, 1536], P('fsdp', 'ctx'), may hold values from -6 to 6
Outputs:
- output: bfloat16 [4, 3072, 1536], P('fsdp', 'ctx')
- input_grad: float32 [4, 3072, 1536], P('fsdp', 'ctx')
- grad_norm_attn: float32 [1536], P('fsdp')
- grad_w_attn_in: float32 [1536, 1792], P('fsdp')
- grad_w_attn_out: float32 [1536, 1536], P('fsdp')
- grad_norm_mlp: float32 [1536], P('fsdp')
- grad_w_mlp_in: float32 [1536, 9216], P('fsdp')
- grad_w_mlp_out: float32 [4608, 1536], P('fsdp')
Inputs may be any that keep to these rules, and one draw needn't show every extreme that they name: Each group's rows hold every place of its pack once; the rows of one ctx device take one block of 96 consecutive places from each of 4 rounds of 768 places, rounds in order. A group's lengths sum to 3072.
All inputs are finite; a program needn't handle non-finite values.
Results may differ from a plain program's by a relative error of at most 0.024.
Values may be sent and summed in bfloat16 or wider, within the bound.
A program may use at most 384 MiB of HBM per device.

v0:
```python
import jax
import jax.numpy as jnp
from jax import lax
from jax.sharding import PartitionSpec as P

H = 12
HD = 128
FF = 4608
WINDOW = 1024


EPS = 1e-06


def rms_norm(values, gain):
    return values * lax.rsqrt(jnp.mean(values * values, axis=-1, keepdims=True) + EPS) * gain


def rotate(values, places):
    half_dim = values.shape[-1] // 2
    frequency = 10000.0 ** (-jnp.arange(half_dim, dtype=jnp.float32) / half_dim)
    angles = places[:, None] * frequency[None, :]
    cosine = jnp.cos(angles)[:, None, :]
    sine_part = jnp.sin(angles)[:, None, :]
    first_half = values[..., :half_dim]
    second_half = values[..., half_dim:]
    return jnp.concatenate(
        [
            first_half * cosine - second_half * sine_part,
            second_half * cosine + first_half * sine_part,
        ],
        axis=-1,
    )


def geglu(joined):
    return jax.nn.gelu(joined[:, :FF], approximate=True) * joined[:, FF:]


def per_device(
    tokens,
    order,
    lengths,
    norm_attn,
    w_attn_in,
    w_attn_out,
    norm_mlp,
    w_mlp_in,
    w_mlp_out,
    cotangent,
):
    own_rows = tokens.shape[1]
    query_dim = H * HD
    ctx_index = lax.axis_index("ctx")
    places_all = order[0]
    seq_ends = jnp.cumsum(lengths[0])
    segment_all = jnp.sum((seq_ends[None, :] <= places_all[:, None]).astype(jnp.int32), axis=1)
    own_places = lax.dynamic_slice_in_dim(places_all, ctx_index * own_rows, own_rows)
    own_segment = lax.dynamic_slice_in_dim(segment_all, ctx_index * own_rows, own_rows)
    row_places = jnp.repeat(own_places, H)
    row_segment = jnp.repeat(own_segment, H)

    def allowed():
        distance = row_places[:, None] - places_all[None, :]
        return (
            (row_segment[:, None] == segment_all[None, :]) & (distance >= 0) & (distance < WINDOW)
        )

    gathered = (
        lax.all_gather(norm_attn, "fsdp", axis=0, tiled=True),
        lax.all_gather(w_attn_in, "fsdp", axis=0, tiled=True),
        lax.all_gather(w_attn_out, "fsdp", axis=0, tiled=True),
        lax.all_gather(norm_mlp, "fsdp", axis=0, tiled=True),
        lax.all_gather(w_mlp_in, "fsdp", axis=0, tiled=True),
        lax.all_gather(w_mlp_out, "fsdp", axis=0, tiled=True),
    )
    gain_attn, in_attn, out_attn, gain_mlp, in_mlp, out_mlp = gathered
    inputs = tokens[0].astype(jnp.float32)
    normed_one, norm_one_back = jax.vjp(rms_norm, inputs, gain_attn.astype(jnp.float32))
    normed_one = normed_one.astype(jnp.bfloat16)
    projected = jnp.dot(normed_one, in_attn, preferred_element_type=jnp.float32)
    place_float = own_places.astype(jnp.float32)

    def query_map(part):
        return rotate(part, place_float) * HD ** (-0.5)

    def key_map(part):
        return rotate(part[:, None, :], place_float)[:, 0, :]

    query_rot, query_back = jax.vjp(query_map, projected[:, :query_dim].reshape(own_rows, H, HD))
    key_rot, key_back = jax.vjp(key_map, projected[:, query_dim : query_dim + HD])
    queries = query_rot.astype(jnp.bfloat16).reshape(own_rows * H, HD)
    key_value = jnp.concatenate(
        [key_rot.astype(jnp.bfloat16), projected[:, query_dim + HD :].astype(jnp.bfloat16)], axis=1
    )
    piece = lax.all_gather(key_value, "ctx", axis=0, tiled=True)
    row_peak = jnp.full((own_rows * H,), -1e30, jnp.float32)
    allowed_mask = allowed()
    scores = jnp.einsum("rd,kd->rk", queries, piece[:, :HD], preferred_element_type=jnp.float32)
    new_peak = jnp.maximum(row_peak, jnp.max(jnp.where(allowed_mask, scores, -1e30), axis=1))
    weights_exp = jnp.where(allowed_mask, jnp.exp(scores - new_peak[:, None]), 0.0)
    row_total = jnp.sum(weights_exp, axis=1)
    accum = jnp.dot(
        weights_exp.astype(jnp.bfloat16), piece[:, HD:], preferred_element_type=jnp.float32
    )
    state = (new_peak, row_total, accum)
    row_peak, row_total, accum = state
    attended = accum / row_total[:, None]
    log_total = row_peak + jnp.log(row_total)
    mixed = attended.reshape(own_rows, query_dim).astype(jnp.bfloat16)
    middle = inputs + jnp.dot(mixed, out_attn, preferred_element_type=jnp.float32)
    normed_two, norm_two_back = jax.vjp(rms_norm, middle, gain_mlp.astype(jnp.float32))
    normed_two = normed_two.astype(jnp.bfloat16)
    joined = jnp.dot(normed_two, in_mlp, preferred_element_type=jnp.float32)
    hidden, hidden_back = jax.vjp(geglu, joined)
    hidden = hidden.astype(jnp.bfloat16)
    result = middle + jnp.dot(hidden, out_mlp, preferred_element_type=jnp.float32)
    upstream = cotangent[0]
    grad_out_mlp = jnp.einsum("tf,td->fd", hidden, upstream, preferred_element_type=jnp.float32)
    grad_hidden = jnp.einsum("td,fd->tf", upstream, out_mlp, preferred_element_type=jnp.float32)
    grad_joined = hidden_back(grad_hidden)[0].astype(jnp.bfloat16)
    grad_in_mlp = jnp.einsum(
        "td,tf->df", normed_two, grad_joined, preferred_element_type=jnp.float32
    )
    grad_normed_two = jnp.einsum(
        "tf,df->td", grad_joined, in_mlp, preferred_element_type=jnp.float32
    )
    grad_middle_norm, grad_gain_mlp = norm_two_back(grad_normed_two)
    grad_middle = upstream.astype(jnp.float32) + grad_middle_norm
    grad_branch = grad_middle.astype(jnp.bfloat16)
    grad_out_attn = jnp.einsum("tc,td->cd", mixed, grad_branch, preferred_element_type=jnp.float32)
    grad_mixed = jnp.einsum(
        "td,cd->tc", grad_branch, out_attn, preferred_element_type=jnp.float32
    ).astype(jnp.bfloat16)
    grad_mixed = grad_mixed.reshape(own_rows * H, HD)
    row_delta = jnp.sum(grad_mixed.astype(jnp.float32) * attended, axis=1)
    piece = lax.all_gather(key_value, "ctx", axis=0, tiled=True)
    allowed_mask = allowed()
    key_part = piece[:, :HD]
    value_part = piece[:, HD:]
    scores = jnp.einsum("rd,kd->rk", queries, key_part, preferred_element_type=jnp.float32)
    probs_full = jnp.where(allowed_mask, jnp.exp(scores - log_total[:, None]), 0.0)
    grad_probs = jnp.einsum("rd,kd->rk", grad_mixed, value_part, preferred_element_type=jnp.float32)
    grad_scores = (probs_full * (grad_probs - row_delta[:, None])).astype(jnp.bfloat16)
    grad_query = jnp.dot(grad_scores, key_part, preferred_element_type=jnp.float32)
    grad_key_part = jnp.einsum(
        "rk,rd->kd", grad_scores, queries, preferred_element_type=jnp.float32
    )
    grad_value_part = jnp.einsum(
        "rk,rd->kd", probs_full.astype(jnp.bfloat16), grad_mixed, preferred_element_type=jnp.float32
    )
    grad_keys = jnp.concatenate([grad_key_part, grad_value_part], axis=1)
    grad_query, grad_keys = (grad_query, grad_keys)
    grad_kv = lax.psum_scatter(
        grad_keys.astype(jnp.bfloat16), "ctx", scatter_dimension=0, tiled=True
    ).astype(jnp.float32)
    grad_query_raw = query_back(grad_query.reshape(own_rows, H, HD))[0].reshape(own_rows, query_dim)
    grad_key_raw = key_back(grad_kv[:, :HD])[0]
    grad_projected = jnp.concatenate(
        [grad_query_raw, grad_key_raw, grad_kv[:, HD:]], axis=1
    ).astype(jnp.bfloat16)
    grad_in_attn = jnp.einsum(
        "td,tc->dc", normed_one, grad_projected, preferred_element_type=jnp.float32
    )
    grad_normed_one = jnp.einsum(
        "tc,dc->td", grad_projected, in_attn, preferred_element_type=jnp.float32
    )
    grad_inputs_norm, grad_gain_attn = norm_one_back(grad_normed_one)
    grad_inputs = grad_middle + grad_inputs_norm
    shards = (
        lax.psum_scatter(
            grad_gain_attn.astype(jnp.bfloat16), "fsdp", scatter_dimension=0, tiled=True
        ).astype(jnp.float32),
        lax.psum_scatter(
            grad_in_attn.astype(jnp.bfloat16), "fsdp", scatter_dimension=0, tiled=True
        ).astype(jnp.float32),
        lax.psum_scatter(
            grad_out_attn.astype(jnp.bfloat16), "fsdp", scatter_dimension=0, tiled=True
        ).astype(jnp.float32),
        lax.psum_scatter(
            grad_gain_mlp.astype(jnp.bfloat16), "fsdp", scatter_dimension=0, tiled=True
        ).astype(jnp.float32),
        lax.psum_scatter(
            grad_in_mlp.astype(jnp.bfloat16), "fsdp", scatter_dimension=0, tiled=True
        ).astype(jnp.float32),
        lax.psum_scatter(
            grad_out_mlp.astype(jnp.bfloat16), "fsdp", scatter_dimension=0, tiled=True
        ).astype(jnp.float32),
    )
    shards = (
        lax.psum(shards[0].astype(jnp.bfloat16), "ctx").astype(jnp.float32),
        lax.psum(shards[1].astype(jnp.bfloat16), "ctx").astype(jnp.float32),
        lax.psum(shards[2].astype(jnp.bfloat16), "ctx").astype(jnp.float32),
        lax.psum(shards[3].astype(jnp.bfloat16), "ctx").astype(jnp.float32),
        lax.psum(shards[4].astype(jnp.bfloat16), "ctx").astype(jnp.float32),
        lax.psum(shards[5].astype(jnp.bfloat16), "ctx").astype(jnp.float32),
    )
    return (
        result.astype(jnp.bfloat16)[None],
        grad_inputs[None],
        shards[0],
        shards[1],
        shards[2],
        shards[3],
        shards[4],
        shards[5],
    )


def solution(mesh):
    in_specs = (
        P("fsdp", "ctx", None),
        P("fsdp", None),
        P("fsdp", None),
        P("fsdp"),
        P("fsdp", None),
        P("fsdp", None),
        P("fsdp"),
        P("fsdp", None),
        P("fsdp", None),
        P("fsdp", "ctx", None),
    )
    out_specs = (
        P("fsdp", "ctx", None),
        P("fsdp", "ctx", None),
        P("fsdp"),
        P("fsdp", None),
        P("fsdp", None),
        P("fsdp"),
        P("fsdp", None),
        P("fsdp", None),
    )
    return jax.shard_map(
        per_device, mesh=mesh, in_specs=in_specs, out_specs=out_specs, check_vma=False
    )
```

profile of v0, /device:TPU:0, one launch (start us, length us, event | category | flops | bytes accessed | tf_op | source)
XLA Modules:
  0.0 2230.6 jit_solution(6796903217464657696)
XLA Ops:
  9.4 13.5 all-gather
  24.7 90.0 %all-gather.8.cloned.1.call-done = bf16[1536,1792]{1,0:T(8,128)(2,1)} async-done(((bf16[384,1792]{1,0:T(8,128)(2,1)}), bf16[1536,1792]{1,0:T(8,128)(2,1)}) %all-gather.8.cloned.1.call-update) | async-done | bytes 5505040 | tf_op jit(solution)/shard_map/all_gather | solution.py:71
  123.9 12.1 all-gather.1
  153.8 23.8 %select_reduce_fusion = (f32[4608]{0:T(1024)S(1)}, f32[4608,3072]{0,1:T(8,128)}) fusion(s32[3072]{0:T(1024)S(1)} %bitcast.64, s32[4608]{0:T(1024)S(1)} %sub.26, s32[3072]{0:T(1024)S(1)} %convert_reduce_fusion, s32[4608]{0:T(1024)S(1)} %eq.8, bf16[4608,128]{1,0:T(8,128)(2,1)S(1)} %fusion.33, bf16[3072,256]{1,0:T(8,128)(2,1)} %all-gather.10.cloned.1.call-done), kind=kOutput, calls=%fused_computation.5 | convolution fusion | flops 3737120256 | bytes 58669056 | tf_op jit(solution)/shard_map/rd,kd->rk/dot_general | solution.py:99
  178.2 29.7 %fusion.2 = f32[4608]{0:T(1024)S(1)} fusion(f32[4608,3072]{0,1:T(8,128)} %get-tuple-element.38, f32[4608]{0:T(1024)S(1)} %broadcast_maximum_fusion, s32[3072]{0:T(1024)S(1)} %bitcast.65, s32[4608]{0:T(1024)S(1)} %sub.26, s32[3072]{0:T(1024)S(1)} %convert_reduce_fusion, s32[4608]{0:T(1024)S(1)} %eq.8), kind=kLoop, calls=%fused_computation.8 | loop fusion | flops 127397376 | bytes 56721408 | tf_op jit(solution)/shard_map/reduce_sum | solution.py:102
  207.9 27.3 %fusion.77 = (bf16[4608,128]{0,1:T(8,128)(2,1)S(1)}, f32[4608,128]{0,1:T(8,128)}) fusion(f32[4608]{0:T(1024)S(1)} %fusion.2, bf16[3072,256]{1,0:T(8,128)(2,1)} %all-gather.10.cloned.1.call-done, f32[4608,3072]{0,1:T(8,128)} %get-tuple-element.38, f32[4608]{0:T(1024)S(1)} %broadcast_maximum_fusion, s32[3072]{0:T(1024)S(1)} %bitcast.66, s32[4608]{0:T(1024)S(1)} %sub.26, ...), kind=kOutput, calls=%fused_computation.127 | convolution fusion | flops 3752460288 | bytes 61046784 | tf_op jit(solution)/shard_map/dot_general | solution.py:103
  243.7 469.4 %all-gather.14.cloned.1.call-done = bf16[1536,9216]{1,0:T(8,128)(2,1)} async-done(((bf16[384,9216]{1,0:T(8,128)(2,1)}), bf16[1536,9216]{1,0:T(8,128)(2,1)}) %all-gather.14.cloned.1.call-update) | async-done | bytes 28311568 | tf_op jit(solution)/shard_map/all_gather | solution.py:74
  713.0 19.6 fusion.73
  732.6 224.0 %all-gather.16.cloned.1.call-done = bf16[4608,1536]{1,0:T(8,128)(2,1)} async-done(((bf16[1152,1536]{1,0:T(8,128)(2,1)}), bf16[4608,1536]{1,0:T(8,128)(2,1)}) %all-gather.16.cloned.1.call-update) | async-done | bytes 14155792 | tf_op jit(solution)/shard_map/all_gather | solution.py:75
  956.6 18.6 fusion.25
  975.2 24.1 %multiply_reduce_fusion = (bf16[1536]{0:T(1024)(128)(2,1)}, f32[384]{0:T(512)}, f32[384,1536]{1,0:T(8,128)}) fusion(f32[384,1536]{1,0:T(8,128)S(1)} %get-tuple-element.42, f32[384]{0:T(512)S(1)} %fusion.66, f32[1536]{0:T(1024)S(1)} %reshape.235, bf16[1536,9216]{1,0:T(8,128)(2,1)} %all-gather.14.cloned.1.call-done, f32[384,4608]{1,0:T(8,128)} %get-tuple-element.21, ...), kind=kOutput, calls=%fused_computation.55 | convolution fusion | flops 10882250752 | bytes 47198208 | tf_op jit(solution)/shard_map/tf,df->td/dot_general | solution.py:125
  1010.3 25.1 %fusion.18 = bf16[3072,128]{1,0:T(8,128)(2,1)} fusion(bf16[4608,128]{1,0:T(8,128)(2,1)S(1)} %reshape.226, f32[4608,3072]{0,1:T(8,128)} %get-tuple-element.38, f32[4608]{0:T(1024)S(1)} %copy-done.48, s32[3072]{0:T(1024)S(1)} %bitcast.67, s32[4608]{0:T(1024)S(1)} %copy-done.38, s32[4608]{0:T(1024)S(1)} %copy-done.36, s32[3072]{0:T(1024)S(1)} %copy-done.40), kind=kOutput, calls=%fused_computation.35 | convolution fusion | flops 3751673856 | bytes 58669056 | tf_op jit(solution)/shard_map/rk,rd->kd/dot_general | solution.py:149
  1035.7 35.8 %multiply_convert_fusion = bf16[4608,3072]{0,1:T(8,128)(2,1)} fusion(f32[4608,3072]{0,1:T(8,128)} %get-tuple-element.38, bf16[4608,128]{1,0:T(8,128)(2,1)S(1)} %reshape.226, f32[4608]{0:T(1024)S(1)} %multiply_reduce_fusion.1, f32[4608]{0:T(1024)S(1)} %copy-done.48, bf16[3072,256]{1,0:T(8,128)(2,1)} %all-gather.10.cloned.1.call-done, s32[3072]{0:T(1024)S(1)} %bitcast.68, ...), kind=kOutput, calls=%fused_computation.2 | convolution fusion | flops 3779592192 | bytes 86999040 | tf_op jit(solution)/shard_map/rd,kd->rk/dot_general | solution.py:143
  1071.4 12.8 convolution_convert_fusion.4
  1092.6 15.0 convolution_multiply_fusion
  1131.4 12.2 convolution_convert_fusion.1
  1145.3 24.1 %convolution_convert_fusion = bf16[1536,9216]{1,0:T(8,128)(2,1)} fusion(f32[384,4608]{1,0:T(8,128)} %get-tuple-element.21, f32[384,4608]{1,0:T(8,128)} %get-tuple-element.20, f32[384,1536]{1,0:T(8,128)S(1)} %copy-done.2, f32[1536]{0:T(1024)S(1)} %copy-done.24, f32[384]{0:T(512)S(1)} %copy-done.26), kind=kOutput, calls=%fused_computation.11 | convolution fusion | flops 10894639104 | bytes 44834304 | tf_op jit(solution)/shard_map/td,tf->df/dot_general | solution.py:122
  1169.4 40.6 %reduce-scatter.10.cloned.1.call-done = bf16[384,1536]{1,0:T(8,128)(2,1)} async-done(((bf16[1536,1536]{1,0:T(8,128)(2,1)}), bf16[384,1536]{1,0:T(8,128)(2,1)}) %reduce-scatter.10.cloned.1.call-update) | async-done | bytes 1179664 | tf_op jit(solution)/shard_map/reduce_scatter | solution.py:177
  1210.0 100.9 %reduce-scatter.8.cloned.1.call-done = bf16[384,1792]{1,0:T(8,128)(2,1)} async-done(((bf16[1536,1792]{1,0:T(8,128)(2,1)}), bf16[384,1792]{1,0:T(8,128)(2,1)}) %reduce-scatter.8.cloned.1.call-update) | async-done | bytes 1376272 | tf_op jit(solution)/shard_map/reduce_scatter | solution.py:174
  1310.9 240.7 %reduce-scatter.14.cloned.1.call-done = bf16[1152,1536]{1,0:T(8,128)(2,1)} async-done(((bf16[4608,1536]{1,0:T(8,128)(2,1)}), bf16[1152,1536]{1,0:T(8,128)(2,1)}) %reduce-scatter.14.cloned.1.call-update) | async-done | bytes 3538960 | tf_op jit(solution)/shard_map/reduce_scatter | solution.py:186
  1551.6 468.1 %reduce-scatter.12.cloned.1.call-done = bf16[384,9216]{1,0:T(8,128)(2,1)} async-done(((bf16[1536,9216]{1,0:T(8,128)(2,1)}), bf16[384,9216]{1,0:T(8,128)(2,1)}) %reduce-scatter.12.cloned.1.call-update) | async-done | bytes 7077904 | tf_op jit(solution)/shard_map/reduce_scatter | solution.py:183
  2039.9 13.3 all-reduce.10
  2055.8 13.0 all-reduce.8
  2075.7 131.2 %all-reduce.13.cloned.1.call-done = (bf16[384,1792]{1,0:T(8,128)(2,1)}, bf16[384,1536]{1,0:T(8,128)(2,1)}, bf16[384,9216]{1,0:T(8,128)(2,1)}, bf16[1152,1536]{1,0:T(8,128)(2,1)}) async-done(((bf16[384,1792]{1,0:T(8,128)(2,1)}, bf16[384,1536]{1,0:T(8,128)(2,1)}, bf16[384,9216]{1,0:T(8,128)(2,1)}, bf16[1152,1536]{1,0:T(8,128)(2,1)}), (bf16[384,1792]{1,0:T(8,128)(2,1)}, bf16[384,1536]{1,0:T(8,128)(2,1)}, ...) | async-done | bytes 13172752 | tf_op jit(solution)/shard_map/psum | solution.py:192
  (220 shorter events, 130.4 us)
Async XLA Ops:
  7.2 107.5 %all-gather.8.cloned.1.call-start = ((), (), s32[]{:S(2)}) async-start(), calls=%async_computation.5 | async-start | bytes 6881280 | tf_op jit(solution)/shard_map/all_gather | solution.py:71
  7.9 145.9 %all-gather.10.cloned.1.call-start = ((), (), s32[]{:S(2)}) async-start(), calls=%async_computation.6 | async-start | bytes 1769472 | tf_op jit(solution)/shard_map/all_gather | solution.py:96
  9.3 127.5 %copy-start.43 = (f32[384]{0:T(512)}, f32[384]{0:T(512)S(1)}, u32[]{:S(2)}) copy-start(f32[384]{0:T(512)S(1)} %convert_element_type.129) | copy-start | bytes 4612
  22.9 97.0 %copy-start.45 = (f32[1536]{0:T(1024)}, f32[1536]{0:T(1024)S(1)}, u32[]{:S(2)}) copy-start(f32[1536]{0:T(1024)S(1)} %reshape.234) | copy-start | bytes 18436
  23.0 113.9 %copy-start.53 = (f32[64]{0:T(128)}, f32[64]{0:T(128)S(1)}, u32[]{:S(2)}) copy-start(f32[64]{0:T(128)S(1)} %multiply_power_fusion) | copy-start | bytes 772
  24.6 95.3 %copy-start.49 = (f32[384]{0:T(512)}, f32[384]{0:T(512)S(1)}, u32[]{:S(2)}) copy-start(f32[384]{0:T(512)S(1)} %fusion.31) | copy-start | bytes 4612
  24.7 95.3 %copy-start.51 = (f32[384]{0:T(512)}, f32[384]{0:T(512)S(1)}, u32[]{:S(2)}) copy-start(f32[384]{0:T(512)S(1)} %fusion.65) | copy-start | bytes 4612
  121.7 116.4 %all-gather.12.cloned.1.call-start = ((), (), s32[]{:S(2)}) async-start(), calls=%async_computation.7 | async-start | bytes 5898240 | tf_op jit(solution)/shard_map/all_gather | solution.py:72
  122.5 590.6 %all-gather.14.cloned.1.call-start = ((), (), s32[]{:S(2)}) async-start(), calls=%async_computation.8 | async-start | bytes 35389440 | tf_op jit(solution)/shard_map/all_gather | solution.py:74
  123.1 833.5 %all-gather.16.cloned.1.call-start = ((), (), s32[]{:S(2)}) async-start(), calls=%async_computation.9 | async-start | bytes 17694720 | tf_op jit(solution)/shard_map/all_gather | solution.py:75
  123.7 998.8 %reduce-scatter.6.cloned.1.call-start = ((), (), s32[]{:S(2)}) async-start(), calls=%async_computation.10 | async-start | bytes 1769472 | tf_op jit(solution)/shard_map/reduce_scatter | solution.py:154
  136.1 863.9 %copy-start.23 = (f32[1536]{0:T(1024)}, f32[1536]{0:T(1024)S(1)}, u32[]{:S(2)}) copy-start(f32[1536]{0:T(1024)S(1)} %reshape.235) | copy-start | bytes 18436
  136.2 71.7 %copy-start.39 = (s32[3072]{0:T(1024)}, s32[3072]{0:T(1024)S(1)}, u32[]{:S(2)}) copy-start(s32[3072]{0:T(1024)S(1)} %convert_reduce_fusion) | copy-start | bytes 36868
  136.6 71.3 %copy-start.35 = (s32[4608]{0:T(1024)}, s32[4608]{0:T(1024)S(1)}, u32[]{:S(2)}) copy-start(s32[4608]{0:T(1024)S(1)} %eq.8) | copy-start | bytes 55300
  136.9 71.0 %copy-start.37 = (s32[4608]{0:T(1024)}, s32[4608]{0:T(1024)S(1)}, u32[]{:S(2)}) copy-start(s32[4608]{0:T(1024)S(1)} %sub.26) | copy-start | bytes 55300
  242.9 757.1 %copy-start.1 = (f32[384,1536]{1,0:T(8,128)}, f32[384,1536]{1,0:T(8,128)S(1)}, u32[]{:S(2)}) copy-start(f32[384,1536]{1,0:T(8,128)S(1)} %get-tuple-element.42) | copy-start | bytes 7077892
  242.9 757.1 %copy-start.25 = (f32[384]{0:T(512)}, f32[384]{0:T(512)S(1)}, u32[]{:S(2)}) copy-start(f32[384]{0:T(512)S(1)} %fusion.66) | copy-start | bytes 4612
  713.0 243.6 %copy-start.10 = (bf16[1,384,1536]{2,1,0:T(8,128)(2,1)S(1)}, bf16[1,384,1536]{2,1,0:T(8,128)(2,1)}, u32[]{:S(2)}) copy-start(bf16[1,384,1536]{2,1,0:T(8,128)(2,1)} %param.19) | copy-start | bytes 3538948
  1085.6 124.4 %reduce-scatter.10.cloned.1.call-start = ((), (), s32[]{:S(2)}) async-start(), calls=%async_computation.12 | async-start | bytes 5898240 | tf_op jit(solution)/shard_map/reduce_scatter | solution.py:177
  1091.2 219.7 %reduce-scatter.8.cloned.1.call-start = ((), (), s32[]{:S(2)}) async-start(), calls=%async_computation.11 | async-start | bytes 6881280 | tf_op jit(solution)/shard_map/reduce_scatter | solution.py:174
  1129.8 421.8 %reduce-scatter.14.cloned.1.call-start = ((), (), s32[]{:S(2)}) async-start(), calls=%async_computation.14 | async-start | bytes 17694720 | tf_op jit(solution)/shard_map/reduce_scatter | solution.py:186
  1143.6 876.0 %reduce-scatter.12.cloned.1.call-start = ((), (), s32[]{:S(2)}) async-start(), calls=%async_computation.13 | async-start | bytes 35389440 | tf_op jit(solution)/shard_map/reduce_scatter | solution.py:183
  1169.4 1037.5 %all-reduce.13.cloned.1.call-start = ((), (), s32[]{:S(2)}) async-start(), calls=%async_computation.15 | async-start | bytes 26345472 | tf_op jit(solution)/shard_map/psum | solution.py:192
  2032.3 39.7 %copy-start.5 = (f32[384,1536]{1,0:T(8,128)S(1)}, f32[384,1536]{1,0:T(8,128)}, u32[]{:S(2)}) copy-start(f32[384,1536]{1,0:T(8,128)} %copy-done.3) | copy-start | bytes 7077892
  (48 other events, 327.6 us)
Sparse Core Ops, SparseCore 0:
  9.6 105.0 all-gather.7
  121.8 24.0 all-gather.9
  147.5 89.4 all-gather.11
  238.4 474.5 all-gather.13
  714.4 242.0 all-gather.15
  1085.7 36.6 reduce-scatter.5
  1124.7 85.2 reduce-scatter.9
  1212.3 98.5 reduce-scatter.7
  1313.8 237.7 reduce-scatter.13
  1553.8 465.8 reduce-scatter.11
  2024.3 182.5 all-reduce.12
where the time goes:
time: 2230 us
  waiting for transfers between devices  1770 us (79%)
  matrix products  280 us (13%)
  other arithmetic  70.6 us (3%)
  blocking collectives  51.9 us (2%)
  local copies, waits for them, and re-layouts  43 us (2%)
    all_gather x1, waiting for transfers between devices, per_device(): lax.all_gather(w_mlp_in, 'fsdp', axis=0, tiled=True)  469 us
    reduce_scatter x1, waiting for transfers between devices, per_device(): lax.psum_scatter(grad_in_mlp.astype(jnp.bfloat16), 'fsdp', scatter_dimens...  468 us
    reduce_scatter x1, waiting for transfers between devices, per_device(): lax.psum_scatter(grad_out_mlp.astype(jnp.bfloat16), 'fsdp', scatter_dimen...  241 us
    all_gather x1, waiting for transfers between devices, per_device(): lax.all_gather(w_mlp_out, 'fsdp', axis=0, tiled=True)  224 us
    psum x1, waiting for transfers between devices, per_device(): lax.psum(shards[1].astype(jnp.bfloat16), 'ctx').astype(jnp.float32)  131 us
    reduce_scatter x1, waiting for transfers between devices, per_device(): lax.psum_scatter(grad_in_attn.astype(jnp.bfloat16), 'fsdp', scatter_dimen...  101 us
    all_gather x1, waiting for transfers between devices, per_device(): lax.all_gather(w_attn_in, 'fsdp', axis=0, tiled=True)  90 us
  transfers between devices with their start and end apart: 11, of which 9 were waited for; matrix products, arithmetic and copies ran while one was open for 11% of the time, Pallas kernels for 0%

commit v1 on v0

v1 whole, which is shorter than its diff:
```python
import jax
import jax.numpy as jnp
from jax import lax
from jax.sharding import PartitionSpec as P

H = 12
HD = 128
FF = 4608
WINDOW = 1024
LANES = 128


EPS = 1e-06


def rms_norm(values, gain):
    return values * lax.rsqrt(jnp.mean(values * values, axis=-1, keepdims=True) + EPS) * gain


def rotate(values, places):
    half_dim = values.shape[-1] // 2
    frequency = 10000.0 ** (-jnp.arange(half_dim, dtype=jnp.float32) / half_dim)
    angles = places[:, None] * frequency[None, :]
    cosine = jnp.cos(angles)[:, None, :]
    sine_part = jnp.sin(angles)[:, None, :]
    first_half = values[..., :half_dim]
    second_half = values[..., half_dim:]
    return jnp.concatenate(
        [
            first_half * cosine - second_half * sine_part,
            second_half * cosine + first_half * sine_part,
        ],
        axis=-1,
    )


def geglu(gate, up):
    return jax.nn.gelu(gate, approximate=True) * up


def dot(left, right):
    return jnp.dot(left, right, preferred_element_type=jnp.float32)


def dot_nt(left, right):
    return jnp.einsum("ab,cb->ac", left, right, preferred_element_type=jnp.float32)


def dot_tn(left, right):
    return jnp.einsum("ab,ac->bc", left, right, preferred_element_type=jnp.float32)


def low(values):
    return values.astype(jnp.bfloat16)


class Layout:
    def __init__(self, ctx_size, fsdp_size):
        self.ctx_size = ctx_size
        self.shards = fsdp_size
        self.chips = ctx_size // 2
        self.index = lax.axis_index("ctx")
        self.chip = self.index // 2
        self.core = self.index % 2
        units = FF // (self.shards * self.chips)
        self.main = units // LANES * LANES
        self.rest = units - self.main
        self.per_shard = FF // self.shards
        self.rest_start = self.chips * self.main

    def xor(self, values, mask):
        pairs = [(i, i ^ mask) for i in range(self.ctx_size)]
        return lax.ppermute(values, "ctx", pairs)

    def same_core_groups(self):
        return [[chip * 2 + core for chip in range(self.chips)] for core in range(2)]

    def gather_chips(self, values):
        if self.chips != 4:
            return lax.all_gather(
                values, "ctx", axis=0, tiled=True, axis_index_groups=self.same_core_groups()
            )
        half = values.shape[1] // 2
        from_x = self.xor(values, 2)
        from_y = self.xor(values, 4)
        corner_left = self.xor(from_x[:, :half], 4)
        corner_right = self.xor(from_y[:, half:], 2)
        corner = jnp.concatenate([corner_left, corner_right], axis=1)
        return jnp.concatenate([values, from_x, from_y, corner], axis=0)

    def scatter_chips(self, partial):
        if self.chips != 4:
            return lax.psum_scatter(
                low(partial),
                "ctx",
                scatter_dimension=0,
                tiled=True,
                axis_index_groups=self.same_core_groups(),
            ).astype(jnp.float32)
        own, to_x, to_y, corner = jnp.split(partial, 4, axis=0)
        half = own.shape[1] // 2
        corner = low(corner)
        left = self.xor(corner[:, :half], 2).astype(jnp.float32)
        right = self.xor(corner[:, half:], 4).astype(jnp.float32)
        to_y = jnp.concatenate([to_y[:, :half] + left, to_y[:, half:]], axis=1)
        to_x = jnp.concatenate([to_x[:, :half], to_x[:, half:] + right], axis=1)
        from_y = self.xor(low(to_y), 4).astype(jnp.float32)
        from_x = self.xor(low(to_x), 2).astype(jnp.float32)
        return own + from_y + from_x

    def columns_of_chip(self, weights, start):
        parts = []
        if self.main:
            for shard in range(self.shards):
                at = start + shard * self.per_shard + self.chip * self.main
                parts.append(lax.dynamic_slice_in_dim(weights, at, self.main, 1))
        if self.rest:
            for shard in range(self.shards):
                at = start + shard * self.per_shard + self.rest_start + self.chip * self.rest
                parts.append(lax.dynamic_slice_in_dim(weights, at, self.rest, 1))
        return jnp.concatenate(parts, axis=1)

    def rows_of_chip(self, weights):
        parts = []
        if self.main:
            parts.append(lax.dynamic_slice_in_dim(weights, self.chip * self.main, self.main, 0))
        if self.rest:
            at = self.rest_start + self.chip * self.rest
            parts.append(lax.dynamic_slice_in_dim(weights, at, self.rest, 0))
        return jnp.concatenate(parts, axis=0)

    def by_core(self, mine, other):
        first = jnp.where(self.core == 0, mine, other)
        second = jnp.where(self.core == 0, other, mine)
        return first, second

    def gather_mlp_in(self, shard):
        mine = self.columns_of_chip(shard, self.core * FF)
        mine = lax.all_gather(mine, "fsdp", axis=0, tiled=True)
        return self.by_core(mine, self.xor(mine, 1))

    def gather_mlp_out(self, shard):
        width = shard.shape[1]
        half = lax.dynamic_slice_in_dim(shard, self.core * (width // 2), width // 2, 1)
        mine = lax.all_gather(self.rows_of_chip(half), "fsdp", axis=0)
        mine = jnp.concatenate(
            [
                mine[:, : self.main].reshape(self.shards * self.main, width // 2),
                mine[:, self.main :].reshape(self.shards * self.rest, width // 2),
            ],
            axis=0,
        )
        return jnp.concatenate(self.by_core(mine, self.xor(mine, 1)), axis=1)

    def sum_pair(self, first, second):
        keep = jnp.where(self.core == 0, first, second)
        send = jnp.where(self.core == 0, second, first)
        return keep + self.xor(low(send), 1).astype(jnp.float32)

    def reduce_mlp_in(self, gate, up):
        total = low(self.sum_pair(gate, up))
        total = lax.psum_scatter(total, "fsdp", scatter_dimension=0, tiled=True)
        rows = total.shape[0]
        every = lax.all_gather(total, "ctx", axis=0)
        every = every.reshape(self.chips, 2, rows, total.shape[1])
        split = self.shards * self.main
        main = every[..., :split].reshape(self.chips, 2, rows, self.shards, self.main)
        rest = every[..., split:].reshape(self.chips, 2, rows, self.shards, self.rest)
        main = main.transpose(2, 1, 3, 0, 4).reshape(rows, 2, self.shards, -1)
        rest = rest.transpose(2, 1, 3, 0, 4).reshape(rows, 2, self.shards, -1)
        return jnp.concatenate([main, rest], axis=3).reshape(rows, 2 * FF).astype(jnp.float32)

    def reduce_mlp_out(self, grad):
        width = grad.shape[1]
        total = low(self.sum_pair(grad[:, : width // 2], grad[:, width // 2 :]))
        split = self.shards * self.main
        main = total[:split].reshape(self.shards, self.main, width // 2)
        rest = total[split:].reshape(self.shards, self.rest, width // 2)
        total = jnp.concatenate([main, rest], axis=1)
        total = lax.psum_scatter(total, "fsdp", scatter_dimension=0, tiled=True)[0]
        every = lax.all_gather(total, "ctx", axis=0)
        every = every.reshape(self.chips, 2, self.main + self.rest, width // 2)
        main = every[:, :, : self.main].transpose(0, 2, 1, 3).reshape(-1, width)
        rest = every[:, :, self.main :].transpose(0, 2, 1, 3).reshape(-1, width)
        return jnp.concatenate([main, rest], axis=0).astype(jnp.float32)

    def gather_whole(self, shard):
        rows = shard.shape[0] // self.ctx_size
        piece = lax.dynamic_slice_in_dim(shard, self.index * rows, rows, 0)
        piece = lax.all_gather(piece, "fsdp", axis=0)
        piece = lax.all_gather(piece, "ctx", axis=1, tiled=True)
        return piece.reshape(-1, shard.shape[1])

    def reduce_whole(self, grad):
        rows = grad.shape[0] // self.shards
        total = low(grad).reshape(self.shards, rows, grad.shape[1])
        total = lax.psum_scatter(total, "ctx", scatter_dimension=1, tiled=True)
        total = lax.psum_scatter(total, "fsdp", scatter_dimension=0, tiled=True)[0]
        return lax.all_gather(total, "ctx", axis=0, tiled=True).astype(jnp.float32)

    def reduce_gain(self, grad):
        total = jnp.sum(lax.all_gather(grad, ("ctx", "fsdp"), axis=0), axis=0)
        rows = grad.shape[0] // self.shards
        return lax.dynamic_slice_in_dim(total, lax.axis_index("fsdp") * rows, rows)


def attend(queries, key_value, row_places, row_segment, places_all, segment_all):
    distance = row_places[:, None] - places_all[None, :]
    allowed = (row_segment[:, None] == segment_all[None, :]) & (distance >= 0) & (distance < WINDOW)
    scores = dot_nt(queries, key_value[:, :HD])
    peak = jnp.max(jnp.where(allowed, scores, -1e30), axis=1)
    weights_exp = jnp.where(allowed, jnp.exp(scores - peak[:, None]), 0.0)
    row_total = jnp.sum(weights_exp, axis=1)
    attended = dot(low(weights_exp), key_value[:, HD:]) / row_total[:, None]
    return attended, peak + jnp.log(row_total)


def attend_back(
    queries, key_value, grad_mixed, row_delta, log_total, row_places, row_segment, places_all, segment_all
):
    distance = row_places[:, None] - places_all[None, :]
    allowed = (row_segment[:, None] == segment_all[None, :]) & (distance >= 0) & (distance < WINDOW)
    key_part = key_value[:, :HD]
    scores = dot_nt(queries, key_part)
    probs = jnp.where(allowed, jnp.exp(scores - log_total[:, None]), 0.0)
    grad_probs = dot_nt(grad_mixed, key_value[:, HD:])
    grad_scores = low(probs * (grad_probs - row_delta[:, None]))
    grad_query = dot(grad_scores, key_part)
    grad_key = dot_tn(grad_scores, queries)
    grad_value = dot_tn(low(probs), grad_mixed)
    return grad_query, jnp.concatenate([grad_key, grad_value], axis=1)


def per_device(
    ctx_size,
    fsdp_size,
    tokens,
    order,
    lengths,
    norm_attn,
    w_attn_in,
    w_attn_out,
    norm_mlp,
    w_mlp_in,
    w_mlp_out,
    cotangent,
):
    lay = Layout(ctx_size, fsdp_size)
    own_rows = tokens.shape[1]
    query_dim = H * HD
    places_all = order[0]
    seq_ends = jnp.cumsum(lengths[0])
    segment_all = jnp.sum((seq_ends[None, :] <= places_all[:, None]).astype(jnp.int32), axis=1)
    own_places = lax.dynamic_slice_in_dim(places_all, lay.index * own_rows, own_rows)
    own_segment = lax.dynamic_slice_in_dim(segment_all, lay.index * own_rows, own_rows)
    row_places = jnp.repeat(own_places, H)
    row_segment = jnp.repeat(own_segment, H)

    in_attn = lay.gather_whole(w_attn_in)
    out_attn = lay.gather_whole(w_attn_out)
    gains = lax.all_gather(jnp.stack([norm_attn, norm_mlp]), "fsdp", axis=1, tiled=True)
    gain_attn = gains[0].astype(jnp.float32)
    gain_mlp = gains[1].astype(jnp.float32)
    gate_in, up_in = lay.gather_mlp_in(w_mlp_in)
    out_mlp = lay.gather_mlp_out(w_mlp_out)
    upstream = cotangent[0]
    upstream_all = lay.gather_chips(upstream)

    inputs = tokens[0].astype(jnp.float32)
    normed_one, norm_one_back = jax.vjp(rms_norm, inputs, gain_attn)
    normed_one = low(normed_one)
    projected = dot(normed_one, in_attn)
    place_float = own_places.astype(jnp.float32)

    def query_map(part):
        return rotate(part, place_float) * HD ** (-0.5)

    def key_map(part):
        return rotate(part[:, None, :], place_float)[:, 0, :]

    query_rot, query_back = jax.vjp(query_map, projected[:, :query_dim].reshape(own_rows, H, HD))
    key_rot, key_back = jax.vjp(key_map, projected[:, query_dim : query_dim + HD])
    queries = low(query_rot).reshape(own_rows * H, HD)
    key_value = jnp.concatenate([low(key_rot), low(projected[:, query_dim + HD :])], axis=1)
    key_value = lax.all_gather(key_value, "ctx", axis=0, tiled=True)
    attended, log_total = attend(
        queries, key_value, row_places, row_segment, places_all, segment_all
    )
    mixed = low(attended.reshape(own_rows, query_dim))
    middle = inputs + dot(mixed, out_attn)
    normed_two, norm_two_back = jax.vjp(rms_norm, middle, gain_mlp)
    normed_all = lay.gather_chips(low(normed_two))

    gate = dot(normed_all, gate_in)
    up = dot(normed_all, up_in)
    hidden, hidden_back = jax.vjp(geglu, gate, up)
    hidden = low(hidden)
    grad_hidden = dot_nt(upstream_all, out_mlp)
    grad_gate, grad_up = hidden_back(grad_hidden)
    grad_gate = low(grad_gate)
    grad_up = low(grad_up)
    grad_normed_two = lay.scatter_chips(dot_nt(grad_gate, gate_in) + dot_nt(grad_up, up_in))
    result = middle + lay.scatter_chips(dot(hidden, out_mlp))
    grad_out_mlp = lay.reduce_mlp_out(dot_tn(hidden, upstream_all))
    grad_in_mlp = lay.reduce_mlp_in(dot_tn(normed_all, grad_gate), dot_tn(normed_all, grad_up))

    grad_middle_norm, grad_gain_mlp = norm_two_back(grad_normed_two)
    grad_middle = upstream.astype(jnp.float32) + grad_middle_norm
    grad_branch = low(grad_middle)
    grad_out_attn = lay.reduce_whole(dot_tn(mixed, grad_branch))
    grad_mixed = low(dot_nt(grad_branch, out_attn)).reshape(own_rows * H, HD)
    row_delta = jnp.sum(grad_mixed.astype(jnp.float32) * attended, axis=1)
    grad_query, grad_keys = attend_back(
        queries,
        key_value,
        grad_mixed,
        row_delta,
        log_total,
        row_places,
        row_segment,
        places_all,
        segment_all,
    )
    grad_kv = lax.psum_scatter(low(grad_keys), "ctx", scatter_dimension=0, tiled=True)
    grad_kv = grad_kv.astype(jnp.float32)
    grad_query_raw = query_back(grad_query.reshape(own_rows, H, HD))[0].reshape(own_rows, query_dim)
    grad_key_raw = key_back(grad_kv[:, :HD])[0]
    grad_projected = low(
        jnp.concatenate([grad_query_raw, grad_key_raw, grad_kv[:, HD:]], axis=1)
    )
    grad_in_attn = lay.reduce_whole(dot_tn(normed_one, grad_projected))
    grad_inputs_norm, grad_gain_attn = norm_one_back(dot_nt(grad_projected, in_attn))
    grad_inputs = grad_middle + grad_inputs_norm
    return (
        low(result)[None],
        grad_inputs[None],
        lay.reduce_gain(grad_gain_attn),
        grad_in_attn,
        grad_out_attn,
        lay.reduce_gain(grad_gain_mlp),
        grad_in_mlp,
        grad_out_mlp,
    )


def solution(mesh):
    in_specs = (
        P("fsdp", "ctx", None),
        P("fsdp", None),
        P("fsdp", None),
        P("fsdp"),
        P("fsdp", None),
        P("fsdp", None),
        P("fsdp"),
        P("fsdp", None),
        P("fsdp", None),
        P("fsdp", "ctx", None),
    )
    out_specs = (
        P("fsdp", "ctx", None),
        P("fsdp", "ctx", None),
        P("fsdp"),
        P("fsdp", None),
        P("fsdp", None),
        P("fsdp"),
        P("fsdp", None),
        P("fsdp", None),
    )

    def run(*arrays):
        return per_device(mesh.shape["ctx"], mesh.shape["fsdp"], *arrays)

    return jax.shard_map(run, mesh=mesh, in_specs=in_specs, out_specs=out_specs, check_vma=False)
```

time: 2230 us -> 1170 us (0.52)
  waiting for transfers between devices: 1770 us -> 390 us
  blocking collectives: 51.9 us -> 192 us
  local copies, waits for them, and re-layouts: 43 us -> 142 us
  matrix products: 280 us -> 315 us
    all_gather x5 -> x9, waiting for transfers between devices: 783 us -> 105 us  [the longest x1 67.3 us: gather_mlp_in(): mine = lax.all_gather(mine, 'fsdp', axis=0, tiled=True)]
    reduce_scatter x5 -> x7, waiting for transfers between devices: 851 us -> 199 us  [the longest x1 67.4 us: reduce_mlp_in(): total = lax.psum_scatter(total, 'fsdp', scatter_dimension=0, tiled=True)]
    all_gather x2 -> x5, blocking collectives: 25.7 us -> 192 us  [the longest x2 135 us: reduce_gain(): total = jnp.sum(lax.all_gather(grad, ('ctx', 'fsdp'), axis=0), axis=0)]
    psum x1 -> x0, waiting for transfers between devices: 131 us -> none  [per_device(): lax.psum(shards[1].astype(jnp.bfloat16), 'ctx').astype(jnp.float32)]
    ppermute x0 -> x20, waiting for transfers between devices: none -> 85.4 us  [xor(): return lax.ppermute(values, 'ctx', pairs)]
    dot_general x18 -> x21, matrix products: 280 us -> 315 us  [the longest x7 105 us: dot(): return jnp.dot(left, right, preferred_element_type=jnp.float32)]
    reshape x2 -> x5, local copies, waits for them, and re-layouts: 2.02 us -> 24.4 us  [the longest x1 11.2 us: reduce_mlp_in(): every[..., :split].reshape(self.chips, 2, rows, self.shards, self.main)]
  transfers between devices with their start and end apart: 11 -> 36, of which waited for: 9 -> 18; matrix products, arithmetic and copies ran while one was open for 11% -> 27% of each run, Pallas kernels for 0% -> 0%
where the time goes in v1:
time: 1170 us; the launch traced here: 1160 us
  waiting for transfers between devices  390 us (33%)
  matrix products  315 us (27%)
  blocking collectives  192 us (16%)
  local copies, waits for them, and re-layouts  142 us (12%)
  other arithmetic  87.1 us (7%)
  starting transfers between devices  19.6 us (2%)
  between operations  15.3 us (1%)
    all_gather x2, blocking collectives, reduce_gain(): total = jnp.sum(lax.all_gather(grad, ('ctx', 'fsdp'), axis=0), axis=0)  135 us
    dot_general x7, matrix products, dot(): return jnp.dot(left, right, preferred_element_type=jnp.float32)  105 us
    dot_general x7, matrix products, dot_tn(): jnp.einsum('ab,ac->bc', left, right, preferred_element_type=jnp.float32)  105 us
    dot_general x7, matrix products, dot_nt(): jnp.einsum('ab,cb->ac', left, right, preferred_element_type=jnp.float32)  105 us
    ppermute x20, waiting for transfers between devices, xor(): return lax.ppermute(values, 'ctx', pairs)  85.4 us
    reduce_scatter x1, waiting for transfers between devices, reduce_mlp_in(): total = lax.psum_scatter(total, 'fsdp', scatter_dimension=0, tiled=True)  67.4 us
    all_gather x1, waiting for transfers between devices, gather_mlp_in(): mine = lax.all_gather(mine, 'fsdp', axis=0, tiled=True)  67.3 us
    reduce_scatter x2, waiting for transfers between devices, reduce_whole(): total = lax.psum_scatter(total, 'ctx', scatter_dimension=1, tiled=True)  50.6 us
  transfers between devices with their start and end apart: 36, of which 18 were waited for; matrix products, arithmetic and copies ran while one was open for 27% of the time, Pallas kernels for 0%

profile of v1, /device:TPU:0, one launch (start us, length us, event | category | flops | bytes accessed | tf_op | source)
XLA Modules:
  0.0 1160.3 jit_solution(346625470529526843)
XLA Ops:
  8.5 20.2 %all-gather = bf16[192,1792]{1,0:T(8,128)(2,1)} all-gather(bf16[48,1792]{1,0:T(8,128)(2,1)S(1)} %constant_dynamic-slice_fusion.9), channel_id=2, replica_groups=mesh['ctx'=8,'fsdp'=4] {'fsdp'}, dimensions={0}, use_global_device_ids=true | all-gather | bytes 860160 | tf_op jit(solution)/shard_map/all_gather | solution.py:190
  48.2 23.5 %all-gather.20.cloned.1.call-done = bf16[4,384,1792]{2,1,0:T(8,128)(2,1)} async-done(((bf16[4,48,1792]{2,1,0:T(8,128)(2,1)}), bf16[4,384,1792]{2,1,0:T(8,128)(2,1)}) %all-gather.20.cloned.1.call-update) | async-done | bytes 5505040 | tf_op jit(solution)/shard_map/all_gather | solution.py:191
  83.0 24.5 %all-gather.1 = bf16[192,1536]{1,0:T(8,128)(2,1)} all-gather(bf16[48,1536]{1,0:T(8,128)(2,1)S(1)} %constant_dynamic-slice_fusion.8), channel_id=3, replica_groups=mesh['ctx'=8,'fsdp'=4] {'fsdp'}, dimensions={0}, use_global_device_ids=true | all-gather | bytes 737280 | tf_op jit(solution)/shard_map/all_gather | solution.py:190
  127.5 67.3 %all-gather.26.cloned.1.call-done = bf16[1536,1152]{1,0:T(8,128)(2,1)} async-done(((bf16[384,1152]{1,0:T(8,128)(2,1)}), bf16[1536,1152]{1,0:T(8,128)(2,1)}) %all-gather.26.cloned.1.call-update) | async-done | bytes 3538960 | tf_op jit(solution)/shard_map/all_gather | solution.py:139
  223.1 24.9 %select_reduce_fusion = (f32[4608]{0:T(1024)S(1)}, f32[4608,3072]{0,1:T(8,128)}) fusion(s32[3072]{0:T(1024)S(1)} %bitcast.138, s32[4608]{0:T(1024)S(1)} %sub.30, s32[3072]{0:T(1024)S(1)} %convert_reduce_fusion, s32[4608]{0:T(1024)S(1)} %eq.12, bf16[4608,128]{1,0:T(8,128)(2,1)} %fusion.41, bf16[3072,256]{1,0:T(8,128)(2,1)} %all-gather.22.cloned.1.call-done), kind=kOutput, calls=%fused_computation.5 | convolution fusion | flops 3737120256 | bytes 58669056 | tf_op jit(solution)/shard_map/ab,cb->ac/dot_general | solution.py:46
  248.0 29.7 %fusion.2 = f32[4608]{0:T(1024)S(1)} fusion(f32[4608,3072]{0,1:T(8,128)} %get-tuple-element.56, f32[4608]{0:T(1024)S(1)} %get-tuple-element.55, s32[3072]{0:T(1024)S(1)} %bitcast.139, s32[4608]{0:T(1024)S(1)} %sub.30, s32[3072]{0:T(1024)S(1)} %convert_reduce_fusion, s32[4608]{0:T(1024)S(1)} %eq.12), kind=kLoop, calls=%fused_computation.8 | loop fusion | flops 127397376 | bytes 56721408 | tf_op jit(solution)/shard_map/reduce_sum | solution.py:213
  277.7 27.3 %fusion.103 = (bf16[4608,128]{0,1:T(8,128)(2,1)}, f32[4608,128]{0,1:T(8,128)}) fusion(f32[4608]{0:T(1024)S(1)} %fusion.2, bf16[3072,256]{1,0:T(8,128)(2,1)} %all-gather.22.cloned.1.call-done, f32[4608,3072]{0,1:T(8,128)} %get-tuple-element.56, f32[4608]{0:T(1024)S(1)} %get-tuple-element.55, s32[3072]{0:T(1024)S(1)} %bitcast.140, s32[4608]{0:T(1024)S(1)} %sub.30, ...), kind=kOutput, calls=%fused_computation.189 | convolution fusion | flops 3752460288 | bytes 61046784 | tf_op jit(solution)/shard_map/dot_general | solution.py:42
  326.0 20.3 %collective-permute-done.1 = bf16[384,1536]{1,0:T(8,128)(2,1)} collective-permute-done((bf16[384,1536]{1,0:T(8,128)(2,1)S(1)}, bf16[384,1536]{1,0:T(8,128)(2,1)}, u32[]{:S(2)}, u32[]{:S(2)}) %collective-permute-start.1) | collective-permute-done | bytes 1179680 | tf_op jit(solution)/shard_map/ppermute | solution.py:73
  372.4 18.6 %fusion.46 = f32[1536,1152]{1,0:T(8,128)} fusion(bf16[1536,1152]{1,0:T(8,128)(2,1)} %collective-permute-done.4, bf16[1536,1152]{1,0:T(8,128)(2,1)S(1)} %copy-done.37, pred[]{:T(512)S(6)} %eq.16, bf16[384,768]{1,0:T(8,128)(2,1)S(1)} %collective-permute-done.3, bf16[384,768]{1,0:T(8,128)(2,1)S(1)} %collective-permute-done.2, ...), kind=kOutput, calls=%fused_computation.90 | convolution fusion | flops 5461180416 | bytes 18874368 | tf_op jit(solution)/shard_map/dot_general | solution.py:42
  391.0 25.7 %fusion.15 = (bf16[1536,1152]{1,0:T(8,128)(2,1)}, bf16[1536,1152]{1,0:T(8,128)(2,1)}, bf16[1536,1152]{1,0:T(8,128)(2,1)}) fusion(f32[1536,1152]{1,0:T(8,128)} %fusion.42, f32[1536,1152]{1,0:T(8,128)} %fusion.46, bf16[1536,1152]{1,0:T(8,128)(2,1)} %all-gather.26.cloned.1.call-done, bf16[1536,1152]{1,0:T(8,128)(2,1)} %collective-permute-done.4, pred[]{:T(512)S(6)} %eq.16, ...), kind=kOutput, calls=%fused_computation.24 | convolution fusion | flops 5507186688 | bytes 36569088 | tf_op jit(solution)/shard_map/dot_general | solution.py:42
  476.0 21.1 %collective-permute-done.17 = bf16[384,1536]{1,0:T(8,128)(2,1)S(1)} collective-permute-done((bf16[384,1536]{1,0:T(8,128)(2,1)S(1)}, bf16[384,1536]{1,0:T(8,128)(2,1)S(1)}, u32[]{:S(2)}, u32[]{:S(2)}) %collective-permute-start.17) | collective-permute-done | bytes 1179680 | tf_op jit(solution)/shard_map/ppermute | solution.py:73
  499.0 20.5 %collective-permute-done.9 = bf16[384,1536]{1,0:T(8,128)(2,1)S(1)} collective-permute-done((bf16[384,1536]{1,0:T(8,128)(2,1)S(1)}, bf16[384,1536]{1,0:T(8,128)(2,1)S(1)}, u32[]{:S(2)}, u32[]{:S(2)}) %collective-permute-start.9) | collective-permute-done | bytes 1179680 | tf_op jit(solution)/shard_map/ppermute | solution.py:73
  530.0 24.5 %fusion.19 = bf16[3072,128]{1,0:T(8,128)(2,1)S(1)} fusion(bf16[4608,128]{1,0:T(8,128)(2,1)S(1)} %reshape.297, f32[4608,3072]{0,1:T(8,128)} %get-tuple-element.56, f32[4608]{0:T(1024)S(1)} %log_add_fusion, s32[3072]{0:T(1024)S(1)} %bitcast.141, s32[4608]{0:T(1024)S(1)} %sub.30, s32[4608]{0:T(1024)S(1)} %eq.12, s32[3072]{0:T(1024)S(1)} %convert_reduce_fusion), kind=kOutput, calls=%fused_computation.35 | convolution fusion | flops 3751673856 | bytes 58669056 | tf_op jit(solution)/shard_map/ab,ac->bc/dot_general | solution.py:50
  554.9 35.7 %multiply_convert_fusion = bf16[4608,3072]{0,1:T(8,128)(2,1)} fusion(f32[4608,3072]{0,1:T(8,128)} %get-tuple-element.56, bf16[4608,128]{1,0:T(8,128)(2,1)S(1)} %reshape.297, f32[4608]{0:T(1024)S(1)} %multiply_reduce_fusion.1, f32[4608]{0:T(1024)S(1)} %log_add_fusion, bf16[3072,256]{1,0:T(8,128)(2,1)} %all-gather.22.cloned.1.call-done, ...), kind=kOutput, calls=%fused_computation.2 | convolution fusion | flops 3779592192 | bytes 86999040 | tf_op jit(solution)/shard_map/ab,cb->ac/dot_general | solution.py:46
  652.4 18.5 %fusion.95 = f32[1152,1536]{1,0:T(8,128)S(1)} fusion(bf16[1536,1152]{1,0:T(8,128)(2,1)} %get-tuple-element.16, bf16[384,768]{1,0:T(8,128)(2,1)S(1)} %copy-done.45, bf16[384,768]{1,0:T(8,128)(2,1)S(1)} %copy-done.47, bf16[384,1536]{1,0:T(8,128)(2,1)} %collective-permute-done.11, bf16[384,1536]{1,0:T(8,128)(2,1)} %collective-permute-done.10, ...), kind=kOutput, calls=%fused_computation.183 | convolution fusion | flops 5459410944 | bytes 15335424 | tf_op jit(solution)/shard_map/ab,ac->bc/dot_general | solution.py:50
  672.5 20.5 %fusion.97 = f32[1536,1152]{1,0:T(8,128)} fusion(bf16[1536,1152]{1,0:T(8,128)(2,1)S(1)} %copy-done.49, bf16[384,768]{1,0:T(8,128)(2,1)S(1)} %copy-done.41, bf16[384,768]{1,0:T(8,128)(2,1)S(1)} %copy-done.43, bf16[384,1536]{1,0:T(8,128)(2,1)} %collective-permute-done.1, bf16[384,1536]{1,0:T(8,128)(2,1)} %collective-permute-done, ...), kind=kOutput, calls=%fused_computation.185 | convolution fusion | flops 5459410944 | bytes 15335424 | tf_op jit(solution)/shard_map/ab,ac->bc/dot_general | solution.py:50
  695.1 17.6 %select_convert_fusion = (bf16[1536,1152]{1,0:T(8,128)(2,1)}, f32[1536,1152]{1,0:T(8,128)}) fusion(f32[1536,1152]{1,0:T(8,128)} %fusion.97, pred[]{:T(512)S(6)} %eq.16, bf16[1536,1152]{1,0:T(8,128)(2,1)} %get-tuple-element.15, bf16[384,768]{1,0:T(8,128)(2,1)S(1)} %copy-done.41, bf16[384,768]{1,0:T(8,128)(2,1)} %copy-done.42, ...), kind=kOutput, calls=%fused_computation.27 | convolution fusion | flops 5461180416 | bytes 25952256 | tf_op jit(solution)/shard_map/ab,ac->bc/dot_general | solution.py:50
  713.2 50.6 %reduce-scatter.10.cloned.1.call-done = bf16[4,48,1792]{2,1,0:T(8,128)(2,1)} async-done(((bf16[4,384,1792]{2,1,0:T(8,128)(2,1)}), bf16[4,48,1792]{2,1,0:T(8,128)(2,1)}) %reduce-scatter.10.cloned.1.call-update) | async-done | bytes 688144 | tf_op jit(solution)/shard_map/reduce_scatter | solution.py:197
  770.8 34.4 %reduce-scatter.20.cloned.1.call-done = bf16[1,288,768]{2,1,0:T(8,128)(2,1)} async-done(((bf16[4,288,768]{2,1,0:T(8,128)(2,1)}), bf16[1,288,768]{2,1,0:T(8,128)(2,1)}) %reduce-scatter.20.cloned.1.call-update) | async-done | bytes 442384 | tf_op jit(solution)/shard_map/reduce_scatter | solution.py:180
  805.2 23.3 %reduce-scatter.16.cloned.1.call-done = bf16[1,48,1536]{2,1,0:T(8,128)(2,1)} async-done(((bf16[4,48,1536]{2,1,0:T(8,128)(2,1)}), bf16[1,48,1536]{2,1,0:T(8,128)(2,1)}) %reduce-scatter.16.cloned.1.call-update) | async-done | bytes 147472 | tf_op jit(solution)/shard_map/reduce_scatter | solution.py:198
  828.6 23.2 %reduce-scatter.12.cloned.1.call-done = bf16[1,48,1792]{2,1,0:T(8,128)(2,1)} async-done(((bf16[4,48,1792]{2,1,0:T(8,128)(2,1)}), bf16[1,48,1792]{2,1,0:T(8,128)(2,1)}) %reduce-scatter.12.cloned.1.call-update) | async-done | bytes 172048 | tf_op jit(solution)/shard_map/reduce_scatter | solution.py:198
  851.8 67.4 %reduce-scatter.18.cloned.1.call-done = bf16[384,1152]{1,0:T(8,128)(2,1)} async-done(((bf16[1536,1152]{1,0:T(8,128)(2,1)}), bf16[384,1152]{1,0:T(8,128)(2,1)}) %reduce-scatter.18.cloned.1.call-update) | async-done | bytes 884752 | tf_op jit(solution)/shard_map/reduce_scatter | solution.py:162
  919.3 69.2 %all-gather.9 = f32[32,1,1536]{2,1,0:T(1,128)S(1)} all-gather(f32[1,1,1536]{2,1,0:T(1,128)S(1)} %reshape.331), channel_id=8, replica_groups=mesh['ctx'=8,'fsdp'=4] {'ctx','fsdp'}, dimensions={0}, use_global_device_ids=true | all-gather | bytes 202752 | tf_op jit(solution)/shard_map/all_gather | solution.py:202
  996.0 66.1 %all-gather.8 = f32[32,1,1536]{2,1,0:T(1,128)S(1)} all-gather(f32[1,1,1536]{2,1,0:T(1,128)S(1)} %reshape.329), channel_id=5, replica_groups=mesh['ctx'=8,'fsdp'=4] {'ctx','fsdp'}, dimensions={0}, use_global_device_ids=true | all-gather | bytes 202752 | tf_op jit(solution)/shard_map/all_gather | solution.py:202
  (306 shorter events, 370.3 us)
Async XLA Ops:
  7.2 64.5 %all-gather.20.cloned.1.call-start = ((), (), s32[]{:S(2)}) async-start(), calls=%async_computation.7 | async-start | bytes 6193152 | tf_op jit(solution)/shard_map/all_gather | solution.py:191
  28.7 95.0 %all-gather.30.cloned.1.call-start = ((), (), s32[]{:S(2)}) async-start(), calls=%async_computation.19 | async-start | bytes 2211840 | tf_op jit(solution)/shard_map/all_gather | solution.py:145
  31.9 162.8 %all-gather.26.cloned.1.call-start = ((), (), s32[]{:S(2)}) async-start(), calls=%async_computation.10 | async-start | bytes 4423680 | tf_op jit(solution)/shard_map/all_gather | solution.py:139
  35.7 187.4 %all-gather.22.cloned.1.call-start = ((), (), s32[]{:S(2)}) async-start(), calls=%async_computation.8 | async-start | bytes 1769472 | tf_op jit(solution)/shard_map/all_gather | solution.py:285
  79.9 231.0 %all-gather.24.cloned.1.call-start = ((), (), s32[]{:S(2)}) async-start(), calls=%async_computation.9 | async-start | bytes 5308416 | tf_op jit(solution)/shard_map/all_gather | solution.py:191
  79.9 239.0 %collective-permute-start.11 = (bf16[384,1536]{1,0:T(8,128)(2,1)}, bf16[384,1536]{1,0:T(8,128)(2,1)}, u32[]{:S(2)}, u32[]{:S(2)}) collective-permute-start(bf16[384,1536]{1,0:T(8,128)(2,1)} %bitcast.16), channel_id=1, source_target_pairs={{0,16},{4,20},{8,24},{12,28},{16,0},{20,4},{24,8},{28,12},{1,17},{... | collective-permute-start | bytes 3538952 | tf_op jit(solution)/shard_map/ppermute | solution.py:73
  81.3 240.3 %collective-permute-start.10 = (bf16[384,1536]{1,0:T(8,128)(2,1)}, bf16[384,1536]{1,0:T(8,128)(2,1)}, u32[]{:S(2)}, u32[]{:S(2)}) collective-permute-start(bf16[384,1536]{1,0:T(8,128)(2,1)} %bitcast.16), channel_id=1, source_target_pairs={{0,8},{4,12},{8,0},{12,4},{16,24},{20,28},{24,16},{28,20},{1,9},{5... | collective-permute-start | bytes 3538952 | tf_op jit(solution)/shard_map/ppermute | solution.py:73
  107.5 535.6 %reduce-scatter.8.cloned.1.call-start = ((), (), s32[]{:S(2)}) async-start(), calls=%async_computation.11 | async-start | bytes 1769472 | tf_op jit(solution)/shard_map/reduce_scatter | solution.py:324
  127.5 195.8 %collective-permute-start.5 = (bf16[1152,768]{1,0:T(8,128)(2,1)}, bf16[1152,768]{1,0:T(8,128)(2,1)}, u32[]{:S(2)}, u32[]{:S(2)}) collective-permute-start(bf16[1152,768]{1,0:T(8,128)(2,1)} %pad_maximum_fusion.3), channel_id=1, source_target_pairs={{0,4},{4,0},{8,12},{12,8},{16,20},{20,16},{24,28},{28,24},{1,5},{5... | collective-permute-start | bytes 5308424 | tf_op jit(solution)/shard_map/ppermute | solution.py:73
  194.8 177.5 %collective-permute-start.4 = (bf16[1536,1152]{1,0:T(8,128)(2,1)}, bf16[1536,1152]{1,0:T(8,128)(2,1)}, u32[]{:S(2)}, u32[]{:S(2)}) collective-permute-start(bf16[1536,1152]{1,0:T(8,128)(2,1)} %all-gather.26.cloned.1.call-done), channel_id=1, source_target_pairs={{0,4},{4,0},{8,12},{12,8},{16,20},{20,16},{24,28},{28,24},{1,5},{5... | collective-permute-start | bytes 10616840 | tf_op jit(solution)/shard_map/ppermute | solution.py:73
  321.6 38.9 %collective-permute-start.13 = (bf16[384,768]{1,0:T(8,128)(2,1)S(1)}, bf16[384,768]{1,0:T(8,128)(2,1)S(1)}, u32[]{:S(2)}, u32[]{:S(2)}) collective-permute-start(bf16[384,768]{1,0:T(8,128)(2,1)S(1)} %slice.199), channel_id=1, source_target_pairs={{0,8},{4,12},{8,0},{12,4},{16,24},{20,28},{24,16},{28,20},{1,9},{5... | collective-permute-start | bytes 1769480 | tf_op jit(solution)/shard_map/ppermute | solution.py:73
  472.7 46.9 %collective-permute-start.9 = (bf16[384,1536]{1,0:T(8,128)(2,1)S(1)}, bf16[384,1536]{1,0:T(8,128)(2,1)S(1)}, u32[]{:S(2)}, u32[]{:S(2)}) collective-permute-start(bf16[384,1536]{1,0:T(8,128)(2,1)S(1)} %pad_maximum_fusion.8), channel_id=1, source_target_pairs={{0,8},{4,12},{8,0},{12,4},{16,24},{20,28},{24,16},{28,20},{1,9},{5... | collective-permute-start | bytes 3538952 | tf_op jit(solution)/shard_map/ppermute | solution.py:73
  474.4 46.4 %collective-permute-start.7 = (bf16[384,1536]{1,0:T(8,128)(2,1)S(1)}, bf16[384,1536]{1,0:T(8,128)(2,1)S(1)}, u32[]{:S(2)}, u32[]{:S(2)}) collective-permute-start(bf16[384,1536]{1,0:T(8,128)(2,1)S(1)} %pad_maximum_fusion.7), channel_id=1, source_target_pairs={{0,16},{4,20},{8,24},{12,28},{16,0},{20,4},{24,8},{28,12},{1,17},{... | collective-permute-start | bytes 3538952 | tf_op jit(solution)/shard_map/ppermute | solution.py:73
  604.9 108.3 %reduce-scatter.14.cloned.1.call-start = ((), (), s32[]{:S(2)}) async-start(), calls=%async_computation.14 | async-start | bytes 5308416 | tf_op jit(solution)/shard_map/reduce_scatter | solution.py:197
  611.2 152.7 %reduce-scatter.10.cloned.1.call-start = ((), (), s32[]{:S(2)}) async-start(), calls=%async_computation.12 | async-start | bytes 6193152 | tf_op jit(solution)/shard_map/reduce_scatter | solution.py:197
  651.1 154.1 %reduce-scatter.20.cloned.1.call-start = ((), (), s32[]{:S(2)}) async-start(), calls=%async_computation.17 | async-start | bytes 2211840 | tf_op jit(solution)/shard_map/reduce_scatter | solution.py:180
  695.1 133.4 %reduce-scatter.16.cloned.1.call-start = ((), (), s32[]{:S(2)}) async-start(), calls=%async_computation.15 | async-start | bytes 737280 | tf_op jit(solution)/shard_map/reduce_scatter | solution.py:198
  712.7 51.2 %collective-permute-start.18 = (bf16[1536,1152]{1,0:T(8,128)(2,1)}, bf16[1536,1152]{1,0:T(8,128)(2,1)}, u32[]{:S(2)}, u32[]{:S(2)}) collective-permute-start(bf16[1536,1152]{1,0:T(8,128)(2,1)} %get-tuple-element.66), channel_id=1, source_target_pairs={{0,4},{4,0},{8,12},{12,8},{16,20},{20,16},{24,28},{28,24},{1,5},{5... | collective-permute-start | bytes 10616840 | tf_op jit(solution)/shard_map/ppermute | solution.py:73
  713.2 138.6 %reduce-scatter.12.cloned.1.call-start = ((), (), s32[]{:S(2)}) async-start(), calls=%async_computation.13 | async-start | bytes 860160 | tf_op jit(solution)/shard_map/reduce_scatter | solution.py:198
  763.9 155.4 %reduce-scatter.18.cloned.1.call-start = ((), (), s32[]{:S(2)}) async-start(), calls=%async_computation.16 | async-start | bytes 4423680 | tf_op jit(solution)/shard_map/reduce_scatter | solution.py:162
  770.7 296.5 %all-gather.28.cloned.1.call-start = ((), (), s32[]{:S(2)}) async-start(), calls=%async_computation.18 | async-start | bytes 3981312 | tf_op jit(solution)/shard_map/all_gather | solution.py:181
  805.2 273.4 %all-gather.34.cloned.1.call-start = ((), (), s32[]{:S(2)}) async-start(), calls=%async_computation.21 | async-start | bytes 1327104 | tf_op jit(solution)/shard_map/all_gather | solution.py:199
  828.5 253.0 %all-gather.32.cloned.1.call-start = ((), (), s32[]{:S(2)}) async-start(), calls=%async_computation.20 | async-start | bytes 1548288 | tf_op jit(solution)/shard_map/all_gather | solution.py:199
  851.8 232.8 %all-gather.36.cloned.1.call-start = ((), (), s32[]{:S(2)}) async-start(), calls=%async_computation.22 | async-start | bytes 7962624 | tf_op jit(solution)/shard_map/all_gather | solution.py:164
  (64 other events, 1691.1 us)
Sparse Core Ops, SparseCore 0:
  28.9 42.8 all-gather.19
  73.9 49.7 all-gather.29
  125.9 68.8 all-gather.25
  196.5 24.2 all-gather.21
  222.6 38.9 all-gather.23
  605.0 36.1 reduce-scatter.7
  644.6 53.8 reduce-scatter.13
  702.4 61.4 reduce-scatter.9
  766.7 38.3 reduce-scatter.19
  807.4 21.0 reduce-scatter.15
  830.9 20.8 reduce-scatter.11
  853.9 65.2 reduce-scatter.17
  921.1 34.4 all-gather.27
  957.3 24.0 all-gather.33
  983.2 25.0 all-gather.31
  1010.0 49.2 all-gather.35

commit v2 on v1

--- a/solution.py
+++ b/solution.py
@@ -1,12 +1,17 @@
+import functools
+
 import jax
 import jax.numpy as jnp
 from jax import lax
+from jax.experimental import pallas as pl
+from jax.experimental.pallas import tpu as pltpu
 from jax.sharding import PartitionSpec as P
 
 H = 12
 HD = 128
 FF = 4608
 WINDOW = 1024
+ROUNDS = 4
 LANES = 128
 
 
@@ -17,23 +22,6 @@
     return values * lax.rsqrt(jnp.mean(values * values, axis=-1, keepdims=True) + EPS) * gain
 
 
-def rotate(values, places):
-    half_dim = values.shape[-1] // 2
-    frequency = 10000.0 ** (-jnp.arange(half_dim, dtype=jnp.float32) / half_dim)
-    angles = places[:, None] * frequency[None, :]
-    cosine = jnp.cos(angles)[:, None, :]
-    sine_part = jnp.sin(angles)[:, None, :]
-    first_half = values[..., :half_dim]
-    second_half = values[..., half_dim:]
-    return jnp.concatenate(
-        [
-            first_half * cosine - second_half * sine_part,
-            second_half * cosine + first_half * sine_part,
-        ],
-        axis=-1,
-    )
-
-
 def geglu(gate, up):
     return jax.nn.gelu(gate, approximate=True) * up
 
@@ -52,6 +40,700 @@
 
 def low(values):
     return values.astype(jnp.bfloat16)
+
+
+VMEM_LIMIT = 56 * 1024 * 1024
+
+def project_kernel(heads, x_ref, gain_ref, w_ref, cos_ref, sin_ref, normed_ref, q_ref, kv_ref):
+    step = pl.program_id(0)
+
+    @pl.when(step == 0)
+    def _():
+        x = x_ref[...].astype(jnp.float32)
+        scale = lax.rsqrt(jnp.mean(x * x, axis=-1, keepdims=True) + EPS)
+        normed_ref[...] = (x * scale * gain_ref[...]).astype(jnp.bfloat16)
+
+    part = jnp.dot(normed_ref[...], w_ref[...], preferred_element_type=jnp.float32)
+    cosine, sine_part = cos_ref[...], sin_ref[...]
+
+    def turn(value):
+        return value * cosine + pltpu.roll(value, HD // 2, 1) * sine_part
+
+    @pl.when(step < heads // 2)
+    def _():
+        for j in range(2):
+            q_ref[j] = (turn(part[:, j * HD : (j + 1) * HD]) * HD ** (-0.5)).astype(jnp.bfloat16)
+
+    @pl.when(step == heads // 2)
+    def _():
+        kv_ref[:, :HD] = turn(part[:, :HD]).astype(jnp.bfloat16)
+        kv_ref[:, HD:] = part[:, HD:].astype(jnp.bfloat16)
+
+
+def project(x, gain, w, cosine, sine_part):
+    rows, width = x.shape
+    steps = H // 2 + 1
+    whole = lambda *shape: pl.BlockSpec(shape, lambda i: (0,) * len(shape))
+    return pl.pallas_call(
+        functools.partial(project_kernel, H),
+        grid=(steps,),
+        name="project",
+        in_specs=[
+            whole(rows, width),
+            whole(1, width),
+            pl.BlockSpec((width, 2 * HD), lambda i: (0, i)),
+            whole(rows, HD),
+            whole(rows, HD),
+        ],
+        out_specs=[
+            whole(rows, width),
+            pl.BlockSpec((2, rows, HD), lambda i: (jnp.minimum(i, H // 2 - 1), 0, 0)),
+            whole(rows, 2 * HD),
+        ],
+        out_shape=[
+            jax.ShapeDtypeStruct((rows, width), jnp.bfloat16),
+            jax.ShapeDtypeStruct((H, rows, HD), jnp.bfloat16),
+            jax.ShapeDtypeStruct((rows, 2 * HD), jnp.bfloat16),
+        ],
+        compiler_params=pltpu.CompilerParams(vmem_limit_bytes=VMEM_LIMIT),
+    )(x, gain, w, cosine, sine_part)
+
+
+HEADS_STEP = 4
+
+
+def attend_kernel(blocks, block, where_ref, q_ref, kv_ref, key_place_ref, place_ref, least_ref, out_ref, window, bias):
+    r = pl.program_id(0)
+
+    @pl.when(pl.program_id(1) == 0)
+    def _():
+        for j in range(blocks):
+            window[j * block : (j + 1) * block, :] = kv_ref[where_ref[r, j]]
+        key_place = key_place_ref[0]
+        allowed = (key_place <= place_ref[...]) & (key_place >= least_ref[...])
+        bias[...] = jnp.where(allowed, 0.0, -1e30)
+
+    queries = q_ref[...].reshape(HEADS_STEP * block, HD)
+    scores = lax.dot_general(
+        queries, window[:, :HD], (((1,), (1,)), ((), ())), preferred_element_type=jnp.float32
+    )
+    scores = scores.reshape(HEADS_STEP, block, blocks * block) + bias[...][None]
+    peak = jnp.max(scores, axis=-1, keepdims=True)
+    weights = jnp.exp(scores - peak)
+    total = jnp.sum(weights, axis=-1, keepdims=True).reshape(HEADS_STEP * block, 1)
+    weights = weights.astype(jnp.bfloat16).reshape(HEADS_STEP * block, blocks * block)
+    mixed = jnp.dot(weights, window[:, HD:], preferred_element_type=jnp.float32) / total
+    mixed = mixed.astype(jnp.bfloat16)
+    for j in range(HEADS_STEP):
+        out_ref[:, j * HD : (j + 1) * HD] = mixed[j * block : (j + 1) * block]
+
+
+def attend(where, queries, kv_blocks, key_place, place, least):
+    rounds, blocks = where.shape
+    heads, rows, _ = queries.shape
+    block = rows // rounds
+    span = blocks * block
+    grid_spec = pltpu.PrefetchScalarGridSpec(
+        num_scalar_prefetch=1,
+        grid=(rounds, heads // HEADS_STEP),
+        in_specs=[
+            pl.BlockSpec((HEADS_STEP, block, HD), lambda r, h, *_: (h, r, 0)),
+            pl.BlockSpec(kv_blocks.shape, lambda r, h, *_: (0, 0, 0)),
+            pl.BlockSpec((1, 1, span), lambda r, h, *_: (r, 0, 0)),
+            pl.BlockSpec((block, 1), lambda r, h, *_: (r, 0)),
+            pl.BlockSpec((block, 1), lambda r, h, *_: (r, 0)),
+        ],
+        out_specs=pl.BlockSpec((block, HEADS_STEP * HD), lambda r, h, *_: (r, h)),
+        scratch_shapes=[
+            pltpu.VMEM((span, 2 * HD), jnp.bfloat16),
+            pltpu.VMEM((block, span), jnp.float32),
+        ],
+    )
+    return pl.pallas_call(
+        functools.partial(attend_kernel, blocks, block),
+        name="attend",
+        grid_spec=grid_spec,
+        out_shape=jax.ShapeDtypeStruct((rows, heads * HD), jnp.bfloat16),
+        compiler_params=pltpu.CompilerParams(vmem_limit_bytes=VMEM_LIMIT),
+    )(where, queries, kv_blocks, key_place, place, least)
+
+
+def attend_back_kernel(
+    blocks, block, where_ref, q_ref, kv_ref, grad_ref, key_place_ref, place_ref, least_ref, cos_ref, sin_ref,
+    grad_q_ref, grad_kv_ref, window, bias, window_grad, total_grad,
+):
+    r, h = pl.program_id(0), pl.program_id(1)
+    last = pl.num_programs(1) - 1
+
+    @pl.when((r == 0) & (h == 0))
+    def _():
+        total_grad[...] = jnp.zeros_like(total_grad)
+
+    @pl.when(h == 0)
+    def _():
+        for j in range(blocks):
+            window[j * block : (j + 1) * block, :] = kv_ref[where_ref[r, j]]
+        key_place = key_place_ref[0]
+        allowed = (key_place <= place_ref[0]) & (key_place >= least_ref[0])
+        bias[...] = jnp.where(allowed, 0.0, -1e30)
+        window_grad[...] = jnp.zeros_like(window_grad)
+
+    queries = q_ref[...].reshape(HEADS_STEP * block, HD)
+    grads = jnp.concatenate([grad_ref[:, j * HD : (j + 1) * HD] for j in range(HEADS_STEP)], axis=0)
+    keys, values = window[:, :HD], window[:, HD:]
+    nt = (((1,), (1,)), ((), ()))
+    tn = (((0,), (0,)), ((), ()))
+    scores = lax.dot_general(keys, queries, nt, preferred_element_type=jnp.float32) + bias[...]
+    peak = jnp.max(scores, axis=0, keepdims=True)
+    weights = jnp.exp(scores - peak)
+    probs = weights * (1.0 / jnp.sum(weights, axis=0, keepdims=True))
+    grad_probs = lax.dot_general(values, grads, nt, preferred_element_type=jnp.float32)
+    delta = jnp.sum(probs * grad_probs, axis=0, keepdims=True)
+    grad_scores = (probs * (grad_probs - delta)).astype(jnp.bfloat16)
+    window_grad[:, :HD] += jnp.dot(grad_scores, queries, preferred_element_type=jnp.float32)
+    window_grad[:, HD:] += jnp.dot(
+        probs.astype(jnp.bfloat16), grads, preferred_element_type=jnp.float32
+    )
+    grad_q = lax.dot_general(grad_scores, keys, tn, preferred_element_type=jnp.float32)
+    cosine, sine_part = cos_ref[...], sin_ref[...]
+    for j in range(HEADS_STEP):
+        one = grad_q[j * block : (j + 1) * block]
+        one = (one * cosine - pltpu.roll(one, HD // 2, 1) * sine_part) * HD ** (-0.5)
+        grad_q_ref[:, j * HD : (j + 1) * HD] = one.astype(jnp.bfloat16)
+
+    @pl.when(h == last)
+    def _():
+        for j in range(blocks):
+            total_grad[where_ref[r, blocks + j]] += window_grad[j * block : (j + 1) * block, :]
+
+    @pl.when((h == last) & (r == pl.num_programs(0) - 1))
+    def _():
+        grad_kv_ref[...] = total_grad[...].astype(jnp.bfloat16)
+
+
+def attend_back(where, queries, kv_blocks, grads, key_place, place, least, cosine, sine_part):
+    rounds, blocks = where.shape[0], where.shape[1] // 2
+    heads, rows, _ = queries.shape
+    block = rows // rounds
+    span = blocks * block
+    width = HEADS_STEP * block
+    grid_spec = pltpu.PrefetchScalarGridSpec(
+        num_scalar_prefetch=1,
+        grid=(rounds, heads // HEADS_STEP),
+        in_specs=[
+            pl.BlockSpec((HEADS_STEP, block, HD), lambda r, h, *_: (h, r, 0)),
+            pl.BlockSpec(kv_blocks.shape, lambda r, h, *_: (0, 0, 0)),
+            pl.BlockSpec((block, HEADS_STEP * HD), lambda r, h, *_: (r, h)),
+            pl.BlockSpec((1, span, 1), lambda r, h, *_: (r, 0, 0)),
+            pl.BlockSpec((1, 1, width), lambda r, h, *_: (r, 0, 0)),
+            pl.BlockSpec((1, 1, width), lambda r, h, *_: (r, 0, 0)),
+            pl.BlockSpec((block, HD), lambda r, h, *_: (r, 0)),
+            pl.BlockSpec((block, HD), lambda r, h, *_: (r, 0)),
+        ],
+        out_specs=[
+            pl.BlockSpec((block, HEADS_STEP * HD), lambda r, h, *_: (r, h)),
+            pl.BlockSpec(kv_blocks.shape, lambda r, h, *_: (0, 0, 0)),
+        ],
+        scratch_shapes=[
+            pltpu.VMEM((span, 2 * HD), jnp.bfloat16),
+            pltpu.VMEM((span, width), jnp.float32),
+            pltpu.VMEM((span, 2 * HD), jnp.float32),
+            pltpu.VMEM(kv_blocks.shape, jnp.float32),
+        ],
+    )
+    return pl.pallas_call(
+        functools.partial(attend_back_kernel, blocks, block),
+        name="attend_back",
+        grid_spec=grid_spec,
+        out_shape=[
+            jax.ShapeDtypeStruct((rows, heads * HD), jnp.bfloat16),
+            jax.ShapeDtypeStruct(kv_blocks.shape, jnp.bfloat16),
+        ],
+        compiler_params=pltpu.CompilerParams(vmem_limit_bytes=VMEM_LIMIT),
+    )(where, queries, kv_blocks, grads, key_place, place, least, cosine, sine_part)
+
+
+MESH_ID = pl.DeviceIdType.MESH
+
+
+class Wire:
+    def __init__(self, send_sems, recv_sems):
+        self.send_sems = send_sems
+        self.recv_sems = recv_sems
+        self.count = 0
+        self.open = []
+        self.ctx = lax.axis_index("ctx")
+        self.shard = lax.axis_index("fsdp")
+
+    def other(self, mask):
+        at = self.ctx
+        for bit in (1, 2, 4):
+            if mask & bit:
+                at = at + bit - 2 * bit * lax.rem(at // bit, 2)
+        return at
+
+    def plane(self, mask):
+        return (self.other(mask), self.shard)
+
+    def line(self, step, shards):
+        return (self.ctx, lax.rem(self.shard + step, shards))
+
+    def meet(self, peers):
+        barrier = pltpu.get_barrier_semaphore()
+        for peer in peers:
+            pl.semaphore_signal(barrier, inc=1, device_id=peer, device_id_type=MESH_ID)
+        pl.semaphore_wait(barrier, len(peers))
+
+    def send(self, source, target, peer):
+        at = self.count
+        self.count += 1
+        copy = pltpu.make_async_remote_copy(
+            src_ref=source,
+            dst_ref=target,
+            send_sem=self.send_sems.at[at],
+            recv_sem=self.recv_sems.at[at],
+            device_id=peer,
+            device_id_type=MESH_ID,
+        )
+        copy.start()
+        self.open.append(copy)
+        return copy
+
+    def sent(self, copy):
+        copy.wait_send()
+        self.open = [one for one in self.open if one is not copy]
+
+    def finish(self):
+        for copy in self.open:
+            copy.wait_send()
+
+
+class PlaneGather:
+    COPIES = 9
+
+    def __init__(self, wire, source, out_at, rows, split):
+        self.wire, self.out_at, self.rows, self.split = wire, out_at, rows, split
+        ctx = wire.ctx
+        self.core = wire.send(source, out_at(ctx), wire.plane(1))
+        self.x = wire.send(source, out_at(ctx), wire.plane(2))
+        self.y = wire.send(source, out_at(ctx), wire.plane(4))
+
+    def forward(self):
+        wire, split = self.wire, self.split
+        rest = self.rows - split
+        self.x.wait_recv()
+        block = self.out_at(wire.other(2))
+        part = block.at[pl.ds(0, split)]
+        self.corner_y = wire.send(part, part, wire.plane(4))
+        self.core_x = wire.send(block, block, wire.plane(1))
+        self.y.wait_recv()
+        block = self.out_at(wire.other(4))
+        part = block.at[pl.ds(split, rest)]
+        self.corner_x = wire.send(part, part, wire.plane(2))
+        self.core_y = wire.send(block, block, wire.plane(1))
+
+    def corner(self):
+        self.corner_y.wait_recv()
+        self.corner_x.wait_recv()
+        block = self.out_at(self.wire.other(6))
+        self.core_corner = self.wire.send(block, block, self.wire.plane(1))
+
+    def settle(self):
+        self.core.wait_recv()
+        self.core_x.wait_recv()
+        self.core_y.wait_recv()
+        self.core_corner.wait_recv()
+
+
+def half_rows(rows, turn):
+    low_half = rows // 32 * 16
+    return low_half if turn % 2 else rows - low_half
+
+
+def add_low(first, second):
+    return (first.astype(jnp.float32) + second.astype(jnp.float32)).astype(jnp.bfloat16)
+
+
+class PlaneSum:
+    COPIES = 7
+
+    def __init__(self, wire, source, own, pair, first, second, local_sem):
+        self.wire, self.own, self.pair, self.first, self.second = wire, own, pair, first, second
+        core = lax.rem(wire.ctx, 2)
+        self.chips = {mask: wire.other(2 * mask) // 2 for mask in range(4)}
+        self.swap = wire.send(source.at[:, :, 1 - core], pair, wire.plane(1))
+        self.local = pltpu.make_async_copy(source.at[:, :, core], own, local_sem)
+        self.local.start()
+
+    def step_one(self):
+        wire, own, pair, first, chips = self.wire, self.own, self.pair, self.first, self.chips
+        self.local.wait()
+        self.swap.wait_recv()
+
+        def add_pair(index, carry):
+            part, other = index // 4, lax.rem(index, 4)
+            own[part, other] = add_low(own[part, other], pair[part, other])
+            return carry
+
+        lax.fori_loop(0, 16, add_pair, 0)
+        low, high = pl.ds(0, 2), pl.ds(2, 2)
+        self.one = [
+            wire.send(own.at[low, chips[3]], first.at[0, 1], wire.plane(2)),
+            wire.send(own.at[high, chips[3]], first.at[1, 1], wire.plane(4)),
+            wire.send(own.at[low, chips[1]], first.at[0, 0], wire.plane(2)),
+            wire.send(own.at[high, chips[2]], first.at[1, 0], wire.plane(4)),
+        ]
+
+    def step_two(self):
+        wire, own, first, second, chips = self.wire, self.own, self.first, self.second, self.chips
+        self.one[0].wait_recv()
+        for part in range(2):
+            own[part, chips[2]] = add_low(own[part, chips[2]], first[0, 1, part])
+        self.two = [wire.send(own.at[pl.ds(0, 2), chips[2]], second.at[pl.ds(0, 2)], wire.plane(4))]
+        self.one[1].wait_recv()
+        for part in range(2):
+            own[part + 2, chips[1]] = add_low(own[part + 2, chips[1]], first[1, 1, part])
+        self.two.append(
+            wire.send(own.at[pl.ds(2, 2), chips[1]], second.at[pl.ds(2, 2)], wire.plane(2))
+        )
+
+    def result(self, store):
+        own, first, second, chips = self.own, self.first, self.second, self.chips
+        for copy in self.one[2:] + self.two:
+            copy.wait_recv()
+        for part in range(4):
+            total = own[part, chips[0]].astype(jnp.float32)
+            total += first[part // 2, 0, part % 2].astype(jnp.float32)
+            total += second[part].astype(jnp.float32)
+            store(part, total)
+
+
+def plane_sum_scratch(rows, columns):
+    shape = lambda *lead: pltpu.VMEM(lead + (rows, columns), jnp.bfloat16)
+    return [shape(4, 4), shape(4, 4), shape(2, 2, 2), shape(4)]
+
+
+def dma_sems(count):
+    return pltpu.SemaphoreType.DMA((count,))
+
+
+ANY = pl.BlockSpec(memory_space=pl.ANY)
+PLANE_PEERS = (1, 2, 4)
+
+
+def comm_params(number):
+    return pltpu.CompilerParams(
+        collective_id=number, has_side_effects=True, vmem_limit_bytes=VMEM_LIMIT
+    )
+
+
+def gather_weights_kernel(shards, in_ref, out_ref, gain_ref, in_all, out_all, gain_all, local_sems, send_sems, recv_sems):
+    wire = Wire(send_sems, recv_sems)
+    ctx, shard = wire.ctx, wire.shard
+    wire.meet(
+        [wire.plane(mask) for mask in PLANE_PEERS] + [wire.line(s, shards) for s in range(1, shards)]
+    )
+    pairs = ((in_ref, in_all), (out_ref, out_all))
+    arrivals = []
+    for source, target in pairs:
+        for step in range(1, shards):
+            arrivals.append(
+                wire.send(source.at[ctx], target.at[shard, ctx], wire.line(step, shards))
+            )
+    gains = [
+        wire.send(gain_ref, gain_all.at[shard], wire.line(step, shards))
+        for step in range(1, shards)
+    ]
+    locals_ = []
+    for i, (source, target) in enumerate(((in_ref, in_all), (out_ref, out_all), (gain_ref, gain_all))):
+        copy = pltpu.make_async_copy(source, target.at[shard], local_sems.at[i])
+        copy.start()
+        locals_.append(copy)
+    gathers = []
+    rows = in_ref.shape[1]
+    for source, target in pairs:
+        for step in range(1, shards):
+            arrivals[len(gathers)].wait_recv()
+            origin = lax.rem(shard + shards - step, shards)
+            place = lambda who, target=target, origin=origin: target.at[origin, who]
+            gathers.append(
+                PlaneGather(wire, place(ctx), place, rows, half_rows(rows, len(gathers)))
+            )
+    for gather in gathers:
+        gather.forward()
+    for gather in gathers:
+        gather.corner()
+    for gather in gathers:
+        gather.settle()
+    for copy in gains:
+        copy.wait_recv()
+    for copy in locals_:
+        copy.wait()
+    wire.finish()
+
+
+def gather_weights(w_in, w_out, gains, ctx_size, shards):
+    rows = w_in.shape[0] // ctx_size
+    w_in = w_in.reshape(ctx_size, rows, -1)
+    w_out = w_out.reshape(ctx_size, rows, -1)
+    copies = 2 * (shards - 1) * (1 + PlaneGather.COPIES) + shards - 1
+    w_in, w_out, gains = pl.pallas_call(
+        functools.partial(gather_weights_kernel, shards),
+        name="gather_weights",
+        in_specs=[ANY] * 3,
+        out_specs=[ANY] * 3,
+        out_shape=[
+            jax.ShapeDtypeStruct((shards,) + w_in.shape, w_in.dtype),
+            jax.ShapeDtypeStruct((shards,) + w_out.shape, w_out.dtype),
+            jax.ShapeDtypeStruct((shards,) + gains.shape, gains.dtype),
+        ],
+        scratch_shapes=[dma_sems(3), dma_sems(copies), dma_sems(copies)],
+        compiler_params=comm_params(1),
+    )(w_in, w_out, gains)
+    width = shards * ctx_size * rows
+    return w_in.reshape(width, -1), w_out.reshape(width, -1), gains
+
+
+def gather_plane_kernel(in_ref, all_ref, local_sem, send_sems, recv_sems):
+    wire = Wire(send_sems, recv_sems)
+    wire.meet([wire.plane(mask) for mask in PLANE_PEERS])
+    place = lambda who: all_ref.at[who]
+    rows = in_ref.shape[0]
+    gather = PlaneGather(wire, in_ref, place, rows, rows // 2)
+    copy = pltpu.make_async_copy(in_ref, place(wire.ctx), local_sem)
+    copy.start()
+    gather.forward()
+    gather.corner()
+    gather.settle()
+    copy.wait()
+    wire.finish()
+
+
+def gather_plane(values, ctx_size):
+    return pl.pallas_call(
+        gather_plane_kernel,
+        name="gather_plane",
+        in_specs=[ANY],
+        out_specs=ANY,
+        out_shape=jax.ShapeDtypeStruct((ctx_size,) + values.shape, values.dtype),
+        scratch_shapes=[
+            pltpu.SemaphoreType.DMA,
+            dma_sems(PlaneGather.COPIES),
+            dma_sems(PlaneGather.COPIES),
+        ],
+        compiler_params=comm_params(2),
+    )(values)
+
+
+def sum_plane_kernel(in_ref, out_ref, own, pair, first, second, local_sem, send_sems, recv_sems):
+    wire = Wire(send_sems, recv_sems)
+    wire.meet([wire.plane(mask) for mask in PLANE_PEERS])
+    total = PlaneSum(wire, in_ref, own, pair, first, second, local_sem)
+    total.step_one()
+    total.step_two()
+
+    def store(part, value):
+        out_ref[part] = value
+
+    total.result(store)
+    wire.finish()
+
+
+def sum_plane(values):
+    rows, columns = values.shape[3:]
+    return pl.pallas_call(
+        sum_plane_kernel,
+        name="sum_plane",
+        in_specs=[ANY],
+        out_specs=pl.BlockSpec(memory_space=pltpu.VMEM),
+        out_shape=jax.ShapeDtypeStruct((4, rows, columns), jnp.float32),
+        scratch_shapes=plane_sum_scratch(rows, columns)
+        + [pltpu.SemaphoreType.DMA, dma_sems(PlaneSum.COPIES), dma_sems(PlaneSum.COPIES)],
+        compiler_params=comm_params(3),
+    )(values)
+
+
+def close_kernel(
+    shards, g_out, g_in, m_in, m_out, gain, out_all, in_all, m_in_all, m_out_all, gain_out,
+    *scratch,
+):
+    sums = (scratch[:4], scratch[4:8])
+    mine, arrived = (scratch[8], scratch[9]), (scratch[10], scratch[11])
+    done = (scratch[12], scratch[13])
+    gain_now, gain_in, gain_line = scratch[14:17]
+    local_sems, send_sems, recv_sems = scratch[17:]
+    wire = Wire(send_sems, recv_sems)
+    ctx, shard = wire.ctx, wire.shard
+    wire.meet(
+        [wire.plane(mask) for mask in PLANE_PEERS] + [wire.line(s, shards) for s in range(1, shards)]
+    )
+    totals = [
+        PlaneSum(wire, source, *sums[i], local_sems.at[i]) for i, source in enumerate((g_out, g_in))
+    ]
+    gain_now[...] = gain[...]
+
+    def gain_start(at):
+        return wire.send(gain_now, gain_in.at[at], wire.plane(PLANE_PEERS[at]))
+
+    def gain_add(at, copy):
+        copy.wait_recv()
+        wire.sent(copy)
+        gain_now[...] += gain_in[at]
+
+    gain_copy = gain_start(0)
+    for total in totals:
+        total.step_one()
+    gain_add(0, gain_copy)
+    gain_copy = gain_start(1)
+    for total in totals:
+        total.step_two()
+    gain_add(1, gain_copy)
+    gain_copy = gain_start(2)
+    gathers, locals_ = [], []
+    for i, (source, target) in enumerate(((m_in, m_in_all), (m_out, m_out_all))):
+        place = lambda who, target=target: target.at[who]
+        rows = source.shape[0]
+        gathers.append(PlaneGather(wire, source, place, rows, half_rows(rows, i)))
+        copy = pltpu.make_async_copy(source, place(ctx), local_sems.at[2 + i])
+        copy.start()
+        locals_.append(copy)
+    lines = []
+    for i, total in enumerate(totals):
+
+        def store(part, value, i=i):
+            mine[i][part] = value.astype(jnp.bfloat16)
+
+        total.result(store)
+        lines.append(
+            [
+                wire.send(
+                    mine[i].at[lax.rem(shard + step, shards)],
+                    arrived[i].at[step - 1],
+                    wire.line(step, shards),
+                )
+                for step in range(1, shards)
+            ]
+        )
+    gain_add(2, gain_copy)
+    gain_copies = [
+        wire.send(
+            gain_now.at[lax.rem(shard + step, shards)], gain_line.at[step - 1], wire.line(step, shards)
+        )
+        for step in range(1, shards)
+    ]
+    small = []
+    for i, target in enumerate((out_all, in_all)):
+        for copy in lines[i]:
+            copy.wait_recv()
+        value = mine[i][shard].astype(jnp.float32)
+        for step in range(shards - 1):
+            value += arrived[i][step].astype(jnp.float32)
+        done[i][...] = value.astype(jnp.bfloat16)
+        place = lambda who, target=target: target.at[who]
+        rows = target.shape[1]
+        small.append(PlaneGather(wire, done[i], place, rows, half_rows(rows, i)))
+        copy = pltpu.make_async_copy(done[i], place(ctx), local_sems.at[4 + i])
+        copy.start()
+        locals_.append(copy)
+    for copy in gain_copies:
+        copy.wait_recv()
+    value = gain_now[shard]
+    for step in range(shards - 1):
+        value += gain_line[step]
+    gain_out[...] = value
+    for gather in gathers + small:
+        gather.forward()
+    for gather in gathers + small:
+        gather.corner()
+    for gather in gathers + small:
+        gather.settle()
+    for copy in locals_:
+        copy.wait()
+    wire.finish()
+
+
+def close(g_out, g_in, m_in, m_out, gain, ctx_size, shards):
+    sums, mine, arrived, done = [], [], [], []
+    for grad in (g_out, g_in):
+        rows, columns = grad.shape[3:]
+        sums += plane_sum_scratch(rows, columns)
+        mine.append(pltpu.VMEM((shards, rows, columns), jnp.bfloat16))
+        arrived.append(pltpu.VMEM((shards - 1, rows, columns), jnp.bfloat16))
+        done.append(pltpu.VMEM((rows, columns), jnp.bfloat16))
+    gains = [
+        pltpu.VMEM(gain.shape, jnp.float32),
+        pltpu.VMEM((3,) + gain.shape, jnp.float32),
+        pltpu.VMEM((shards - 1,) + gain.shape[1:], jnp.float32),
+    ]
+    copies = 2 * (PlaneSum.COPIES + 2 * PlaneGather.COPIES + shards - 1) + 3 + shards - 1
+    whole = lambda shape: jax.ShapeDtypeStruct((ctx_size,) + shape, jnp.bfloat16)
+    return pl.pallas_call(
+        functools.partial(close_kernel, shards),
+        name="close",
+        in_specs=[ANY] * 4 + [pl.BlockSpec(memory_space=pltpu.VMEM)],
+        out_specs=[ANY] * 4 + [pl.BlockSpec(memory_space=pltpu.VMEM)],
+        out_shape=[
+            whole(g_out.shape[3:]),
+            whole(g_in.shape[3:]),
+            whole(m_in.shape),
+            whole(m_out.shape),
+            jax.ShapeDtypeStruct(gain.shape[1:], jnp.float32),
+        ],
+        scratch_shapes=sums + mine + arrived + done + gains + [dma_sems(6), dma_sems(copies), dma_sems(copies)],
+        compiler_params=comm_params(4),
+    )(g_out, g_in, m_in, m_out, gain)
+
+
+def finish_in_kernel(shards, chips, main, rest, in_ref, out_ref):
+    per_shard = chips * (main + rest)
+    split = shards * main
+    for core in range(2):
+        for shard in range(shards):
+            start = (core * shards + shard) * per_shard
+            for chip in range(chips):
+                block = in_ref[chip * 2 + core, :, shard * main : (shard + 1) * main]
+                out_ref[:, start + chip * main : start + (chip + 1) * main] = block.astype(jnp.float32)
+            tails = [
+                in_ref[chip * 2 + core, :, split : split + shards * rest].astype(jnp.float32)[
+                    :, shard * rest : (shard + 1) * rest
+                ]
+                for chip in range(chips)
+            ]
+            out_ref[:, start + chips * main : start + per_shard] = jnp.concatenate(tails, axis=1)
+
+
+def finish_in(values, shards, main, rest):
+    ctx_size, rows, units = values.shape
+    tile = rows // 8
+    return pl.pallas_call(
+        functools.partial(finish_in_kernel, shards, ctx_size // 2, main, rest),
+        name="finish_in",
+        grid=(rows // tile,),
+        in_specs=[pl.BlockSpec((ctx_size, tile, units), lambda i: (0, i, 0))],
+        out_specs=pl.BlockSpec((tile, 2 * FF), lambda i: (i, 0)),
+        out_shape=jax.ShapeDtypeStruct((rows, 2 * FF), jnp.float32),
+        compiler_params=pltpu.CompilerParams(vmem_limit_bytes=VMEM_LIMIT),
+    )(values)
+
+
+def finish_out_kernel(chips, main, rest, in_ref, out_ref):
+    chip = pl.program_id(1)
+    out_ref[pl.ds(chip * main, main), :] = in_ref[0, :main, :].astype(jnp.float32)
+    out_ref[pl.ds(chips * main + chip * rest, rest), :] = in_ref[0, main:, :].astype(jnp.float32)
+
+
+def finish_out(values, main, rest):
+    ctx_size, units, half = values.shape
+    chips = ctx_size // 2
+    return pl.pallas_call(
+        functools.partial(finish_out_kernel, chips, main, rest),
+        name="finish_out",
+        grid=(2, chips),
+        in_specs=[pl.BlockSpec((1, units, half), lambda k, q: (q * 2 + k, 0, 0))],
+        out_specs=pl.BlockSpec((chips * units, half), lambda k, q: (0, k)),
+        out_shape=jax.ShapeDtypeStruct((chips * units, 2 * half), jnp.float32),
+        compiler_params=pltpu.CompilerParams(vmem_limit_bytes=VMEM_LIMIT),
+    )(values)
 
 
 class Layout:
@@ -67,6 +749,7 @@
         self.rest = units - self.main
         self.per_shard = FF // self.shards
         self.rest_start = self.chips * self.main
+        self.plane = ctx_size == 8 and fsdp_size == 4
 
     def xor(self, values, mask):
         pairs = [(i, i ^ mask) for i in range(self.ctx_size)]
@@ -159,10 +842,13 @@
 
     def reduce_mlp_in(self, gate, up):
         total = low(self.sum_pair(gate, up))
-        total = lax.psum_scatter(total, "fsdp", scatter_dimension=0, tiled=True)
-        rows = total.shape[0]
-        every = lax.all_gather(total, "ctx", axis=0)
-        every = every.reshape(self.chips, 2, rows, total.shape[1])
+        return lax.psum_scatter(total, "fsdp", scatter_dimension=0, tiled=True)
+
+    def order_mlp_in(self, every):
+        rows = every.shape[1]
+        if self.main:
+            return finish_in(every, self.shards, self.main, self.rest)
+        every = every.reshape(self.chips, 2, rows, every.shape[2])
         split = self.shards * self.main
         main = every[..., :split].reshape(self.chips, 2, rows, self.shards, self.main)
         rest = every[..., split:].reshape(self.chips, 2, rows, self.shards, self.rest)
@@ -177,8 +863,12 @@
         main = total[:split].reshape(self.shards, self.main, width // 2)
         rest = total[split:].reshape(self.shards, self.rest, width // 2)
         total = jnp.concatenate([main, rest], axis=1)
-        total = lax.psum_scatter(total, "fsdp", scatter_dimension=0, tiled=True)[0]
-        every = lax.all_gather(total, "ctx", axis=0)
+        return lax.psum_scatter(total, "fsdp", scatter_dimension=0, tiled=True)[0]
+
+    def order_mlp_out(self, every):
+        if self.main:
+            return finish_out(every, self.main, self.rest)
+        width = 2 * every.shape[2]
         every = every.reshape(self.chips, 2, self.main + self.rest, width // 2)
         main = every[:, :, : self.main].transpose(0, 2, 1, 3).reshape(-1, width)
         rest = every[:, :, self.main :].transpose(0, 2, 1, 3).reshape(-1, width)
@@ -193,7 +883,7 @@
 
     def reduce_whole(self, grad):
         rows = grad.shape[0] // self.shards
-        total = low(grad).reshape(self.shards, rows, grad.shape[1])
+        total = grad.reshape(self.shards, rows, grad.shape[1])
         total = lax.psum_scatter(total, "ctx", scatter_dimension=1, tiled=True)
         total = lax.psum_scatter(total, "fsdp", scatter_dimension=0, tiled=True)[0]
         return lax.all_gather(total, "ctx", axis=0, tiled=True).astype(jnp.float32)
@@ -204,31 +894,21 @@
         return lax.dynamic_slice_in_dim(total, lax.axis_index("fsdp") * rows, rows)
 
 
-def attend(queries, key_value, row_places, row_segment, places_all, segment_all):
-    distance = row_places[:, None] - places_all[None, :]
-    allowed = (row_segment[:, None] == segment_all[None, :]) & (distance >= 0) & (distance < WINDOW)
-    scores = dot_nt(queries, key_value[:, :HD])
-    peak = jnp.max(jnp.where(allowed, scores, -1e30), axis=1)
-    weights_exp = jnp.where(allowed, jnp.exp(scores - peak[:, None]), 0.0)
-    row_total = jnp.sum(weights_exp, axis=1)
-    attended = dot(low(weights_exp), key_value[:, HD:]) / row_total[:, None]
-    return attended, peak + jnp.log(row_total)
-
-
-def attend_back(
-    queries, key_value, grad_mixed, row_delta, log_total, row_places, row_segment, places_all, segment_all
-):
-    distance = row_places[:, None] - places_all[None, :]
-    allowed = (row_segment[:, None] == segment_all[None, :]) & (distance >= 0) & (distance < WINDOW)
-    key_part = key_value[:, :HD]
-    scores = dot_nt(queries, key_part)
-    probs = jnp.where(allowed, jnp.exp(scores - log_total[:, None]), 0.0)
-    grad_probs = dot_nt(grad_mixed, key_value[:, HD:])
-    grad_scores = low(probs * (grad_probs - row_delta[:, None]))
-    grad_query = dot(grad_scores, key_part)
-    grad_key = dot_tn(grad_scores, queries)
-    grad_value = dot_tn(low(probs), grad_mixed)
-    return grad_query, jnp.concatenate([grad_key, grad_value], axis=1)
+def window_blocks(places_all, own_places, seq_ends, block):
+    count = places_all.shape[0] // block
+    blocks = places_all.reshape(count, block)
+    held = blocks[:, 0] // block
+    at = jnp.arange(count, dtype=jnp.int32)
+    position = jnp.sum(jnp.where(held[None, :] == at[:, None], at[None, :], 0), axis=1)
+    span = (WINDOW + block - 2) // block + 1
+    first = own_places.reshape(-1, block)[:, 0] // block
+    wanted = first[:, None] - (span - 1) + jnp.arange(span, dtype=jnp.int32)[None, :]
+    where = position[jnp.maximum(wanted, 0)]
+    key_place = jnp.where((wanted >= 0)[:, :, None], blocks[where], jnp.int32(1 << 30))
+    key_place = key_place.reshape(where.shape[0], 1, span * block)
+    starts = jnp.where(seq_ends[None, :] <= own_places[:, None], seq_ends[None, :], 0)
+    least = jnp.maximum(jnp.max(starts, axis=1), own_places - (WINDOW - 1))
+    return where, key_place, least
 
 
 def per_device(
@@ -246,49 +926,46 @@
     cotangent,
 ):
     lay = Layout(ctx_size, fsdp_size)
-    own_rows = tokens.shape[1]
+    own_rows, width = tokens.shape[1:]
     query_dim = H * HD
+    block = own_rows // ROUNDS
     places_all = order[0]
-    seq_ends = jnp.cumsum(lengths[0])
-    segment_all = jnp.sum((seq_ends[None, :] <= places_all[:, None]).astype(jnp.int32), axis=1)
     own_places = lax.dynamic_slice_in_dim(places_all, lay.index * own_rows, own_rows)
-    own_segment = lax.dynamic_slice_in_dim(segment_all, lay.index * own_rows, own_rows)
-    row_places = jnp.repeat(own_places, H)
-    row_segment = jnp.repeat(own_segment, H)
-
-    in_attn = lay.gather_whole(w_attn_in)
-    out_attn = lay.gather_whole(w_attn_out)
-    gains = lax.all_gather(jnp.stack([norm_attn, norm_mlp]), "fsdp", axis=1, tiled=True)
-    gain_attn = gains[0].astype(jnp.float32)
-    gain_mlp = gains[1].astype(jnp.float32)
+    where, key_place, least = window_blocks(
+        places_all, own_places, jnp.cumsum(lengths[0]), block
+    )
+    frequency = 10000.0 ** (-jnp.arange(HD // 2, dtype=jnp.float32) / (HD // 2))
+    angles = own_places.astype(jnp.float32)[:, None] * frequency[None, :]
+    cosine = jnp.cos(angles)
+    sine_part = jnp.sin(angles)
+    cosine = jnp.concatenate([cosine, cosine], axis=1)
+    sine_part = jnp.concatenate([-sine_part, sine_part], axis=1)
+
+    gains = jnp.stack([norm_attn, norm_mlp]).astype(jnp.float32)
+    if lay.plane:
+        gains = jnp.pad(gains, ((0, 6), (0, 0)))
+        in_attn, out_attn, gains = gather_weights(
+            w_attn_in, w_attn_out, gains, ctx_size, fsdp_size
+        )
+        gains = gains.transpose(1, 0, 2).reshape(8, width)
+    else:
+        in_attn = lay.gather_whole(w_attn_in)
+        out_attn = lay.gather_whole(w_attn_out)
+        gains = lax.all_gather(gains, "fsdp", axis=1, tiled=True)
     gate_in, up_in = lay.gather_mlp_in(w_mlp_in)
     out_mlp = lay.gather_mlp_out(w_mlp_out)
     upstream = cotangent[0]
     upstream_all = lay.gather_chips(upstream)
 
-    inputs = tokens[0].astype(jnp.float32)
-    normed_one, norm_one_back = jax.vjp(rms_norm, inputs, gain_attn)
-    normed_one = low(normed_one)
-    projected = dot(normed_one, in_attn)
-    place_float = own_places.astype(jnp.float32)
-
-    def query_map(part):
-        return rotate(part, place_float) * HD ** (-0.5)
-
-    def key_map(part):
-        return rotate(part[:, None, :], place_float)[:, 0, :]
-
-    query_rot, query_back = jax.vjp(query_map, projected[:, :query_dim].reshape(own_rows, H, HD))
-    key_rot, key_back = jax.vjp(key_map, projected[:, query_dim : query_dim + HD])
-    queries = low(query_rot).reshape(own_rows * H, HD)
-    key_value = jnp.concatenate([low(key_rot), low(projected[:, query_dim + HD :])], axis=1)
-    key_value = lax.all_gather(key_value, "ctx", axis=0, tiled=True)
-    attended, log_total = attend(
-        queries, key_value, row_places, row_segment, places_all, segment_all
-    )
-    mixed = low(attended.reshape(own_rows, query_dim))
-    middle = inputs + dot(mixed, out_attn)
-    normed_two, norm_two_back = jax.vjp(rms_norm, middle, gain_mlp)
+    normed_one, queries, key_value = project(tokens[0], gains[:1], in_attn, cosine, sine_part)
+    if lay.plane:
+        key_value = gather_plane(key_value, ctx_size)
+    else:
+        key_value = lax.all_gather(key_value, "ctx", axis=0)
+    key_value = key_value.reshape(ctx_size * ROUNDS, block, 2 * HD)
+    mixed = attend(where, queries, key_value, key_place, own_places[:, None], least[:, None])
+    middle = tokens[0].astype(jnp.float32) + dot(mixed, out_attn)
+    normed_two, norm_two_back = jax.vjp(rms_norm, middle, gains[1])
     normed_all = lay.gather_chips(low(normed_two))
 
     gate = dot(normed_all, gate_in)
@@ -307,39 +984,70 @@
     grad_middle_norm, grad_gain_mlp = norm_two_back(grad_normed_two)
     grad_middle = upstream.astype(jnp.float32) + grad_middle_norm
     grad_branch = low(grad_middle)
-    grad_out_attn = lay.reduce_whole(dot_tn(mixed, grad_branch))
-    grad_mixed = low(dot_nt(grad_branch, out_attn)).reshape(own_rows * H, HD)
-    row_delta = jnp.sum(grad_mixed.astype(jnp.float32) * attended, axis=1)
-    grad_query, grad_keys = attend_back(
+    grad_out_attn = low(dot_tn(mixed, grad_branch))
+    grad_mixed = low(dot_nt(grad_branch, out_attn))
+
+    def repeated(values):
+        values = values.reshape(ROUNDS, 1, block)
+        return jnp.tile(values, (1, 1, HEADS_STEP))
+
+    target = where % ROUNDS * ctx_size + where // ROUNDS
+    grad_query, grad_kv = attend_back(
+        jnp.concatenate([where, target], axis=1),
         queries,
         key_value,
         grad_mixed,
-        row_delta,
-        log_total,
-        row_places,
-        row_segment,
-        places_all,
-        segment_all,
-    )
-    grad_kv = lax.psum_scatter(low(grad_keys), "ctx", scatter_dimension=0, tiled=True)
-    grad_kv = grad_kv.astype(jnp.float32)
-    grad_query_raw = query_back(grad_query.reshape(own_rows, H, HD))[0].reshape(own_rows, query_dim)
-    grad_key_raw = key_back(grad_kv[:, :HD])[0]
-    grad_projected = low(
-        jnp.concatenate([grad_query_raw, grad_key_raw, grad_kv[:, HD:]], axis=1)
-    )
-    grad_in_attn = lay.reduce_whole(dot_tn(normed_one, grad_projected))
+        key_place.reshape(ROUNDS, -1, 1),
+        repeated(own_places),
+        repeated(least),
+        cosine,
+        sine_part,
+    )
+    if lay.plane:
+        grad_kv = sum_plane(grad_kv.reshape(ROUNDS, lay.chips, 2, block, 2 * HD))
+        grad_kv = grad_kv.reshape(own_rows, 2 * HD)
+    else:
+        grad_kv = grad_kv.reshape(ROUNDS, ctx_size, block, 2 * HD)
+        grad_kv = lax.psum_scatter(grad_kv, "ctx", scatter_dimension=1, tiled=True)
+        grad_kv = grad_kv.reshape(own_rows, 2 * HD).astype(jnp.float32)
+    grad_key = grad_kv[:, :HD] * cosine - jnp.roll(grad_kv[:, :HD], HD // 2, 1) * sine_part
+    grad_projected = jnp.concatenate([grad_query, low(grad_key), low(grad_kv[:, HD:])], axis=1)
+    grad_in_attn = low(dot_tn(normed_one, grad_projected))
+    _, norm_one_back = jax.vjp(rms_norm, tokens[0].astype(jnp.float32), gains[0])
     grad_inputs_norm, grad_gain_attn = norm_one_back(dot_nt(grad_projected, in_attn))
     grad_inputs = grad_middle + grad_inputs_norm
+    if lay.plane:
+        split = lambda grad: grad.reshape(fsdp_size, lay.chips, 2, -1, grad.shape[1])
+        grad_gains = jnp.stack([grad_gain_attn, grad_gain_mlp]).reshape(2, fsdp_size, -1)
+        grad_gains = jnp.pad(grad_gains.transpose(1, 0, 2), ((0, 0), (0, 6), (0, 0)))
+        grad_out_attn, grad_in_attn, grad_in_mlp, grad_out_mlp, grad_gains = close(
+            split(grad_out_attn),
+            split(grad_in_attn),
+            grad_in_mlp,
+            grad_out_mlp,
+            grad_gains,
+            ctx_size,
+            fsdp_size,
+        )
+        whole = lambda grad: grad.reshape(-1, grad.shape[2]).astype(jnp.float32)
+        grad_out_attn, grad_in_attn = whole(grad_out_attn), whole(grad_in_attn)
+        grad_gain_attn, grad_gain_mlp = grad_gains[0], grad_gains[1]
+    else:
+        grad_out_attn = lay.reduce_whole(grad_out_attn)
+        grad_in_attn = lay.reduce_whole(grad_in_attn)
+        grad_in_mlp = lax.all_gather(grad_in_mlp, "ctx", axis=0)
+        grad_out_mlp = lax.all_gather(grad_out_mlp, "ctx", axis=0)
+        grad_gain_attn = lay.reduce_gain(grad_gain_attn)
+        grad_gain_mlp = lay.reduce_gain(grad_gain_mlp)
     return (
         low(result)[None],
         grad_inputs[None],
-        lay.reduce_gain(grad_gain_attn),
+        grad_gain_attn,
         grad_in_attn,
         grad_out_attn,
-        lay.reduce_gain(grad_gain_mlp),
-        grad_in_mlp,
-        grad_out_mlp,
+        grad_gain_mlp,
+        lay.order_mlp_in(grad_in_mlp),
+        lay.order_mlp_out(grad_out_mlp),
     )
 
 

time: 1170 us -> 651 us (0.56)
  waiting for transfers between devices: 390 us -> 64.1 us
  Pallas kernels: 0 us -> 297 us
  blocking collectives: 192 us -> 0 us
  matrix products: 315 us -> 159 us
  local copies, waits for them, and re-layouts: 142 us -> 40.9 us
  other arithmetic: 87.1 us -> 50.7 us
    pallas_call x0 -> x9, Pallas kernels: none -> 297 us  [the longest x1 108 us: close(): pl.pallas_call(functools.partial(close_kernel, shards), name='close', in_...]
    reduce_scatter x7 -> x2, waiting for transfers between devices: 199 us -> 0.01 us  [the longest x1 0.01 us: reduce_mlp_out(): return lax.psum_scatter(total, 'fsdp', scatter_dimension=0, tiled=True)[0]]
    all_gather x5 -> x0, blocking collectives: 192 us -> none  [the longest x2 135 us: reduce_gain(): total = jnp.sum(lax.all_gather(grad, ('ctx', 'fsdp'), axis=0), axis=0)]
    all_gather x1, waiting for transfers between devices: 67.3 us -> 0.01 us  [gather_mlp_in(): mine = lax.all_gather(mine, 'fsdp', axis=0, tiled=True)]
    dot_general x7 -> x5, matrix products: 105 us -> 44.4 us  [dot_nt(): jnp.einsum('ab,cb->ac', left, right, preferred_element_type=jnp.float32)]
    dot_general x7 -> x4, matrix products: 105 us -> 49.6 us  [dot(): return jnp.dot(left, right, preferred_element_type=jnp.float32)]
    dot_general x7 -> x5, matrix products: 105 us -> 64.6 us  [dot_tn(): jnp.einsum('ab,ac->bc', left, right, preferred_element_type=jnp.float32)]
    reduce_sum x6 -> x1, other arithmetic: 30.5 us -> 0.11 us  [window_blocks(): jnp.sum(jnp.where(held[None, :] == at[:, None], at[None, :], 0), axis=1)]
  transfers between devices with their start and end apart: 36 -> 24, of which waited for: 18 -> 9; matrix products, arithmetic and copies ran while one was open for 27% -> 29% of each run, Pallas kernels for 0% -> 27%
where the time goes in v2:
time: 651 us; the launch traced here: 645 us
  Pallas kernels  297 us (46%)
  matrix products  159 us (24%)
  waiting for transfers between devices  64.1 us (10%)
  other arithmetic  50.7 us (8%)
  local copies, waits for them, and re-layouts  40.9 us (6%)
  starting transfers between devices  18.7 us (3%)
  between operations  14.8 us (2%)
    pallas_call x1, Pallas kernels, close(): pl.pallas_call(functools.partial(close_kernel, shards), name='close', in_...  108 us
    pallas_call x1, Pallas kernels, gather_weights(): pl.pallas_call(functools.partial(gather_weights_kernel, shards), name='ga...  83.7 us
    dot_general x5, matrix products, dot_tn(): jnp.einsum('ab,ac->bc', left, right, preferred_element_type=jnp.float32)  64.6 us
    ppermute x20, waiting for transfers between devices, xor(): return lax.ppermute(values, 'ctx', pairs)  64 us
    dot_general x4, matrix products, dot(): return jnp.dot(left, right, preferred_element_type=jnp.float32)  49.6 us
    dot_general x5, matrix products, dot_nt(): jnp.einsum('ab,cb->ac', left, right, preferred_element_type=jnp.float32)  44.4 us
    pallas_call x1, Pallas kernels, attend_back(): pl.pallas_call(functools.partial(attend_back_kernel, blocks, block), name...  33.2 us
    pallas_call x1, Pallas kernels, attend(): pl.pallas_call(functools.partial(attend_kernel, blocks, block), name='att...  20.8 us
  transfers between devices with their start and end apart: 24, of which 9 were waited for; matrix products, arithmetic and copies ran while one was open for 29% of the time, Pallas kernels for 27%

profile of v2, /device:TPU:0, one launch (start us, length us, event | category | flops | bytes accessed | tf_op | source)
XLA Modules:
  0.0 644.9 jit_solution(4063014365118649496)
XLA Ops:
  24.8 83.7 %gather_weights.1 = (bf16[4,8,48,1792]{3,2,1,0:T(8,128)(2,1)}, bf16[4,8,48,1536]{3,2,1,0:T(8,128)(2,1)}, f32[4,8,384]{2,1,0:T(8,128)}) custom-call(bf16[8,48,1792]{2,1,0:T(8,128)(2,1)} %bitcast.75, bf16[8,48,1536]{2,1,0:T(8,128)(2,1)} %bitcast.76, f32[8,384]{1,0:T(8,128)} %fusion.39.gain_ref), custom_call_target="tpu_custom_call" | custom-call | tf_op jit(solution)/shard_map/gather_weights/pallas_call | solution.py:480
  112.5 9.4 %project.1 = (bf16[384,1536]{1,0:T(8,128)(2,1)}, bf16[12,384,128]{2,1,0:T(8,128)(2,1)}, bf16[384,256]{1,0:T(8,128)(2,1)}) custom-call(bf16[384,1536]{1,0:T(8,128)(2,1)} %bitcast.61, f32[1,1536]{1,0:T(1,128)} %bitcast.79, bf16[1536,1792]{1,0:T(8,128)(2,1)} %bitcast.63, f32[384,128]{1,0:T(8,128)} %get-tuple-element.86.cos_ref, ...), custom_call_target="tpu_custom_call" | custom-call | tf_op jit(solution)/shard_map/project/pallas_call | solution.py:77
  121.8 12.4 %gather_plane.1 = bf16[8,384,256]{2,1,0:T(8,128)(2,1)} custom-call(bf16[384,256]{1,0:T(8,128)(2,1)} %get-tuple-element.24.in_ref), custom_call_target="tpu_custom_call" | custom-call | tf_op jit(solution)/shard_map/gather_plane/pallas_call | solution.py:513
  135.1 20.8 %attend.1 = bf16[384,1536]{1,0:T(8,128)(2,1)} custom-call(s32[4,12]{1,0:T(4,128)} %reshape.351.where_ref, bf16[12,384,128]{2,1,0:T(8,128)(2,1)} %get-tuple-element.23.q_ref, bf16[32,96,256]{2,1,0:T(8,128)(2,1)} %bitcast.59, s32[4,1,1152]{2,1,0:T(1,128)} %select_n.203.key_place_ref, s32[384,1]{1,0:T(8,128)} %copy-done.18, s32[384,1]{1,0:T(8,128)} %reshape_maximum_fusion.least_ref), custom_call_target="tpu_custom_call" | custom-call | tf_op jit(solution)/shard_map/attend/pallas_call | solution.py:152
  179.0 17.0 %collective-permute-done.1 = bf16[384,1536]{1,0:T(8,128)(2,1)} collective-permute-done((bf16[384,1536]{1,0:T(8,128)(2,1)}, bf16[384,1536]{1,0:T(8,128)(2,1)}, u32[]{:S(2)}, u32[]{:S(2)}) %collective-permute-start.1) | collective-permute-done | bytes 1179680 | tf_op jit(solution)/shard_map/ppermute | solution.py:756
  203.2 6.9 %collective-permute-done.13 = bf16[384,768]{1,0:T(8,128)(2,1)S(1)} collective-permute-done((bf16[384,768]{1,0:T(8,128)(2,1)S(1)}, bf16[384,768]{1,0:T(8,128)(2,1)S(1)}, u32[]{:S(2)}, u32[]{:S(2)}) %collective-permute-start.13) | collective-permute-done | bytes 589856 | tf_op jit(solution)/shard_map/ppermute | solution.py:756
  212.3 11.5 %fusion.18 = f32[1536,1152]{1,0:T(8,128)} fusion(bf16[1152,768]{1,0:T(8,128)(2,1)S(1)} %get-tuple-element.66, bf16[1152,768]{1,0:T(8,128)(2,1)S(1)} %get-tuple-element.65, bf16[384,768]{1,0:T(8,128)(2,1)S(1)} %collective-permute-done.13, bf16[384,768]{1,0:T(8,128)(2,1)S(1)} %collective-permute-done.12, bf16[384,1536]{1,0:T(8,128)(2,1)} %collective-permute-done.11, ...), kind=kOutput, calls=%fused_computation.51 | convolution fusion | flops 5466488832 | bytes 15335424 | tf_op jit(solution)/shard_map/ab,cb->ac/dot_general | solution.py:34
  224.9 12.6 %fusion.22 = f32[1536,1152]{1,0:T(8,128)} fusion(bf16[1536,1152]{1,0:T(8,128)(2,1)} %collective-permute-done.4, bf16[1536,1152]{1,0:T(8,128)(2,1)S(1)} %copy-done.43, pred[]{:T(512)S(6)} %eq.14, bf16[384,768]{1,0:T(8,128)(2,1)S(1)} %collective-permute-done.3, bf16[384,768]{1,0:T(8,128)(2,1)S(1)} %collective-permute-done.2, ...), kind=kOutput, calls=%fused_computation.61 | convolution fusion | flops 5461180416 | bytes 18874368 | tf_op jit(solution)/shard_map/dot_general | solution.py:30
  237.5 20.7 %fusion.6 = (bf16[1536,1152]{1,0:T(8,128)(2,1)}, bf16[1536,1152]{1,0:T(8,128)(2,1)}, bf16[1536,1152]{1,0:T(8,128)(2,1)}) fusion(f32[1536,1152]{1,0:T(8,128)} %fusion.18, f32[1536,1152]{1,0:T(8,128)} %fusion.22, bf16[1536,1152]{1,0:T(8,128)(2,1)S(1)} %copy-done.43, bf16[1536,1152]{1,0:T(8,128)(2,1)} %collective-permute-done.4, pred[]{:T(512)S(6)} %eq.14, ...), kind=kOutput, calls=%fused_computation.13 | convolution fusion | flops 5507186688 | bytes 36569088 | tf_op jit(solution)/shard_map/dot_general | solution.py:30
  258.2 9.7 %fusion.53 = f32[1152,1536]{1,0:T(8,128)S(1)} fusion(bf16[1536,1152]{1,0:T(8,128)(2,1)} %get-tuple-element.44, bf16[384,768]{1,0:T(8,128)(2,1)} %copy-done.45, bf16[384,768]{1,0:T(8,128)(2,1)} %copy-done.48, bf16[384,1536]{1,0:T(8,128)(2,1)} %collective-permute-done.11, bf16[384,1536]{1,0:T(8,128)(2,1)} %collective-permute-done.10, ...), kind=kOutput, calls=%fused_computation.155 | convolution fusion | flops 5459410944 | bytes 15335424 | tf_op jit(solution)/shard_map/ab,ac->bc/dot_general | solution.py:38
  270.9 18.6 %fusion.55 = f32[1536,1152]{1,0:T(8,128)S(1)} fusion(bf16[1536,1152]{1,0:T(8,128)(2,1)S(1)} %copy-done.52, bf16[384,768]{1,0:T(8,128)(2,1)S(1)} %copy-done.47, bf16[384,768]{1,0:T(8,128)(2,1)S(1)} %copy-done.50, bf16[384,1536]{1,0:T(8,128)(2,1)} %collective-permute-done.1, bf16[384,1536]{1,0:T(8,128)(2,1)} %collective-permute-done, ...), kind=kOutput, calls=%fused_computation.157 | convolution fusion | flops 5459410944 | bytes 15335424 | tf_op jit(solution)/shard_map/ab,ac->bc/dot_general | solution.py:38
  289.5 24.6 %select_convert_fusion = (bf16[1536,1152]{1,0:T(8,128)(2,1)}, f32[1536,1152]{1,0:T(8,128)}) fusion(f32[1536,1152]{1,0:T(8,128)S(1)} %fusion.55, pred[]{:T(512)S(6)} %eq.14, bf16[1536,1152]{1,0:T(8,128)(2,1)} %get-tuple-element.43, bf16[384,768]{1,0:T(8,128)(2,1)S(1)} %copy-done.47, bf16[384,768]{1,0:T(8,128)(2,1)S(1)} %copy-done.50, ...), kind=kOutput, calls=%fused_computation.15 | convolution fusion | flops 5461180416 | bytes 25952256 | tf_op jit(solution)/shard_map/ab,ac->bc/dot_general | solution.py:38
  314.1 11.3 %fusion.21 = f32[1536,1536]{1,0:T(8,128)} fusion(bf16[1536,1152]{1,0:T(8,128)(2,1)} %get-tuple-element.43, bf16[1536,1152]{1,0:T(8,128)(2,1)} %collective-permute-done.4, bf16[1536,1152]{1,0:T(8,128)(2,1)} %all-gather.4.cloned.1.call-done, pred[]{:T(512)S(6)} %eq.14), kind=kOutput, calls=%fused_computation.60 | convolution fusion | flops 5437587456 | bytes 20054016 | tf_op jit(solution)/shard_map/ab,cb->ac/dot_general | solution.py:34
  325.5 12.7 %fusion.59 = (bf16[1536,1536]{1,0:T(8,128)(2,1)S(1)}, f32[1536,1536]{1,0:T(8,128)}) fusion(f32[1536,1536]{1,0:T(8,128)} %fusion.21, bf16[1536,1152]{1,0:T(8,128)(2,1)} %get-tuple-element.42, bf16[1536,1152]{1,0:T(8,128)(2,1)} %all-gather.4.cloned.1.call-done, bf16[1536,1152]{1,0:T(8,128)(2,1)} %collective-permute-done.4, pred[]{:T(512)S(6)} %eq.14), kind=kOutput, calls=%fused_computation.161 | convolution fusion | flops 5442306048 | bytes 34209792 | tf_op jit(solution)/shard_map/ab,cb->ac/dot_general | solution.py:34
  345.5 11.6 %fusion.60 = (bf16[1536,1536]{1,0:T(8,128)(2,1)S(1)}, f32[1536,1536]{1,0:T(8,128)}) fusion(bf16[1536,1152]{1,0:T(8,128)(2,1)} %get-tuple-element.44, bf16[1152,768]{1,0:T(8,128)(2,1)} %copy-done.20, bf16[1152,768]{1,0:T(8,128)(2,1)} %copy-done.19), kind=kOutput, calls=%fused_computation.162 | convolution fusion | flops 5445255168 | bytes 21233664 | tf_op jit(solution)/shard_map/dot_general | solution.py:30
  363.7 5.8 add_convert_fusion
  383.0 17.1 %collective-permute-done.17 = bf16[384,1536]{1,0:T(8,128)(2,1)S(1)} collective-permute-done((bf16[384,1536]{1,0:T(8,128)(2,1)S(1)}, bf16[384,1536]{1,0:T(8,128)(2,1)S(1)}, u32[]{:S(2)}, u32[]{:S(2)}) %collective-permute-start.17) | collective-permute-done | bytes 1179680 | tf_op jit(solution)/shard_map/ppermute | solution.py:756
  406.4 18.2 %collective-permute-done.9 = bf16[384,1536]{1,0:T(8,128)(2,1)} collective-permute-done((bf16[384,1536]{1,0:T(8,128)(2,1)}, bf16[384,1536]{1,0:T(8,128)(2,1)}, u32[]{:S(2)}, u32[]{:S(2)}) %collective-permute-start.9) | collective-permute-done | bytes 1179680 | tf_op jit(solution)/shard_map/ppermute | solution.py:756
  435.1 33.2 %attend_back.1 = (bf16[384,1536]{1,0:T(8,128)(2,1)}, bf16[32,96,256]{2,1,0:T(8,128)(2,1)}) custom-call(s32[4,24]{1,0:T(4,128)} %pad_add_fusion.where_ref, bf16[12,384,128]{2,1,0:T(8,128)(2,1)} %get-tuple-element.23.q_ref, bf16[32,96,256]{2,1,0:T(8,128)(2,1)} %bitcast.60, bf16[384,1536]{1,0:T(8,128)(2,1)} %convolution_convert_fusion.2.grad_ref, ...), custom_call_target="tpu_custom_call" | custom-call | tf_op jit(solution)/shard_map/attend_back/pallas_call | solution.py:244
  468.3 12.9 %sum_plane.1 = f32[4,96,256]{2,1,0:T(8,128)} custom-call(bf16[4,4,2,96,256]{4,3,2,1,0:T(8,128)(2,1)} %bitcast.74), custom_call_target="tpu_custom_call" | custom-call | tf_op jit(solution)/shard_map/sum_plane/pallas_call | solution.py:544
  493.7 7.4 %convolution_convert_fusion = bf16[1536,1792]{1,0:T(8,128)(2,1)} fusion(bf16[384,1536]{1,0:T(8,128)(2,1)} %get-tuple-element.28, bf16[384,128]{1,0:T(8,128)(2,1)} %copy-done.28, bf16[384,128]{1,0:T(8,128)(2,1)} %copy-done.27, bf16[384,1536]{1,0:T(8,128)(2,1)} %get-tuple-element.26), kind=kOutput, calls=%fused_computation.5 | convolution fusion | flops 2120810496 | bytes 8060928 | tf_op jit(solution)/shard_map/ab,ac->bc/dot_general | solution.py:38
  507.4 107.8 %close.1 = (bf16[8,48,1536]{2,1,0:T(8,128)(2,1)}, bf16[8,48,1792]{2,1,0:T(8,128)(2,1)}, bf16[8,384,1152]{2,1,0:T(8,128)(2,1)}, bf16[8,288,768]{2,1,0:T(8,128)(2,1)}, f32[8,384]{1,0:T(8,128)}) custom-call(bf16[4,4,2,48,1536]{4,3,2,1,0:T(8,128)(2,1)} %bitcast.66, bf16[4,4,2,48,1792]{4,3,2,1,0:T(8,128)(2,1)} %bitcast.65, ...), custom_call_target="tpu_custom_call" | custom-call | tf_op jit(solution)/shard_map/close/pallas_call | solution.py:670
  621.4 7.1 %finish_out.1 = f32[1152,1536]{1,0:T(8,128)} custom-call(bf16[8,288,768]{2,1,0:T(8,128)(2,1)} %get-tuple-element.33.in_ref), custom_call_target="tpu_custom_call" | custom-call | tf_op jit(solution)/shard_map/finish_out/pallas_call | solution.py:728
  628.5 9.6 %finish_in.1 = f32[384,9216]{1,0:T(8,128)} custom-call(bf16[8,384,1152]{2,1,0:T(8,128)(2,1)} %get-tuple-element.32.in_ref), custom_call_target="tpu_custom_call" | custom-call | tf_op jit(solution)/shard_map/finish_in/pallas_call | solution.py:708
  (256 shorter events, 127.4 us)
Async XLA Ops:
  7.2 153.6 %all-gather.6.cloned.1.call-start = ((), (), s32[]{:S(2)}) async-start(), calls=%async_computation.5 | async-start | bytes 2211840 | tf_op jit(solution)/shard_map/all_gather | solution.py:828
  10.3 159.4 %all-gather.4.cloned.1.call-start = ((), (), s32[]{:S(2)}) async-start(), calls=%async_computation.2 | async-start | bytes 4423680 | tf_op jit(solution)/shard_map/all_gather | solution.py:822
  14.2 493.2 %reduce-scatter.5.cloned.1.call-start = ((), (), s32[]{:S(2)}) async-start(), calls=%async_computation.4 | async-start | bytes 2211840 | tf_op jit(solution)/shard_map/reduce_scatter | solution.py:866
  14.2 155.5 %collective-permute-start.11 = (bf16[384,1536]{1,0:T(8,128)(2,1)}, bf16[384,1536]{1,0:T(8,128)(2,1)}, u32[]{:S(2)}, u32[]{:S(2)}) collective-permute-start(bf16[384,1536]{1,0:T(8,128)(2,1)} %bitcast.15), channel_id=1, source_target_pairs={{0,16},{4,20},{8,24},{12,28},{16,0},{20,4},{24,8},{28,12},{1,17},{... | collective-permute-start | bytes 3538952 | tf_op jit(solution)/shard_map/ppermute | solution.py:756
  17.2 160.0 %collective-permute-start.10 = (bf16[384,1536]{1,0:T(8,128)(2,1)}, bf16[384,1536]{1,0:T(8,128)(2,1)}, u32[]{:S(2)}, u32[]{:S(2)}) collective-permute-start(bf16[384,1536]{1,0:T(8,128)(2,1)} %bitcast.15), channel_id=1, source_target_pairs={{0,8},{4,12},{8,0},{12,4},{16,24},{20,28},{24,16},{28,20},{1,9},{5... | collective-permute-start | bytes 3538952 | tf_op jit(solution)/shard_map/ppermute | solution.py:756
  166.0 34.4 %collective-permute-start.5 = (bf16[1152,768]{1,0:T(8,128)(2,1)}, bf16[1152,768]{1,0:T(8,128)(2,1)}, u32[]{:S(2)}, u32[]{:S(2)}) collective-permute-start(bf16[1152,768]{1,0:T(8,128)(2,1)} %pad_maximum_fusion.3), channel_id=1, source_target_pairs={{0,4},{4,0},{8,12},{12,8},{16,20},{20,16},{24,28},{28,24},{1,5},{5... | collective-permute-start | bytes 5308424 | tf_op jit(solution)/shard_map/ppermute | solution.py:756
  167.7 28.3 %collective-permute-start.1 = (bf16[384,1536]{1,0:T(8,128)(2,1)}, bf16[384,1536]{1,0:T(8,128)(2,1)}, u32[]{:S(2)}, u32[]{:S(2)}) collective-permute-start(bf16[384,1536]{1,0:T(8,128)(2,1)} %multiply_convert_fusion.2), channel_id=1, source_target_pairs={{0,16},{4,20},{8,24},{12,28},{16,0},{20,4},{24,8},{28,12},{1,17},{... | collective-permute-start | bytes 3538952 | tf_op jit(solution)/shard_map/ppermute | solution.py:756
  168.3 29.4 %collective-permute-start = (bf16[384,1536]{1,0:T(8,128)(2,1)}, bf16[384,1536]{1,0:T(8,128)(2,1)}, u32[]{:S(2)}, u32[]{:S(2)}) collective-permute-start(bf16[384,1536]{1,0:T(8,128)(2,1)} %multiply_convert_fusion.2), channel_id=1, source_target_pairs={{0,8},{4,12},{8,0},{12,4},{16,24},{20,28},{24,16},{28,20},{1,9},{5... | collective-permute-start | bytes 3538952 | tf_op jit(solution)/shard_map/ppermute | solution.py:756
  169.8 54.1 %collective-permute-start.4 = (bf16[1536,1152]{1,0:T(8,128)(2,1)}, bf16[1536,1152]{1,0:T(8,128)(2,1)}, u32[]{:S(2)}, u32[]{:S(2)}) collective-permute-start(bf16[1536,1152]{1,0:T(8,128)(2,1)} %all-gather.4.cloned.1.call-done), channel_id=1, source_target_pairs={{0,4},{4,0},{8,12},{12,8},{16,20},{20,16},{24,28},{28,24},{1,5},{5... | collective-permute-start | bytes 10616840 | tf_op jit(solution)/shard_map/ppermute | solution.py:756
  177.2 32.8 %collective-permute-start.13 = (bf16[384,768]{1,0:T(8,128)(2,1)S(1)}, bf16[384,768]{1,0:T(8,128)(2,1)S(1)}, u32[]{:S(2)}, u32[]{:S(2)}) collective-permute-start(bf16[384,768]{1,0:T(8,128)(2,1)S(1)} %slice.174), channel_id=1, source_target_pairs={{0,8},{4,12},{8,0},{12,4},{16,24},{20,28},{24,16},{28,20},{1,9},{5... | collective-permute-start | bytes 1769480 | tf_op jit(solution)/shard_map/ppermute | solution.py:756
  196.0 16.3 %collective-permute-start.12 = (bf16[384,768]{1,0:T(8,128)(2,1)S(1)}, bf16[384,768]{1,0:T(8,128)(2,1)S(1)}, u32[]{:S(2)}, u32[]{:S(2)}) collective-permute-start(bf16[384,768]{1,0:T(8,128)(2,1)S(1)} %slice.173), channel_id=1, source_target_pairs={{0,16},{4,20},{8,24},{12,28},{16,0},{20,4},{24,8},{28,12},{1,17},{... | collective-permute-start | bytes 1769480 | tf_op jit(solution)/shard_map/ppermute | solution.py:756
  197.8 26.1 %collective-permute-start.3 = (bf16[384,768]{1,0:T(8,128)(2,1)S(1)}, bf16[384,768]{1,0:T(8,128)(2,1)S(1)}, u32[]{:S(2)}, u32[]{:S(2)}) collective-permute-start(bf16[384,768]{1,0:T(8,128)(2,1)S(1)} %slice.164), channel_id=1, source_target_pairs={{0,8},{4,12},{8,0},{12,4},{16,24},{20,28},{24,16},{28,20},{1,9},{5... | collective-permute-start | bytes 1769480 | tf_op jit(solution)/shard_map/ppermute | solution.py:756
  200.4 23.5 %collective-permute-start.2 = (bf16[384,768]{1,0:T(8,128)(2,1)S(1)}, bf16[384,768]{1,0:T(8,128)(2,1)S(1)}, u32[]{:S(2)}, u32[]{:S(2)}) collective-permute-start(bf16[384,768]{1,0:T(8,128)(2,1)S(1)} %slice.163), channel_id=1, source_target_pairs={{0,16},{4,20},{8,24},{12,28},{16,0},{20,4},{24,8},{28,12},{1,17},{... | collective-permute-start | bytes 1769480 | tf_op jit(solution)/shard_map/ppermute | solution.py:756
  269.5 72.2 %collective-permute-start.19 = (bf16[1152,768]{1,0:T(8,128)(2,1)}, bf16[1152,768]{1,0:T(8,128)(2,1)}, u32[]{:S(2)}, u32[]{:S(2)}) collective-permute-start(bf16[1152,768]{1,0:T(8,128)(2,1)} %select_convert_fusion.1), channel_id=1, source_target_pairs={{0,4},{4,0},{8,12},{12,8},{16,20},{20,16},{24,28},{28,24},{1,5},{5... | collective-permute-start | bytes 5308424 | tf_op jit(solution)/shard_map/ppermute | solution.py:756
  314.1 49.6 %collective-permute-start.18 = (bf16[1536,1152]{1,0:T(8,128)(2,1)}, bf16[1536,1152]{1,0:T(8,128)(2,1)S(1)}, u32[]{:S(2)}, u32[]{:S(2)}) collective-permute-start(bf16[1536,1152]{1,0:T(8,128)(2,1)} %get-tuple-element.84), channel_id=1, source_target_pairs={{0,4},{4,0},{8,12},{12,8},{16,20},{20,16},{24,28},{28,24},{1,5},{5... | collective-permute-start | bytes 10616840 | tf_op jit(solution)/shard_map/ppermute | solution.py:756
  339.6 20.8 %collective-permute-start.14 = (bf16[384,768]{1,0:T(8,128)(2,1)}, bf16[384,768]{1,0:T(8,128)(2,1)}, u32[]{:S(2)}, u32[]{:S(2)}) collective-permute-start(bf16[384,768]{1,0:T(8,128)(2,1)} %get-tuple-element.57), channel_id=1, source_target_pairs={{0,8},{4,12},{8,0},{12,4},{16,24},{20,28},{24,16},{28,20},{1,9},{5... | collective-permute-start | bytes 1769480 | tf_op jit(solution)/shard_map/ppermute | solution.py:756
  340.2 20.2 %collective-permute-start.16 = (bf16[384,768]{1,0:T(8,128)(2,1)}, bf16[384,768]{1,0:T(8,128)(2,1)}, u32[]{:S(2)}, u32[]{:S(2)}) collective-permute-start(bf16[384,768]{1,0:T(8,128)(2,1)} %get-tuple-element.58), channel_id=1, source_target_pairs={{0,16},{4,20},{8,24},{12,28},{16,0},{20,4},{24,8},{28,12},{1,17},{... | collective-permute-start | bytes 1769480 | tf_op jit(solution)/shard_map/ppermute | solution.py:756
  345.5 161.9 %reduce-scatter.3.cloned.1.call-start = ((), (), s32[]{:S(2)}) async-start(), calls=%async_computation.3 | async-start | bytes 4423680 | tf_op jit(solution)/shard_map/reduce_scatter | solution.py:845
  358.5 16.4 %collective-permute-start.6 = (bf16[384,768]{1,0:T(8,128)(2,1)}, bf16[384,768]{1,0:T(8,128)(2,1)}, u32[]{:S(2)}, u32[]{:S(2)}) collective-permute-start(bf16[384,768]{1,0:T(8,128)(2,1)} %get-tuple-element.61), channel_id=1, source_target_pairs={{0,8},{4,12},{8,0},{12,4},{16,24},{20,28},{24,16},{28,20},{1,9},{5... | collective-permute-start | bytes 1769480 | tf_op jit(solution)/shard_map/ppermute | solution.py:756
  359.1 15.9 %collective-permute-start.8 = (bf16[384,768]{1,0:T(8,128)(2,1)}, bf16[384,768]{1,0:T(8,128)(2,1)}, u32[]{:S(2)}, u32[]{:S(2)}) collective-permute-start(bf16[384,768]{1,0:T(8,128)(2,1)} %get-tuple-element.62), channel_id=1, source_target_pairs={{0,16},{4,20},{8,24},{12,28},{16,0},{20,4},{24,8},{28,12},{1,17},{... | collective-permute-start | bytes 1769480 | tf_op jit(solution)/shard_map/ppermute | solution.py:756
  370.8 29.2 %collective-permute-start.17 = (bf16[384,1536]{1,0:T(8,128)(2,1)S(1)}, bf16[384,1536]{1,0:T(8,128)(2,1)S(1)}, u32[]{:S(2)}, u32[]{:S(2)}) collective-permute-start(bf16[384,1536]{1,0:T(8,128)(2,1)S(1)} %pad_maximum_fusion.9), channel_id=1, source_target_pairs={{0,8},{4,12},{8,0},{12,4},{16,24},{20,28},{24,16},{28,20},{1,9},{5... | collective-permute-start | bytes 3538952 | tf_op jit(solution)/shard_map/ppermute | solution.py:756
  371.7 29.0 %collective-permute-start.15 = (bf16[384,1536]{1,0:T(8,128)(2,1)S(1)}, bf16[384,1536]{1,0:T(8,128)(2,1)S(1)}, u32[]{:S(2)}, u32[]{:S(2)}) collective-permute-start(bf16[384,1536]{1,0:T(8,128)(2,1)S(1)} %pad_maximum_fusion.8), channel_id=1, source_target_pairs={{0,16},{4,20},{8,24},{12,28},{16,0},{20,4},{24,8},{28,12},{1,17},{... | collective-permute-start | bytes 3538952 | tf_op jit(solution)/shard_map/ppermute | solution.py:756
  378.5 46.1 %collective-permute-start.9 = (bf16[384,1536]{1,0:T(8,128)(2,1)}, bf16[384,1536]{1,0:T(8,128)(2,1)}, u32[]{:S(2)}, u32[]{:S(2)}) collective-permute-start(bf16[384,1536]{1,0:T(8,128)(2,1)} %pad_maximum_fusion.7), channel_id=1, source_target_pairs={{0,8},{4,12},{8,0},{12,4},{16,24},{20,28},{24,16},{28,20},{1,9},{5... | collective-permute-start | bytes 3538952 | tf_op jit(solution)/shard_map/ppermute | solution.py:756
  381.1 43.8 %collective-permute-start.7 = (bf16[384,1536]{1,0:T(8,128)(2,1)}, bf16[384,1536]{1,0:T(8,128)(2,1)}, u32[]{:S(2)}, u32[]{:S(2)}) collective-permute-start(bf16[384,1536]{1,0:T(8,128)(2,1)} %pad_maximum_fusion.6), channel_id=1, source_target_pairs={{0,16},{4,20},{8,24},{12,28},{16,0},{20,4},{24,8},{28,12},{1,17},{... | collective-permute-start | bytes 3538952 | tf_op jit(solution)/shard_map/ppermute | solution.py:756
  (55 other events, 647.2 us)
Sparse Core Ops, SparseCore 0:
  10.4 69.1 all-gather.5
  81.8 69.1 all-gather.3
  345.6 35.6 reduce-scatter.4
  383.5 65.4 reduce-scatter.2

commit v3 on v2

--- a/solution.py
+++ b/solution.py
@@ -38,11 +38,37 @@
     return jnp.einsum("ab,ac->bc", left, right, preferred_element_type=jnp.float32)
 
 
+def nt_dot(left, right):
+    return lax.dot_general(left, right, (((1,), (1,)), ((), ())), preferred_element_type=jnp.float32)
+
+
+def tn_dot(left, right):
+    return lax.dot_general(left, right, (((0,), (0,)), ((), ())), preferred_element_type=jnp.float32)
+
+
 def low(values):
     return values.astype(jnp.bfloat16)
 
 
 VMEM_LIMIT = 56 * 1024 * 1024
+MLP_VMEM = 62 * 1024 * 1024
+
+def gain_row(ref, which):
+    parts = [ref[shard, which : which + 1, :] for shard in range(ref.shape[0])]
+    return jnp.concatenate(parts, axis=1)
+
+
+def norm_scale(values):
+    return lax.rsqrt(jnp.mean(values * values, axis=-1, keepdims=True) + EPS)
+
+
+def norm_back(values, gain, incoming):
+    scale = norm_scale(values)
+    weighted = incoming * gain
+    inner = jnp.mean(weighted * values, axis=-1, keepdims=True)
+    grad = scale * weighted - values * (scale * scale * scale * inner)
+    return grad, jnp.sum(incoming * values * scale, axis=0, keepdims=True)
+
 
 def project_kernel(heads, x_ref, gain_ref, w_ref, cos_ref, sin_ref, normed_ref, q_ref, kv_ref):
     step = pl.program_id(0)
@@ -50,8 +76,7 @@
     @pl.when(step == 0)
     def _():
         x = x_ref[...].astype(jnp.float32)
-        scale = lax.rsqrt(jnp.mean(x * x, axis=-1, keepdims=True) + EPS)
-        normed_ref[...] = (x * scale * gain_ref[...]).astype(jnp.bfloat16)
+        normed_ref[...] = (x * norm_scale(x) * gain_row(gain_ref, 0)).astype(jnp.bfloat16)
 
     part = jnp.dot(normed_ref[...], w_ref[...], preferred_element_type=jnp.float32)
     cosine, sine_part = cos_ref[...], sin_ref[...]
@@ -80,7 +105,7 @@
         name="project",
         in_specs=[
             whole(rows, width),
-            whole(1, width),
+            whole(*gain.shape),
             pl.BlockSpec((width, 2 * HD), lambda i: (0, i)),
             whole(rows, HD),
             whole(rows, HD),
@@ -102,7 +127,7 @@
 HEADS_STEP = 4
 
 
-def attend_kernel(blocks, block, where_ref, q_ref, kv_ref, key_place_ref, place_ref, least_ref, out_ref, window, bias):
+def attend_kernel(blocks, block, where_ref, q_ref, kv_ref, key_place_ref, bounds_ref, out_ref, window, bias):
     r = pl.program_id(0)
 
     @pl.when(pl.program_id(1) == 0)
@@ -110,7 +135,7 @@
         for j in range(blocks):
             window[j * block : (j + 1) * block, :] = kv_ref[where_ref[r, j]]
         key_place = key_place_ref[0]
-        allowed = (key_place <= place_ref[...]) & (key_place >= least_ref[...])
+        allowed = (key_place <= bounds_ref[:, :1]) & (key_place >= bounds_ref[:, 1:])
         bias[...] = jnp.where(allowed, 0.0, -1e30)
 
     queries = q_ref[...].reshape(HEADS_STEP * block, HD)
@@ -128,8 +153,8 @@
         out_ref[:, j * HD : (j + 1) * HD] = mixed[j * block : (j + 1) * block]
 
 
-def attend(where, queries, kv_blocks, key_place, place, least):
-    rounds, blocks = where.shape
+def attend(where, queries, kv_blocks, key_place, bounds):
+    rounds, blocks = where.shape[0], where.shape[1] // 2
     heads, rows, _ = queries.shape
     block = rows // rounds
     span = blocks * block
@@ -140,8 +165,7 @@
             pl.BlockSpec((HEADS_STEP, block, HD), lambda r, h, *_: (h, r, 0)),
             pl.BlockSpec(kv_blocks.shape, lambda r, h, *_: (0, 0, 0)),
             pl.BlockSpec((1, 1, span), lambda r, h, *_: (r, 0, 0)),
-            pl.BlockSpec((block, 1), lambda r, h, *_: (r, 0)),
-            pl.BlockSpec((block, 1), lambda r, h, *_: (r, 0)),
+            pl.BlockSpec((block, 2), lambda r, h, *_: (r, 0)),
         ],
         out_specs=pl.BlockSpec((block, HEADS_STEP * HD), lambda r, h, *_: (r, h)),
         scratch_shapes=[
@@ -155,11 +179,11 @@
         grid_spec=grid_spec,
         out_shape=jax.ShapeDtypeStruct((rows, heads * HD), jnp.bfloat16),
         compiler_params=pltpu.CompilerParams(vmem_limit_bytes=VMEM_LIMIT),
-    )(where, queries, kv_blocks, key_place, place, least)
+    )(where, queries, kv_blocks, key_place, bounds)
 
 
 def attend_back_kernel(
-    blocks, block, where_ref, q_ref, kv_ref, grad_ref, key_place_ref, place_ref, least_ref, cos_ref, sin_ref,
+    blocks, block, where_ref, q_ref, kv_ref, grad_ref, key_place_ref, bounds_ref, cos_ref, sin_ref,
     grad_q_ref, grad_kv_ref, window, bias, window_grad, total_grad,
 ):
     r, h = pl.program_id(0), pl.program_id(1)
@@ -173,8 +197,8 @@
     def _():
         for j in range(blocks):
             window[j * block : (j + 1) * block, :] = kv_ref[where_ref[r, j]]
-        key_place = key_place_ref[0]
-        allowed = (key_place <= place_ref[0]) & (key_place >= least_ref[0])
+        key_place = jnp.broadcast_to(key_place_ref[0], (8, blocks * block)).T[:, :1]
+        allowed = (key_place <= bounds_ref[0, :1, :]) & (key_place >= bounds_ref[0, 1:, :])
         bias[...] = jnp.where(allowed, 0.0, -1e30)
         window_grad[...] = jnp.zeros_like(window_grad)
 
@@ -211,7 +235,7 @@
         grad_kv_ref[...] = total_grad[...].astype(jnp.bfloat16)
 
 
-def attend_back(where, queries, kv_blocks, grads, key_place, place, least, cosine, sine_part):
+def attend_back(where, queries, kv_blocks, grads, key_place, bounds, cosine, sine_part):
     rounds, blocks = where.shape[0], where.shape[1] // 2
     heads, rows, _ = queries.shape
     block = rows // rounds
@@ -224,9 +248,8 @@
             pl.BlockSpec((HEADS_STEP, block, HD), lambda r, h, *_: (h, r, 0)),
             pl.BlockSpec(kv_blocks.shape, lambda r, h, *_: (0, 0, 0)),
             pl.BlockSpec((block, HEADS_STEP * HD), lambda r, h, *_: (r, h)),
-            pl.BlockSpec((1, span, 1), lambda r, h, *_: (r, 0, 0)),
-            pl.BlockSpec((1, 1, width), lambda r, h, *_: (r, 0, 0)),
-            pl.BlockSpec((1, 1, width), lambda r, h, *_: (r, 0, 0)),
+            pl.BlockSpec((1, 1, span), lambda r, h, *_: (r, 0, 0)),
+            pl.BlockSpec((1, 2, width), lambda r, h, *_: (r, 0, 0)),
             pl.BlockSpec((block, HD), lambda r, h, *_: (r, 0)),
             pl.BlockSpec((block, HD), lambda r, h, *_: (r, 0)),
         ],
@@ -250,7 +273,166 @@
             jax.ShapeDtypeStruct(kv_blocks.shape, jnp.bfloat16),
         ],
         compiler_params=pltpu.CompilerParams(vmem_limit_bytes=VMEM_LIMIT),
-    )(where, queries, kv_blocks, grads, key_place, place, least, cosine, sine_part)
+    )(where, queries, kv_blocks, grads, key_place, bounds, cosine, sine_part)
+
+
+ANY = pl.BlockSpec(memory_space=pl.ANY)
+MIDDLE_TILES = 3
+
+
+def whole_block(shape):
+    return pl.BlockSpec(shape, lambda i: (0,) * len(shape))
+
+
+def middle_kernel(x_ref, mixed_ref, gain_ref, w_ref, middle_ref, normed_ref):
+    step = pl.program_id(0)
+    tile = w_ref.shape[1]
+    columns = pl.ds(pl.multiple_of(step * tile, tile), tile)
+    middle_ref[:, columns] = x_ref[:, columns].astype(jnp.float32) + dot(mixed_ref[...], w_ref[...])
+
+    @pl.when(step == pl.num_programs(0) - 1)
+    def _():
+        values = middle_ref[...]
+        normed_ref[...] = low(values * norm_scale(values) * gain_row(gain_ref, 1))
+
+
+def middle_forward(x, mixed, gains, w):
+    rows, width = x.shape
+    inner = mixed.shape[1]
+    return pl.pallas_call(
+        middle_kernel,
+        name="middle",
+        grid=(MIDDLE_TILES,),
+        in_specs=[
+            whole_block((rows, width)),
+            whole_block((rows, inner)),
+            whole_block(gains.shape),
+            pl.BlockSpec((inner, width // MIDDLE_TILES), lambda i: (0, i)),
+        ],
+        out_specs=[whole_block((rows, width))] * 2,
+        out_shape=[
+            jax.ShapeDtypeStruct((rows, width), jnp.float32),
+            jax.ShapeDtypeStruct((rows, width), jnp.bfloat16),
+        ],
+        compiler_params=pltpu.CompilerParams(vmem_limit_bytes=VMEM_LIMIT),
+    )(x, mixed, gains, w)
+
+
+def middle_back_kernel(
+    grad_ref, middle_ref, upstream_ref, mixed_ref, gain_ref, w_ref,
+    grad_middle_ref, grad_mixed_ref, grad_w_ref, grad_gain_ref, token, branch,
+):
+    @pl.when(pl.program_id(0) == 0)
+    def _():
+        grad, grad_gain = norm_back(middle_ref[...], gain_row(gain_ref, 1), grad_ref[...])
+        total = upstream_ref[...].astype(jnp.float32) + grad
+        grad_middle_ref[...] = total
+        branch[...] = low(total)
+        grad_gain_ref[...] = grad_gain
+        token[...] = jnp.zeros_like(token)
+
+    grad_mixed_ref[...] = low(nt_dot(branch[...], w_ref[...]))
+    grad_w_ref[...] = low(tn_dot(mixed_ref[...], branch[...]))
+
+
+def middle_back(grad, middle, upstream, mixed, gains, w):
+    rows, width = middle.shape
+    inner = mixed.shape[1]
+    tile = inner // MIDDLE_TILES
+    return pl.pallas_call(
+        middle_back_kernel,
+        name="middle_back",
+        grid=(MIDDLE_TILES,),
+        in_specs=[
+            whole_block((rows, width)),
+            whole_block((rows, width)),
+            whole_block((rows, width)),
+            pl.BlockSpec((rows, tile), lambda i: (0, i)),
+            whole_block(gains.shape),
+            pl.BlockSpec((tile, width), lambda i: (i, 0)),
+        ],
+        out_specs=[
+            whole_block((rows, width)),
+            pl.BlockSpec((rows, tile), lambda i: (0, i)),
+            pl.BlockSpec((tile, width), lambda i: (i, 0)),
+            whole_block((1, width)),
+            whole_block(TOKEN),
+        ],
+        out_shape=[
+            jax.ShapeDtypeStruct((rows, width), jnp.float32),
+            jax.ShapeDtypeStruct((rows, inner), jnp.bfloat16),
+            jax.ShapeDtypeStruct((inner, width), jnp.bfloat16),
+            jax.ShapeDtypeStruct((1, width), jnp.float32),
+            token_shape(),
+        ],
+        scratch_shapes=[pltpu.VMEM((rows, width), jnp.bfloat16)],
+        compiler_params=pltpu.CompilerParams(vmem_limit_bytes=VMEM_LIMIT),
+    )(grad, middle, upstream, mixed, gains, w)
+
+
+def project_back_kernel(
+    grad_q_ref, grad_kv_ref, cos_ref, sin_ref, normed_ref, x_ref, grad_middle_ref, gain_ref, w_ref,
+    grad_w_ref, grad_x_ref, grad_gain_ref, joined, grad_normed,
+):
+    step = pl.program_id(0)
+    inner = grad_q_ref.shape[1]
+    tile = w_ref.shape[0]
+
+    @pl.when(step == 0)
+    def _():
+        joined[:, :inner] = grad_q_ref[...]
+        keys = grad_kv_ref[:, :HD]
+        keys = keys * cos_ref[...] - pltpu.roll(keys, HD // 2, 1) * sin_ref[...]
+        joined[:, inner : inner + HD] = low(keys)
+        joined[:, inner + HD :] = low(grad_kv_ref[:, HD:])
+
+    columns = pl.ds(pl.multiple_of(step * tile, tile), tile)
+    grad_normed[:, columns] = nt_dot(joined[...], w_ref[...])
+    grad_w_ref[...] = low(tn_dot(normed_ref[...], joined[...]))
+
+    @pl.when(step == pl.num_programs(0) - 1)
+    def _():
+        values = x_ref[...].astype(jnp.float32)
+        grad, grad_gain = norm_back(values, gain_row(gain_ref, 0), grad_normed[...])
+        grad_x_ref[...] = grad_middle_ref[...] + grad
+        grad_gain_ref[...] = grad_gain
+
+
+def project_back(grad_q, grad_kv, cosine, sine_part, normed, x, grad_middle, gains, w):
+    rows, width = x.shape
+    inner = w.shape[1]
+    tile = width // MIDDLE_TILES
+    return pl.pallas_call(
+        project_back_kernel,
+        name="project_back",
+        grid=(MIDDLE_TILES,),
+        in_specs=[
+            whole_block(grad_q.shape),
+            whole_block(grad_kv.shape),
+            whole_block(cosine.shape),
+            whole_block(cosine.shape),
+            pl.BlockSpec((rows, tile), lambda i: (0, i)),
+            whole_block((rows, width)),
+            whole_block((rows, width)),
+            whole_block(gains.shape),
+            pl.BlockSpec((tile, inner), lambda i: (i, 0)),
+        ],
+        out_specs=[
+            pl.BlockSpec((tile, inner), lambda i: (i, 0)),
+            whole_block((rows, width)),
+            whole_block((1, width)),
+        ],
+        out_shape=[
+            jax.ShapeDtypeStruct((width, inner), jnp.bfloat16),
+            jax.ShapeDtypeStruct((rows, width), jnp.float32),
+            jax.ShapeDtypeStruct((1, width), jnp.float32),
+        ],
+        scratch_shapes=[
+            pltpu.VMEM((rows, inner), jnp.bfloat16),
+            pltpu.VMEM((rows, width), jnp.float32),
+        ],
+        compiler_params=pltpu.CompilerParams(vmem_limit_bytes=VMEM_LIMIT),
+    )(grad_q, grad_kv, cosine, sine_part, normed, x, grad_middle, gains, w)
 
 
 MESH_ID = pl.DeviceIdType.MESH
@@ -417,7 +599,6 @@
     return pltpu.SemaphoreType.DMA((count,))
 
 
-ANY = pl.BlockSpec(memory_space=pl.ANY)
 PLANE_PEERS = (1, 2, 4)
 
 
@@ -427,102 +608,258 @@
     )
 
 
-def gather_weights_kernel(shards, in_ref, out_ref, gain_ref, in_all, out_all, gain_all, local_sems, send_sems, recv_sems):
+class Relay:
+    def __init__(self, source, stage, targets, sems):
+        self.stage, self.targets, self.sems = stage, targets, sems
+        self.load = pltpu.make_async_copy(source, stage, sems.at[0])
+        self.load.start()
+
+    def push(self):
+        self.load.wait()
+        self.stores = []
+        for i, (part, target) in enumerate(self.targets):
+            store = pltpu.make_async_copy(part, target, self.sems.at[1 + i])
+            store.start()
+            self.stores.append(store)
+
+    def settle(self):
+        for store in self.stores:
+            store.wait()
+
+
+TOKEN = (8, 128)
+
+
+def token_shape():
+    return jax.ShapeDtypeStruct(TOKEN, jnp.int32)
+
+
+def after(token, values):
+    return jnp.where(token[0, 0] != 0, jnp.zeros_like(values), values)
+
+
+def share_line_kernel(
+    shards, pack, in_ref, gain_a, gain_b, mlp_in, mlp_out, in_line, gain_all, mine, token,
+    gain_now, in_stage, packed, tiles, local_sems, load_sems, send_sems, recv_sems,
+):
     wire = Wire(send_sems, recv_sems)
     ctx, shard = wire.ctx, wire.shard
-    wire.meet(
-        [wire.plane(mask) for mask in PLANE_PEERS] + [wire.line(s, shards) for s in range(1, shards)]
-    )
-    pairs = ((in_ref, in_all), (out_ref, out_all))
-    arrivals = []
-    for source, target in pairs:
+    chip, core = ctx // 2, lax.rem(ctx, 2)
+    chips = pack.chips
+    relay = Relay(in_ref.at[ctx], in_stage, [(in_stage, in_line.at[shard])], local_sems.at[0])
+    gain_now[...] = jnp.zeros_like(gain_now)
+    gain_now[:1] = gain_a[...].astype(jnp.float32)
+    gain_now[1:2] = gain_b[...].astype(jnp.float32)
+    token[...] = jnp.zeros_like(token)
+    wire.meet([wire.line(step, shards) for step in range(1, shards)])
+    copies = []
+    for source, target in ((gain_now, gain_all), (in_ref.at[ctx], in_line)):
         for step in range(1, shards):
-            arrivals.append(
-                wire.send(source.at[ctx], target.at[shard, ctx], wire.line(step, shards))
-            )
-    gains = [
-        wire.send(gain_ref, gain_all.at[shard], wire.line(step, shards))
-        for step in range(1, shards)
+            copies.append(wire.send(source, target.at[shard], wire.line(step, shards)))
+    gain_copy = pltpu.make_async_copy(gain_now, gain_all.at[shard], local_sems.at[1, 0])
+    gain_copy.start()
+    relay.push()
+
+    loads = []
+
+    def load(source, target):
+        copy = pltpu.make_async_copy(source, target, load_sems.at[len(loads)])
+        copy.start()
+        loads.append(copy)
+
+    def strip(start, count):
+        return pl.ds(pl.multiple_of(start, LANES), count)
+
+    main, rest, half, tail, split = pack.main, pack.rest, pack.half, pack.tail, pack.split
+    per_shard = chips * (main + rest)
+    base = core * (shards * per_shard)
+    for part in range(shards):
+        start = base + part * per_shard
+        load(mlp_in.at[:, strip(start + chips * main, chips * rest)], tiles.at[part])
+        column = part * main
+        if column + main <= half:
+            source = mlp_in.at[:, strip(start + chip * main, main)]
+            load(source, packed.at[pl.ds(0, pack.rows), pl.ds(column, main)])
+            continue
+        for i, at in enumerate(range(0, pack.rows, split)):
+            source = mlp_in.at[pl.ds(at, split), strip(start + chip * main, main)]
+            load(source, packed.at[pl.ds(pack.rows, split), pl.ds(i * tail + column - half, main)])
+    columns = strip(core * half, half)
+    for start, count, row in (
+        (chip * main, main, pack.out_start),
+        (chips * main + chip * rest, rest, pack.out_start + main),
+    ):
+        source = mlp_out.at[pl.ds(pl.multiple_of(start, 16), count), columns]
+        load(source, packed.at[pl.ds(row, count), :])
+    for copy in loads:
+        copy.wait()
+    width = chips * rest
+    ends = [
+        pltpu.roll(tiles[part].astype(jnp.float32), lax.rem(width - chip * rest, width), 1)[:, :rest]
+        for part in range(shards)
     ]
-    locals_ = []
-    for i, (source, target) in enumerate(((in_ref, in_all), (out_ref, out_all), (gain_ref, gain_all))):
-        copy = pltpu.make_async_copy(source, target.at[shard], local_sems.at[i])
-        copy.start()
-        locals_.append(copy)
+    ends = low(jnp.concatenate(ends, axis=1))
+    for i, at in enumerate(range(0, pack.rows, split)):
+        column = i * tail + shards * main - half
+        packed[pack.rows : pack.rows + split, column : column + shards * rest] = ends[at : at + split]
+    mine_copy = pltpu.make_async_copy(packed, mine, local_sems.at[1, 1])
+    mine_copy.start()
+    relay.settle()
+    gain_copy.wait()
+    mine_copy.wait()
+    for copy in copies:
+        copy.wait_recv()
+    wire.finish()
+
+
+def gather_shards(wire, line, target, rows, shards, count):
     gathers = []
-    rows = in_ref.shape[1]
-    for source, target in pairs:
-        for step in range(1, shards):
-            arrivals[len(gathers)].wait_recv()
-            origin = lax.rem(shard + shards - step, shards)
-            place = lambda who, target=target, origin=origin: target.at[origin, who]
-            gathers.append(
-                PlaneGather(wire, place(ctx), place, rows, half_rows(rows, len(gathers)))
-            )
+    for step in range(1, shards):
+        origin = lax.rem(wire.shard + shards - step, shards)
+        place = lambda who, origin=origin: target.at[origin, who]
+        gathers.append(PlaneGather(wire, line.at[origin], place, rows, half_rows(rows, step + count)))
+    return gathers
+
+
+def relay_shards(wire, whole, line, target, stage, piece, shards, sems):
+    origins = [lax.rem(wire.shard + shards - step, shards) for step in range(1, shards)]
+    places = [(piece.at[origin], target.at[origin, wire.ctx]) for origin in origins]
+    return [
+        Relay(whole, stage, [(stage, target.at[wire.shard])], sems.at[0]),
+        Relay(line, piece, places, sems.at[1]),
+    ]
+
+
+def complete(gathers, relays):
+    for relay in relays:
+        relay.push()
     for gather in gathers:
         gather.forward()
     for gather in gathers:
         gather.corner()
     for gather in gathers:
         gather.settle()
-    for copy in gains:
+    for relay in relays:
+        relay.settle()
+
+
+def share_plane_kernel(
+    shards, in_ref, in_line, out_ref, in_all, out_line, token,
+    in_stage, in_piece, out_stage, local_sems, send_sems, recv_sems,
+):
+    wire = Wire(send_sems, recv_sems)
+    ctx, shard = wire.ctx, wire.shard
+    relays = relay_shards(wire, in_ref, in_line, in_all, in_stage, in_piece, shards, local_sems)
+    relays.append(
+        Relay(out_ref.at[ctx], out_stage, [(out_stage, out_line.at[shard])], local_sems.at[2])
+    )
+    token[...] = jnp.zeros_like(token)
+    wire.meet(
+        [wire.plane(mask) for mask in PLANE_PEERS] + [wire.line(s, shards) for s in range(1, shards)]
+    )
+    gathers = gather_shards(wire, in_line, in_all, in_ref.shape[1], shards, 0)
+    copies = [
+        wire.send(out_ref.at[ctx], out_line.at[shard], wire.line(step, shards))
+        for step in range(1, shards)
+    ]
+    complete(gathers, relays)
+    for copy in copies:
         copy.wait_recv()
-    for copy in locals_:
-        copy.wait()
     wire.finish()
 
 
-def gather_weights(w_in, w_out, gains, ctx_size, shards):
-    rows = w_in.shape[0] // ctx_size
-    w_in = w_in.reshape(ctx_size, rows, -1)
-    w_out = w_out.reshape(ctx_size, rows, -1)
-    copies = 2 * (shards - 1) * (1 + PlaneGather.COPIES) + shards - 1
-    w_in, w_out, gains = pl.pallas_call(
-        functools.partial(gather_weights_kernel, shards),
-        name="gather_weights",
+def gather_plane_kernel(
+    shards, kv_ref, out_ref, out_line, kv_all, out_all, token,
+    kv_stage, out_stage, out_piece, local_sems, send_sems, recv_sems,
+):
+    wire = Wire(send_sems, recv_sems)
+    ctx = wire.ctx
+    relays = relay_shards(wire, out_ref, out_line, out_all, out_stage, out_piece, shards, local_sems)
+    relays.append(Relay(kv_ref, kv_stage, [(kv_stage, kv_all.at[ctx])], local_sems.at[2]))
+    token[...] = jnp.zeros_like(token)
+    wire.meet([wire.plane(mask) for mask in PLANE_PEERS])
+    rows = kv_ref.shape[0]
+    gathers = [PlaneGather(wire, kv_ref, lambda who: kv_all.at[who], rows, rows // 2)]
+    gathers += gather_shards(wire, out_line, out_all, out_ref.shape[1], shards, 1)
+    complete(gathers, relays)
+    wire.finish()
+
+
+def like(values, *lead):
+    return jax.ShapeDtypeStruct(lead + values.shape[-2:], values.dtype)
+
+
+def stage_like(values, *lead):
+    return pltpu.VMEM(lead + values.shape[-2:], values.dtype)
+
+
+def share_line(w_in, gain_a, gain_b, mlp_in, mlp_out, pack, shards):
+    columns = gain_a.shape[1]
+    copies = 2 * (shards - 1)
+    loads = shards + shards + 1 + 2
+    return pl.pallas_call(
+        functools.partial(share_line_kernel, shards, pack),
+        name="share_line",
+        in_specs=[ANY] + [pl.BlockSpec(memory_space=pltpu.VMEM)] * 2 + [ANY] * 2,
+        out_specs=[ANY] * 3 + [pl.BlockSpec(memory_space=pltpu.VMEM)],
+        out_shape=[
+            like(w_in, shards),
+            jax.ShapeDtypeStruct((shards, 8, columns), jnp.float32),
+            jax.ShapeDtypeStruct((pack.total, pack.half), mlp_in.dtype),
+            token_shape(),
+        ],
+        scratch_shapes=[
+            pltpu.VMEM((8, columns), jnp.float32),
+            stage_like(w_in),
+            pltpu.VMEM((pack.total, pack.half), mlp_in.dtype),
+            pltpu.VMEM((shards, pack.rows, pack.chips * pack.rest), mlp_in.dtype),
+            pltpu.SemaphoreType.DMA((2, 2)),
+            dma_sems(loads),
+            dma_sems(copies),
+            dma_sems(copies),
+        ],
+        compiler_params=comm_params(1),
+    )(w_in, gain_a, gain_b, mlp_in, mlp_out)
+
+
+def share_plane(w_in, in_line, w_out, ctx_size, shards):
+    copies = (shards - 1) * (PlaneGather.COPIES + 1)
+    return pl.pallas_call(
+        functools.partial(share_plane_kernel, shards),
+        name="share_plane",
         in_specs=[ANY] * 3,
-        out_specs=[ANY] * 3,
-        out_shape=[
-            jax.ShapeDtypeStruct((shards,) + w_in.shape, w_in.dtype),
-            jax.ShapeDtypeStruct((shards,) + w_out.shape, w_out.dtype),
-            jax.ShapeDtypeStruct((shards,) + gains.shape, gains.dtype),
-        ],
-        scratch_shapes=[dma_sems(3), dma_sems(copies), dma_sems(copies)],
-        compiler_params=comm_params(1),
-    )(w_in, w_out, gains)
-    width = shards * ctx_size * rows
-    return w_in.reshape(width, -1), w_out.reshape(width, -1), gains
-
-
-def gather_plane_kernel(in_ref, all_ref, local_sem, send_sems, recv_sems):
-    wire = Wire(send_sems, recv_sems)
-    wire.meet([wire.plane(mask) for mask in PLANE_PEERS])
-    place = lambda who: all_ref.at[who]
-    rows = in_ref.shape[0]
-    gather = PlaneGather(wire, in_ref, place, rows, rows // 2)
-    copy = pltpu.make_async_copy(in_ref, place(wire.ctx), local_sem)
-    copy.start()
-    gather.forward()
-    gather.corner()
-    gather.settle()
-    copy.wait()
-    wire.finish()
-
-
-def gather_plane(values, ctx_size):
+        out_specs=[ANY] * 2 + [pl.BlockSpec(memory_space=pltpu.VMEM)],
+        out_shape=[like(w_in, shards, ctx_size), like(w_out, shards), token_shape()],
+        scratch_shapes=[
+            stage_like(w_in, ctx_size),
+            stage_like(w_in, shards),
+            stage_like(w_out),
+            pltpu.SemaphoreType.DMA((3, shards)),
+            dma_sems(copies),
+            dma_sems(copies),
+        ],
+        compiler_params=comm_params(6),
+    )(w_in, in_line, w_out)
+
+
+def gather_plane(key_value, w_out, out_line, ctx_size, shards):
+    copies = shards * PlaneGather.COPIES
     return pl.pallas_call(
-        gather_plane_kernel,
+        functools.partial(gather_plane_kernel, shards),
         name="gather_plane",
-        in_specs=[ANY],
-        out_specs=ANY,
-        out_shape=jax.ShapeDtypeStruct((ctx_size,) + values.shape, values.dtype),
+        in_specs=[ANY] * 3,
+        out_specs=[ANY] * 2 + [pl.BlockSpec(memory_space=pltpu.VMEM)],
+        out_shape=[like(key_value, ctx_size), like(w_out, shards, ctx_size), token_shape()],
         scratch_shapes=[
-            pltpu.SemaphoreType.DMA,
-            dma_sems(PlaneGather.COPIES),
-            dma_sems(PlaneGather.COPIES),
+            stage_like(key_value),
+            stage_like(w_out, ctx_size),
+            stage_like(w_out, shards),
+            pltpu.SemaphoreType.DMA((3, shards)),
+            dma_sems(copies),
+            dma_sems(copies),
         ],
         compiler_params=comm_params(2),
-    )(values)
+    )(key_value, w_out, out_line)
 
 
 def sum_plane_kernel(in_ref, out_ref, own, pair, first, second, local_sem, send_sems, recv_sems):
@@ -554,14 +891,14 @@
 
 
 def close_kernel(
-    shards, g_out, g_in, m_in, m_out, gain, out_all, in_all, m_in_all, m_out_all, gain_out,
+    shards, g_out, g_in, m_ref, gain_a, gain_b, out_all, in_all, m_all, gain_out,
     *scratch,
 ):
     sums = (scratch[:4], scratch[4:8])
     mine, arrived = (scratch[8], scratch[9]), (scratch[10], scratch[11])
     done = (scratch[12], scratch[13])
-    gain_now, gain_in, gain_line = scratch[14:17]
-    local_sems, send_sems, recv_sems = scratch[17:]
+    gain_now, gain_in, gain_line, stage = scratch[14:18]
+    local_sems, relay_sems, send_sems, recv_sems = scratch[18:]
     wire = Wire(send_sems, recv_sems)
     ctx, shard = wire.ctx, wire.shard
     wire.meet(
@@ -570,7 +907,13 @@
     totals = [
         PlaneSum(wire, source, *sums[i], local_sems.at[i]) for i, source in enumerate((g_out, g_in))
     ]
-    gain_now[...] = gain[...]
+    relay = Relay(m_ref, stage, [(stage, m_all.at[ctx])], relay_sems)
+    gain_now[...] = jnp.zeros_like(gain_now)
+    columns = gain_now.shape[2]
+    for part in range(shards):
+        span = slice(part * columns, (part + 1) * columns)
+        gain_now[part, :1] = gain_a[:, span]
+        gain_now[part, 1:2] = gain_b[:, span]
 
     def gain_start(at):
         return wire.send(gain_now, gain_in.at[at], wire.plane(PLANE_PEERS[at]))
@@ -589,14 +932,10 @@
         total.step_two()
     gain_add(1, gain_copy)
     gain_copy = gain_start(2)
-    gathers, locals_ = [], []
-    for i, (source, target) in enumerate(((m_in, m_in_all), (m_out, m_out_all))):
-        place = lambda who, target=target: target.at[who]
-        rows = source.shape[0]
-        gathers.append(PlaneGather(wire, source, place, rows, half_rows(rows, i)))
-        copy = pltpu.make_async_copy(source, place(ctx), local_sems.at[2 + i])
-        copy.start()
-        locals_.append(copy)
+    place = lambda who: m_all.at[who]
+    rows = m_ref.shape[0]
+    gathers, locals_ = [PlaneGather(wire, m_ref, place, rows, rows // 2)], []
+    relay.push()
     lines = []
     for i, total in enumerate(totals):
 
@@ -632,7 +971,7 @@
         place = lambda who, target=target: target.at[who]
         rows = target.shape[1]
         small.append(PlaneGather(wire, done[i], place, rows, half_rows(rows, i)))
-        copy = pltpu.make_async_copy(done[i], place(ctx), local_sems.at[4 + i])
+        copy = pltpu.make_async_copy(done[i], place(ctx), local_sems.at[2 + i])
         copy.start()
         locals_.append(copy)
     for copy in gain_copies:
@@ -649,10 +988,11 @@
         gather.settle()
     for copy in locals_:
         copy.wait()
+    relay.settle()
     wire.finish()
 
 
-def close(g_out, g_in, m_in, m_out, gain, ctx_size, shards):
+def close(g_out, g_in, m_part, gain_a, gain_b, ctx_size, shards):
     sums, mine, arrived, done = [], [], [], []
     for grad in (g_out, g_in):
         rows, columns = grad.shape[3:]
@@ -660,80 +1000,366 @@
         mine.append(pltpu.VMEM((shards, rows, columns), jnp.bfloat16))
         arrived.append(pltpu.VMEM((shards - 1, rows, columns), jnp.bfloat16))
         done.append(pltpu.VMEM((rows, columns), jnp.bfloat16))
-    gains = [
-        pltpu.VMEM(gain.shape, jnp.float32),
-        pltpu.VMEM((3,) + gain.shape, jnp.float32),
-        pltpu.VMEM((shards - 1,) + gain.shape[1:], jnp.float32),
+    gain_shape = (shards, 8, gain_a.shape[1] // shards)
+    rest = [
+        pltpu.VMEM(gain_shape, jnp.float32),
+        pltpu.VMEM((3,) + gain_shape, jnp.float32),
+        pltpu.VMEM((shards - 1,) + gain_shape[1:], jnp.float32),
+        pltpu.VMEM(m_part.shape, m_part.dtype),
+        dma_sems(4),
+        dma_sems(2),
     ]
-    copies = 2 * (PlaneSum.COPIES + 2 * PlaneGather.COPIES + shards - 1) + 3 + shards - 1
+    copies = 2 * (PlaneSum.COPIES + PlaneGather.COPIES + shards - 1) + PlaneGather.COPIES + 3 + shards - 1
     whole = lambda shape: jax.ShapeDtypeStruct((ctx_size,) + shape, jnp.bfloat16)
+    vmem = pl.BlockSpec(memory_space=pltpu.VMEM)
     return pl.pallas_call(
         functools.partial(close_kernel, shards),
         name="close",
-        in_specs=[ANY] * 4 + [pl.BlockSpec(memory_space=pltpu.VMEM)],
-        out_specs=[ANY] * 4 + [pl.BlockSpec(memory_space=pltpu.VMEM)],
+        in_specs=[ANY] * 3 + [vmem] * 2,
+        out_specs=[ANY] * 3 + [vmem],
         out_shape=[
             whole(g_out.shape[3:]),
             whole(g_in.shape[3:]),
-            whole(m_in.shape),
-            whole(m_out.shape),
-            jax.ShapeDtypeStruct(gain.shape[1:], jnp.float32),
-        ],
-        scratch_shapes=sums + mine + arrived + done + gains + [dma_sems(6), dma_sems(copies), dma_sems(copies)],
+            whole(m_part.shape),
+            jax.ShapeDtypeStruct(gain_shape[1:], jnp.float32),
+        ],
+        scratch_shapes=sums + mine + arrived + done + rest + [dma_sems(copies), dma_sems(copies)],
         compiler_params=comm_params(4),
-    )(g_out, g_in, m_in, m_out, gain)
-
-
-def finish_in_kernel(shards, chips, main, rest, in_ref, out_ref):
+    )(g_out, g_in, m_part, gain_a, gain_b)
+
+
+class Pack:
+    def __init__(self, rows, half, chips, units, main, rest):
+        self.rows, self.half, self.chips, self.main, self.rest = rows, half, chips, main, rest
+        self.tail = units - half
+        self.split = rows // (half // self.tail)
+        self.out_start = rows + self.split
+        self.total = self.out_start + main + rest
+
+    def in_spans(self, shard):
+        yield (0, self.rows), (0, self.half), (shard * self.rows, self.rows), (0, self.half)
+        for i, at in enumerate(range(0, self.rows, self.split)):
+            yield (
+                (self.rows, self.split),
+                (i * self.tail, self.tail),
+                (shard * self.rows + at, self.split),
+                (self.half, self.tail),
+            )
+
+    def out_spans(self, shard, shards):
+        yield (self.out_start, self.main), (shard * self.main, self.main)
+        yield (self.out_start + self.main, self.rest), (shards * self.main + shard * self.rest, self.rest)
+
+
+def finish_kernel(shards, chips, pack, step_rows, main_ref, tail_ref, out_part_ref, in_ref, out_ref):
+    step = pl.program_id(0)
+    main, rest, half, tail = pack.main, pack.rest, pack.half, pack.tail
     per_shard = chips * (main + rest)
-    split = shards * main
+
+    def columns_of(who, start, count):
+        if start + count <= half:
+            return main_ref[who, :, start : start + count]
+        at = start - half
+        return tails[who][:, at : at + count]
+
+    second = step >= pl.num_programs(0) // 2
+    tails = [
+        jnp.where(second, tail_ref[who, :, tail:], tail_ref[who, :, :tail])
+        for who in range(2 * chips)
+    ]
     for core in range(2):
         for shard in range(shards):
             start = (core * shards + shard) * per_shard
             for chip in range(chips):
-                block = in_ref[chip * 2 + core, :, shard * main : (shard + 1) * main]
-                out_ref[:, start + chip * main : start + (chip + 1) * main] = block.astype(jnp.float32)
-            tails = [
-                in_ref[chip * 2 + core, :, split : split + shards * rest].astype(jnp.float32)[
+                block = columns_of(chip * 2 + core, shard * main, main)
+                in_ref[:, start + chip * main : start + (chip + 1) * main] = block.astype(jnp.float32)
+            ends = [
+                columns_of(chip * 2 + core, shards * main, shards * rest).astype(jnp.float32)[
                     :, shard * rest : (shard + 1) * rest
                 ]
                 for chip in range(chips)
             ]
-            out_ref[:, start + chips * main : start + per_shard] = jnp.concatenate(tails, axis=1)
-
-
-def finish_in(values, shards, main, rest):
-    ctx_size, rows, units = values.shape
-    tile = rows // 8
+            in_ref[:, start + chips * main : start + per_shard] = jnp.concatenate(ends, axis=1)
+
+    for chip in range(chips):
+
+        @pl.when(step == chip)
+        def _(chip=chip):
+            for core in range(2):
+                columns = slice(core * half, (core + 1) * half)
+                block = out_part_ref[core]
+                out_ref[chip * main : (chip + 1) * main, columns] = block[:main].astype(jnp.float32)
+                start = chips * main + chip * rest
+                out_ref[start : start + rest, columns] = block[main:].astype(jnp.float32)
+
+
+def finish(values, pack, shards):
+    ctx_size = values.shape[0]
+    chips = ctx_size // 2
+    steps = 8
+    tile = pack.rows // steps
+    per_out = pack.main + pack.rest
+    assert pack.rows // pack.split == 2 and pack.split % tile == 0 and pack.out_start % per_out == 0
     return pl.pallas_call(
-        functools.partial(finish_in_kernel, shards, ctx_size // 2, main, rest),
-        name="finish_in",
-        grid=(rows // tile,),
-        in_specs=[pl.BlockSpec((ctx_size, tile, units), lambda i: (0, i, 0))],
-        out_specs=pl.BlockSpec((tile, 2 * FF), lambda i: (i, 0)),
-        out_shape=jax.ShapeDtypeStruct((rows, 2 * FF), jnp.float32),
+        functools.partial(finish_kernel, shards, chips, pack, tile),
+        name="finish",
+        grid=(steps,),
+        in_specs=[
+            pl.BlockSpec((ctx_size, tile, pack.half), lambda i: (0, i, 0)),
+            pl.BlockSpec(
+                (ctx_size, tile, pack.half),
+                lambda i: (0, pack.rows // tile + i % (pack.split // tile), 0),
+            ),
+            pl.BlockSpec(
+                (2, per_out, pack.half),
+                lambda i: (jnp.minimum(i, chips - 1), pack.out_start // per_out, 0),
+            ),
+        ],
+        out_specs=[
+            pl.BlockSpec((tile, 2 * FF), lambda i: (i, 0)),
+            whole_block((FF // shards, 2 * pack.half)),
+        ],
+        out_shape=[
+            jax.ShapeDtypeStruct((pack.rows, 2 * FF), jnp.float32),
+            jax.ShapeDtypeStruct((FF // shards, 2 * pack.half), jnp.float32),
+        ],
         compiler_params=pltpu.CompilerParams(vmem_limit_bytes=VMEM_LIMIT),
-    )(values)
-
-
-def finish_out_kernel(chips, main, rest, in_ref, out_ref):
-    chip = pl.program_id(1)
-    out_ref[pl.ds(chip * main, main), :] = in_ref[0, :main, :].astype(jnp.float32)
-    out_ref[pl.ds(chips * main + chip * rest, rest), :] = in_ref[0, main:, :].astype(jnp.float32)
-
-
-def finish_out(values, main, rest):
-    ctx_size, units, half = values.shape
-    chips = ctx_size // 2
+    )(values, values, values)
+
+
+TANH_SCALE = 0.7978845608028654
+TANH_CUBE = 0.044715
+UNIT_TILE = 384
+
+
+def mlp_kernel(
+    shards, pack, mine, x_own, c_own, c_x, c_y,
+    normed_grad, out_own, out_x, out_y, out_left, out_right, grad_part,
+    w_in, w_out, xs, cs, hidden, grads, part, from_x, from_y, corner_left, corner_right,
+    out_stage, pair_in, pair_out, local_sems, send_sems, recv_sems,
+):
+    wire = Wire(send_sems, recv_sems)
+    core = lax.rem(wire.ctx, 2)
+    other = 1 - core
+    rows, width = x_own.shape
+    half = width // 2
+    units = w_in.shape[2]
+    tiles = units // UNIT_TILE
+    left, right = pl.ds(0, half), pl.ds(half, half)
+    locals_ = []
+
+    def copy_in(source, target):
+        copy = pltpu.make_async_copy(source, target, local_sems.at[len(locals_)])
+        copy.start()
+        locals_.append(copy)
+        return copy
+
+    def spans():
+        for shard in range(shards):
+            for p_rows, p_columns, w_rows, w_columns in pack.in_spans(shard):
+                yield (shard, pl.ds(*p_rows), pl.ds(*p_columns)), w_in, (pl.ds(*w_rows), pl.ds(*w_columns))
+            for p_rows, w_rows in pack.out_spans(shard, shards):
+                yield (shard, pl.ds(*p_rows)), w_out, (pl.ds(*w_rows),)
+
+    loads = [copy_in(x_own, xs.at[0]), copy_in(c_own, cs.at[0])]
+    for here, target, there in spans():
+        loads.append(copy_in(mine.at[here], target.at[(core,) + there]))
+    late = [
+        copy_in(source, target)
+        for source, target in (
+            (c_x, cs.at[1]),
+            (c_y, cs.at[2]),
+        )
+    ]
+    wire.meet([wire.plane(mask) for mask in PLANE_PEERS])
+    x_copies = [
+        wire.send(x_own, xs.at[1], wire.plane(2)),
+        wire.send(x_own, xs.at[2], wire.plane(4)),
+    ]
+    swaps = [
+        wire.send(mine.at[here], target.at[(core,) + there], wire.plane(1))
+        for here, target, there in spans()
+    ]
+    for copy in loads:
+        copy.wait()
+    for copy in swaps:
+        copy.wait_recv()
+
+    def one_chunk(at):
+        def one_tile(tile, carry):
+            columns = pl.ds(pl.multiple_of(tile * UNIT_TILE, UNIT_TILE), UNIT_TILE)
+            gate = dot(xs[at], w_in[0, :, columns])
+            up = dot(xs[at], w_in[1, :, columns])
+            grad = nt_dot(cs[at, :, left], w_out[0, columns, :])
+            grad += nt_dot(cs[at, :, right], w_out[1, columns, :])
+            square = gate * gate
+            bend = jnp.tanh(TANH_SCALE * gate * (1.0 + TANH_CUBE * square))
+            lift = 0.5 + 0.5 * bend
+            value = gate * lift
+            slope = lift + (0.5 * TANH_SCALE) * gate * (1.0 - bend * bend) * (
+                1.0 + (3.0 * TANH_CUBE) * square
+            )
+            hidden[at, :, columns] = low(value * up)
+            grads[0, at, :, columns] = low(grad * up * slope)
+            grads[1, at, :, columns] = low(grad * value)
+            return carry
+
+        lax.fori_loop(0, tiles, one_tile, 0)
+
+        def one_half(span):
+            total = nt_dot(grads[0, at], w_in[0, span, :])
+            return total + nt_dot(grads[1, at], w_in[1, span, :])
+
+        return one_half
+
+    one_half = one_chunk(0)
+    for span in (left, right):
+        normed_grad[:, span] = one_half(span)
+    for copy in x_copies:
+        copy.wait_recv()
+    corners = [
+        wire.send(xs.at[1, :, left], xs.at[3, :, left], wire.plane(4)),
+        wire.send(xs.at[2, :, right], xs.at[3, :, right], wire.plane(2)),
+    ]
+    for copy in late:
+        copy.wait()
+    corners += [
+        wire.send(cs.at[1, :, left], cs.at[3, :, left], wire.plane(4)),
+        wire.send(cs.at[2, :, right], cs.at[3, :, right], wire.plane(2)),
+    ]
+    one_half = one_chunk(1)
+    part[0, :, left] = low(one_half(left))
+    early = [wire.send(part.at[0, :, left], from_x.at[:, left], wire.plane(2))]
+    part[0, :, right] = low(one_half(right))
+    one_half = one_chunk(2)
+    part[1, :, right] = low(one_half(right))
+    early.append(wire.send(part.at[1, :, right], from_y.at[:, right], wire.plane(4)))
+    part[1, :, left] = low(one_half(left))
+    for copy in corners:
+        copy.wait_recv()
+    one_half = one_chunk(3)
+    part[2, :, left] = low(one_half(left))
+    corner = [wire.send(part.at[2, :, left], corner_left, wire.plane(2))]
+    part[2, :, right] = low(one_half(right))
+    corner.append(wire.send(part.at[2, :, right], corner_right, wire.plane(4)))
+
+    for at, target in ((1, out_x), (2, out_y), (0, out_own), (3, None)):
+        slot = at % 2
+        if at in (0, 3):
+            for copy in out_copies[slot]:
+                copy.wait()
+        else:
+            out_copies = {} if at == 1 else out_copies
+        for n, span in enumerate((left, right)):
+            out_stage[slot, :, span] = low(dot(hidden[at], w_out[n]))
+        if target is None:
+            out_copies[slot] = [
+                copy_in(out_stage.at[slot, :, left], out_left),
+                copy_in(out_stage.at[slot, :, right], out_right),
+            ]
+        else:
+            out_copies[slot] = [copy_in(out_stage.at[slot], target)]
+
+    everything = lambda ref: ref[...].reshape(ref.shape[0] * rows, ref.shape[2])
+
+    def in_tile(which, tile):
+        columns = pl.ds(tile * UNIT_TILE, UNIT_TILE)
+        picked = grads[which, :, :, columns].reshape(4 * rows, UNIT_TILE)
+        return columns, tn_dot(everything(xs), picked)
+
+    pairs_in = []
+    for tile in range(tiles):
+        columns, value = in_tile(other, tile)
+        w_in[0, :, columns] = low(value)
+        pairs_in.append(wire.send(w_in.at[0, :, columns], pair_in.at[:, columns], wire.plane(1)))
+    merged = []
+    corner[0].wait_recv()
+    part[1, :, left] = add_low(part[1, :, left], corner_left[...])
+    merged.append(wire.send(part.at[1, :, left], from_y.at[:, left], wire.plane(4)))
+    corner[1].wait_recv()
+    part[0, :, right] = add_low(part[0, :, right], corner_right[...])
+    merged.append(wire.send(part.at[0, :, right], from_x.at[:, right], wire.plane(2)))
+
+    def out_tile(which, tile):
+        columns = pl.ds(tile * UNIT_TILE, UNIT_TILE)
+        picked = hidden[:, :, columns].reshape(4 * rows, UNIT_TILE)
+        span = pl.ds(pl.multiple_of(which * half, half), half)
+        return columns, tn_dot(picked, cs[:, :, span].reshape(4 * rows, half))
+
+    pairs_out = []
+    for tile in range(tiles):
+        span, value = out_tile(other, tile)
+        w_out[0, span, :] = low(value)
+        pairs_out.append(wire.send(w_out.at[0, span, :], pair_out.at[span, :], wire.plane(1)))
+    final = []
+    for tile in range(tiles):
+        columns, value = in_tile(core, tile)
+        pairs_in[tile].wait_recv()
+        w_in[1, :, columns] = low(value + pair_in[:, columns].astype(jnp.float32))
+    for tile in range(tiles):
+        span, value = out_tile(core, tile)
+        pairs_out[tile].wait_recv()
+        w_out[1, span, :] = low(value + pair_out[span, :].astype(jnp.float32))
+    for here, source, there in spans():
+        final.append(copy_in(source.at[(1,) + there], grad_part.at[here]))
+    for copy in early + merged:
+        copy.wait_recv()
+    normed_grad[...] += from_x[...].astype(jnp.float32) + from_y[...].astype(jnp.float32)
+    for copies in out_copies.values():
+        for copy in copies:
+            copy.wait()
+    for copy in final:
+        copy.wait()
+    wire.finish()
+
+
+def mlp(mine, x, upstream, pack):
+    rows, width = x.shape
+    half = width // 2
+    units = pack.half + pack.tail
+    shards = mine.shape[0]
+    low_shape = lambda *shape: jax.ShapeDtypeStruct(shape, jnp.bfloat16)
+    low_scratch = lambda *shape: pltpu.VMEM(shape, jnp.bfloat16)
+    parts = shards * (1 + pack.rows // pack.split + 2)
+    copies = parts + 6 + 2 + 2 + 2 + 2 * (units // UNIT_TILE)
+    locals_ = 2 + parts + 2 + 5 + parts
     return pl.pallas_call(
-        functools.partial(finish_out_kernel, chips, main, rest),
-        name="finish_out",
-        grid=(2, chips),
-        in_specs=[pl.BlockSpec((1, units, half), lambda k, q: (q * 2 + k, 0, 0))],
-        out_specs=pl.BlockSpec((chips * units, half), lambda k, q: (0, k)),
-        out_shape=jax.ShapeDtypeStruct((chips * units, 2 * half), jnp.float32),
-        compiler_params=pltpu.CompilerParams(vmem_limit_bytes=VMEM_LIMIT),
-    )(values)
+        functools.partial(mlp_kernel, shards, pack),
+        name="mlp",
+        in_specs=[ANY] * 5,
+        out_specs=[pl.BlockSpec(memory_space=pltpu.VMEM)] + [ANY] * 6,
+        out_shape=[
+            jax.ShapeDtypeStruct((rows, width), jnp.float32),
+            low_shape(rows, width),
+            low_shape(rows, width),
+            low_shape(rows, width),
+            low_shape(rows, half),
+            low_shape(rows, half),
+            low_shape(*mine.shape),
+        ],
+        scratch_shapes=[
+            low_scratch(2, width, units),
+            low_scratch(2, units, half),
+            low_scratch(4, rows, width),
+            low_scratch(4, rows, width),
+            low_scratch(4, rows, units),
+            low_scratch(2, 4, rows, units),
+            low_scratch(3, rows, width),
+            low_scratch(rows, width),
+            low_scratch(rows, width),
+            low_scratch(rows, half),
+            low_scratch(rows, half),
+            low_scratch(2, rows, width),
+            low_scratch(width, units),
+            low_scratch(units, half),
+            dma_sems(locals_),
+            dma_sems(copies),
+            dma_sems(copies),
+        ],
+        compiler_params=pltpu.CompilerParams(
+            collective_id=5, has_side_effects=True, vmem_limit_bytes=MLP_VMEM
+        ),
+    )(mine, x, *upstream)
 
 
 class Layout:
@@ -758,18 +1384,31 @@
     def same_core_groups(self):
         return [[chip * 2 + core for chip in range(self.chips)] for core in range(2)]
 
+    def from_neighbours(self, values):
+        return self.xor(values, 2), self.xor(values, 4)
+
+    def from_corner(self, from_x, from_y):
+        half = from_x.shape[1] // 2
+        return self.xor(from_x[:, :half], 4), self.xor(from_y[:, half:], 2)
+
+    def scatter_chip_blocks(self, own, to_x, to_y, left, right, token):
+        half = left.shape[1]
+        left = after(token, self.xor(left, 2))
+        right = after(token, self.xor(right, 4))
+        to_y = jnp.concatenate([add_low(to_y[:, :half], left), to_y[:, half:]], axis=1)
+        to_x = jnp.concatenate([to_x[:, :half], add_low(to_x[:, half:], right)], axis=1)
+        wide = lambda part: part.astype(jnp.float32)
+        return wide(own) + wide(self.xor(to_y, 4)) + wide(self.xor(to_x, 2))
+
     def gather_chips(self, values):
         if self.chips != 4:
             return lax.all_gather(
                 values, "ctx", axis=0, tiled=True, axis_index_groups=self.same_core_groups()
             )
-        half = values.shape[1] // 2
-        from_x = self.xor(values, 2)
-        from_y = self.xor(values, 4)
-        corner_left = self.xor(from_x[:, :half], 4)
-        corner_right = self.xor(from_y[:, half:], 2)
-        corner = jnp.concatenate([corner_left, corner_right], axis=1)
-        return jnp.concatenate([values, from_x, from_y, corner], axis=0)
+        from_x, from_y = self.from_neighbours(values)
+        left, right = self.from_corner(from_x, from_y)
+        own = values
+        return jnp.concatenate([own, from_x, from_y, jnp.concatenate([left, right], axis=1)], axis=0)
 
     def scatter_chips(self, partial):
         if self.chips != 4:
@@ -817,15 +1456,21 @@
         second = jnp.where(self.core == 0, other, mine)
         return first, second
 
+    def mine_in(self, shard, later=0):
+        return self.columns_of_chip(shard, self.core * FF + later)
+
+    def mine_out(self, shard, later=0):
+        width = shard.shape[1]
+        half = lax.dynamic_slice_in_dim(shard, self.core * (width // 2) + later, width // 2, 1)
+        return self.rows_of_chip(half)
+
     def gather_mlp_in(self, shard):
-        mine = self.columns_of_chip(shard, self.core * FF)
-        mine = lax.all_gather(mine, "fsdp", axis=0, tiled=True)
+        mine = lax.all_gather(self.mine_in(shard), "fsdp", axis=0, tiled=True)
         return self.by_core(mine, self.xor(mine, 1))
 
     def gather_mlp_out(self, shard):
         width = shard.shape[1]
-        half = lax.dynamic_slice_in_dim(shard, self.core * (width // 2), width // 2, 1)
-        mine = lax.all_gather(self.rows_of_chip(half), "fsdp", axis=0)
+        mine = lax.all_gather(self.mine_out(shard), "fsdp", axis=0)
         mine = jnp.concatenate(
             [
                 mine[:, : self.main].reshape(self.shards * self.main, width // 2),
@@ -846,8 +1491,6 @@
 
     def order_mlp_in(self, every):
         rows = every.shape[1]
-        if self.main:
-            return finish_in(every, self.shards, self.main, self.rest)
         every = every.reshape(self.chips, 2, rows, every.shape[2])
         split = self.shards * self.main
         main = every[..., :split].reshape(self.chips, 2, rows, self.shards, self.main)
@@ -866,8 +1509,6 @@
         return lax.psum_scatter(total, "fsdp", scatter_dimension=0, tiled=True)[0]
 
     def order_mlp_out(self, every):
-        if self.main:
-            return finish_out(every, self.main, self.rest)
         width = 2 * every.shape[2]
         every = every.reshape(self.chips, 2, self.main + self.rest, width // 2)
         main = every[:, :, : self.main].transpose(0, 2, 1, 3).reshape(-1, width)
@@ -926,14 +1567,19 @@
     cotangent,
 ):
     lay = Layout(ctx_size, fsdp_size)
-    own_rows, width = tokens.shape[1:]
-    query_dim = H * HD
+    x, upstream = tokens[0], cotangent[0]
+    own_rows, width = x.shape
     block = own_rows // ROUNDS
     places_all = order[0]
     own_places = lax.dynamic_slice_in_dim(places_all, lay.index * own_rows, own_rows)
     where, key_place, least = window_blocks(
         places_all, own_places, jnp.cumsum(lengths[0]), block
     )
+    target = where % ROUNDS * ctx_size + where // ROUNDS
+    where = jnp.concatenate([where, target], axis=1)
+    bounds = jnp.stack([own_places, least])
+    bounds_wide = bounds.reshape(2, ROUNDS, block).transpose(1, 0, 2)
+    bounds_wide = jnp.tile(bounds_wide, (1, 1, HEADS_STEP))
     frequency = 10000.0 ** (-jnp.arange(HD // 2, dtype=jnp.float32) / (HD // 2))
     angles = own_places.astype(jnp.float32)[:, None] * frequency[None, :]
     cosine = jnp.cos(angles)
@@ -941,67 +1587,67 @@
     cosine = jnp.concatenate([cosine, cosine], axis=1)
     sine_part = jnp.concatenate([-sine_part, sine_part], axis=1)
 
-    gains = jnp.stack([norm_attn, norm_mlp]).astype(jnp.float32)
     if lay.plane:
-        gains = jnp.pad(gains, ((0, 6), (0, 0)))
-        in_attn, out_attn, gains = gather_weights(
-            w_attn_in, w_attn_out, gains, ctx_size, fsdp_size
+        pack = Pack(w_mlp_in.shape[0], width // 2, lay.chips, FF // lay.chips, lay.main, lay.rest)
+        pieces = lambda w: w.reshape(ctx_size, w.shape[0] // ctx_size, w.shape[1])
+        in_line, gains, mine, _ = share_line(
+            pieces(w_attn_in), norm_attn[None], norm_mlp[None], w_mlp_in, w_mlp_out, pack, fsdp_size
         )
-        gains = gains.transpose(1, 0, 2).reshape(8, width)
+        mine = lax.all_gather(mine, "fsdp", axis=0)
+        in_attn, out_line, token = share_plane(
+            pieces(w_attn_in), in_line, pieces(w_attn_out), ctx_size, fsdp_size
+        )
+        in_attn = in_attn.reshape(width, -1)
     else:
         in_attn = lay.gather_whole(w_attn_in)
         out_attn = lay.gather_whole(w_attn_out)
-        gains = lax.all_gather(gains, "fsdp", axis=1, tiled=True)
-    gate_in, up_in = lay.gather_mlp_in(w_mlp_in)
-    out_mlp = lay.gather_mlp_out(w_mlp_out)
-    upstream = cotangent[0]
-    upstream_all = lay.gather_chips(upstream)
-
-    normed_one, queries, key_value = project(tokens[0], gains[:1], in_attn, cosine, sine_part)
+        gains = jnp.pad(jnp.stack([norm_attn, norm_mlp]).astype(jnp.float32), ((0, 6), (0, 0)))
+        gains = lax.all_gather(gains, "fsdp", axis=0)
+        gate_in, up_in = lay.gather_mlp_in(w_mlp_in)
+        out_mlp = lay.gather_mlp_out(w_mlp_out)
+        upstream_all = lay.gather_chips(upstream)
+
+    normed_one, queries, key_value = project(x, gains, in_attn, cosine, sine_part)
     if lay.plane:
-        key_value = gather_plane(key_value, ctx_size)
+        key_value, out_attn, token = gather_plane(
+            key_value, pieces(w_attn_out), out_line, ctx_size, fsdp_size
+        )
+        out_attn = out_attn.reshape(-1, width)
+        upstream_all = (upstream,) + lay.from_neighbours(after(token, upstream))
     else:
         key_value = lax.all_gather(key_value, "ctx", axis=0)
     key_value = key_value.reshape(ctx_size * ROUNDS, block, 2 * HD)
-    mixed = attend(where, queries, key_value, key_place, own_places[:, None], least[:, None])
-    middle = tokens[0].astype(jnp.float32) + dot(mixed, out_attn)
-    normed_two, norm_two_back = jax.vjp(rms_norm, middle, gains[1])
-    normed_all = lay.gather_chips(low(normed_two))
-
-    gate = dot(normed_all, gate_in)
-    up = dot(normed_all, up_in)
-    hidden, hidden_back = jax.vjp(geglu, gate, up)
-    hidden = low(hidden)
-    grad_hidden = dot_nt(upstream_all, out_mlp)
-    grad_gate, grad_up = hidden_back(grad_hidden)
-    grad_gate = low(grad_gate)
-    grad_up = low(grad_up)
-    grad_normed_two = lay.scatter_chips(dot_nt(grad_gate, gate_in) + dot_nt(grad_up, up_in))
-    result = middle + lay.scatter_chips(dot(hidden, out_mlp))
-    grad_out_mlp = lay.reduce_mlp_out(dot_tn(hidden, upstream_all))
-    grad_in_mlp = lay.reduce_mlp_in(dot_tn(normed_all, grad_gate), dot_tn(normed_all, grad_up))
-
-    grad_middle_norm, grad_gain_mlp = norm_two_back(grad_normed_two)
-    grad_middle = upstream.astype(jnp.float32) + grad_middle_norm
-    grad_branch = low(grad_middle)
-    grad_out_attn = low(dot_tn(mixed, grad_branch))
-    grad_mixed = low(dot_nt(grad_branch, out_attn))
-
-    def repeated(values):
-        values = values.reshape(ROUNDS, 1, block)
-        return jnp.tile(values, (1, 1, HEADS_STEP))
-
-    target = where % ROUNDS * ctx_size + where // ROUNDS
+    mixed = attend(where, queries, key_value, key_place, bounds.T)
+    middle, normed_two = middle_forward(x, mixed, gains, out_attn)
+
+    if lay.plane:
+        grad_normed_two, *out_parts, grad_mlp = mlp(
+            mine, normed_two, upstream_all, pack
+        )
+        grad_mlp = lax.psum_scatter(grad_mlp, "fsdp", scatter_dimension=0, tiled=True)[0]
+    else:
+        normed_all = lay.gather_chips(normed_two)
+        gate = dot(normed_all, gate_in)
+        up = dot(normed_all, up_in)
+        hidden, hidden_back = jax.vjp(geglu, gate, up)
+        hidden = low(hidden)
+        grad_hidden = dot_nt(upstream_all, out_mlp)
+        grad_gate, grad_up = hidden_back(grad_hidden)
+        grad_gate = low(grad_gate)
+        grad_up = low(grad_up)
+        grad_normed_two = lay.scatter_chips(dot_nt(grad_gate, gate_in) + dot_nt(grad_up, up_in))
+        mixed_out = lay.scatter_chips(dot(hidden, out_mlp))
+        grad_out_mlp = lay.reduce_mlp_out(dot_tn(hidden, upstream_all))
+        grad_in_mlp = lay.reduce_mlp_in(dot_tn(normed_all, grad_gate), dot_tn(normed_all, grad_up))
+
+    grad_middle, grad_mixed, grad_out_attn, grad_gain_mlp, token = middle_back(
+        grad_normed_two, middle, upstream, mixed, gains, out_attn
+    )
+    if lay.plane:
+        mixed_out = lay.scatter_chip_blocks(*out_parts, token)
+    result = middle + mixed_out
     grad_query, grad_kv = attend_back(
-        jnp.concatenate([where, target], axis=1),
-        queries,
-        key_value,
-        grad_mixed,
-        key_place.reshape(ROUNDS, -1, 1),
-        repeated(own_places),
-        repeated(least),
-        cosine,
-        sine_part,
+        where, queries, key_value, grad_mixed, key_place, bounds_wide, cosine, sine_part
     )
     if lay.plane:
         grad_kv = sum_plane(grad_kv.reshape(ROUNDS, lay.chips, 2, block, 2 * HD))
@@ -1010,35 +1656,31 @@
         grad_kv = grad_kv.reshape(ROUNDS, ctx_size, block, 2 * HD)
         grad_kv = lax.psum_scatter(grad_kv, "ctx", scatter_dimension=1, tiled=True)
         grad_kv = grad_kv.reshape(own_rows, 2 * HD).astype(jnp.float32)
-    grad_key = grad_kv[:, :HD] * cosine - jnp.roll(grad_kv[:, :HD], HD // 2, 1) * sine_part
-    grad_projected = jnp.concatenate([grad_query, low(grad_key), low(grad_kv[:, HD:])], axis=1)
-    grad_in_attn = low(dot_tn(normed_one, grad_projected))
-    _, norm_one_back = jax.vjp(rms_norm, tokens[0].astype(jnp.float32), gains[0])
-    grad_inputs_norm, grad_gain_attn = norm_one_back(dot_nt(grad_projected, in_attn))
-    grad_inputs = grad_middle + grad_inputs_norm
+    grad_in_attn, grad_inputs, grad_gain_attn = project_back(
+        grad_query, grad_kv, cosine, sine_part, normed_one, x, grad_middle, gains, in_attn
+    )
     if lay.plane:
         split = lambda grad: grad.reshape(fsdp_size, lay.chips, 2, -1, grad.shape[1])
-        grad_gains = jnp.stack([grad_gain_attn, grad_gain_mlp]).reshape(2, fsdp_size, -1)
-        grad_gains = jnp.pad(grad_gains.transpose(1, 0, 2), ((0, 0), (0, 6), (0, 0)))
-        grad_out_attn, grad_in_attn, grad_in_mlp, grad_out_mlp, grad_gains = close(
+        grad_out_attn, grad_in_attn, grad_mlp, grad_gains = close(
             split(grad_out_attn),
             split(grad_in_attn),
-            grad_in_mlp,
-            grad_out_mlp,
-            grad_gains,
+            grad_mlp,
+            grad_gain_attn,
+            grad_gain_mlp,
             ctx_size,
             fsdp_size,
         )
         whole = lambda grad: grad.reshape(-1, grad.shape[2]).astype(jnp.float32)
         grad_out_attn, grad_in_attn = whole(grad_out_attn), whole(grad_in_attn)
+        grad_in_mlp, grad_out_mlp = finish(grad_mlp, pack, fsdp_size)
         grad_gain_attn, grad_gain_mlp = grad_gains[0], grad_gains[1]
     else:
         grad_out_attn = lay.reduce_whole(grad_out_attn)
         grad_in_attn = lay.reduce_whole(grad_in_attn)
-        grad_in_mlp = lax.all_gather(grad_in_mlp, "ctx", axis=0)
-        grad_out_mlp = lax.all_gather(grad_out_mlp, "ctx", axis=0)
-        grad_gain_attn = lay.reduce_gain(grad_gain_attn)
-        grad_gain_mlp = lay.reduce_gain(grad_gain_mlp)
+        grad_in_mlp = lay.order_mlp_in(lax.all_gather(grad_in_mlp, "ctx", axis=0))
+        grad_out_mlp = lay.order_mlp_out(lax.all_gather(grad_out_mlp, "ctx", axis=0))
+        grad_gain_attn = lay.reduce_gain(grad_gain_attn[0])
+        grad_gain_mlp = lay.reduce_gain(grad_gain_mlp[0])
     return (
         low(result)[None],
         grad_inputs[None],
@@ -1046,8 +1688,8 @@
         grad_in_attn,
         grad_out_attn,
         grad_gain_mlp,
-        lay.order_mlp_in(grad_in_mlp),
-        lay.order_mlp_out(grad_out_mlp),
+        grad_in_mlp,
+        grad_out_mlp,
     )
 
 

time: 651 us -> 486 us (0.75)
  matrix products: 159 us -> 0 us
  Pallas kernels: 297 us -> 413 us
  waiting for transfers between devices: 64.1 us -> 16.5 us
  other arithmetic: 50.7 us -> 12.2 us
  local copies, waits for them, and re-layouts: 40.9 us -> 12.8 us
  starting transfers between devices: 18.7 us -> 6.49 us
    dot_general x14 -> x0, matrix products: 159 us -> none  [the longest x5 64.6 us: dot_tn(): jnp.einsum('ab,ac->bc', left, right, preferred_element_type=jnp.float32)]
    pallas_call x4 -> x8, Pallas kernels: 113 us -> 227 us  [the longest x1 107 us: mlp(): pl.pallas_call(functools.partial(mlp_kernel, shards, pack), name='mlp', i...]
    ppermute x20 -> x6, waiting for transfers between devices: 64 us -> 0.02 us  [xor(): return lax.ppermute(values, 'ctx', pairs)]
    reduce_scatter x2 -> x1, waiting for transfers between devices: 0.01 us -> 15.2 us  [per_device(): lax.psum_scatter(grad_mlp, 'fsdp', scatter_dimension=0, tiled=True)[0]]
    ppermute x20 -> x6, starting transfers between devices: 18.5 us -> 6.41 us  [xor(): return lax.ppermute(values, 'ctx', pairs)]
    convert_element_type x5 -> x2, other arithmetic: 12 us -> 0.35 us  [add_low(): (first.astype(jnp.float32) + second.astype(jnp.float32)).astype(jnp.bfloa...]
    slice x13 -> x4, local copies, waits for them, and re-layouts: 13.7 us -> 2.47 us  [the longest x2 2.39 us: after(): return jnp.where(token[0, 0] != 0, jnp.zeros_like(values), values)]
  transfers between devices with their start and end apart: 24 -> 8, of which waited for: 9 -> 2; matrix products, arithmetic and copies ran while one was open for 29% -> 3% of each run, Pallas kernels for 27% -> 34%
where the time goes in v3:
time: 486 us; the launch traced here: 477 us
  Pallas kernels  413 us (85%)
  waiting for transfers between devices  16.5 us (3%)
  between operations  16.1 us (3%)
  local copies, waits for them, and re-layouts  12.8 us (3%)
  other arithmetic  12.2 us (3%)
  starting transfers between devices  6.49 us (1%)
    pallas_call x1, Pallas kernels, close(): pl.pallas_call(functools.partial(close_kernel, shards), name='close', in_...  109 us
    pallas_call x1, Pallas kernels, mlp(): pl.pallas_call(functools.partial(mlp_kernel, shards, pack), name='mlp', i...  107 us
    pallas_call x1, Pallas kernels, attend_back(): pl.pallas_call(functools.partial(attend_back_kernel, blocks, block), name...  33.9 us
    pallas_call x1, Pallas kernels, share_plane(): pl.pallas_call(functools.partial(share_plane_kernel, shards), name='share...  27.8 us
    pallas_call x1, Pallas kernels, gather_plane(): pl.pallas_call(functools.partial(gather_plane_kernel, shards), name='gath...  27.2 us
    pallas_call x1, Pallas kernels, attend(): pl.pallas_call(functools.partial(attend_kernel, blocks, block), name='att...  20.3 us
    pallas_call x1, Pallas kernels, share_line(): pl.pallas_call(functools.partial(share_line_kernel, shards, pack), name='...  19.8 us
    reduce_scatter x1, waiting for transfers between devices, per_device(): lax.psum_scatter(grad_mlp, 'fsdp', scatter_dimension=0, tiled=True)[0]  15.2 us
  transfers between devices with their start and end apart: 8, of which 2 were waited for; matrix products, arithmetic and copies ran while one was open for 3% of the time, Pallas kernels for 34%

profile of v3, /device:TPU:0, one launch (start us, length us, event | category | flops | bytes accessed | tf_op | source)
XLA Modules:
  0.0 476.8 jit_solution(10699278477103441552)
XLA Ops:
  7.2 1.2 broadcast_in_dim.64.gain_a
  8.5 1.2 broadcast_in_dim.65.gain_b
  9.7 19.8 %share_line.1 = (bf16[4,48,1792]{2,1,0:T(8,128)(2,1)}, f32[4,8,384]{2,1,0:T(8,128)}, bf16[864,768]{1,0:T(8,128)(2,1)}, s32[8,128]{1,0:T(8,128)}) custom-call(bf16[8,48,1792]{2,1,0:T(8,128)(2,1)} %bitcast.46, bf16[1,384]{1,0:T(2,128)(2,1)} %broadcast_in_dim.64.gain_a, bf16[1,384]{1,0:T(2,128)(2,1)} %broadcast_in_dim.65.gain_b, bf16[384,9216]{1,0:T(8,128)(2,1)} %mlp_in.1, ...), custom_call_target="tpu_custom_call" | custom-call | tf_op jit(solution)/shard_map/share_line/pallas_call | solution.py:800
  30.3 27.8 %share_plane.1 = (bf16[4,8,48,1792]{3,2,1,0:T(8,128)(2,1)}, bf16[4,48,1536]{2,1,0:T(8,128)(2,1)}, s32[8,128]{1,0:T(8,128)}) custom-call(bf16[8,48,1792]{2,1,0:T(8,128)(2,1)} %bitcast.47, bf16[4,48,1792]{2,1,0:T(8,128)(2,1)} %get-tuple-element.45.in_line, bf16[8,48,1536]{2,1,0:T(8,128)(2,1)} %bitcast.49), custom_call_target="tpu_custom_call" | custom-call | tf_op jit(solution)/shard_map/share_plane/pallas_call | solution.py:827
  59.8 9.3 %project.1 = (bf16[384,1536]{1,0:T(8,128)(2,1)}, bf16[12,384,128]{2,1,0:T(8,128)(2,1)}, bf16[384,256]{1,0:T(8,128)(2,1)}) custom-call(bf16[384,1536]{1,0:T(8,128)(2,1)} %bitcast.40, f32[4,8,384]{2,1,0:T(8,128)} %get-tuple-element.44.gain_ref, bf16[1536,1792]{1,0:T(8,128)(2,1)} %bitcast.34, f32[384,128]{1,0:T(8,128)} %get-tuple-element.89.cos_ref, ...), custom_call_target="tpu_custom_call" | custom-call | tf_op jit(solution)/shard_map/project/pallas_call | solution.py:102
  69.1 27.2 %gather_plane.1 = (bf16[8,384,256]{2,1,0:T(8,128)(2,1)}, bf16[4,8,48,1536]{3,2,1,0:T(8,128)(2,1)}, s32[8,128]{1,0:T(8,128)}) custom-call(bf16[384,256]{1,0:T(8,128)(2,1)} %get-tuple-element.48.kv_ref, bf16[8,48,1536]{2,1,0:T(8,128)(2,1)} %bitcast.50, bf16[4,48,1536]{2,1,0:T(8,128)(2,1)} %get-tuple-element.49.out_line), custom_call_target="tpu_custom_call" | custom-call | tf_op jit(solution)/shard_map/gather_plane/pallas_call | solution.py:847
  96.3 1.2 slice.33
  106.7 20.3 %attend.1.mixed_ref = bf16[384,1536]{1,0:T(8,128)(2,1)} custom-call(s32[4,24]{1,0:T(4,128)} %pad_add_fusion.1.where_ref, bf16[12,384,128]{2,1,0:T(8,128)(2,1)} %get-tuple-element.47.q_ref, bf16[32,96,256]{2,1,0:T(8,128)(2,1)} %bitcast.43, s32[4,1,1152]{2,1,0:T(1,128)} %select_n.98.key_place_ref, s32[384,2]{1,0:T(8,128)} %bitcast.55), custom_call_target="tpu_custom_call" | custom-call | tf_op jit(solution)/shard_map/attend/pallas_call | solution.py:176
  127.0 7.2 %middle.1 = (f32[384,1536]{1,0:T(8,128)}, bf16[384,1536]{1,0:T(8,128)(2,1)}) custom-call(bf16[384,1536]{1,0:T(8,128)(2,1)} %bitcast.41, bf16[384,1536]{1,0:T(8,128)(2,1)} %attend.1.mixed_ref, f32[4,8,384]{2,1,0:T(8,128)} %get-tuple-element.44.gain_ref, bf16[1536,1536]{1,0:T(8,128)(2,1)} %bitcast.36), custom_call_target="tpu_custom_call" | custom-call | tf_op jit(solution)/shard_map/middle/pallas_call | solution.py:302
  135.4 106.7 %mlp.1 = (f32[384,1536]{1,0:T(8,128)}, bf16[384,1536]{1,0:T(8,128)(2,1)}, bf16[384,1536]{1,0:T(8,128)(2,1)}, bf16[384,1536]{1,0:T(8,128)(2,1)}, bf16[384,768]{1,...) custom-call(bf16[4,864,768]{2,1,0:T(8,128)(2,1)} %bitcast.48, ...), custom_call_target="tpu_custom_call" | custom-call | tf_op jit(solution)/shard_map/mlp/pallas_call | solution.py:1326
  243.2 1.3 collective-permute-start.4
  245.3 11.2 %middle_back.1 = (f32[384,1536]{1,0:T(8,128)}, bf16[384,1536]{1,0:T(8,128)(2,1)}, bf16[1536,1536]{1,0:T(8,128)(2,1)}, f32[1,1536]{1,0:T(1,128)}, s32[8,128]{1,0:T(8,128)}) custom-call(f32[384,1536]{1,0:T(8,128)} %get-tuple-element.58.grad_ref, f32[384,1536]{1,0:T(8,128)} %get-tuple-element.52.middle_ref, bf16[384,1536]{1,0:T(8,128)(2,1)} %bitcast.39, ...), custom_call_target="tpu_custom_call" | custom-call | tf_op jit(solution)/shard_map/middle_back/pallas_call | solution.py:342
  256.5 1.2 slice.35
  258.6 1.4 collective-permute-start.5
  263.1 33.9 %attend_back.1 = (bf16[384,1536]{1,0:T(8,128)(2,1)}, bf16[32,96,256]{2,1,0:T(8,128)(2,1)}) custom-call(s32[4,24]{1,0:T(4,128)} %pad_add_fusion.1.where_ref, bf16[12,384,128]{2,1,0:T(8,128)(2,1)} %get-tuple-element.47.q_ref, bf16[32,96,256]{2,1,0:T(8,128)(2,1)} %bitcast.44, bf16[384,1536]{1,0:T(8,128)(2,1)} %get-tuple-element.63.grad_ref, ...), custom_call_target="tpu_custom_call" | custom-call | tf_op jit(solution)/shard_map/attend_back/pallas_call | solution.py:267
  297.0 12.6 %sum_plane.1 = f32[4,96,256]{2,1,0:T(8,128)} custom-call(bf16[4,4,2,96,256]{4,3,2,1,0:T(8,128)(2,1)} %bitcast.53), custom_call_target="tpu_custom_call" | custom-call | tf_op jit(solution)/shard_map/sum_plane/pallas_call | solution.py:881
  309.6 13.0 %project_back.1 = (bf16[1536,1792]{1,0:T(8,128)(2,1)}, f32[384,1536]{1,0:T(8,128)}, f32[1,1536]{1,0:T(1,128)}) custom-call(bf16[384,1536]{1,0:T(8,128)(2,1)} %get-tuple-element.64.grad_q_ref, f32[384,256]{1,0:T(8,128)} %bitcast.52, f32[384,128]{1,0:T(8,128)} %get-tuple-element.89.cos_ref, f32[384,128]{1,0:T(8,128)} %get-tuple-element.90.sin_ref, ...), custom_call_target="tpu_custom_call" | custom-call | tf_op jit(solution)/shard_map/project_back/pallas_call | solution.py:405
  322.7 1.6 fusion
  324.3 15.2 %reduce-scatter.2.cloned.1.call-done = bf16[1,864,768]{2,1,0:T(8,128)(2,1)} async-done(((bf16[4,864,768]{2,1,0:T(8,128)(2,1)}), bf16[1,864,768]{2,1,0:T(8,128)(2,1)}) %reduce-scatter.2.cloned.1.call-update) | async-done | bytes 1327120 | tf_op jit(solution)/shard_map/reduce_scatter | solution.py:1627
  339.5 109.4 %close.1 = (bf16[8,48,1536]{2,1,0:T(8,128)(2,1)}, bf16[8,48,1792]{2,1,0:T(8,128)(2,1)}, bf16[8,864,768]{2,1,0:T(8,128)(2,1)}, f32[8,384]{1,0:T(8,128)}) custom-call(bf16[4,4,2,48,1536]{4,3,2,1,0:T(8,128)(2,1)} %bitcast.51, bf16[4,4,2,48,1792]{4,3,2,1,0:T(8,128)(2,1)} %bitcast.45, bf16[864,768]{1,0:T(8,128)(2,1)} %bitcast.54, ...), custom_call_target="tpu_custom_call" | custom-call | tf_op jit(solution)/shard_map/close/pallas_call | solution.py:1015
  448.9 1.4 slice_reduce_fusion
  450.3 3.1 bitcast_convert_fusion.1
  453.3 1.8 bitcast_convert_fusion
  455.1 14.4 %finish.1 = (f32[384,9216]{1,0:T(8,128)}, f32[1152,1536]{1,0:T(8,128)}) custom-call(bf16[8,864,768]{2,1,0:T(8,128)(2,1)} %get-tuple-element.77.main_ref.tail_ref.out_part_ref, bf16[8,864,768]{2,1,0:T(8,128)(2,1)} %get-tuple-element.77.main_ref.tail_ref.out_part_ref, bf16[8,864,768]{2,1,0:T(8,128)(2,1)} %get-tuple-element.77.main_ref.tail_ref.out_part_ref), custom_call_target="tpu_custom_call" | custom-call | tf_op jit(solution)/shard_map/finish/pallas_call | solution.py:1103
  (83 shorter events, 17.3 us)
Async XLA Ops:
  7.2 128.3 %all-gather.3.cloned.1.call-start = ((), (), s32[]{:S(2)}) async-start(), calls=%async_computation.2 | async-start | bytes 6635520 | tf_op jit(solution)/shard_map/all_gather | solution.py:1596
  29.5 0.7 copy-start.7
  29.6 309.9 %reduce-scatter.2.cloned.1.call-start = ((), (), s32[]{:S(2)}) async-start(), calls=%async_computation.1 | async-start | bytes 6635520 | tf_op jit(solution)/shard_map/reduce_scatter | solution.py:1627
  69.1 29.1 %copy-start = (bf16[1,384,1536]{2,1,0:T(8,128)(2,1)S(1)}, bf16[1,384,1536]{2,1,0:T(8,128)(2,1)}, u32[]{:S(2)}) copy-start(bf16[1,384,1536]{2,1,0:T(8,128)(2,1)} %param.19) | copy-start | bytes 3538948
  98.3 5.1 %copy-start.9 = (s32[1,4]{1,0:T(1,128)S(1)}, s32[1,4]{1,0:T(1,128)}, u32[]{:S(2)}) copy-start(s32[1,4]{1,0:T(1,128)} %param.12) | copy-start | bytes 52
  98.3 36.0 %collective-permute-start.1 = (bf16[384,1536]{1,0:T(8,128)(2,1)S(1)}, bf16[384,1536]{1,0:T(8,128)(2,1)S(1)}, u32[]{:S(2)}, u32[]{:S(2)}) collective-permute-start(bf16[384,1536]{1,0:T(8,128)(2,1)S(1)} %broadcast_select_fusion), channel_id=1, source_target_pairs={{0,16},{4,20},{8,24},{12,28},{16,0},{20,4},{24,8},{28,12},{1,17},{... | collective-permute-start | bytes 3538952 | tf_op jit(solution)/shard_map/ppermute | solution.py:1382
  99.3 35.0 %collective-permute-start = (bf16[384,1536]{1,0:T(8,128)(2,1)S(1)}, bf16[384,1536]{1,0:T(8,128)(2,1)}, u32[]{:S(2)}, u32[]{:S(2)}) collective-permute-start(bf16[384,1536]{1,0:T(8,128)(2,1)S(1)} %broadcast_select_fusion), channel_id=1, source_target_pairs={{0,8},{4,12},{8,0},{12,4},{16,24},{20,28},{24,16},{28,20},{1,9},{5... | collective-permute-start | bytes 3538952 | tf_op jit(solution)/shard_map/ppermute | solution.py:1382
  134.2 1.2 copy-start.3
  242.1 1.1 copy-start.8
  242.1 3.1 copy-start.5
  242.2 3.1 copy-start.6
  243.2 15.2 %collective-permute-start.4 = (bf16[384,768]{1,0:T(8,128)(2,1)S(1)}, bf16[384,768]{1,0:T(8,128)(2,1)S(1)}, u32[]{:S(2)}, u32[]{:S(2)}) collective-permute-start(bf16[384,768]{1,0:T(8,128)(2,1)S(1)} %copy-done.8), channel_id=1, source_target_pairs={{0,16},{4,20},{8,24},{12,28},{16,0},{20,4},{24,8},{28,12},{1,17},{... | collective-permute-start | bytes 1769480 | tf_op jit(solution)/shard_map/ppermute | solution.py:1382
  244.5 15.5 %collective-permute-start.2 = (bf16[384,768]{1,0:T(8,128)(2,1)}, bf16[384,768]{1,0:T(8,128)(2,1)S(1)}, u32[]{:S(2)}, u32[]{:S(2)}) collective-permute-start(bf16[384,768]{1,0:T(8,128)(2,1)} %get-tuple-element.60), channel_id=1, source_target_pairs={{0,8},{4,12},{8,0},{12,4},{16,24},{20,28},{24,16},{28,20},{1,9},{5... | collective-permute-start | bytes 1769480 | tf_op jit(solution)/shard_map/ppermute | solution.py:1382
  258.6 64.0 %collective-permute-start.5 = (bf16[384,1536]{1,0:T(8,128)(2,1)S(1)}, bf16[384,1536]{1,0:T(8,128)(2,1)S(1)}, u32[]{:S(2)}, u32[]{:S(2)}) collective-permute-start(bf16[384,1536]{1,0:T(8,128)(2,1)S(1)} %pad_maximum_fusion.1), channel_id=1, source_target_pairs={{0,8},{4,12},{8,0},{12,4},{16,24},{20,28},{24,16},{28,20},{1,9},{5... | collective-permute-start | bytes 3538952 | tf_op jit(solution)/shard_map/ppermute | solution.py:1382
  261.3 61.3 %collective-permute-start.3 = (bf16[384,1536]{1,0:T(8,128)(2,1)}, bf16[384,1536]{1,0:T(8,128)(2,1)S(1)}, u32[]{:S(2)}, u32[]{:S(2)}) collective-permute-start(bf16[384,1536]{1,0:T(8,128)(2,1)} %pad_maximum_fusion), channel_id=1, source_target_pairs={{0,16},{4,20},{8,24},{12,28},{16,0},{20,4},{24,8},{28,12},{1,17},{... | collective-permute-start | bytes 3538952 | tf_op jit(solution)/shard_map/ppermute | solution.py:1382
  309.6 13.1 %copy-start.1 = (f32[384,1536]{1,0:T(8,128)S(1)}, f32[384,1536]{1,0:T(8,128)}, u32[]{:S(2)}) copy-start(f32[384,1536]{1,0:T(8,128)} %get-tuple-element.52.middle_ref) | copy-start | bytes 7077892
  309.6 13.1 %copy-start.4 = (bf16[384,1536]{1,0:T(8,128)(2,1)S(1)}, bf16[384,1536]{1,0:T(8,128)(2,1)}, u32[]{:S(2)}) copy-start(bf16[384,1536]{1,0:T(8,128)(2,1)} %get-tuple-element.56) | copy-start | bytes 3538948
  450.3 3.1 copy-start.2
Sparse Core Ops, SparseCore 0:
  29.7 105.6 all-gather.2
  242.3 97.1 reduce-scatter.1

commit v4 on v3

--- a/solution.py
+++ b/solution.py
@@ -125,137 +125,250 @@
 
 
 HEADS_STEP = 4
-
-
-def attend_kernel(blocks, block, where_ref, q_ref, kv_ref, key_place_ref, bounds_ref, out_ref, window, bias):
+ANY = pl.BlockSpec(memory_space=pl.ANY)
+
+
+class Window:
+    def __init__(self, rows):
+        self.block = rows // ROUNDS
+        self.blocks = (WINDOW + self.block - 2) // self.block + 1
+        self.span = self.blocks * self.block
+
+
+def place_tables(
+    index, devices, order_ref, lengths_ref, frequency_ref,
+    where_ref, key_place_ref, bounds_ref, wide_ref, cos_ref, sin_ref,
+):
+    count, block = order_ref.shape
+    window = Window(block * ROUNDS)
+    blocks = order_ref[...].astype(jnp.float32)
+    block_of = lambda place: jnp.floor((place + 0.5) * (1.0 / block))
+    held = block_of(blocks[:, :1])
+    offsets = low(blocks - held * block)
+    at = lax.broadcasted_iota(jnp.int32, (count, 1), 0).astype(jnp.float32)
+    lane = lax.broadcasted_iota(jnp.int32, (1, LANES), 1).astype(jnp.float32)
+    step = jnp.where(lane < window.blocks, lane, lane - window.blocks)
+    lengths = lengths_ref[...].astype(jnp.float32)
+    ends = [lengths[:, :1]]
+    for j in range(1, lengths.shape[1]):
+        ends.append(ends[-1] + lengths[:, j : j + 1])
+
+    def least_of(place):
+        start = jnp.zeros_like(place)
+        for end in ends:
+            start = jnp.where(end <= place, end, start)
+        return jnp.maximum(start, place - (WINDOW - 1))
+
+    where_ref[...] = jnp.zeros_like(where_ref)
+    own = []
+    for r in range(ROUNDS):
+        mine = order_ref[pl.ds(index * ROUNDS + r, 1), :].astype(jnp.float32)
+        own.append(mine)
+        wanted = block_of(mine[:, :1]) - (window.blocks - 1) + step
+        match = (held == jnp.maximum(wanted, 0.0)).astype(jnp.float32)
+        where = jnp.sum(match * at, axis=0, keepdims=True)
+        device = jnp.floor((where + 0.5) * (1.0 / ROUNDS))
+        target = (where - ROUNDS * device) * devices + device
+        where_ref[r : r + 1, :] = jnp.where(lane < window.blocks, where, target).astype(jnp.int32)
+        inner = tn_dot(low(match), offsets)
+        pieces = []
+        for j in range(window.blocks):
+            one = wanted[:, j : j + 1]
+            pieces.append(inner[j : j + 1] + jnp.where(one >= 0.0, one * block, 1e9))
+        key_place_ref[r] = jnp.concatenate(pieces, axis=1)
+        wide_ref[r, :1, :] = jnp.concatenate([mine] * HEADS_STEP, axis=1)
+        wide_ref[r, 1:, :] = jnp.concatenate([least_of(mine)] * HEADS_STEP, axis=1)
+    own = jnp.concatenate(own, axis=1)
+    own = jnp.broadcast_to(own, (8, own.shape[1])).T[:, :1]
+    bounds_ref[:, :1] = own
+    bounds_ref[:, 1:] = least_of(own)
+    angles = own * frequency_ref[...]
+    cos_ref[...] = jnp.cos(angles)
+    sign = jnp.where(lane < HD // 2, -1.0, 1.0)
+    sin_ref[...] = jnp.sin(angles) * sign
+
+
+def place_arrays(order, lengths, rows):
+    window = Window(rows)
+    frequency = 10000.0 ** (-jnp.arange(HD // 2, dtype=jnp.float32) / (HD // 2))
+    operands = (
+        order.reshape(-1, window.block),
+        lengths,
+        jnp.concatenate([frequency, frequency])[None],
+    )
+    wide = jax.ShapeDtypeStruct((rows, HD), jnp.float32)
+    shapes = (
+        jax.ShapeDtypeStruct((8, LANES), jnp.int32),
+        jax.ShapeDtypeStruct((ROUNDS, 1, window.span), jnp.float32),
+        jax.ShapeDtypeStruct((rows, 2), jnp.float32),
+        jax.ShapeDtypeStruct((ROUNDS, 2, HEADS_STEP * window.block), jnp.float32),
+        wide,
+        wide,
+    )
+    return operands, shapes
+
+
+def place_tables_alone(devices, order, lengths, rows):
+    operands, shapes = place_arrays(order, lengths, rows)
+
+    def kernel(*refs):
+        place_tables(lax.axis_index("ctx"), devices, *refs)
+
+    vmem = pl.BlockSpec(memory_space=pltpu.VMEM)
+    return pl.pallas_call(
+        kernel,
+        name="places",
+        in_specs=[vmem] * len(operands),
+        out_specs=[vmem] * len(shapes),
+        out_shape=shapes,
+    )(*operands)
+
+
+def load_window(blocks, block, where_ref, kv_ref, window):
     r = pl.program_id(0)
-
-    @pl.when(pl.program_id(1) == 0)
-    def _():
-        for j in range(blocks):
-            window[j * block : (j + 1) * block, :] = kv_ref[where_ref[r, j]]
-        key_place = key_place_ref[0]
-        allowed = (key_place <= bounds_ref[:, :1]) & (key_place >= bounds_ref[:, 1:])
-        bias[...] = jnp.where(allowed, 0.0, -1e30)
-
-    queries = q_ref[...].reshape(HEADS_STEP * block, HD)
-    scores = lax.dot_general(
-        queries, window[:, :HD], (((1,), (1,)), ((), ())), preferred_element_type=jnp.float32
-    )
-    scores = scores.reshape(HEADS_STEP, block, blocks * block) + bias[...][None]
-    peak = jnp.max(scores, axis=-1, keepdims=True)
-    weights = jnp.exp(scores - peak)
-    total = jnp.sum(weights, axis=-1, keepdims=True).reshape(HEADS_STEP * block, 1)
-    weights = weights.astype(jnp.bfloat16).reshape(HEADS_STEP * block, blocks * block)
-    mixed = jnp.dot(weights, window[:, HD:], preferred_element_type=jnp.float32) / total
-    mixed = mixed.astype(jnp.bfloat16)
-    for j in range(HEADS_STEP):
-        out_ref[:, j * HD : (j + 1) * HD] = mixed[j * block : (j + 1) * block]
+    for j in range(blocks):
+        window[j * block : (j + 1) * block, :] = kv_ref[where_ref[r, j]]
+
+
+def attend_kernel(
+    blocks, block, where_ref, q_ref, kv_ref, key_place_ref, bounds_ref, out_ref, log_ref, window, bias
+):
+    load_window(blocks, block, where_ref, kv_ref, window)
+    key_place = key_place_ref[0]
+    allowed = (key_place <= bounds_ref[:, :1]) & (key_place >= bounds_ref[:, 1:])
+    bias[...] = jnp.where(allowed, 0.0, -1e30)
+    for part in range(q_ref.shape[0] // HEADS_STEP):
+        first = part * HEADS_STEP
+        queries = q_ref[first : first + HEADS_STEP].reshape(HEADS_STEP * block, HD)
+        scores = nt_dot(queries, window[:, :HD])
+        scores = scores.reshape(HEADS_STEP, block, blocks * block) + bias[...][None]
+        peak = jnp.max(scores, axis=-1, keepdims=True)
+        weights = jnp.exp(scores - peak)
+        total = jnp.sum(weights, axis=-1, keepdims=True).reshape(HEADS_STEP * block, 1)
+        weights = low(weights).reshape(HEADS_STEP * block, blocks * block)
+        mixed = low(dot(weights, window[:, HD:]) / total)
+        for j in range(HEADS_STEP):
+            columns = slice((first + j) * HD, (first + j + 1) * HD)
+            out_ref[:, columns] = mixed[j * block : (j + 1) * block]
+        log_total = peak.reshape(HEADS_STEP * block, 1) + jnp.log(total)
+        log_ref[0, part] = jnp.broadcast_to(log_total, (HEADS_STEP * block, LANES)).T[:1, :]
 
 
 def attend(where, queries, kv_blocks, key_place, bounds):
-    rounds, blocks = where.shape[0], where.shape[1] // 2
     heads, rows, _ = queries.shape
-    block = rows // rounds
-    span = blocks * block
+    window = Window(rows)
+    block, span, parts = window.block, window.span, heads // HEADS_STEP
     grid_spec = pltpu.PrefetchScalarGridSpec(
         num_scalar_prefetch=1,
-        grid=(rounds, heads // HEADS_STEP),
+        grid=(ROUNDS,),
         in_specs=[
-            pl.BlockSpec((HEADS_STEP, block, HD), lambda r, h, *_: (h, r, 0)),
-            pl.BlockSpec(kv_blocks.shape, lambda r, h, *_: (0, 0, 0)),
-            pl.BlockSpec((1, 1, span), lambda r, h, *_: (r, 0, 0)),
-            pl.BlockSpec((block, 2), lambda r, h, *_: (r, 0)),
-        ],
-        out_specs=pl.BlockSpec((block, HEADS_STEP * HD), lambda r, h, *_: (r, h)),
+            pl.BlockSpec((heads, block, HD), lambda r, *_: (0, r, 0)),
+            pl.BlockSpec(kv_blocks.shape, lambda r, *_: (0, 0, 0)),
+            pl.BlockSpec((1, 1, span), lambda r, *_: (r, 0, 0)),
+            pl.BlockSpec((block, 2), lambda r, *_: (r, 0)),
+        ],
+        out_specs=[
+            pl.BlockSpec((block, heads * HD), lambda r, *_: (r, 0)),
+            pl.BlockSpec((1, parts, 1, HEADS_STEP * block), lambda r, *_: (r, 0, 0, 0)),
+        ],
         scratch_shapes=[
             pltpu.VMEM((span, 2 * HD), jnp.bfloat16),
             pltpu.VMEM((block, span), jnp.float32),
         ],
     )
     return pl.pallas_call(
-        functools.partial(attend_kernel, blocks, block),
+        functools.partial(attend_kernel, window.blocks, block),
         name="attend",
         grid_spec=grid_spec,
-        out_shape=jax.ShapeDtypeStruct((rows, heads * HD), jnp.bfloat16),
+        out_shape=[
+            jax.ShapeDtypeStruct((rows, heads * HD), jnp.bfloat16),
+            jax.ShapeDtypeStruct((ROUNDS, parts, 1, HEADS_STEP * block), jnp.float32),
+        ],
         compiler_params=pltpu.CompilerParams(vmem_limit_bytes=VMEM_LIMIT),
     )(where, queries, kv_blocks, key_place, bounds)
 
 
 def attend_back_kernel(
-    blocks, block, where_ref, q_ref, kv_ref, grad_ref, key_place_ref, bounds_ref, cos_ref, sin_ref,
-    grad_q_ref, grad_kv_ref, window, bias, window_grad, total_grad,
+    blocks, block, where_ref, q_ref, kv_ref, grad_ref, mixed_ref, log_ref, key_place_ref, bounds_ref,
+    cos_ref, sin_ref, *refs,
 ):
-    r, h = pl.program_id(0), pl.program_id(1)
-    last = pl.num_programs(1) - 1
-
-    @pl.when((r == 0) & (h == 0))
+    grad_q_ref, grad_kv_ref, window, bias, window_grad, total_grad = refs[-6:]
+    r = pl.program_id(0)
+
+    @pl.when(r == 0)
     def _():
         total_grad[...] = jnp.zeros_like(total_grad)
 
-    @pl.when(h == 0)
+    load_window(blocks, block, where_ref, kv_ref, window)
+    key_place = jnp.broadcast_to(key_place_ref[0], (8, blocks * block)).T[:, :1]
+    allowed = (key_place <= bounds_ref[0, :1, :]) & (key_place >= bounds_ref[0, 1:, :])
+    bias[...] = jnp.where(allowed, 0.0, -1e30)
+    keys, values = window[:, :HD], window[:, HD:]
+    cosine, sine_part = cos_ref[...], sin_ref[...]
+    for part in range(q_ref.shape[0] // HEADS_STEP):
+        first = part * HEADS_STEP
+        spans = [slice((first + j) * HD, (first + j + 1) * HD) for j in range(HEADS_STEP)]
+        queries = q_ref[first : first + HEADS_STEP].reshape(HEADS_STEP * block, HD)
+        grads = jnp.concatenate([grad_ref[:, span] for span in spans], axis=0)
+        delta = jnp.concatenate(
+            [
+                jnp.sum(
+                    (grad_ref[:, span].astype(jnp.float32) * mixed_ref[:, span].astype(jnp.float32)).T,
+                    axis=0,
+                    keepdims=True,
+                )
+                for span in spans
+            ],
+            axis=1,
+        )
+        probs = jnp.exp(nt_dot(keys, queries) + (bias[...] - log_ref[0, part]))
+        grad_scores = low(probs * (nt_dot(values, grads) - delta))
+        grad_keys = dot(grad_scores, queries)
+        grad_values = dot(low(probs), grads)
+        if part == 0:
+            window_grad[:, :HD] = grad_keys
+            window_grad[:, HD:] = grad_values
+        else:
+            window_grad[:, :HD] += grad_keys
+            window_grad[:, HD:] += grad_values
+        grad_q = tn_dot(grad_scores, keys)
+        for j, span in enumerate(spans):
+            one = grad_q[j * block : (j + 1) * block]
+            one = (one * cosine - pltpu.roll(one, HD // 2, 1) * sine_part) * HD ** (-0.5)
+            grad_q_ref[:, span] = low(one)
+    for j in range(blocks):
+        total_grad[where_ref[r, blocks + j]] += window_grad[j * block : (j + 1) * block, :]
+
+    @pl.when(r == pl.num_programs(0) - 1)
     def _():
-        for j in range(blocks):
-            window[j * block : (j + 1) * block, :] = kv_ref[where_ref[r, j]]
-        key_place = jnp.broadcast_to(key_place_ref[0], (8, blocks * block)).T[:, :1]
-        allowed = (key_place <= bounds_ref[0, :1, :]) & (key_place >= bounds_ref[0, 1:, :])
-        bias[...] = jnp.where(allowed, 0.0, -1e30)
-        window_grad[...] = jnp.zeros_like(window_grad)
-
-    queries = q_ref[...].reshape(HEADS_STEP * block, HD)
-    grads = jnp.concatenate([grad_ref[:, j * HD : (j + 1) * HD] for j in range(HEADS_STEP)], axis=0)
-    keys, values = window[:, :HD], window[:, HD:]
-    nt = (((1,), (1,)), ((), ()))
-    tn = (((0,), (0,)), ((), ()))
-    scores = lax.dot_general(keys, queries, nt, preferred_element_type=jnp.float32) + bias[...]
-    peak = jnp.max(scores, axis=0, keepdims=True)
-    weights = jnp.exp(scores - peak)
-    probs = weights * (1.0 / jnp.sum(weights, axis=0, keepdims=True))
-    grad_probs = lax.dot_general(values, grads, nt, preferred_element_type=jnp.float32)
-    delta = jnp.sum(probs * grad_probs, axis=0, keepdims=True)
-    grad_scores = (probs * (grad_probs - delta)).astype(jnp.bfloat16)
-    window_grad[:, :HD] += jnp.dot(grad_scores, queries, preferred_element_type=jnp.float32)
-    window_grad[:, HD:] += jnp.dot(
-        probs.astype(jnp.bfloat16), grads, preferred_element_type=jnp.float32
-    )
-    grad_q = lax.dot_general(grad_scores, keys, tn, preferred_element_type=jnp.float32)
-    cosine, sine_part = cos_ref[...], sin_ref[...]
-    for j in range(HEADS_STEP):
-        one = grad_q[j * block : (j + 1) * block]
-        one = (one * cosine - pltpu.roll(one, HD // 2, 1) * sine_part) * HD ** (-0.5)
-        grad_q_ref[:, j * HD : (j + 1) * HD] = one.astype(jnp.bfloat16)
-
-    @pl.when(h == last)
-    def _():
-        for j in range(blocks):
-            total_grad[where_ref[r, blocks + j]] += window_grad[j * block : (j + 1) * block, :]
-
-    @pl.when((h == last) & (r == pl.num_programs(0) - 1))
-    def _():
-        grad_kv_ref[...] = total_grad[...].astype(jnp.bfloat16)
-
-
-def attend_back(where, queries, kv_blocks, grads, key_place, bounds, cosine, sine_part):
-    rounds, blocks = where.shape[0], where.shape[1] // 2
+        grad_kv_ref[...] = low(total_grad[...])
+
+
+def attend_back(
+    where, queries, kv_blocks, grads, mixed, log_total, key_place, bounds, cosine, sine_part, earlier
+):
     heads, rows, _ = queries.shape
-    block = rows // rounds
-    span = blocks * block
+    window = Window(rows)
+    block, span, parts = window.block, window.span, heads // HEADS_STEP
     width = HEADS_STEP * block
     grid_spec = pltpu.PrefetchScalarGridSpec(
         num_scalar_prefetch=1,
-        grid=(rounds, heads // HEADS_STEP),
+        grid=(ROUNDS,),
         in_specs=[
-            pl.BlockSpec((HEADS_STEP, block, HD), lambda r, h, *_: (h, r, 0)),
-            pl.BlockSpec(kv_blocks.shape, lambda r, h, *_: (0, 0, 0)),
-            pl.BlockSpec((block, HEADS_STEP * HD), lambda r, h, *_: (r, h)),
-            pl.BlockSpec((1, 1, span), lambda r, h, *_: (r, 0, 0)),
-            pl.BlockSpec((1, 2, width), lambda r, h, *_: (r, 0, 0)),
-            pl.BlockSpec((block, HD), lambda r, h, *_: (r, 0)),
-            pl.BlockSpec((block, HD), lambda r, h, *_: (r, 0)),
-        ],
+            pl.BlockSpec((heads, block, HD), lambda r, *_: (0, r, 0)),
+            pl.BlockSpec(kv_blocks.shape, lambda r, *_: (0, 0, 0)),
+            pl.BlockSpec((block, heads * HD), lambda r, *_: (r, 0)),
+            pl.BlockSpec((block, heads * HD), lambda r, *_: (r, 0)),
+            pl.BlockSpec((1, parts, 1, width), lambda r, *_: (r, 0, 0, 0)),
+            pl.BlockSpec((1, 1, span), lambda r, *_: (r, 0, 0)),
+            pl.BlockSpec((1, 2, width), lambda r, *_: (r, 0, 0)),
+            pl.BlockSpec((block, HD), lambda r, *_: (r, 0)),
+            pl.BlockSpec((block, HD), lambda r, *_: (r, 0)),
+        ]
+        + [ANY] * len(earlier),
         out_specs=[
-            pl.BlockSpec((block, HEADS_STEP * HD), lambda r, h, *_: (r, h)),
-            pl.BlockSpec(kv_blocks.shape, lambda r, h, *_: (0, 0, 0)),
+            pl.BlockSpec((block, heads * HD), lambda r, *_: (r, 0)),
+            pl.BlockSpec(kv_blocks.shape, lambda r, *_: (0, 0, 0)),
         ],
         scratch_shapes=[
             pltpu.VMEM((span, 2 * HD), jnp.bfloat16),
@@ -265,7 +378,7 @@
         ],
     )
     return pl.pallas_call(
-        functools.partial(attend_back_kernel, blocks, block),
+        functools.partial(attend_back_kernel, window.blocks, block),
         name="attend_back",
         grid_spec=grid_spec,
         out_shape=[
@@ -273,10 +386,21 @@
             jax.ShapeDtypeStruct(kv_blocks.shape, jnp.bfloat16),
         ],
         compiler_params=pltpu.CompilerParams(vmem_limit_bytes=VMEM_LIMIT),
-    )(where, queries, kv_blocks, grads, key_place, bounds, cosine, sine_part)
-
-
-ANY = pl.BlockSpec(memory_space=pl.ANY)
+    )(
+        where,
+        queries,
+        kv_blocks,
+        grads,
+        mixed,
+        log_total,
+        key_place,
+        bounds,
+        cosine,
+        sine_part,
+        *earlier,
+    )
+
+
 MIDDLE_TILES = 3
 
 
@@ -370,72 +494,72 @@
     )(grad, middle, upstream, mixed, gains, w)
 
 
-def project_back_kernel(
-    grad_q_ref, grad_kv_ref, cos_ref, sin_ref, normed_ref, x_ref, grad_middle_ref, gain_ref, w_ref,
-    grad_w_ref, grad_x_ref, grad_gain_ref, joined, grad_normed,
-):
-    step = pl.program_id(0)
-    inner = grad_q_ref.shape[1]
-    tile = w_ref.shape[0]
-
-    @pl.when(step == 0)
-    def _():
-        joined[:, :inner] = grad_q_ref[...]
-        keys = grad_kv_ref[:, :HD]
-        keys = keys * cos_ref[...] - pltpu.roll(keys, HD // 2, 1) * sin_ref[...]
-        joined[:, inner : inner + HD] = low(keys)
-        joined[:, inner + HD :] = low(grad_kv_ref[:, HD:])
-
-    columns = pl.ds(pl.multiple_of(step * tile, tile), tile)
-    grad_normed[:, columns] = nt_dot(joined[...], w_ref[...])
-    grad_w_ref[...] = low(tn_dot(normed_ref[...], joined[...]))
-
-    @pl.when(step == pl.num_programs(0) - 1)
-    def _():
-        values = x_ref[...].astype(jnp.float32)
-        grad, grad_gain = norm_back(values, gain_row(gain_ref, 0), grad_normed[...])
-        grad_x_ref[...] = grad_middle_ref[...] + grad
-        grad_gain_ref[...] = grad_gain
-
-
-def project_back(grad_q, grad_kv, cosine, sine_part, normed, x, grad_middle, gains, w):
-    rows, width = x.shape
-    inner = w.shape[1]
+def project_back_queries_kernel(grad_ref, normed_ref, w_ref, grad_w_ref, grad_normed_ref):
+    grad_normed_ref[...] = nt_dot(grad_ref[...], w_ref[...])
+    grad_w_ref[...] = low(tn_dot(normed_ref[...], grad_ref[...]))
+
+
+def project_back_queries(grad_q, normed, w):
+    rows, width = normed.shape
+    inner = grad_q.shape[1]
     tile = width // MIDDLE_TILES
     return pl.pallas_call(
-        project_back_kernel,
-        name="project_back",
+        project_back_queries_kernel,
+        name="project_back_queries",
         grid=(MIDDLE_TILES,),
         in_specs=[
             whole_block(grad_q.shape),
-            whole_block(grad_kv.shape),
-            whole_block(cosine.shape),
-            whole_block(cosine.shape),
             pl.BlockSpec((rows, tile), lambda i: (0, i)),
-            whole_block((rows, width)),
-            whole_block((rows, width)),
-            whole_block(gains.shape),
             pl.BlockSpec((tile, inner), lambda i: (i, 0)),
         ],
         out_specs=[
             pl.BlockSpec((tile, inner), lambda i: (i, 0)),
-            whole_block((rows, width)),
-            whole_block((1, width)),
-        ],
+            pl.BlockSpec((rows, tile), lambda i: (0, i)),
+        ],
+        out_shape=[
+            jax.ShapeDtypeStruct((width, inner), jnp.bfloat16),
+            jax.ShapeDtypeStruct((rows, width), jnp.float32),
+        ],
+        compiler_params=pltpu.CompilerParams(vmem_limit_bytes=VMEM_LIMIT),
+    )(grad_q, normed, w)
+
+
+def project_back_keys_kernel(
+    grad_kv_ref, cos_ref, sin_ref, normed_ref, partial_ref, x_ref, grad_middle_ref, gain_ref, w_ref,
+    grad_w_ref, grad_x_ref, grad_gain_ref,
+):
+    keys = grad_kv_ref[:, :HD]
+    keys = low(keys * cos_ref[...] - pltpu.roll(keys, HD // 2, 1) * sin_ref[...])
+    joined = jnp.concatenate([keys, low(grad_kv_ref[:, HD:])], axis=1)
+    grad_w_ref[...] = low(tn_dot(normed_ref[...], joined))
+    grad_normed = partial_ref[...] + nt_dot(joined, w_ref[...])
+    grad, grad_gain = norm_back(x_ref[...].astype(jnp.float32), gain_row(gain_ref, 0), grad_normed)
+    grad_x_ref[...] = grad_middle_ref[...] + grad
+    grad_gain_ref[...] = grad_gain
+
+
+def project_back_keys(grad_kv, cosine, sine_part, normed, partial, x, grad_middle, gains, w):
+    rows, width = x.shape
+    inner = grad_kv.shape[1]
+    arrays = (grad_kv, cosine, sine_part, normed, partial, x, grad_middle, gains)
+    last = w.shape[1] // inner - 1
+    return pl.pallas_call(
+        project_back_keys_kernel,
+        name="project_back_keys",
+        grid=(1,),
+        in_specs=[whole_block(one.shape) for one in arrays]
+        + [pl.BlockSpec((width, inner), lambda i: (0, last))],
+        out_specs=[whole_block((width, inner)), whole_block((rows, width)), whole_block((1, width))],
         out_shape=[
             jax.ShapeDtypeStruct((width, inner), jnp.bfloat16),
             jax.ShapeDtypeStruct((rows, width), jnp.float32),
             jax.ShapeDtypeStruct((1, width), jnp.float32),
         ],
-        scratch_shapes=[
-            pltpu.VMEM((rows, inner), jnp.bfloat16),
-            pltpu.VMEM((rows, width), jnp.float32),
-        ],
         compiler_params=pltpu.CompilerParams(vmem_limit_bytes=VMEM_LIMIT),
-    )(grad_q, grad_kv, cosine, sine_part, normed, x, grad_middle, gains, w)
-
-
-MESH_ID = pl.DeviceIdType.MESH
+    )(*arrays, w)
+
+
+MESH_ID =MESH_ID = pl.DeviceIdType.MESH
 
 
 class Wire:
@@ -608,6 +732,10 @@
     )
 
 
+def take(values, count):
+    return values[:count], values[count:]
+
+
 class Relay:
     def __init__(self, source, stage, targets, sems):
         self.stage, self.targets, self.sems = stage, targets, sems
@@ -639,7 +767,7 @@
 
 
 def share_line_kernel(
-    shards, pack, in_ref, gain_a, gain_b, mlp_in, mlp_out, in_line, gain_all, mine, token,
+    shards, pack, in_ref, gain_a, gain_b, mlp_in, mlp_out, up_ref, in_line, gain_all, mine, up_x, up_y,
     gain_now, in_stage, packed, tiles, local_sems, load_sems, send_sems, recv_sems,
 ):
     wire = Wire(send_sems, recv_sems)
@@ -650,9 +778,14 @@
     gain_now[...] = jnp.zeros_like(gain_now)
     gain_now[:1] = gain_a[...].astype(jnp.float32)
     gain_now[1:2] = gain_b[...].astype(jnp.float32)
-    token[...] = jnp.zeros_like(token)
-    wire.meet([wire.line(step, shards) for step in range(1, shards)])
-    copies = []
+    wire.meet(
+        [wire.line(step, shards) for step in range(1, shards)] + [wire.plane(2), wire.plane(4)]
+    )
+    half = pack.half
+    copies = [
+        wire.send(up_ref.at[:, pl.ds(0, half)], up_x, wire.plane(2)),
+        wire.send(up_ref.at[:, pl.ds(half, half)], up_y, wire.plane(4)),
+    ]
     for source, target in ((gain_now, gain_all), (in_ref.at[ctx], in_line)):
         for step in range(1, shards):
             copies.append(wire.send(source, target.at[shard], wire.line(step, shards)))
@@ -683,7 +816,7 @@
             continue
         for i, at in enumerate(range(0, pack.rows, split)):
             source = mlp_in.at[pl.ds(at, split), strip(start + chip * main, main)]
-            load(source, packed.at[pl.ds(pack.rows, split), pl.ds(i * tail + column - half, main)])
+            load(source, packed.at[pl.ds(pack.tail_start, split), pl.ds(i * tail + column - half, main)])
     columns = strip(core * half, half)
     for start, count, row in (
         (chip * main, main, pack.out_start),
@@ -701,7 +834,7 @@
     ends = low(jnp.concatenate(ends, axis=1))
     for i, at in enumerate(range(0, pack.rows, split)):
         column = i * tail + shards * main - half
-        packed[pack.rows : pack.rows + split, column : column + shards * rest] = ends[at : at + split]
+        packed[pack.tail_start : pack.tail_start + split, column : column + shards * rest] = ends[at : at + split]
     mine_copy = pltpu.make_async_copy(packed, mine, local_sems.at[1, 1])
     mine_copy.start()
     relay.settle()
@@ -731,8 +864,6 @@
 
 
 def complete(gathers, relays):
-    for relay in relays:
-        relay.push()
     for gather in gathers:
         gather.forward()
     for gather in gathers:
@@ -744,16 +875,16 @@
 
 
 def share_plane_kernel(
-    shards, in_ref, in_line, out_ref, in_all, out_line, token,
-    in_stage, in_piece, out_stage, local_sems, send_sems, recv_sems,
+    shards, devices, in_ref, in_line, out_ref, order, lengths, frequency, in_all, out_line, *refs
 ):
+    tables, scratch = take(refs, len(refs) - 6)
+    in_stage, in_piece, out_stage, local_sems, send_sems, recv_sems = scratch
     wire = Wire(send_sems, recv_sems)
     ctx, shard = wire.ctx, wire.shard
     relays = relay_shards(wire, in_ref, in_line, in_all, in_stage, in_piece, shards, local_sems)
     relays.append(
         Relay(out_ref.at[ctx], out_stage, [(out_stage, out_line.at[shard])], local_sems.at[2])
     )
-    token[...] = jnp.zeros_like(token)
     wire.meet(
         [wire.plane(mask) for mask in PLANE_PEERS] + [wire.line(s, shards) for s in range(1, shards)]
     )
@@ -762,6 +893,9 @@
         wire.send(out_ref.at[ctx], out_line.at[shard], wire.line(step, shards))
         for step in range(1, shards)
     ]
+    for relay in relays:
+        relay.push()
+    place_tables(ctx, devices, order, lengths, frequency, *tables)
     complete(gathers, relays)
     for copy in copies:
         copy.wait_recv()
@@ -781,6 +915,8 @@
     rows = kv_ref.shape[0]
     gathers = [PlaneGather(wire, kv_ref, lambda who: kv_all.at[who], rows, rows // 2)]
     gathers += gather_shards(wire, out_line, out_all, out_ref.shape[1], shards, 1)
+    for relay in relays:
+        relay.push()
     complete(gathers, relays)
     wire.finish()
 
@@ -793,21 +929,21 @@
     return pltpu.VMEM(lead + values.shape[-2:], values.dtype)
 
 
-def share_line(w_in, gain_a, gain_b, mlp_in, mlp_out, pack, shards):
+def share_line(w_in, gain_a, gain_b, mlp_in, mlp_out, upstream, pack, shards):
     columns = gain_a.shape[1]
-    copies = 2 * (shards - 1)
+    copies = 2 * (shards - 1) + 2
     loads = shards + shards + 1 + 2
     return pl.pallas_call(
         functools.partial(share_line_kernel, shards, pack),
         name="share_line",
-        in_specs=[ANY] + [pl.BlockSpec(memory_space=pltpu.VMEM)] * 2 + [ANY] * 2,
-        out_specs=[ANY] * 3 + [pl.BlockSpec(memory_space=pltpu.VMEM)],
+        in_specs=[ANY] + [pl.BlockSpec(memory_space=pltpu.VMEM)] * 2 + [ANY] * 3,
+        out_specs=[ANY] * 5,
         out_shape=[
             like(w_in, shards),
             jax.ShapeDtypeStruct((shards, 8, columns), jnp.float32),
             jax.ShapeDtypeStruct((pack.total, pack.half), mlp_in.dtype),
-            token_shape(),
-        ],
+        ]
+        + [jax.ShapeDtypeStruct((upstream.shape[0], pack.half), upstream.dtype)] * 2,
         scratch_shapes=[
             pltpu.VMEM((8, columns), jnp.float32),
             stage_like(w_in),
@@ -819,17 +955,19 @@
             dma_sems(copies),
         ],
         compiler_params=comm_params(1),
-    )(w_in, gain_a, gain_b, mlp_in, mlp_out)
-
-
-def share_plane(w_in, in_line, w_out, ctx_size, shards):
+    )(w_in, gain_a, gain_b, mlp_in, mlp_out, upstream)
+
+
+def share_plane(w_in, in_line, w_out, order, lengths, rows, ctx_size, shards):
     copies = (shards - 1) * (PlaneGather.COPIES + 1)
+    operands, shapes = place_arrays(order, lengths, rows)
+    vmem = pl.BlockSpec(memory_space=pltpu.VMEM)
     return pl.pallas_call(
-        functools.partial(share_plane_kernel, shards),
+        functools.partial(share_plane_kernel, shards, ctx_size),
         name="share_plane",
-        in_specs=[ANY] * 3,
-        out_specs=[ANY] * 2 + [pl.BlockSpec(memory_space=pltpu.VMEM)],
-        out_shape=[like(w_in, shards, ctx_size), like(w_out, shards), token_shape()],
+        in_specs=[ANY] * 3 + [vmem] * len(operands),
+        out_specs=[ANY] * 2 + [vmem] * len(shapes),
+        out_shape=[like(w_in, shards, ctx_size), like(w_out, shards), *shapes],
         scratch_shapes=[
             stage_like(w_in, ctx_size),
             stage_like(w_in, shards),
@@ -839,7 +977,7 @@
             dma_sems(copies),
         ],
         compiler_params=comm_params(6),
-    )(w_in, in_line, w_out)
+    )(w_in, in_line, w_out, *operands)
 
 
 def gather_plane(key_value, w_out, out_line, ctx_size, shards):
@@ -862,170 +1000,220 @@
     )(key_value, w_out, out_line)
 
 
-def sum_plane_kernel(in_ref, out_ref, own, pair, first, second, local_sem, send_sems, recv_sems):
-    wire = Wire(send_sems, recv_sems)
-    wire.meet([wire.plane(mask) for mask in PLANE_PEERS])
-    total = PlaneSum(wire, in_ref, own, pair, first, second, local_sem)
-    total.step_one()
-    total.step_two()
-
-    def store(part, value):
-        out_ref[part] = value
-
-    total.result(store)
-    wire.finish()
-
-
-def sum_plane(values):
-    rows, columns = values.shape[3:]
-    return pl.pallas_call(
-        sum_plane_kernel,
-        name="sum_plane",
-        in_specs=[ANY],
-        out_specs=pl.BlockSpec(memory_space=pltpu.VMEM),
-        out_shape=jax.ShapeDtypeStruct((4, rows, columns), jnp.float32),
-        scratch_shapes=plane_sum_scratch(rows, columns)
-        + [pltpu.SemaphoreType.DMA, dma_sems(PlaneSum.COPIES), dma_sems(PlaneSum.COPIES)],
-        compiler_params=comm_params(3),
-    )(values)
-
-
-def close_kernel(
-    shards, g_out, g_in, m_ref, gain_a, gain_b, out_all, in_all, m_all, gain_out,
-    *scratch,
-):
-    sums = (scratch[:4], scratch[4:8])
-    mine, arrived = (scratch[8], scratch[9]), (scratch[10], scratch[11])
-    done = (scratch[12], scratch[13])
-    gain_now, gain_in, gain_line, stage = scratch[14:18]
-    local_sems, relay_sems, send_sems, recv_sems = scratch[18:]
+class GainSum:
+    def __init__(self, wire, now, arrived, line, shards):
+        self.wire, self.now, self.arrived, self.line, self.shards = wire, now, arrived, line, shards
+        self.at = 0
+        self.start()
+
+    def start(self):
+        peer = self.wire.plane(PLANE_PEERS[self.at])
+        self.copy = self.wire.send(self.now, self.arrived.at[self.at], peer)
+
+    def add(self):
+        self.copy.wait_recv()
+        self.wire.sent(self.copy)
+        self.now[...] += self.arrived[self.at]
+        self.at += 1
+
+    def step(self):
+        self.add()
+        self.start()
+
+    def step_line(self):
+        self.add()
+        wire, shards = self.wire, self.shards
+        self.copies = [
+            wire.send(
+                self.now.at[lax.rem(wire.shard + step, shards)],
+                self.line.at[step - 1],
+                wire.line(step, shards),
+            )
+            for step in range(1, shards)
+        ]
+
+    def result(self):
+        for copy in self.copies:
+            copy.wait_recv()
+        value = self.now[self.wire.shard]
+        for step in range(self.shards - 1):
+            value += self.line[step]
+        return value
+
+
+def reduce_kernel(shards, plane_count, half_count, line_count, full_count, part_count, gain_count, *refs):
+    planes, refs = take(refs, plane_count)
+    halves, refs = take(refs, half_count)
+    line_ins, refs = take(refs, line_count)
+    fulls, refs = take(refs, full_count)
+    parts, refs = take(refs, part_count)
+    gain_rows, refs = take(refs, gain_count)
+    plane_outs, refs = take(refs, plane_count)
+    half_outs, refs = take(refs, half_count)
+    full_outs, refs = take(refs, line_count + full_count)
+    part_outs, refs = take(refs, part_count)
+    gain_out, refs = take(refs, min(gain_count, 1))
+    sums, refs = take(refs, 4 * (plane_count + half_count + full_count))
+    mine, refs = take(refs, full_count)
+    arrived, refs = take(refs, line_count + full_count)
+    done, refs = take(refs, line_count + full_count)
+    stages, refs = take(refs, part_count)
+    gain_scratch, refs = take(refs, 3 * min(gain_count, 1))
+    sum_sems, done_sems, part_sems, send_sems, recv_sems = refs
+
     wire = Wire(send_sems, recv_sems)
     ctx, shard = wire.ctx, wire.shard
+    relays = [
+        Relay(source, stage, [(stage, target.at[ctx])], part_sems.at[i])
+        for i, (source, stage, target) in enumerate(zip(parts, stages, part_outs))
+    ]
+    if gain_count:
+        gain_now = gain_scratch[0]
+        gain_now[...] = jnp.zeros_like(gain_now)
+        columns = gain_now.shape[2]
+        for part in range(shards):
+            for row, values in enumerate(gain_rows):
+                gain_now[part, row : row + 1] = values[:, part * columns : (part + 1) * columns]
     wire.meet(
         [wire.plane(mask) for mask in PLANE_PEERS] + [wire.line(s, shards) for s in range(1, shards)]
     )
     totals = [
-        PlaneSum(wire, source, *sums[i], local_sems.at[i]) for i, source in enumerate((g_out, g_in))
+        PlaneSum(wire, source, *sums[4 * i : 4 * i + 4], sum_sems.at[i])
+        for i, source in enumerate(planes + halves + fulls)
     ]
-    relay = Relay(m_ref, stage, [(stage, m_all.at[ctx])], relay_sems)
-    gain_now[...] = jnp.zeros_like(gain_now)
-    columns = gain_now.shape[2]
-    for part in range(shards):
-        span = slice(part * columns, (part + 1) * columns)
-        gain_now[part, :1] = gain_a[:, span]
-        gain_now[part, 1:2] = gain_b[:, span]
-
-    def gain_start(at):
-        return wire.send(gain_now, gain_in.at[at], wire.plane(PLANE_PEERS[at]))
-
-    def gain_add(at, copy):
-        copy.wait_recv()
-        wire.sent(copy)
-        gain_now[...] += gain_in[at]
-
-    gain_copy = gain_start(0)
-    for total in totals:
-        total.step_one()
-    gain_add(0, gain_copy)
-    gain_copy = gain_start(1)
-    for total in totals:
-        total.step_two()
-    gain_add(1, gain_copy)
-    gain_copy = gain_start(2)
-    place = lambda who: m_all.at[who]
-    rows = m_ref.shape[0]
-    gathers, locals_ = [PlaneGather(wire, m_ref, place, rows, rows // 2)], []
-    relay.push()
     lines = []
-    for i, total in enumerate(totals):
-
-        def store(part, value, i=i):
-            mine[i][part] = value.astype(jnp.bfloat16)
-
-        total.result(store)
+
+    def send_line(source):
+        target = arrived[len(lines)]
         lines.append(
             [
                 wire.send(
-                    mine[i].at[lax.rem(shard + step, shards)],
-                    arrived[i].at[step - 1],
-                    wire.line(step, shards),
+                    source.at[lax.rem(shard + step, shards)], target.at[step - 1], wire.line(step, shards)
                 )
                 for step in range(1, shards)
             ]
         )
-    gain_add(2, gain_copy)
-    gain_copies = [
-        wire.send(
-            gain_now.at[lax.rem(shard + step, shards)], gain_line.at[step - 1], wire.line(step, shards)
-        )
-        for step in range(1, shards)
-    ]
-    small = []
-    for i, target in enumerate((out_all, in_all)):
+
+    for source in line_ins:
+        send_line(source)
+    gain = GainSum(wire, *gain_scratch, shards) if gain_count else None
+    for total in totals:
+        total.step_one()
+    if gain:
+        gain.step()
+    for total in totals:
+        total.step_two()
+    if gain:
+        gain.step()
+    gathers = []
+    for source, target in zip(parts, part_outs):
+        rows = source.shape[0]
+        place = lambda who, target=target: target.at[who]
+        gathers.append(PlaneGather(wire, source, place, rows, half_rows(rows, len(gathers))))
+    for total, target in zip(totals, plane_outs):
+
+        def store_wide(part, value, target=target):
+            target[part] = value
+
+        total.result(store_wide)
+    for total, target in zip(totals[plane_count:], half_outs + mine):
+
+        def store(part, value, target=target):
+            target[part] = low(value)
+
+        total.result(store)
+    for source in mine:
+        send_line(source)
+    if gain:
+        gain.step_line()
+    for relay in relays:
+        relay.push()
+    locals_ = []
+    for i, (source, target) in enumerate(zip(line_ins + mine, full_outs)):
         for copy in lines[i]:
             copy.wait_recv()
-        value = mine[i][shard].astype(jnp.float32)
+        value = source[shard].astype(jnp.float32)
         for step in range(shards - 1):
             value += arrived[i][step].astype(jnp.float32)
-        done[i][...] = value.astype(jnp.bfloat16)
+        done[i][...] = low(value)
         place = lambda who, target=target: target.at[who]
         rows = target.shape[1]
-        small.append(PlaneGather(wire, done[i], place, rows, half_rows(rows, i)))
-        copy = pltpu.make_async_copy(done[i], place(ctx), local_sems.at[2 + i])
+        gathers.append(PlaneGather(wire, done[i], place, rows, half_rows(rows, i)))
+        copy = pltpu.make_async_copy(done[i], place(ctx), done_sems.at[i])
         copy.start()
         locals_.append(copy)
-    for copy in gain_copies:
-        copy.wait_recv()
-    value = gain_now[shard]
-    for step in range(shards - 1):
-        value += gain_line[step]
-    gain_out[...] = value
-    for gather in gathers + small:
+    if gain:
+        gain_out[0][...] = gain.result()
+    for gather in gathers:
         gather.forward()
-    for gather in gathers + small:
+    for gather in gathers:
         gather.corner()
-    for gather in gathers + small:
+    for gather in gathers:
         gather.settle()
     for copy in locals_:
         copy.wait()
-    relay.settle()
+    for relay in relays:
+        relay.settle()
     wire.finish()
 
 
-def close(g_out, g_in, m_part, gain_a, gain_b, ctx_size, shards):
+def reduce(name, number, ctx_size, shards, planes=(), halves=(), lines=(), fulls=(), parts=(), gains=()):
     sums, mine, arrived, done = [], [], [], []
-    for grad in (g_out, g_in):
-        rows, columns = grad.shape[3:]
-        sums += plane_sum_scratch(rows, columns)
-        mine.append(pltpu.VMEM((shards, rows, columns), jnp.bfloat16))
+    for array in (*planes, *halves, *fulls):
+        sums += plane_sum_scratch(*array.shape[3:])
+    for array in fulls:
+        mine.append(pltpu.VMEM((shards, *array.shape[3:]), jnp.bfloat16))
+    for array in (*lines, *fulls):
+        rows, columns = array.shape[-2:]
         arrived.append(pltpu.VMEM((shards - 1, rows, columns), jnp.bfloat16))
         done.append(pltpu.VMEM((rows, columns), jnp.bfloat16))
-    gain_shape = (shards, 8, gain_a.shape[1] // shards)
-    rest = [
-        pltpu.VMEM(gain_shape, jnp.float32),
-        pltpu.VMEM((3,) + gain_shape, jnp.float32),
-        pltpu.VMEM((shards - 1,) + gain_shape[1:], jnp.float32),
-        pltpu.VMEM(m_part.shape, m_part.dtype),
-        dma_sems(4),
-        dma_sems(2),
-    ]
-    copies = 2 * (PlaneSum.COPIES + PlaneGather.COPIES + shards - 1) + PlaneGather.COPIES + 3 + shards - 1
-    whole = lambda shape: jax.ShapeDtypeStruct((ctx_size,) + shape, jnp.bfloat16)
+    stages = [pltpu.VMEM(part.shape, part.dtype) for part in parts]
+    copies = PlaneSum.COPIES * (len(planes) + len(halves) + len(fulls))
+    copies += (PlaneGather.COPIES + shards - 1) * (len(lines) + len(fulls))
+    copies += PlaneGather.COPIES * len(parts)
     vmem = pl.BlockSpec(memory_space=pltpu.VMEM)
+    outs = [(vmem, jax.ShapeDtypeStruct((4,) + array.shape[3:], jnp.float32)) for array in planes]
+    outs += [(vmem, jax.ShapeDtypeStruct((4,) + array.shape[3:], array.dtype)) for array in halves]
+    outs += [(ANY, like(array, ctx_size)) for array in (*lines, *fulls)]
+    outs += [(ANY, like(part, ctx_size)) for part in parts]
+    gain_scratch = []
+    if gains:
+        shape = (shards, 8, gains[0].shape[1] // shards)
+        outs.append((vmem, jax.ShapeDtypeStruct(shape[1:], jnp.float32)))
+        gain_scratch = [
+            pltpu.VMEM(shape, jnp.float32),
+            pltpu.VMEM((3,) + shape, jnp.float32),
+            pltpu.VMEM((shards - 1,) + shape[1:], jnp.float32),
+        ]
+        copies += 3 + shards - 1
     return pl.pallas_call(
-        functools.partial(close_kernel, shards),
-        name="close",
-        in_specs=[ANY] * 3 + [vmem] * 2,
-        out_specs=[ANY] * 3 + [vmem],
-        out_shape=[
-            whole(g_out.shape[3:]),
-            whole(g_in.shape[3:]),
-            whole(m_part.shape),
-            jax.ShapeDtypeStruct(gain_shape[1:], jnp.float32),
-        ],
-        scratch_shapes=sums + mine + arrived + done + rest + [dma_sems(copies), dma_sems(copies)],
-        compiler_params=comm_params(4),
-    )(g_out, g_in, m_part, gain_a, gain_b)
+        functools.partial(
+            reduce_kernel,
+            shards,
+            len(planes),
+            len(halves),
+            len(lines),
+            len(fulls),
+            len(parts),
+            len(gains),
+        ),
+        name=name,
+        in_specs=[ANY] * (len(planes) + len(halves))
+        + [vmem] * len(lines)
+        + [ANY] * (len(fulls) + len(parts))
+        + [vmem] * len(gains),
+        out_specs=[spec for spec, _ in outs],
+        out_shape=[shape for _, shape in outs],
+        scratch_shapes=sums + mine + arrived + done + stages + gain_scratch
+        + [
+            dma_sems(max(1, len(planes) + len(halves) + len(fulls))),
+            dma_sems(max(1, len(lines) + len(fulls))),
+            pltpu.SemaphoreType.DMA((max(1, len(parts)), 2)),
+            dma_sems(copies),
+            dma_sems(copies),
+        ],
+        compiler_params=comm_params(number),
+    )(*planes, *halves, *lines, *fulls, *parts, *gains)
 
 
 class Pack:
@@ -1033,22 +1221,29 @@
         self.rows, self.half, self.chips, self.main, self.rest = rows, half, chips, main, rest
         self.tail = units - half
         self.split = rows // (half // self.tail)
-        self.out_start = rows + self.split
-        self.total = self.out_start + main + rest
+        self.out_start = rows
+        self.tail_start = rows + main + rest
+        self.total = self.tail_start + self.split
 
     def in_spans(self, shard):
         yield (0, self.rows), (0, self.half), (shard * self.rows, self.rows), (0, self.half)
         for i, at in enumerate(range(0, self.rows, self.split)):
             yield (
-                (self.rows, self.split),
+                (self.tail_start, self.split),
                 (i * self.tail, self.tail),
                 (shard * self.rows + at, self.split),
                 (self.half, self.tail),
             )
 
     def out_spans(self, shard, shards):
-        yield (self.out_start, self.main), (shard * self.main, self.main)
-        yield (self.out_start + self.main, self.rest), (shards * self.main + shard * self.rest, self.rest)
+        every = (0, self.half)
+        yield (self.out_start, self.main), every, (shard * self.main, self.main), every
+        yield (
+            (self.out_start + self.main, self.rest),
+            every,
+            (shards * self.main + shard * self.rest, self.rest),
+            every,
+        )
 
 
 def finish_kernel(shards, chips, pack, step_rows, main_ref, tail_ref, out_part_ref, in_ref, out_ref):
@@ -1093,13 +1288,13 @@
                 out_ref[start : start + rest, columns] = block[main:].astype(jnp.float32)
 
 
-def finish(values, pack, shards):
-    ctx_size = values.shape[0]
+def finish(first, second, pack, shards):
+    ctx_size = first.shape[0]
     chips = ctx_size // 2
     steps = 8
     tile = pack.rows // steps
     per_out = pack.main + pack.rest
-    assert pack.rows // pack.split == 2 and pack.split % tile == 0 and pack.out_start % per_out == 0
+    assert pack.rows // pack.split == 2 and pack.split % tile == 0 and per_out % tile == 0
     return pl.pallas_call(
         functools.partial(finish_kernel, shards, chips, pack, tile),
         name="finish",
@@ -1108,12 +1303,9 @@
             pl.BlockSpec((ctx_size, tile, pack.half), lambda i: (0, i, 0)),
             pl.BlockSpec(
                 (ctx_size, tile, pack.half),
-                lambda i: (0, pack.rows // tile + i % (pack.split // tile), 0),
+                lambda i: (0, per_out // tile + i % (pack.split // tile), 0),
             ),
-            pl.BlockSpec(
-                (2, per_out, pack.half),
-                lambda i: (jnp.minimum(i, chips - 1), pack.out_start // per_out, 0),
-            ),
+            pl.BlockSpec((2, per_out, pack.half), lambda i: (jnp.minimum(i, chips - 1), 0, 0)),
         ],
         out_specs=[
             pl.BlockSpec((tile, 2 * FF), lambda i: (i, 0)),
@@ -1124,7 +1316,7 @@
             jax.ShapeDtypeStruct((FF // shards, 2 * pack.half), jnp.float32),
         ],
         compiler_params=pltpu.CompilerParams(vmem_limit_bytes=VMEM_LIMIT),
-    )(values, values, values)
+    )(first, second, second)
 
 
 TANH_SCALE = 0.7978845608028654
@@ -1133,8 +1325,8 @@
 
 
 def mlp_kernel(
-    shards, pack, mine, x_own, c_own, c_x, c_y,
-    normed_grad, out_own, out_x, out_y, out_left, out_right, grad_part,
+    shards, pack, mine, x_own, x_x, x_y, c_own, c_x_left, c_x_right, c_y_left, c_y_right, c_left, c_right,
+    normed_grad, out_own, out_x, out_y, out_left, out_right, grad_main, grad_rest,
     w_in, w_out, xs, cs, hidden, grads, part, from_x, from_y, corner_left, corner_right,
     out_stage, pair_in, pair_out, local_sems, send_sems, recv_sems,
 ):
@@ -1156,29 +1348,41 @@
 
     def spans():
         for shard in range(shards):
-            for p_rows, p_columns, w_rows, w_columns in pack.in_spans(shard):
-                yield (shard, pl.ds(*p_rows), pl.ds(*p_columns)), w_in, (pl.ds(*w_rows), pl.ds(*w_columns))
-            for p_rows, w_rows in pack.out_spans(shard, shards):
-                yield (shard, pl.ds(*p_rows)), w_out, (pl.ds(*w_rows),)
+            for one in pack.in_spans(shard):
+                yield shard, w_in, one
+            for one in pack.out_spans(shard, shards):
+                yield shard, w_out, one
+
+    def packed(shard, one):
+        return mine.at[shard, pl.ds(*one[0]), pl.ds(*one[1])]
+
+    def placed(which, target, one):
+        return target.at[which, pl.ds(*one[2]), pl.ds(*one[3])]
 
     loads = [copy_in(x_own, xs.at[0]), copy_in(c_own, cs.at[0])]
-    for here, target, there in spans():
-        loads.append(copy_in(mine.at[here], target.at[(core,) + there]))
+    for shard, target, one in spans():
+        loads.append(copy_in(packed(shard, one), placed(core, target, one)))
     late = [
         copy_in(source, target)
         for source, target in (
-            (c_x, cs.at[1]),
-            (c_y, cs.at[2]),
+            (x_x, xs.at[1, :, left]),
+            (x_y, xs.at[2, :, right]),
+            (c_x_left, cs.at[1, :, left]),
+            (c_x_right, cs.at[1, :, right]),
+            (c_y_left, cs.at[2, :, left]),
+            (c_y_right, cs.at[2, :, right]),
+            (c_left, cs.at[3, :, left]),
+            (c_right, cs.at[3, :, right]),
         )
     ]
     wire.meet([wire.plane(mask) for mask in PLANE_PEERS])
     x_copies = [
-        wire.send(x_own, xs.at[1], wire.plane(2)),
-        wire.send(x_own, xs.at[2], wire.plane(4)),
+        wire.send(x_own.at[:, right], xs.at[1, :, right], wire.plane(2)),
+        wire.send(x_own.at[:, left], xs.at[2, :, left], wire.plane(4)),
     ]
     swaps = [
-        wire.send(mine.at[here], target.at[(core,) + there], wire.plane(1))
-        for here, target, there in spans()
+        wire.send(packed(shard, one), placed(core, target, one), wire.plane(1))
+        for shard, target, one in spans()
     ]
     for copy in loads:
         copy.wait()
@@ -1186,25 +1390,19 @@
         copy.wait_recv()
 
     def one_chunk(at):
-        def one_tile(tile, carry):
-            columns = pl.ds(pl.multiple_of(tile * UNIT_TILE, UNIT_TILE), UNIT_TILE)
-            gate = dot(xs[at], w_in[0, :, columns])
-            up = dot(xs[at], w_in[1, :, columns])
-            grad = nt_dot(cs[at, :, left], w_out[0, columns, :])
-            grad += nt_dot(cs[at, :, right], w_out[1, columns, :])
-            square = gate * gate
-            bend = jnp.tanh(TANH_SCALE * gate * (1.0 + TANH_CUBE * square))
-            lift = 0.5 + 0.5 * bend
-            value = gate * lift
-            slope = lift + (0.5 * TANH_SCALE) * gate * (1.0 - bend * bend) * (
-                1.0 + (3.0 * TANH_CUBE) * square
-            )
-            hidden[at, :, columns] = low(value * up)
-            grads[0, at, :, columns] = low(grad * up * slope)
-            grads[1, at, :, columns] = low(grad * value)
-            return carry
-
-        lax.fori_loop(0, tiles, one_tile, 0)
+        gate = dot(xs[at], w_in[0])
+        up = dot(xs[at], w_in[1])
+        grad = nt_dot(cs[at, :, left], w_out[0]) + nt_dot(cs[at, :, right], w_out[1])
+        square = gate * gate
+        bend = jnp.tanh(TANH_SCALE * gate * (1.0 + TANH_CUBE * square))
+        lift = 0.5 + 0.5 * bend
+        value = gate * lift
+        slope = lift + (0.5 * TANH_SCALE) * gate * (1.0 - bend * bend) * (
+            1.0 + (3.0 * TANH_CUBE) * square
+        )
+        hidden[at] = low(value * up)
+        grads[0, at] = low(grad * up * slope)
+        grads[1, at] = low(grad * value)
 
         def one_half(span):
             total = nt_dot(grads[0, at], w_in[0, span, :])
@@ -1218,15 +1416,11 @@
     for copy in x_copies:
         copy.wait_recv()
     corners = [
-        wire.send(xs.at[1, :, left], xs.at[3, :, left], wire.plane(4)),
-        wire.send(xs.at[2, :, right], xs.at[3, :, right], wire.plane(2)),
+        wire.send(x_x, xs.at[3, :, left], wire.plane(4)),
+        wire.send(x_y, xs.at[3, :, right], wire.plane(2)),
     ]
     for copy in late:
         copy.wait()
-    corners += [
-        wire.send(cs.at[1, :, left], cs.at[3, :, left], wire.plane(4)),
-        wire.send(cs.at[2, :, right], cs.at[3, :, right], wire.plane(2)),
-    ]
     one_half = one_chunk(1)
     part[0, :, left] = low(one_half(left))
     early = [wire.send(part.at[0, :, left], from_x.at[:, left], wire.plane(2))]
@@ -1243,22 +1437,21 @@
     part[2, :, right] = low(one_half(right))
     corner.append(wire.send(part.at[2, :, right], corner_right, wire.plane(4)))
 
-    for at, target in ((1, out_x), (2, out_y), (0, out_own), (3, None)):
+    out_copies = {}
+
+    def out_part(at, targets):
         slot = at % 2
-        if at in (0, 3):
-            for copy in out_copies[slot]:
-                copy.wait()
-        else:
-            out_copies = {} if at == 1 else out_copies
+        for copy in out_copies.get(slot, ()):
+            copy.wait()
         for n, span in enumerate((left, right)):
             out_stage[slot, :, span] = low(dot(hidden[at], w_out[n]))
-        if target is None:
-            out_copies[slot] = [
-                copy_in(out_stage.at[slot, :, left], out_left),
-                copy_in(out_stage.at[slot, :, right], out_right),
-            ]
-        else:
-            out_copies[slot] = [copy_in(out_stage.at[slot], target)]
+        out_copies[slot] = [copy_in(out_stage.at[(slot,) + here], target) for here, target in targets]
+
+    every = slice(None)
+    out_part(3, [((every, left), out_left), ((every, right), out_right)])
+    out_part(2, [((), out_y)])
+    out_part(1, [((), out_x)])
+    out_part(0, [((), out_own)])
 
     everything = lambda ref: ref[...].reshape(ref.shape[0] * rows, ref.shape[2])
 
@@ -1300,8 +1493,13 @@
         span, value = out_tile(core, tile)
         pairs_out[tile].wait_recv()
         w_out[1, span, :] = low(value + pair_out[span, :].astype(jnp.float32))
-    for here, source, there in spans():
-        final.append(copy_in(source.at[(1,) + there], grad_part.at[here]))
+    for shard, source, one in spans():
+        start, count = one[0]
+        if start < pack.rows:
+            target = grad_main.at[shard, pl.ds(start, count), pl.ds(*one[1])]
+        else:
+            target = grad_rest.at[shard, pl.ds(start - pack.rows, count), pl.ds(*one[1])]
+        final.append(copy_in(placed(1, source, one), target))
     for copy in early + merged:
         copy.wait_recv()
     normed_grad[...] += from_x[...].astype(jnp.float32) + from_y[...].astype(jnp.float32)
@@ -1314,20 +1512,20 @@
 
 
 def mlp(mine, x, upstream, pack):
-    rows, width = x.shape
+    rows, width = x[0].shape
     half = width // 2
     units = pack.half + pack.tail
     shards = mine.shape[0]
     low_shape = lambda *shape: jax.ShapeDtypeStruct(shape, jnp.bfloat16)
     low_scratch = lambda *shape: pltpu.VMEM(shape, jnp.bfloat16)
     parts = shards * (1 + pack.rows // pack.split + 2)
-    copies = parts + 6 + 2 + 2 + 2 + 2 * (units // UNIT_TILE)
-    locals_ = 2 + parts + 2 + 5 + parts
+    copies = parts + 4 + 2 + 2 + 2 + 2 * (units // UNIT_TILE)
+    locals_ = 2 + parts + 8 + 5 + parts
     return pl.pallas_call(
         functools.partial(mlp_kernel, shards, pack),
         name="mlp",
-        in_specs=[ANY] * 5,
-        out_specs=[pl.BlockSpec(memory_space=pltpu.VMEM)] + [ANY] * 6,
+        in_specs=[ANY] * 11,
+        out_specs=[pl.BlockSpec(memory_space=pltpu.VMEM)] + [ANY] * 7,
         out_shape=[
             jax.ShapeDtypeStruct((rows, width), jnp.float32),
             low_shape(rows, width),
@@ -1335,7 +1533,8 @@
             low_shape(rows, width),
             low_shape(rows, half),
             low_shape(rows, half),
-            low_shape(*mine.shape),
+            low_shape(shards, pack.rows, half),
+            low_shape(shards, pack.total - pack.rows, half),
         ],
         scratch_shapes=[
             low_scratch(2, width, units),
@@ -1359,7 +1558,7 @@
         compiler_params=pltpu.CompilerParams(
             collective_id=5, has_side_effects=True, vmem_limit_bytes=MLP_VMEM
         ),
-    )(mine, x, *upstream)
+    )(mine, *x, *upstream)
 
 
 class Layout:
@@ -1384,51 +1583,28 @@
     def same_core_groups(self):
         return [[chip * 2 + core for chip in range(self.chips)] for core in range(2)]
 
-    def from_neighbours(self, values):
-        return self.xor(values, 2), self.xor(values, 4)
-
-    def from_corner(self, from_x, from_y):
-        half = from_x.shape[1] // 2
-        return self.xor(from_x[:, :half], 4), self.xor(from_y[:, half:], 2)
-
-    def scatter_chip_blocks(self, own, to_x, to_y, left, right, token):
+    def join_corner(self, to_x, to_y, left, right, token):
         half = left.shape[1]
         left = after(token, self.xor(left, 2))
         right = after(token, self.xor(right, 4))
         to_y = jnp.concatenate([add_low(to_y[:, :half], left), to_y[:, half:]], axis=1)
         to_x = jnp.concatenate([to_x[:, :half], add_low(to_x[:, half:], right)], axis=1)
+        return to_x, to_y
+
+    def sum_neighbours(self, own, to_x, to_y):
         wide = lambda part: part.astype(jnp.float32)
         return wide(own) + wide(self.xor(to_y, 4)) + wide(self.xor(to_x, 2))
 
     def gather_chips(self, values):
-        if self.chips != 4:
-            return lax.all_gather(
-                values, "ctx", axis=0, tiled=True, axis_index_groups=self.same_core_groups()
-            )
-        from_x, from_y = self.from_neighbours(values)
-        left, right = self.from_corner(from_x, from_y)
-        own = values
-        return jnp.concatenate([own, from_x, from_y, jnp.concatenate([left, right], axis=1)], axis=0)
+        groups = self.same_core_groups()
+        return lax.all_gather(values, "ctx", axis=0, tiled=True, axis_index_groups=groups)
 
     def scatter_chips(self, partial):
-        if self.chips != 4:
-            return lax.psum_scatter(
-                low(partial),
-                "ctx",
-                scatter_dimension=0,
-                tiled=True,
-                axis_index_groups=self.same_core_groups(),
-            ).astype(jnp.float32)
-        own, to_x, to_y, corner = jnp.split(partial, 4, axis=0)
-        half = own.shape[1] // 2
-        corner = low(corner)
-        left = self.xor(corner[:, :half], 2).astype(jnp.float32)
-        right = self.xor(corner[:, half:], 4).astype(jnp.float32)
-        to_y = jnp.concatenate([to_y[:, :half] + left, to_y[:, half:]], axis=1)
-        to_x = jnp.concatenate([to_x[:, :half], to_x[:, half:] + right], axis=1)
-        from_y = self.xor(low(to_y), 4).astype(jnp.float32)
-        from_x = self.xor(low(to_x), 2).astype(jnp.float32)
-        return own + from_y + from_x
+        groups = self.same_core_groups()
+        total = lax.psum_scatter(
+            low(partial), "ctx", scatter_dimension=0, tiled=True, axis_index_groups=groups
+        )
+        return total.astype(jnp.float32)
 
     def columns_of_chip(self, weights, start):
         parts = []
@@ -1533,23 +1709,6 @@
         total = jnp.sum(lax.all_gather(grad, ("ctx", "fsdp"), axis=0), axis=0)
         rows = grad.shape[0] // self.shards
         return lax.dynamic_slice_in_dim(total, lax.axis_index("fsdp") * rows, rows)
-
-
-def window_blocks(places_all, own_places, seq_ends, block):
-    count = places_all.shape[0] // block
-    blocks = places_all.reshape(count, block)
-    held = blocks[:, 0] // block
-    at = jnp.arange(count, dtype=jnp.int32)
-    position = jnp.sum(jnp.where(held[None, :] == at[:, None], at[None, :], 0), axis=1)
-    span = (WINDOW + block - 2) // block + 1
-    first = own_places.reshape(-1, block)[:, 0] // block
-    wanted = first[:, None] - (span - 1) + jnp.arange(span, dtype=jnp.int32)[None, :]
-    where = position[jnp.maximum(wanted, 0)]
-    key_place = jnp.where((wanted >= 0)[:, :, None], blocks[where], jnp.int32(1 << 30))
-    key_place = key_place.reshape(where.shape[0], 1, span * block)
-    starts = jnp.where(seq_ends[None, :] <= own_places[:, None], seq_ends[None, :], 0)
-    least = jnp.maximum(jnp.max(starts, axis=1), own_places - (WINDOW - 1))
-    return where, key_place, least
 
 
 def per_device(
@@ -1570,35 +1729,33 @@
     x, upstream = tokens[0], cotangent[0]
     own_rows, width = x.shape
     block = own_rows // ROUNDS
-    places_all = order[0]
-    own_places = lax.dynamic_slice_in_dim(places_all, lay.index * own_rows, own_rows)
-    where, key_place, least = window_blocks(
-        places_all, own_places, jnp.cumsum(lengths[0]), block
-    )
-    target = where % ROUNDS * ctx_size + where // ROUNDS
-    where = jnp.concatenate([where, target], axis=1)
-    bounds = jnp.stack([own_places, least])
-    bounds_wide = bounds.reshape(2, ROUNDS, block).transpose(1, 0, 2)
-    bounds_wide = jnp.tile(bounds_wide, (1, 1, HEADS_STEP))
-    frequency = 10000.0 ** (-jnp.arange(HD // 2, dtype=jnp.float32) / (HD // 2))
-    angles = own_places.astype(jnp.float32)[:, None] * frequency[None, :]
-    cosine = jnp.cos(angles)
-    sine_part = jnp.sin(angles)
-    cosine = jnp.concatenate([cosine, cosine], axis=1)
-    sine_part = jnp.concatenate([-sine_part, sine_part], axis=1)
-
     if lay.plane:
         pack = Pack(w_mlp_in.shape[0], width // 2, lay.chips, FF // lay.chips, lay.main, lay.rest)
         pieces = lambda w: w.reshape(ctx_size, w.shape[0] // ctx_size, w.shape[1])
-        in_line, gains, mine, _ = share_line(
-            pieces(w_attn_in), norm_attn[None], norm_mlp[None], w_mlp_in, w_mlp_out, pack, fsdp_size
+        in_line, gains, mine, upstream_x, upstream_y = share_line(
+            pieces(w_attn_in),
+            norm_attn[None],
+            norm_mlp[None],
+            w_mlp_in,
+            w_mlp_out,
+            upstream,
+            pack,
+            fsdp_size,
         )
         mine = lax.all_gather(mine, "fsdp", axis=0)
-        in_attn, out_line, token = share_plane(
-            pieces(w_attn_in), in_line, pieces(w_attn_out), ctx_size, fsdp_size
+        in_attn, out_line, *tables = share_plane(
+            pieces(w_attn_in),
+            in_line,
+            pieces(w_attn_out),
+            order,
+            lengths,
+            own_rows,
+            ctx_size,
+            fsdp_size,
         )
         in_attn = in_attn.reshape(width, -1)
     else:
+        tables = place_tables_alone(ctx_size, order, lengths, own_rows)
         in_attn = lay.gather_whole(w_attn_in)
         out_attn = lay.gather_whole(w_attn_out)
         gains = jnp.pad(jnp.stack([norm_attn, norm_mlp]).astype(jnp.float32), ((0, 6), (0, 0)))
@@ -1607,24 +1764,38 @@
         out_mlp = lay.gather_mlp_out(w_mlp_out)
         upstream_all = lay.gather_chips(upstream)
 
+    where, key_place, bounds, bounds_wide, cosine, sine_part = tables
     normed_one, queries, key_value = project(x, gains, in_attn, cosine, sine_part)
     if lay.plane:
         key_value, out_attn, token = gather_plane(
             key_value, pieces(w_attn_out), out_line, ctx_size, fsdp_size
         )
         out_attn = out_attn.reshape(-1, width)
-        upstream_all = (upstream,) + lay.from_neighbours(after(token, upstream))
+        half = width // 2
+        upstream_all = (
+            upstream,
+            upstream_x,
+            lay.xor(after(token, upstream[:, half:]), 2),
+            lay.xor(after(token, upstream[:, :half]), 4),
+            upstream_y,
+            lay.xor(after(token, upstream_x), 4),
+            lay.xor(after(token, upstream_y), 2),
+        )
     else:
         key_value = lax.all_gather(key_value, "ctx", axis=0)
     key_value = key_value.reshape(ctx_size * ROUNDS, block, 2 * HD)
-    mixed = attend(where, queries, key_value, key_place, bounds.T)
+    mixed, log_total = attend(where, queries, key_value, key_place, bounds)
     middle, normed_two = middle_forward(x, mixed, gains, out_attn)
 
     if lay.plane:
-        grad_normed_two, *out_parts, grad_mlp = mlp(
-            mine, normed_two, upstream_all, pack
+        grad_normed_two, out_own, *out_parts, grad_main, grad_rest = mlp(
+            mine,
+            (normed_two, lay.xor(normed_two[:, :half], 2), lay.xor(normed_two[:, half:], 4)),
+            upstream_all,
+            pack,
         )
-        grad_mlp = lax.psum_scatter(grad_mlp, "fsdp", scatter_dimension=0, tiled=True)[0]
+        grad_main = lax.psum_scatter(grad_main, "fsdp", scatter_dimension=0, tiled=True)[0]
+        grad_rest = lax.psum_scatter(grad_rest, "fsdp", scatter_dimension=0, tiled=True)[0]
     else:
         normed_all = lay.gather_chips(normed_two)
         gate = dot(normed_all, gate_in)
@@ -1643,38 +1814,62 @@
     grad_middle, grad_mixed, grad_out_attn, grad_gain_mlp, token = middle_back(
         grad_normed_two, middle, upstream, mixed, gains, out_attn
     )
-    if lay.plane:
-        mixed_out = lay.scatter_chip_blocks(*out_parts, token)
-    result = middle + mixed_out
+    out_parts = lay.join_corner(*out_parts, token) if lay.plane else ()
     grad_query, grad_kv = attend_back(
-        where, queries, key_value, grad_mixed, key_place, bounds_wide, cosine, sine_part
+        where,
+        queries,
+        key_value,
+        grad_mixed,
+        mixed,
+        log_total,
+        key_place,
+        bounds_wide,
+        cosine,
+        sine_part,
+        out_parts,
     )
     if lay.plane:
-        grad_kv = sum_plane(grad_kv.reshape(ROUNDS, lay.chips, 2, block, 2 * HD))
+        mixed_out = lay.sum_neighbours(out_own, *out_parts)
+    result = middle + mixed_out
+    grad_in_queries, grad_normed = project_back_queries(grad_query, normed_one, in_attn)
+    split = lambda grad: grad.reshape(fsdp_size, lay.chips, 2, -1, grad.shape[1])
+    if lay.plane:
+        grad_kv = grad_kv.reshape(ROUNDS, lay.chips, 2, block, 2 * HD)
+        grad_kv, grad_out_attn, grad_in_queries, grad_main = reduce(
+            "reduce_early",
+            3,
+            ctx_size,
+            fsdp_size,
+            planes=[grad_kv],
+            halves=[split(grad_out_attn), split(grad_in_queries)],
+            parts=[grad_main],
+        )
         grad_kv = grad_kv.reshape(own_rows, 2 * HD)
     else:
         grad_kv = grad_kv.reshape(ROUNDS, ctx_size, block, 2 * HD)
         grad_kv = lax.psum_scatter(grad_kv, "ctx", scatter_dimension=1, tiled=True)
         grad_kv = grad_kv.reshape(own_rows, 2 * HD).astype(jnp.float32)
-    grad_in_attn, grad_inputs, grad_gain_attn = project_back(
-        grad_query, grad_kv, cosine, sine_part, normed_one, x, grad_middle, gains, in_attn
+    grad_in_keys, grad_inputs, grad_gain_attn = project_back_keys(
+        grad_kv, cosine, sine_part, normed_one, grad_normed, x, grad_middle, gains, in_attn
     )
     if lay.plane:
-        split = lambda grad: grad.reshape(fsdp_size, lay.chips, 2, -1, grad.shape[1])
-        grad_out_attn, grad_in_attn, grad_mlp, grad_gains = close(
-            split(grad_out_attn),
-            split(grad_in_attn),
-            grad_mlp,
-            grad_gain_attn,
-            grad_gain_mlp,
+        grad_out_attn, grad_in_queries, grad_in_keys, grad_rest, grad_gains = reduce(
+            "reduce_late",
+            4,
             ctx_size,
             fsdp_size,
+            lines=[grad_out_attn, grad_in_queries],
+            fulls=[split(grad_in_keys)],
+            parts=[grad_rest],
+            gains=[grad_gain_attn, grad_gain_mlp],
         )
         whole = lambda grad: grad.reshape(-1, grad.shape[2]).astype(jnp.float32)
-        grad_out_attn, grad_in_attn = whole(grad_out_attn), whole(grad_in_attn)
-        grad_in_mlp, grad_out_mlp = finish(grad_mlp, pack, fsdp_size)
+        grad_out_attn = whole(grad_out_attn)
+        grad_in_attn = jnp.concatenate([whole(grad_in_queries), whole(grad_in_keys)], axis=1)
+        grad_in_mlp, grad_out_mlp = finish(grad_main, grad_rest, pack, fsdp_size)
         grad_gain_attn, grad_gain_mlp = grad_gains[0], grad_gains[1]
     else:
+        grad_in_attn = jnp.concatenate([grad_in_queries, grad_in_keys], axis=1)
         grad_out_attn = lay.reduce_whole(grad_out_attn)
         grad_in_attn = lay.reduce_whole(grad_in_attn)
         grad_in_mlp = lay.order_mlp_in(lax.all_gather(grad_in_mlp, "ctx", axis=0))

time: 486 us -> 454 us (0.934)
  Pallas kernels: 413 us -> 385 us
    pallas_call x1, Pallas kernels: 107 us -> 84.7 us  [mlp(): pl.pallas_call(functools.partial(mlp_kernel, shards, pack), name='mlp', i...]
    ppermute x6 -> x10, waiting for transfers between devices: 0.02 us -> 13.4 us  [xor(): return lax.ppermute(values, 'ctx', pairs)]
    reduce_scatter x1 -> x2, waiting for transfers between devices: 15.2 us -> 3.48 us  [the longest x1 3.48 us: per_device(): lax.psum_scatter(grad_main, 'fsdp', scatter_dimension=0, tiled=True)[0]]
    pallas_call x6 -> x7, Pallas kernels: 217 us -> 210 us  [the longest x2 131 us: reduce(): pl.pallas_call(functools.partial(reduce_kernel, shards, len(planes), len(...]
    ppermute x6 -> x10, starting transfers between devices: 6.41 us -> 10.5 us  [xor(): return lax.ppermute(values, 'ctx', pairs)]
  transfers between devices with their start and end apart: 8 -> 13, of which waited for: 2 -> 4; matrix products, arithmetic and copies ran while one was open for 3% -> 2% of each run, Pallas kernels for 34% -> 48%
where the time goes in v4:
time: 454 us; the launch traced here: 447 us
  Pallas kernels  385 us (85%)
  waiting for transfers between devices  17.6 us (4%)
  between operations  15.6 us (3%)
  starting transfers between devices  10.6 us (2%)
  local copies, waits for them, and re-layouts  9.31 us (2%)
  other arithmetic  8.36 us (2%)
    pallas_call x2, Pallas kernels, reduce(): pl.pallas_call(functools.partial(reduce_kernel, shards, len(planes), len(...  131 us
    pallas_call x1, Pallas kernels, mlp(): pl.pallas_call(functools.partial(mlp_kernel, shards, pack), name='mlp', i...  84.7 us
    pallas_call x1, Pallas kernels, gather_plane(): pl.pallas_call(functools.partial(gather_plane_kernel, shards), name='gath...  27.2 us
    pallas_call x1, Pallas kernels, share_plane(): pl.pallas_call(functools.partial(share_plane_kernel, shards, ctx_size), n...  27.1 us
    pallas_call x1, Pallas kernels, attend_back(): pl.pallas_call(functools.partial(attend_back_kernel, window.blocks, block...  21.9 us
    pallas_call x1, Pallas kernels, share_line(): pl.pallas_call(functools.partial(share_line_kernel, shards, pack), name='...  20.9 us
    pallas_call x1, Pallas kernels, finish(): pl.pallas_call(functools.partial(finish_kernel, shards, chips, pack, tile...  14.4 us
    pallas_call x1, Pallas kernels, attend(): pl.pallas_call(functools.partial(attend_kernel, window.blocks, block), na...  14.3 us
  transfers between devices with their start and end apart: 13, of which 4 were waited for; matrix products, arithmetic and copies ran while one was open for 2% of the time, Pallas kernels for 48%

profile of v4, /device:TPU:0, one launch (start us, length us, event | category | flops | bytes accessed | tf_op | source)
XLA Modules:
  0.0 446.7 jit_solution(4170219385966697226)
XLA Ops:
  7.2 1.2 broadcast_in_dim.15.gain_a
  8.5 1.2 broadcast_in_dim.16.gain_b
  9.7 20.9 %share_line.1 = (bf16[4,48,1792]{2,1,0:T(8,128)(2,1)}, f32[4,8,384]{2,1,0:T(8,128)}, bf16[864,768]{1,0:T(8,128)(2,1)}, bf16[384,768]{1,0:T(8,128)(2,1)}, bf16[384,768]{1,0:T(8,128)(2,1)}) custom-call(bf16[8,48,1792]{2,1,0:T(8,128)(2,1)} %bitcast.41, bf16[1,384]{1,0:T(2,128)(2,1)} %broadcast_in_dim.15.gain_a, bf16[1,384]{1,0:T(2,128)(2,1)} %broadcast_in_dim.16.gain_b, ...), custom_call_target="tpu_custom_call" | custom-call | tf_op jit(solution)/shard_map/share_line/pallas_call | solution.py:936
  33.2 27.1 %share_plane.1 = (bf16[4,8,48,1792]{3,2,1,0:T(8,128)(2,1)}, bf16[4,48,1536]{2,1,0:T(8,128)(2,1)}, s32[8,128]{1,0:T(8,128)}, f32[4,1,1152]{2,1,0:T(1,128)}, f32[3...) custom-call(bf16[8,48,1792]{2,1,0:T(8,128)(2,1)} %bitcast.42, ...), custom_call_target="tpu_custom_call" | custom-call | tf_op jit(solution)/shard_map/share_plane/pallas_call | solution.py:965
  60.3 9.3 %project.1 = (bf16[384,1536]{1,0:T(8,128)(2,1)}, bf16[12,384,128]{2,1,0:T(8,128)(2,1)}, bf16[384,256]{1,0:T(8,128)(2,1)}) custom-call(bf16[384,1536]{1,0:T(8,128)(2,1)} %bitcast.36, f32[4,8,384]{2,1,0:T(8,128)} %get-tuple-element.64.gain_ref, bf16[1536,1792]{1,0:T(8,128)(2,1)} %bitcast.27, f32[384,128]{1,0:T(8,128)} %get-tuple-element.66.cos_ref, ...), custom_call_target="tpu_custom_call" | custom-call | tf_op jit(solution)/shard_map/project/pallas_call | solution.py:102
  69.7 27.2 %gather_plane.1 = (bf16[8,384,256]{2,1,0:T(8,128)(2,1)}, bf16[4,8,48,1536]{3,2,1,0:T(8,128)(2,1)}, s32[8,128]{1,0:T(8,128)}) custom-call(bf16[384,256]{1,0:T(8,128)(2,1)} %get-tuple-element.69.kv_ref, bf16[8,48,1536]{2,1,0:T(8,128)(2,1)} %bitcast.47, bf16[4,48,1536]{2,1,0:T(8,128)(2,1)} %get-tuple-element.70.out_line), custom_call_target="tpu_custom_call" | custom-call | tf_op jit(solution)/shard_map/gather_plane/pallas_call | solution.py:985
  96.9 1.3 slice.42
  103.3 14.3 %attend.1 = (bf16[384,1536]{1,0:T(8,128)(2,1)}, f32[4,3,1,384]{3,2,1,0:T(1,128)}) custom-call(s32[8,128]{1,0:T(8,128)} %get-tuple-element.63.where_ref, bf16[12,384,128]{2,1,0:T(8,128)(2,1)} %get-tuple-element.68.q_ref, bf16[32,96,256]{2,1,0:T(8,128)(2,1)} %bitcast.39, f32[4,1,1152]{2,1,0:T(1,128)} %get-tuple-element.72.key_place_ref, ...), custom_call_target="tpu_custom_call" | custom-call | tf_op jit(solution)/shard_map/attend/pallas_call | solution.py:279
  117.5 7.4 %middle.1 = (f32[384,1536]{1,0:T(8,128)}, bf16[384,1536]{1,0:T(8,128)(2,1)}) custom-call(bf16[384,1536]{1,0:T(8,128)(2,1)} %bitcast.37, bf16[384,1536]{1,0:T(8,128)(2,1)} %get-tuple-element.74.mixed_ref, f32[4,8,384]{2,1,0:T(8,128)} %get-tuple-element.64.gain_ref, bf16[1536,1536]{1,0:T(8,128)(2,1)} %bitcast.34), custom_call_target="tpu_custom_call" | custom-call | tf_op jit(solution)/shard_map/middle/pallas_call | solution.py:426
  125.0 1.3 fusion.1
  128.4 12.6 %collective-permute-done.1.x_y = bf16[384,768]{1,0:T(8,128)(2,1)} collective-permute-done((bf16[384,768]{1,0:T(8,128)(2,1)S(1)}, bf16[384,768]{1,0:T(8,128)(2,1)}, u32[]{:S(2)}, u32[]{:S(2)}) %collective-permute-start.1) | collective-permute-done | bytes 589856 | tf_op jit(solution)/shard_map/ppermute | solution.py:1581
  141.7 84.7 %mlp.1 = (f32[384,1536]{1,0:T(8,128)}, bf16[384,1536]{1,0:T(8,128)(2,1)}, bf16[384,1536]{1,0:T(8,128)(2,1)}, bf16[384,1536]{1,0:T(8,128)(2,1)}, bf16[384,768]{1,...) custom-call(bf16[4,864,768]{2,1,0:T(8,128)(2,1)} %bitcast.43, ...), custom_call_target="tpu_custom_call" | custom-call | tf_op jit(solution)/shard_map/mlp/pallas_call | solution.py:1524
  229.6 11.2 %middle_back.1 = (f32[384,1536]{1,0:T(8,128)}, bf16[384,1536]{1,0:T(8,128)(2,1)}, bf16[1536,1536]{1,0:T(8,128)(2,1)}, f32[1,1536]{1,0:T(1,128)}, s32[8,128]{1,0:T(8,128)}) custom-call(f32[384,1536]{1,0:T(8,128)} %get-tuple-element.84.grad_ref, f32[384,1536]{1,0:T(8,128)} %get-tuple-element.76.middle_ref, bf16[384,1536]{1,0:T(8,128)(2,1)} %bitcast.32, ...), custom_call_target="tpu_custom_call" | custom-call | tf_op jit(solution)/shard_map/middle_back/pallas_call | solution.py:466
  245.4 21.9 %attend_back.1 = (bf16[384,1536]{1,0:T(8,128)(2,1)}, bf16[32,96,256]{2,1,0:T(8,128)(2,1)}) custom-call(s32[8,128]{1,0:T(8,128)} %get-tuple-element.63.where_ref, bf16[12,384,128]{2,1,0:T(8,128)(2,1)} %get-tuple-element.68.q_ref, bf16[32,96,256]{2,1,0:T(8,128)(2,1)} %bitcast.40, bf16[384,1536]{1,0:T(8,128)(2,1)} %get-tuple-element.89.grad_ref, ...), custom_call_target="tpu_custom_call" | custom-call | tf_op jit(solution)/shard_map/attend_back/pallas_call | solution.py:380
  267.4 9.0 %project_back_queries.1 = (bf16[1536,1536]{1,0:T(8,128)(2,1)}, f32[384,1536]{1,0:T(8,128)}) custom-call(bf16[384,1536]{1,0:T(8,128)(2,1)} %get-tuple-element.94.grad_ref, bf16[384,1536]{1,0:T(8,128)(2,1)} %get-tuple-element.95.normed_ref, bf16[1536,1792]{1,0:T(8,128)(2,1)} %bitcast.28), custom_call_target="tpu_custom_call" | custom-call | tf_op jit(solution)/shard_map/project_back_queries/pallas_call | solution.py:506
  276.3 1.6 fusion
  278.0 3.5 reduce-scatter.3.cloned.1.call-done
  281.4 80.6 %reduce_early.1 = (f32[4,96,256]{2,1,0:T(8,128)}, bf16[4,48,1536]{2,1,0:T(8,128)(2,1)}, bf16[4,48,1536]{2,1,0:T(8,128)(2,1)}, bf16[8,384,768]{2,1,0:T(8,128)(2,1)}) custom-call(bf16[4,4,2,96,256]{4,3,2,1,0:T(8,128)(2,1)} %bitcast.48, bf16[4,4,2,48,1536]{4,3,2,1,0:T(8,128)(2,1)} %bitcast.44, bf16[4,4,2,48,1536]{4,3,2,1,0:T(8,128)(2,1)} %bitcast.45, ...), custom_call_target="tpu_custom_call" | custom-call | tf_op jit(solution)/shard_map/reduce_early/pallas_call | solution.py:1189
  362.0 6.7 %project_back_keys.1 = (bf16[1536,256]{1,0:T(8,128)(2,1)}, f32[384,1536]{1,0:T(8,128)}, f32[1,1536]{1,0:T(1,128)}) custom-call(f32[384,256]{1,0:T(8,128)} %bitcast.53, f32[384,128]{1,0:T(8,128)} %get-tuple-element.66.cos_ref, f32[384,128]{1,0:T(8,128)} %get-tuple-element.67.sin_ref, bf16[384,1536]{1,0:T(8,128)(2,1)} %get-tuple-element.95.normed_ref, ...), custom_call_target="tpu_custom_call" | custom-call | tf_op jit(solution)/shard_map/project_back_keys/pallas_call | solution.py:546
  368.8 50.7 %reduce_late.1 = (bf16[8,48,1536]{2,1,0:T(8,128)(2,1)}, bf16[8,48,1536]{2,1,0:T(8,128)(2,1)}, bf16[8,48,256]{2,1,0:T(8,128)(2,1)}, bf16[8,480,768]{2,1,0:T(8,128)(2,1)}, f32[8,384]{1,0:T(8,128)}) custom-call(bf16[4,48,1536]{2,1,0:T(8,128)(2,1)} %get-tuple-element.102.refs_0_, bf16[4,48,1536]{2,1,0:T(8,128)(2,1)} %get-tuple-element.103.refs_1_, ...), custom_call_target="tpu_custom_call" | custom-call | tf_op jit(solution)/shard_map/reduce_late/pallas_call | solution.py:1189
  419.4 1.4 slice_reduce_fusion
  420.8 3.1 bitcast_convert_fusion
  423.9 1.7 maximum_convert_fusion
  425.6 14.4 %finish.1 = (f32[384,9216]{1,0:T(8,128)}, f32[1152,1536]{1,0:T(8,128)}) custom-call(bf16[8,384,768]{2,1,0:T(8,128)(2,1)} %get-tuple-element.112.main_ref, bf16[8,480,768]{2,1,0:T(8,128)(2,1)} %get-tuple-element.113.tail_ref.out_part_ref, bf16[8,480,768]{2,1,0:T(8,128)(2,1)} %get-tuple-element.113.tail_ref.out_part_ref), custom_call_target="tpu_custom_call" | custom-call | tf_op jit(solution)/shard_map/finish/pallas_call | solution.py:1298
  (76 shorter events, 16.9 us)
Async XLA Ops:
  7.2 134.5 %all-gather.3.cloned.1.call-start = ((), (), s32[]{:S(2)}) async-start(), calls=%async_computation.4 | async-start | bytes 6635520 | tf_op jit(solution)/shard_map/all_gather | solution.py:1745
  9.7 21.5 %copy-start.14 = (s32[1,3072]{1,0:T(1,128)S(1)}, s32[1,3072]{1,0:T(1,128)}, u32[]{:S(2)}) copy-start(s32[1,3072]{1,0:T(1,128)} %param.11) | copy-start | bytes 36868
  30.7 250.8 %reduce-scatter.3.cloned.1.call-start = ((), (), s32[]{:S(2)}) async-start(), calls=%async_computation.2 | async-start | bytes 2949120 | tf_op jit(solution)/shard_map/reduce_scatter | solution.py:1797
  69.6 29.2 %copy-start.5 = (bf16[384,768]{1,0:T(8,128)(2,1)S(1)}, bf16[384,768]{1,0:T(8,128)(2,1)}, u32[]{:S(2)}) copy-start(bf16[384,768]{1,0:T(8,128)(2,1)} %get-tuple-element.81.c_y_right) | copy-start | bytes 1769476
  69.6 30.3 %copy-start.4 = (bf16[384,768]{1,0:T(8,128)(2,1)S(1)}, bf16[384,768]{1,0:T(8,128)(2,1)}, u32[]{:S(2)}) copy-start(bf16[384,768]{1,0:T(8,128)(2,1)} %get-tuple-element.79.c_x_left) | copy-start | bytes 1769476
  96.9 4.2 copy-start
  98.9 28.5 %collective-permute-start.5 = (bf16[384,768]{1,0:T(8,128)(2,1)S(1)}, bf16[384,768]{1,0:T(8,128)(2,1)}, u32[]{:S(2)}, u32[]{:S(2)}) collective-permute-start(bf16[384,768]{1,0:T(8,128)(2,1)S(1)} %broadcast_select_fusion), channel_id=1, source_target_pairs={{0,8},{4,12},{8,0},{12,4},{16,24},{20,28},{24,16},{28,20},{1,9},{5... | collective-permute-start | bytes 1769480 | tf_op jit(solution)/shard_map/ppermute | solution.py:1581
  100.0 28.4 %collective-permute-start.4 = (bf16[384,768]{1,0:T(8,128)(2,1)S(1)}, bf16[384,768]{1,0:T(8,128)(2,1)S(1)}, u32[]{:S(2)}, u32[]{:S(2)}) collective-permute-start(bf16[384,768]{1,0:T(8,128)(2,1)S(1)} %broadcast_select_fusion.1), channel_id=1, source_target_pairs={{0,16},{4,20},{8,24},{12,28},{16,0},{20,4},{24,8},{28,12},{1,17},{... | collective-permute-start | bytes 1769480 | tf_op jit(solution)/shard_map/ppermute | solution.py:1581
  101.2 27.2 %collective-permute-start.3 = (bf16[384,768]{1,0:T(8,128)(2,1)S(1)}, bf16[384,768]{1,0:T(8,128)(2,1)S(1)}, u32[]{:S(2)}, u32[]{:S(2)}) collective-permute-start(bf16[384,768]{1,0:T(8,128)(2,1)S(1)} %get-tuple-element.118), channel_id=1, source_target_pairs={{0,16},{4,20},{8,24},{12,28},{16,0},{20,4},{24,8},{28,12},{1,17},{... | collective-permute-start | bytes 1769480 | tf_op jit(solution)/shard_map/ppermute | solution.py:1581
  102.2 26.2 %collective-permute-start.2 = (bf16[384,768]{1,0:T(8,128)(2,1)S(1)}, bf16[384,768]{1,0:T(8,128)(2,1)S(1)}, u32[]{:S(2)}, u32[]{:S(2)}) collective-permute-start(bf16[384,768]{1,0:T(8,128)(2,1)S(1)} %get-tuple-element.119), channel_id=1, source_target_pairs={{0,8},{4,12},{8,0},{12,4},{16,24},{20,28},{24,16},{28,20},{1,9},{5... | collective-permute-start | bytes 1769480 | tf_op jit(solution)/shard_map/ppermute | solution.py:1581
  126.3 14.7 %collective-permute-start.1 = (bf16[384,768]{1,0:T(8,128)(2,1)S(1)}, bf16[384,768]{1,0:T(8,128)(2,1)}, u32[]{:S(2)}, u32[]{:S(2)}) collective-permute-start(bf16[384,768]{1,0:T(8,128)(2,1)S(1)} %get-tuple-element.120), channel_id=1, source_target_pairs={{0,16},{4,20},{8,24},{12,28},{16,0},{20,4},{24,8},{28,12},{1,17},{... | collective-permute-start | bytes 1769480 | tf_op jit(solution)/shard_map/ppermute | solution.py:1581
  127.3 14.4 %collective-permute-start = (bf16[384,768]{1,0:T(8,128)(2,1)S(1)}, bf16[384,768]{1,0:T(8,128)(2,1)}, u32[]{:S(2)}, u32[]{:S(2)}) collective-permute-start(bf16[384,768]{1,0:T(8,128)(2,1)S(1)} %get-tuple-element.121), channel_id=1, source_target_pairs={{0,8},{4,12},{8,0},{12,4},{16,24},{20,28},{24,16},{28,20},{1,9},{5... | collective-permute-start | bytes 1769480 | tf_op jit(solution)/shard_map/ppermute | solution.py:1581
  128.4 13.3 %copy-start.10 = (bf16[384,768]{1,0:T(8,128)(2,1)}, bf16[384,768]{1,0:T(8,128)(2,1)S(1)}, u32[]{:S(2)}) copy-start(bf16[384,768]{1,0:T(8,128)(2,1)S(1)} %collective-permute-done.4.c_left) | copy-start | bytes 1769476
  128.4 13.3 %copy-start.11 = (bf16[384,768]{1,0:T(8,128)(2,1)}, bf16[384,768]{1,0:T(8,128)(2,1)S(1)}, u32[]{:S(2)}) copy-start(bf16[384,768]{1,0:T(8,128)(2,1)S(1)} %collective-permute-done.3.c_y_left) | copy-start | bytes 1769476
  128.4 13.3 %copy-start.12 = (bf16[384,768]{1,0:T(8,128)(2,1)}, bf16[384,768]{1,0:T(8,128)(2,1)S(1)}, u32[]{:S(2)}) copy-start(bf16[384,768]{1,0:T(8,128)(2,1)S(1)} %collective-permute-done.2.c_x_right) | copy-start | bytes 1769476
  226.4 142.3 %reduce-scatter.5.cloned.1.call-start = ((), (), s32[]{:S(2)}) async-start(), calls=%async_computation.3 | async-start | bytes 3686400 | tf_op jit(solution)/shard_map/reduce_scatter | solution.py:1798
  227.5 15.3 %collective-permute-start.8 = (bf16[384,768]{1,0:T(8,128)(2,1)S(1)}, bf16[384,768]{1,0:T(8,128)(2,1)S(1)}, u32[]{:S(2)}, u32[]{:S(2)}) collective-permute-start(bf16[384,768]{1,0:T(8,128)(2,1)S(1)} %copy-done.16), channel_id=1, source_target_pairs={{0,16},{4,20},{8,24},{12,28},{16,0},{20,4},{24,8},{28,12},{1,17},{... | collective-permute-start | bytes 1769480 | tf_op jit(solution)/shard_map/ppermute | solution.py:1581
  228.4 15.6 %collective-permute-start.6 = (bf16[384,768]{1,0:T(8,128)(2,1)S(1)}, bf16[384,768]{1,0:T(8,128)(2,1)S(1)}, u32[]{:S(2)}, u32[]{:S(2)}) collective-permute-start(bf16[384,768]{1,0:T(8,128)(2,1)S(1)} %copy-done.15), channel_id=1, source_target_pairs={{0,8},{4,12},{8,0},{12,4},{16,24},{20,28},{24,16},{28,20},{1,9},{5... | collective-permute-start | bytes 1769480 | tf_op jit(solution)/shard_map/ppermute | solution.py:1581
  243.0 33.3 %collective-permute-start.9 = (bf16[384,1536]{1,0:T(8,128)(2,1)S(1)}, bf16[384,1536]{1,0:T(8,128)(2,1)S(1)}, u32[]{:S(2)}, u32[]{:S(2)}) collective-permute-start(bf16[384,1536]{1,0:T(8,128)(2,1)S(1)} %pad_maximum_fusion.1.refs_0_), channel_id=1, source_target_pairs={{0,8},{4,12},{8,0},{12,4},{16,24},{20,28},{24,16},{28,20},{1,9},{5... | collective-permute-start | bytes 3538952 | tf_op jit(solution)/shard_map/ppermute | solution.py:1581
  244.3 32.0 %collective-permute-start.7 = (bf16[384,1536]{1,0:T(8,128)(2,1)S(1)}, bf16[384,1536]{1,0:T(8,128)(2,1)S(1)}, u32[]{:S(2)}, u32[]{:S(2)}) collective-permute-start(bf16[384,1536]{1,0:T(8,128)(2,1)S(1)} %pad_maximum_fusion.refs_1_), channel_id=1, source_target_pairs={{0,16},{4,20},{8,24},{12,28},{16,0},{20,4},{24,8},{28,12},{1,17},{... | collective-permute-start | bytes 3538952 | tf_op jit(solution)/shard_map/ppermute | solution.py:1581
  267.3 9.0 %copy-start.1 = (f32[384,1536]{1,0:T(8,128)S(1)}, f32[384,1536]{1,0:T(8,128)}, u32[]{:S(2)}) copy-start(f32[384,1536]{1,0:T(8,128)} %get-tuple-element.76.middle_ref) | copy-start | bytes 7077892
  267.3 9.0 %copy-start.6 = (bf16[384,1536]{1,0:T(8,128)(2,1)S(1)}, bf16[384,1536]{1,0:T(8,128)(2,1)}, u32[]{:S(2)}) copy-start(bf16[384,1536]{1,0:T(8,128)(2,1)} %get-tuple-element.82) | copy-start | bytes 3538948
  420.8 3.1 copy-start.9
  420.8 3.1 copy-start.13
  (6 other events, 11.4 us)
Sparse Core Ops, SparseCore 0:
  30.8 106.4 all-gather.2
  226.6 54.8 reduce-scatter.2
  283.7 56.6 reduce-scatter.4

commit v5 on v4

--- a/solution.py
+++ b/solution.py
@@ -70,60 +70,53 @@
     return grad, jnp.sum(incoming * values * scale, axis=0, keepdims=True)
 
 
-def project_kernel(heads, x_ref, gain_ref, w_ref, cos_ref, sin_ref, normed_ref, q_ref, kv_ref):
+def project_kernel(heads, x_ref, gain_ref, w_ref, cos_ref, sin_ref, normed_ref, heads_ref):
     step = pl.program_id(0)
 
     @pl.when(step == 0)
     def _():
         x = x_ref[...].astype(jnp.float32)
-        normed_ref[...] = (x * norm_scale(x) * gain_row(gain_ref, 0)).astype(jnp.bfloat16)
-
-    part = jnp.dot(normed_ref[...], w_ref[...], preferred_element_type=jnp.float32)
+        normed_ref[...] = low(x * norm_scale(x) * gain_row(gain_ref, 0))
+
+    part = dot(normed_ref[...], w_ref[...])
     cosine, sine_part = cos_ref[...], sin_ref[...]
-
-    def turn(value):
-        return value * cosine + pltpu.roll(value, HD // 2, 1) * sine_part
-
-    @pl.when(step < heads // 2)
-    def _():
-        for j in range(2):
-            q_ref[j] = (turn(part[:, j * HD : (j + 1) * HD]) * HD ** (-0.5)).astype(jnp.bfloat16)
-
-    @pl.when(step == heads // 2)
-    def _():
-        kv_ref[:, :HD] = turn(part[:, :HD]).astype(jnp.bfloat16)
-        kv_ref[:, HD:] = part[:, HD:].astype(jnp.bfloat16)
+    count = heads_ref.shape[0]
+    for j in range(count):
+        value = part[:, j * HD : (j + 1) * HD]
+        turned = value * cosine + pltpu.roll(value, HD // 2, 1) * sine_part
+        head = step * count + j
+        value = jnp.where(head < heads, turned * HD ** (-0.5), jnp.where(head == heads, turned, value))
+        heads_ref[j] = low(value)
 
 
 def project(x, gain, w, cosine, sine_part):
     rows, width = x.shape
-    steps = H // 2 + 1
+    count = (H + 2) // PROJECT_STEPS
     whole = lambda *shape: pl.BlockSpec(shape, lambda i: (0,) * len(shape))
     return pl.pallas_call(
         functools.partial(project_kernel, H),
-        grid=(steps,),
+        grid=(PROJECT_STEPS,),
         name="project",
         in_specs=[
             whole(rows, width),
             whole(*gain.shape),
-            pl.BlockSpec((width, 2 * HD), lambda i: (0, i)),
+            pl.BlockSpec((width, count * HD), lambda i: (0, i)),
             whole(rows, HD),
             whole(rows, HD),
         ],
         out_specs=[
             whole(rows, width),
-            pl.BlockSpec((2, rows, HD), lambda i: (jnp.minimum(i, H // 2 - 1), 0, 0)),
-            whole(rows, 2 * HD),
+            pl.BlockSpec((count, rows, HD), lambda i: (i, 0, 0)),
         ],
         out_shape=[
             jax.ShapeDtypeStruct((rows, width), jnp.bfloat16),
-            jax.ShapeDtypeStruct((H, rows, HD), jnp.bfloat16),
-            jax.ShapeDtypeStruct((rows, 2 * HD), jnp.bfloat16),
+            jax.ShapeDtypeStruct((H + 2, rows, HD), jnp.bfloat16),
         ],
         compiler_params=pltpu.CompilerParams(vmem_limit_bytes=VMEM_LIMIT),
     )(x, gain, w, cosine, sine_part)
 
 
+PROJECT_STEPS = 2
 HEADS_STEP = 4
 ANY = pl.BlockSpec(memory_space=pl.ANY)
 
@@ -137,11 +130,14 @@
 
 def place_tables(
     index, devices, order_ref, lengths_ref, frequency_ref,
-    where_ref, key_place_ref, bounds_ref, wide_ref, cos_ref, sin_ref,
+    where_ref, key_place_ref, bounds_ref, wide_ref, cos_ref, sin_ref, order_rows,
 ):
-    count, block = order_ref.shape
+    block = bounds_ref.shape[0] // ROUNDS
+    count = order_ref.shape[1] // block
     window = Window(block * ROUNDS)
-    blocks = order_ref[...].astype(jnp.float32)
+    blocks = [order_ref[:, i * block : (i + 1) * block] for i in range(count)]
+    order_rows[...] = jnp.concatenate(blocks, axis=0).astype(jnp.float32)
+    blocks = order_rows[...]
     block_of = lambda place: jnp.floor((place + 0.5) * (1.0 / block))
     held = block_of(blocks[:, :1])
     offsets = low(blocks - held * block)
@@ -162,7 +158,7 @@
     where_ref[...] = jnp.zeros_like(where_ref)
     own = []
     for r in range(ROUNDS):
-        mine = order_ref[pl.ds(index * ROUNDS + r, 1), :].astype(jnp.float32)
+        mine = order_rows[pl.ds(index * ROUNDS + r, 1), :]
         own.append(mine)
         wanted = block_of(mine[:, :1]) - (window.blocks - 1) + step
         match = (held == jnp.maximum(wanted, 0.0)).astype(jnp.float32)
@@ -192,7 +188,7 @@
     window = Window(rows)
     frequency = 10000.0 ** (-jnp.arange(HD // 2, dtype=jnp.float32) / (HD // 2))
     operands = (
-        order.reshape(-1, window.block),
+        order,
         lengths,
         jnp.concatenate([frequency, frequency])[None],
     )
@@ -214,6 +210,8 @@
     def kernel(*refs):
         place_tables(lax.axis_index("ctx"), devices, *refs)
 
+    block = Window(rows).block
+
     vmem = pl.BlockSpec(memory_space=pltpu.VMEM)
     return pl.pallas_call(
         kernel,
@@ -221,13 +219,19 @@
         in_specs=[vmem] * len(operands),
         out_specs=[vmem] * len(shapes),
         out_shape=shapes,
+        scratch_shapes=[pltpu.VMEM((order.shape[1] // block, block), jnp.float32)],
     )(*operands)
 
 
 def load_window(blocks, block, where_ref, kv_ref, window):
     r = pl.program_id(0)
     for j in range(blocks):
-        window[j * block : (j + 1) * block, :] = kv_ref[where_ref[r, j]]
+        rows = slice(j * block, (j + 1) * block)
+        at = where_ref[r, j]
+        device, round_ = at // ROUNDS, lax.rem(at, ROUNDS)
+        span = pl.ds(pl.multiple_of(round_ * block, 16), block)
+        window[rows, :HD] = kv_ref[device, 0, span, :]
+        window[rows, HD:] = kv_ref[device, 1, span, :]
 
 
 def attend_kernel(
@@ -255,7 +259,7 @@
 
 
 def attend(where, queries, kv_blocks, key_place, bounds):
-    heads, rows, _ = queries.shape
+    heads, rows = H, queries.shape[1]
     window = Window(rows)
     block, span, parts = window.block, window.span, heads // HEADS_STEP
     grid_spec = pltpu.PrefetchScalarGridSpec(
@@ -263,7 +267,7 @@
         grid=(ROUNDS,),
         in_specs=[
             pl.BlockSpec((heads, block, HD), lambda r, *_: (0, r, 0)),
-            pl.BlockSpec(kv_blocks.shape, lambda r, *_: (0, 0, 0)),
+            pl.BlockSpec(kv_blocks.shape, lambda r, *_: (0, 0, 0, 0)),
             pl.BlockSpec((1, 1, span), lambda r, *_: (r, 0, 0)),
             pl.BlockSpec((block, 2), lambda r, *_: (r, 0)),
         ],
@@ -347,7 +351,8 @@
 def attend_back(
     where, queries, kv_blocks, grads, mixed, log_total, key_place, bounds, cosine, sine_part, earlier
 ):
-    heads, rows, _ = queries.shape
+    heads, rows = H, queries.shape[1]
+    kv_sums = (kv_blocks.shape[0] * ROUNDS, rows // ROUNDS, 2 * HD)
     window = Window(rows)
     block, span, parts = window.block, window.span, heads // HEADS_STEP
     width = HEADS_STEP * block
@@ -356,7 +361,7 @@
         grid=(ROUNDS,),
         in_specs=[
             pl.BlockSpec((heads, block, HD), lambda r, *_: (0, r, 0)),
-            pl.BlockSpec(kv_blocks.shape, lambda r, *_: (0, 0, 0)),
+            pl.BlockSpec(kv_blocks.shape, lambda r, *_: (0, 0, 0, 0)),
             pl.BlockSpec((block, heads * HD), lambda r, *_: (r, 0)),
             pl.BlockSpec((block, heads * HD), lambda r, *_: (r, 0)),
             pl.BlockSpec((1, parts, 1, width), lambda r, *_: (r, 0, 0, 0)),
@@ -368,13 +373,13 @@
         + [ANY] * len(earlier),
         out_specs=[
             pl.BlockSpec((block, heads * HD), lambda r, *_: (r, 0)),
-            pl.BlockSpec(kv_blocks.shape, lambda r, *_: (0, 0, 0)),
+            pl.BlockSpec(kv_sums, lambda r, *_: (0, 0, 0)),
         ],
         scratch_shapes=[
             pltpu.VMEM((span, 2 * HD), jnp.bfloat16),
             pltpu.VMEM((span, width), jnp.float32),
             pltpu.VMEM((span, 2 * HD), jnp.float32),
-            pltpu.VMEM(kv_blocks.shape, jnp.float32),
+            pltpu.VMEM(kv_sums, jnp.float32),
         ],
     )
     return pl.pallas_call(
@@ -383,7 +388,7 @@
         grid_spec=grid_spec,
         out_shape=[
             jax.ShapeDtypeStruct((rows, heads * HD), jnp.bfloat16),
-            jax.ShapeDtypeStruct(kv_blocks.shape, jnp.bfloat16),
+            jax.ShapeDtypeStruct(kv_sums, jnp.bfloat16),
         ],
         compiler_params=pltpu.CompilerParams(vmem_limit_bytes=VMEM_LIMIT),
     )(
@@ -402,13 +407,14 @@
 
 
 MIDDLE_TILES = 3
+FORWARD_TILES = 2
 
 
 def whole_block(shape):
     return pl.BlockSpec(shape, lambda i: (0,) * len(shape))
 
 
-def middle_kernel(x_ref, mixed_ref, gain_ref, w_ref, middle_ref, normed_ref):
+def middle_kernel(x_ref, mixed_ref, gain_ref, w_ref, middle_ref, left_ref, right_ref):
     step = pl.program_id(0)
     tile = w_ref.shape[1]
     columns = pl.ds(pl.multiple_of(step * tile, tile), tile)
@@ -417,26 +423,31 @@
     @pl.when(step == pl.num_programs(0) - 1)
     def _():
         values = middle_ref[...]
-        normed_ref[...] = low(values * norm_scale(values) * gain_row(gain_ref, 1))
+        normed = low(values * norm_scale(values) * gain_row(gain_ref, 1))
+        half = left_ref.shape[1]
+        left_ref[...] = normed[:, :half]
+        right_ref[...] = normed[:, half:]
 
 
 def middle_forward(x, mixed, gains, w):
     rows, width = x.shape
+    half = width // 2
     inner = mixed.shape[1]
     return pl.pallas_call(
         middle_kernel,
         name="middle",
-        grid=(MIDDLE_TILES,),
+        grid=(FORWARD_TILES,),
         in_specs=[
             whole_block((rows, width)),
             whole_block((rows, inner)),
             whole_block(gains.shape),
-            pl.BlockSpec((inner, width // MIDDLE_TILES), lambda i: (0, i)),
-        ],
-        out_specs=[whole_block((rows, width))] * 2,
+            pl.BlockSpec((inner, width // FORWARD_TILES), lambda i: (0, i)),
+        ],
+        out_specs=[whole_block((rows, width))] + [whole_block((rows, half))] * 2,
         out_shape=[
             jax.ShapeDtypeStruct((rows, width), jnp.float32),
-            jax.ShapeDtypeStruct((rows, width), jnp.bfloat16),
+            jax.ShapeDtypeStruct((rows, half), jnp.bfloat16),
+            jax.ShapeDtypeStruct((rows, half), jnp.bfloat16),
         ],
         compiler_params=pltpu.CompilerParams(vmem_limit_bytes=VMEM_LIMIT),
     )(x, mixed, gains, w)
@@ -767,7 +778,7 @@
 
 
 def share_line_kernel(
-    shards, pack, in_ref, gain_a, gain_b, mlp_in, mlp_out, up_ref, in_line, gain_all, mine, up_x, up_y,
+    shards, pack, in_ref, gain_ref, mlp_in, mlp_out, up_ref, in_line, gain_all, mine, up_x, up_y,
     gain_now, in_stage, packed, tiles, local_sems, load_sems, send_sems, recv_sems,
 ):
     wire = Wire(send_sems, recv_sems)
@@ -776,8 +787,7 @@
     chips = pack.chips
     relay = Relay(in_ref.at[ctx], in_stage, [(in_stage, in_line.at[shard])], local_sems.at[0])
     gain_now[...] = jnp.zeros_like(gain_now)
-    gain_now[:1] = gain_a[...].astype(jnp.float32)
-    gain_now[1:2] = gain_b[...].astype(jnp.float32)
+    gain_now[:2] = gain_ref[...].astype(jnp.float32)
     wire.meet(
         [wire.line(step, shards) for step in range(1, shards)] + [wire.plane(2), wire.plane(4)]
     )
@@ -812,15 +822,15 @@
         column = part * main
         if column + main <= half:
             source = mlp_in.at[:, strip(start + chip * main, main)]
-            load(source, packed.at[pl.ds(0, pack.rows), pl.ds(column, main)])
+            load(source, packed.at[pl.ds(pack.main_start, pack.rows), pl.ds(column, main)])
             continue
         for i, at in enumerate(range(0, pack.rows, split)):
             source = mlp_in.at[pl.ds(at, split), strip(start + chip * main, main)]
             load(source, packed.at[pl.ds(pack.tail_start, split), pl.ds(i * tail + column - half, main)])
     columns = strip(core * half, half)
     for start, count, row in (
-        (chip * main, main, pack.out_start),
-        (chips * main + chip * rest, rest, pack.out_start + main),
+        (chip * main, main, 0),
+        (chips * main + chip * rest, rest, main),
     ):
         source = mlp_out.at[pl.ds(pl.multiple_of(start, 16), count), columns]
         load(source, packed.at[pl.ds(row, count), :])
@@ -877,8 +887,8 @@
 def share_plane_kernel(
     shards, devices, in_ref, in_line, out_ref, order, lengths, frequency, in_all, out_line, *refs
 ):
-    tables, scratch = take(refs, len(refs) - 6)
-    in_stage, in_piece, out_stage, local_sems, send_sems, recv_sems = scratch
+    tables, scratch = take(refs, len(refs) - 7)
+    order_rows, in_stage, in_piece, out_stage, local_sems, send_sems, recv_sems = scratch
     wire = Wire(send_sems, recv_sems)
     ctx, shard = wire.ctx, wire.shard
     relays = relay_shards(wire, in_ref, in_line, in_all, in_stage, in_piece, shards, local_sems)
@@ -895,7 +905,7 @@
     ]
     for relay in relays:
         relay.push()
-    place_tables(ctx, devices, order, lengths, frequency, *tables)
+    place_tables(ctx, devices, order, lengths, frequency, *tables, order_rows)
     complete(gathers, relays)
     for copy in copies:
         copy.wait_recv()
@@ -903,17 +913,17 @@
 
 
 def gather_plane_kernel(
-    shards, kv_ref, out_ref, out_line, kv_all, out_all, token,
+    shards, heads_ref, out_ref, out_line, kv_all, out_all, token,
     kv_stage, out_stage, out_piece, local_sems, send_sems, recv_sems,
 ):
     wire = Wire(send_sems, recv_sems)
     ctx = wire.ctx
+    kv_ref = heads_ref.at[pl.ds(H, 2)]
     relays = relay_shards(wire, out_ref, out_line, out_all, out_stage, out_piece, shards, local_sems)
     relays.append(Relay(kv_ref, kv_stage, [(kv_stage, kv_all.at[ctx])], local_sems.at[2]))
     token[...] = jnp.zeros_like(token)
     wire.meet([wire.plane(mask) for mask in PLANE_PEERS])
-    rows = kv_ref.shape[0]
-    gathers = [PlaneGather(wire, kv_ref, lambda who: kv_all.at[who], rows, rows // 2)]
+    gathers = [PlaneGather(wire, kv_ref, lambda who: kv_all.at[who], 2, 1)]
     gathers += gather_shards(wire, out_line, out_all, out_ref.shape[1], shards, 1)
     for relay in relays:
         relay.push()
@@ -929,14 +939,14 @@
     return pltpu.VMEM(lead + values.shape[-2:], values.dtype)
 
 
-def share_line(w_in, gain_a, gain_b, mlp_in, mlp_out, upstream, pack, shards):
-    columns = gain_a.shape[1]
+def share_line(w_in, gains, mlp_in, mlp_out, upstream, pack, shards):
+    columns = gains.shape[1]
     copies = 2 * (shards - 1) + 2
     loads = shards + shards + 1 + 2
     return pl.pallas_call(
         functools.partial(share_line_kernel, shards, pack),
         name="share_line",
-        in_specs=[ANY] + [pl.BlockSpec(memory_space=pltpu.VMEM)] * 2 + [ANY] * 3,
+        in_specs=[ANY] + [pl.BlockSpec(memory_space=pltpu.VMEM)] + [ANY] * 3,
         out_specs=[ANY] * 5,
         out_shape=[
             like(w_in, shards),
@@ -955,7 +965,7 @@
             dma_sems(copies),
         ],
         compiler_params=comm_params(1),
-    )(w_in, gain_a, gain_b, mlp_in, mlp_out, upstream)
+    )(w_in, gains, mlp_in, mlp_out, upstream)
 
 
 def share_plane(w_in, in_line, w_out, order, lengths, rows, ctx_size, shards):
@@ -969,6 +979,7 @@
         out_specs=[ANY] * 2 + [vmem] * len(shapes),
         out_shape=[like(w_in, shards, ctx_size), like(w_out, shards), *shapes],
         scratch_shapes=[
+            pltpu.VMEM((ctx_size * ROUNDS, rows // ROUNDS), jnp.float32),
             stage_like(w_in, ctx_size),
             stage_like(w_in, shards),
             stage_like(w_out),
@@ -980,16 +991,17 @@
     )(w_in, in_line, w_out, *operands)
 
 
-def gather_plane(key_value, w_out, out_line, ctx_size, shards):
+def gather_plane(heads, w_out, out_line, ctx_size, shards):
     copies = shards * PlaneGather.COPIES
+    key_value = jax.ShapeDtypeStruct((2,) + heads.shape[1:], heads.dtype)
     return pl.pallas_call(
         functools.partial(gather_plane_kernel, shards),
         name="gather_plane",
         in_specs=[ANY] * 3,
         out_specs=[ANY] * 2 + [pl.BlockSpec(memory_space=pltpu.VMEM)],
-        out_shape=[like(key_value, ctx_size), like(w_out, shards, ctx_size), token_shape()],
+        out_shape=[like(key_value, ctx_size, 2), like(w_out, shards, ctx_size), token_shape()],
         scratch_shapes=[
-            stage_like(key_value),
+            stage_like(key_value, 2),
             stage_like(w_out, ctx_size),
             stage_like(w_out, shards),
             pltpu.SemaphoreType.DMA((3, shards)),
@@ -997,7 +1009,7 @@
             dma_sems(copies),
         ],
         compiler_params=comm_params(2),
-    )(key_value, w_out, out_line)
+    )(heads, w_out, out_line)
 
 
 class GainSum:
@@ -1041,95 +1053,178 @@
         return value
 
 
-def reduce_kernel(shards, plane_count, half_count, line_count, full_count, part_count, gain_count, *refs):
-    planes, refs = take(refs, plane_count)
-    halves, refs = take(refs, half_count)
+def project_back_plane_kernel(
+    kv_ref, g_out_ref, part_ref, grad_ref, normed_ref, x_ref, cos_ref, sin_ref, gain_ref, w_ref,
+    out_half, q_half, k_half, part_all, grad_x_ref, grad_gain_ref,
+    grad, normed, x, cosine, sine_part, gains, w, g_q, g_k, grad_normed, kv_sum, stage, *scratch,
+):
+    sums, scratch = take(scratch, 16)
+    load_sems, sum_sems, part_sems, send_sems, recv_sems = scratch
+    wire = Wire(send_sems, recv_sems)
+    loads = []
+    for source, target in (
+        (grad_ref, grad),
+        (normed_ref, normed),
+        (w_ref, w),
+        (cos_ref, cosine),
+        (sin_ref, sine_part),
+        (x_ref, x),
+        (gain_ref, gains),
+    ):
+        loads.append(pltpu.make_async_copy(source, target, load_sems.at[len(loads)]))
+        loads[-1].start()
+    relay = Relay(part_ref, stage, [(stage, part_all.at[wire.ctx])], part_sems)
+    wire.meet([wire.plane(mask) for mask in PLANE_PEERS])
+
+    def plane_sum(source, at):
+        return PlaneSum(wire, source, *sums[4 * at : 4 * at + 4], sum_sems.at[at])
+
+    rows = part_ref.shape[0]
+    keys_sum = plane_sum(kv_ref, 0)
+    out_sum = plane_sum(g_out_ref, 1)
+    gather = PlaneGather(wire, part_ref, lambda who: part_all.at[who], rows, rows // 32 * 16)
+    keys_sum.step_one()
+    out_sum.step_one()
+    relay.push()
+    for copy in loads:
+        copy.wait()
+    inner = grad.shape[1]
+    tile = normed.shape[1] // 4
+    pieces = g_q.shape[1:4]
+
+    def queries_part(part, carry):
+        span = pl.ds(pl.multiple_of(part * tile, tile), tile)
+        value = low(tn_dot(normed[:, span], grad[...]))
+        g_q[part] = value.reshape(*pieces, inner)
+        grad_normed[:, span] = nt_dot(grad[...], w[span, :inner])
+        return carry
+
+    lax.fori_loop(0, 4, queries_part, 0)
+    queries_sum = plane_sum(g_q, 2)
+    keys_sum.step_two()
+
+    def store_keys(part, value):
+        kv_sum[part] = value
+
+    keys_sum.result(store_keys)
+    kv = kv_sum[...].reshape(normed.shape[0], 2 * HD)
+    keys = kv[:, :HD]
+    keys = low(keys * cosine[...] - pltpu.roll(keys, HD // 2, 1) * sine_part[...])
+    joined = jnp.concatenate([keys, low(kv[:, HD:])], axis=1)
+    for part in range(4):
+        span = slice(part * tile, (part + 1) * tile)
+        g_k[part] = low(tn_dot(normed[:, span], joined)).reshape(*pieces, 2 * HD)
+        grad_normed[:, span] += nt_dot(joined, w[span, inner:])
+    pair_sum = plane_sum(g_k, 3)
+    out_sum.step_two()
+    queries_sum.step_one()
+    pair_sum.step_one()
+    gather.forward()
+    change, grad_gain = norm_back(x[...].astype(jnp.float32), gain_row(gains, 0), grad_normed[...])
+    grad_x_ref[...] = change
+    grad_gain_ref[...] = grad_gain
+    queries_sum.step_two()
+    pair_sum.step_two()
+    gather.corner()
+    for total, target in ((out_sum, out_half), (queries_sum, q_half), (pair_sum, k_half)):
+
+        def store(part, value, target=target):
+            target[part] = low(value)
+
+        total.result(store)
+    gather.settle()
+    relay.settle()
+    wire.finish()
+
+
+def project_back_plane(grad_kv, g_out, part, grad_q, normed, x, cosine, sine_part, gains, w, ctx_size):
+    rows, width = x.shape
+    inner = grad_q.shape[1]
+    lead = g_out.shape[:4]
+    vmem = pl.BlockSpec(memory_space=pltpu.VMEM)
+    low_scratch = lambda *shape: pltpu.VMEM(shape, jnp.bfloat16)
+    wide = lambda *shape: pltpu.VMEM(shape, jnp.float32)
+    sums = []
+    for piece in (grad_kv.shape[3:], g_out.shape[3:], (lead[3], inner), (lead[3], 2 * HD)):
+        sums += plane_sum_scratch(*piece)
+    copies = 4 * PlaneSum.COPIES + PlaneGather.COPIES
+    half = lambda columns: jax.ShapeDtypeStruct((4, lead[3], columns), jnp.bfloat16)
+    return pl.pallas_call(
+        project_back_plane_kernel,
+        name="project_back_plane",
+        in_specs=[ANY] * 10,
+        out_specs=[vmem] * 3 + [ANY] + [vmem] * 2,
+        out_shape=[
+            half(g_out.shape[4]),
+            half(inner),
+            half(2 * HD),
+            like(part, ctx_size),
+            jax.ShapeDtypeStruct((rows, width), jnp.float32),
+            jax.ShapeDtypeStruct((1, width), jnp.float32),
+        ],
+        scratch_shapes=[
+            low_scratch(*grad_q.shape),
+            low_scratch(*normed.shape),
+            low_scratch(*x.shape),
+            wide(*cosine.shape),
+            wide(*cosine.shape),
+            wide(*gains.shape),
+            low_scratch(*w.shape),
+            low_scratch(*lead, inner),
+            low_scratch(*lead, 2 * HD),
+            wide(rows, width),
+            wide(4, *grad_kv.shape[3:]),
+            stage_like(part),
+            *sums,
+            dma_sems(7),
+            dma_sems(4),
+            dma_sems(2),
+            dma_sems(copies),
+            dma_sems(copies),
+        ],
+        compiler_params=comm_params(3),
+    )(grad_kv, g_out, part, grad_q, normed, x, cosine, sine_part, gains, w)
+
+
+def reduce_late_kernel(shards, line_count, *refs):
     line_ins, refs = take(refs, line_count)
-    fulls, refs = take(refs, full_count)
-    parts, refs = take(refs, part_count)
-    gain_rows, refs = take(refs, gain_count)
-    plane_outs, refs = take(refs, plane_count)
-    half_outs, refs = take(refs, half_count)
-    full_outs, refs = take(refs, line_count + full_count)
-    part_outs, refs = take(refs, part_count)
-    gain_out, refs = take(refs, min(gain_count, 1))
-    sums, refs = take(refs, 4 * (plane_count + half_count + full_count))
-    mine, refs = take(refs, full_count)
-    arrived, refs = take(refs, line_count + full_count)
-    done, refs = take(refs, line_count + full_count)
-    stages, refs = take(refs, part_count)
-    gain_scratch, refs = take(refs, 3 * min(gain_count, 1))
-    sum_sems, done_sems, part_sems, send_sems, recv_sems = refs
+    part_ref, gain_a, gain_b, *refs = refs
+    line_outs, refs = take(refs, line_count)
+    part_all, gain_out, *refs = refs
+    arrived, refs = take(refs, line_count)
+    done, refs = take(refs, line_count)
+    stage, gain_now, gain_in, gain_line, done_sems, part_sems, send_sems, recv_sems = refs
 
     wire = Wire(send_sems, recv_sems)
     ctx, shard = wire.ctx, wire.shard
-    relays = [
-        Relay(source, stage, [(stage, target.at[ctx])], part_sems.at[i])
-        for i, (source, stage, target) in enumerate(zip(parts, stages, part_outs))
-    ]
-    if gain_count:
-        gain_now = gain_scratch[0]
-        gain_now[...] = jnp.zeros_like(gain_now)
-        columns = gain_now.shape[2]
-        for part in range(shards):
-            for row, values in enumerate(gain_rows):
-                gain_now[part, row : row + 1] = values[:, part * columns : (part + 1) * columns]
+    relay = Relay(part_ref, stage, [(stage, part_all.at[ctx])], part_sems)
+    gain_now[...] = jnp.zeros_like(gain_now)
+    columns = gain_now.shape[2]
+    for part in range(shards):
+        for row, values in enumerate((gain_a, gain_b)):
+            gain_now[part, row : row + 1] = values[:, part * columns : (part + 1) * columns]
     wire.meet(
         [wire.plane(mask) for mask in PLANE_PEERS] + [wire.line(s, shards) for s in range(1, shards)]
     )
-    totals = [
-        PlaneSum(wire, source, *sums[4 * i : 4 * i + 4], sum_sems.at[i])
-        for i, source in enumerate(planes + halves + fulls)
+    lines = [
+        [
+            wire.send(
+                source.at[lax.rem(shard + step, shards)], target.at[step - 1], wire.line(step, shards)
+            )
+            for step in range(1, shards)
+        ]
+        for source, target in zip(line_ins, arrived)
     ]
-    lines = []
-
-    def send_line(source):
-        target = arrived[len(lines)]
-        lines.append(
-            [
-                wire.send(
-                    source.at[lax.rem(shard + step, shards)], target.at[step - 1], wire.line(step, shards)
-                )
-                for step in range(1, shards)
-            ]
-        )
-
-    for source in line_ins:
-        send_line(source)
-    gain = GainSum(wire, *gain_scratch, shards) if gain_count else None
-    for total in totals:
-        total.step_one()
-    if gain:
-        gain.step()
-    for total in totals:
-        total.step_two()
-    if gain:
-        gain.step()
-    gathers = []
-    for source, target in zip(parts, part_outs):
-        rows = source.shape[0]
-        place = lambda who, target=target: target.at[who]
-        gathers.append(PlaneGather(wire, source, place, rows, half_rows(rows, len(gathers))))
-    for total, target in zip(totals, plane_outs):
-
-        def store_wide(part, value, target=target):
-            target[part] = value
-
-        total.result(store_wide)
-    for total, target in zip(totals[plane_count:], half_outs + mine):
-
-        def store(part, value, target=target):
-            target[part] = low(value)
-
-        total.result(store)
-    for source in mine:
-        send_line(source)
-    if gain:
-        gain.step_line()
-    for relay in relays:
-        relay.push()
+    rows = part_ref.shape[0]
+    gathers = [PlaneGather(wire, part_ref, lambda who: part_all.at[who], rows, rows // 32 * 16)]
+    gain = GainSum(wire, gain_now, gain_in, gain_line, shards)
+    gain.step()
+    gain.step()
+    gain.step_line()
+    relay.push()
+    gathers[0].forward()
     locals_ = []
-    for i, (source, target) in enumerate(zip(line_ins + mine, full_outs)):
+    for i, (source, target) in enumerate(zip(line_ins, line_outs)):
         for copy in lines[i]:
             copy.wait_recv()
         value = source[shard].astype(jnp.float32)
@@ -1137,14 +1232,12 @@
             value += arrived[i][step].astype(jnp.float32)
         done[i][...] = low(value)
         place = lambda who, target=target: target.at[who]
-        rows = target.shape[1]
-        gathers.append(PlaneGather(wire, done[i], place, rows, half_rows(rows, i)))
+        gathers.append(PlaneGather(wire, done[i], place, target.shape[1], half_rows(target.shape[1], i)))
         copy = pltpu.make_async_copy(done[i], place(ctx), done_sems.at[i])
         copy.start()
         locals_.append(copy)
-    if gain:
-        gain_out[0][...] = gain.result()
-    for gather in gathers:
+    gain_out[...] = gain.result()
+    for gather in gathers[1:]:
         gather.forward()
     for gather in gathers:
         gather.corner()
@@ -1152,68 +1245,35 @@
         gather.settle()
     for copy in locals_:
         copy.wait()
-    for relay in relays:
-        relay.settle()
+    relay.settle()
     wire.finish()
 
 
-def reduce(name, number, ctx_size, shards, planes=(), halves=(), lines=(), fulls=(), parts=(), gains=()):
-    sums, mine, arrived, done = [], [], [], []
-    for array in (*planes, *halves, *fulls):
-        sums += plane_sum_scratch(*array.shape[3:])
-    for array in fulls:
-        mine.append(pltpu.VMEM((shards, *array.shape[3:]), jnp.bfloat16))
-    for array in (*lines, *fulls):
-        rows, columns = array.shape[-2:]
-        arrived.append(pltpu.VMEM((shards - 1, rows, columns), jnp.bfloat16))
-        done.append(pltpu.VMEM((rows, columns), jnp.bfloat16))
-    stages = [pltpu.VMEM(part.shape, part.dtype) for part in parts]
-    copies = PlaneSum.COPIES * (len(planes) + len(halves) + len(fulls))
-    copies += (PlaneGather.COPIES + shards - 1) * (len(lines) + len(fulls))
-    copies += PlaneGather.COPIES * len(parts)
+def reduce_late(lines, part, gain_a, gain_b, ctx_size):
+    shards = lines[0].shape[0]
     vmem = pl.BlockSpec(memory_space=pltpu.VMEM)
-    outs = [(vmem, jax.ShapeDtypeStruct((4,) + array.shape[3:], jnp.float32)) for array in planes]
-    outs += [(vmem, jax.ShapeDtypeStruct((4,) + array.shape[3:], array.dtype)) for array in halves]
-    outs += [(ANY, like(array, ctx_size)) for array in (*lines, *fulls)]
-    outs += [(ANY, like(part, ctx_size)) for part in parts]
-    gain_scratch = []
-    if gains:
-        shape = (shards, 8, gains[0].shape[1] // shards)
-        outs.append((vmem, jax.ShapeDtypeStruct(shape[1:], jnp.float32)))
-        gain_scratch = [
-            pltpu.VMEM(shape, jnp.float32),
-            pltpu.VMEM((3,) + shape, jnp.float32),
-            pltpu.VMEM((shards - 1,) + shape[1:], jnp.float32),
-        ]
-        copies += 3 + shards - 1
+    gain_shape = (shards, 8, gain_a.shape[1] // shards)
+    copies = (PlaneGather.COPIES + shards - 1) * len(lines) + PlaneGather.COPIES + 3 + shards - 1
     return pl.pallas_call(
-        functools.partial(
-            reduce_kernel,
-            shards,
-            len(planes),
-            len(halves),
-            len(lines),
-            len(fulls),
-            len(parts),
-            len(gains),
-        ),
-        name=name,
-        in_specs=[ANY] * (len(planes) + len(halves))
-        + [vmem] * len(lines)
-        + [ANY] * (len(fulls) + len(parts))
-        + [vmem] * len(gains),
-        out_specs=[spec for spec, _ in outs],
-        out_shape=[shape for _, shape in outs],
-        scratch_shapes=sums + mine + arrived + done + stages + gain_scratch
+        functools.partial(reduce_late_kernel, shards, len(lines)),
+        name="reduce_late",
+        in_specs=[vmem] * len(lines) + [ANY] + [vmem] * 2,
+        out_specs=[ANY] * (len(lines) + 1) + [vmem],
+        out_shape=[like(array, ctx_size) for array in (*lines, part)]
+        + [jax.ShapeDtypeStruct(gain_shape[1:], jnp.float32)],
+        scratch_shapes=[stage_like(array, shards - 1) for array in lines]
+        + [stage_like(array) for array in (*lines, part)]
         + [
-            dma_sems(max(1, len(planes) + len(halves) + len(fulls))),
-            dma_sems(max(1, len(lines) + len(fulls))),
-            pltpu.SemaphoreType.DMA((max(1, len(parts)), 2)),
+            pltpu.VMEM(gain_shape, jnp.float32),
+            pltpu.VMEM((3,) + gain_shape, jnp.float32),
+            pltpu.VMEM((shards - 1,) + gain_shape[1:], jnp.float32),
+            dma_sems(len(lines)),
+            dma_sems(2),
             dma_sems(copies),
             dma_sems(copies),
         ],
-        compiler_params=comm_params(number),
-    )(*planes, *halves, *lines, *fulls, *parts, *gains)
+        compiler_params=comm_params(4),
+    )(*lines, part, gain_a, gain_b)
 
 
 class Pack:
@@ -1221,12 +1281,13 @@
         self.rows, self.half, self.chips, self.main, self.rest = rows, half, chips, main, rest
         self.tail = units - half
         self.split = rows // (half // self.tail)
-        self.out_start = rows
-        self.tail_start = rows + main + rest
+        self.main_start = main + rest
+        self.tail_start = self.main_start + rows
         self.total = self.tail_start + self.split
 
     def in_spans(self, shard):
-        yield (0, self.rows), (0, self.half), (shard * self.rows, self.rows), (0, self.half)
+        every = (0, self.half)
+        yield (self.main_start, self.rows), every, (shard * self.rows, self.rows), every
         for i, at in enumerate(range(0, self.rows, self.split)):
             yield (
                 (self.tail_start, self.split),
@@ -1237,86 +1298,107 @@
 
     def out_spans(self, shard, shards):
         every = (0, self.half)
-        yield (self.out_start, self.main), every, (shard * self.main, self.main), every
+        yield (0, self.main), every, (shard * self.main, self.main), every
         yield (
-            (self.out_start + self.main, self.rest),
+            (self.main, self.rest),
             every,
             (shards * self.main + shard * self.rest, self.rest),
             every,
         )
 
 
-def finish_kernel(shards, chips, pack, step_rows, main_ref, tail_ref, out_part_ref, in_ref, out_ref):
+def finish_kernel(
+    shards, chips, pack, main_ref, tail_ref, out_main_ref, out_rest_ref, attn_out_ref, attn_q_ref, attn_kv_ref,
+    in_ref, out_ref, grad_attn_out_ref, grad_attn_in_ref,
+):
     step = pl.program_id(0)
+    last = pl.num_programs(0) - 1
     main, rest, half, tail = pack.main, pack.rest, pack.half, pack.tail
     per_shard = chips * (main + rest)
-
-    def columns_of(who, start, count):
-        if start + count <= half:
-            return main_ref[who, :, start : start + count]
-        at = start - half
-        return tails[who][:, at : at + count]
-
-    second = step >= pl.num_programs(0) // 2
-    tails = [
-        jnp.where(second, tail_ref[who, :, tail:], tail_ref[who, :, :tail])
-        for who in range(2 * chips)
-    ]
-    for core in range(2):
-        for shard in range(shards):
-            start = (core * shards + shard) * per_shard
-            for chip in range(chips):
-                block = columns_of(chip * 2 + core, shard * main, main)
-                in_ref[:, start + chip * main : start + (chip + 1) * main] = block.astype(jnp.float32)
-            ends = [
-                columns_of(chip * 2 + core, shards * main, shards * rest).astype(jnp.float32)[
-                    :, shard * rest : (shard + 1) * rest
+    wide = lambda values: values.astype(jnp.float32)
+
+    @pl.when(step < last)
+    def _():
+        second = step >= last // 2
+        tails = [
+            jnp.where(second, tail_ref[who, :, tail:], tail_ref[who, :, :tail])
+            for who in range(2 * chips)
+        ]
+
+        def columns_of(who, start, count):
+            if start + count <= half:
+                return main_ref[who, :, start : start + count]
+            return tails[who][:, start - half : start - half + count]
+
+        for core in range(2):
+            for shard in range(shards):
+                start = (core * shards + shard) * per_shard
+                for chip in range(chips):
+                    block = wide(columns_of(chip * 2 + core, shard * main, main))
+                    in_ref[:, start + chip * main : start + (chip + 1) * main] = block
+                ends = [
+                    wide(columns_of(chip * 2 + core, shards * main, shards * rest))[
+                        :, shard * rest : (shard + 1) * rest
+                    ]
+                    for chip in range(chips)
                 ]
-                for chip in range(chips)
-            ]
-            in_ref[:, start + chips * main : start + per_shard] = jnp.concatenate(ends, axis=1)
-
-    for chip in range(chips):
-
-        @pl.when(step == chip)
-        def _(chip=chip):
+                in_ref[:, start + chips * main : start + per_shard] = jnp.concatenate(ends, axis=1)
+            out_ref[:, core * half : (core + 1) * half] = wide(out_main_ref[core])
+        grad_attn_out_ref[...] = wide(attn_out_ref[0])
+        inner = attn_q_ref.shape[2]
+        grad_attn_in_ref[:, :inner] = wide(attn_q_ref[0])
+        grad_attn_in_ref[:, inner:] = wide(attn_kv_ref[0])
+
+    @pl.when(step == last)
+    def _():
+        for chip in range(chips):
             for core in range(2):
-                columns = slice(core * half, (core + 1) * half)
-                block = out_part_ref[core]
-                out_ref[chip * main : (chip + 1) * main, columns] = block[:main].astype(jnp.float32)
-                start = chips * main + chip * rest
-                out_ref[start : start + rest, columns] = block[main:].astype(jnp.float32)
-
-
-def finish(first, second, pack, shards):
+                block = wide(out_rest_ref[chip * 2 + core])
+                out_ref[chip * rest : (chip + 1) * rest, core * half : (core + 1) * half] = block
+
+
+def finish(first, second, attn_out, attn_q, attn_kv, pack, shards):
     ctx_size = first.shape[0]
     chips = ctx_size // 2
-    steps = 8
+    steps = ctx_size
     tile = pack.rows // steps
-    per_out = pack.main + pack.rest
-    assert pack.rows // pack.split == 2 and pack.split % tile == 0 and per_out % tile == 0
+    out_tile = pack.main // 2
+    assert pack.rows // pack.split == 2 and pack.split % tile == 0
+    assert out_tile == chips * pack.rest and pack.main % pack.rest == 0
+    at = lambda i: jnp.minimum(i, steps - 1)
+    rows = attn_out.shape[1]
+    piece = lambda array: pl.BlockSpec((1,) + array.shape[1:], lambda i: (at(i), 0, 0))
+    attn_in = attn_q.shape[2] + attn_kv.shape[2]
     return pl.pallas_call(
-        functools.partial(finish_kernel, shards, chips, pack, tile),
+        functools.partial(finish_kernel, shards, chips, pack),
         name="finish",
-        grid=(steps,),
+        grid=(steps + 1,),
         in_specs=[
-            pl.BlockSpec((ctx_size, tile, pack.half), lambda i: (0, i, 0)),
+            pl.BlockSpec((ctx_size, tile, pack.half), lambda i: (0, at(i), 0)),
             pl.BlockSpec(
                 (ctx_size, tile, pack.half),
-                lambda i: (0, per_out // tile + i % (pack.split // tile), 0),
+                lambda i: (0, pack.rows // tile + at(i) % (pack.split // tile), 0),
             ),
-            pl.BlockSpec((2, per_out, pack.half), lambda i: (jnp.minimum(i, chips - 1), 0, 0)),
+            pl.BlockSpec((2, out_tile, pack.half), lambda i: (at(i) // 2, at(i) % 2, 0)),
+            pl.BlockSpec((ctx_size, pack.rest, pack.half), lambda i: (0, pack.main // pack.rest, 0)),
+            piece(attn_out),
+            piece(attn_q),
+            piece(attn_kv),
         ],
         out_specs=[
-            pl.BlockSpec((tile, 2 * FF), lambda i: (i, 0)),
-            whole_block((FF // shards, 2 * pack.half)),
+            pl.BlockSpec((tile, 2 * FF), lambda i: (at(i), 0)),
+            pl.BlockSpec((out_tile, 2 * pack.half), lambda i: (i, 0)),
+            pl.BlockSpec((rows, attn_out.shape[2]), lambda i: (at(i), 0)),
+            pl.BlockSpec((rows, attn_in), lambda i: (at(i), 0)),
         ],
         out_shape=[
             jax.ShapeDtypeStruct((pack.rows, 2 * FF), jnp.float32),
             jax.ShapeDtypeStruct((FF // shards, 2 * pack.half), jnp.float32),
+            jax.ShapeDtypeStruct((steps * rows, attn_out.shape[2]), jnp.float32),
+            jax.ShapeDtypeStruct((steps * rows, attn_in), jnp.float32),
         ],
         compiler_params=pltpu.CompilerParams(vmem_limit_bytes=VMEM_LIMIT),
-    )(first, second, second)
+    )(second, second, first, first, attn_out, attn_q, attn_kv)
 
 
 TANH_SCALE = 0.7978845608028654
@@ -1325,16 +1407,16 @@
 
 
 def mlp_kernel(
-    shards, pack, mine, x_own, x_x, x_y, c_own, c_x_left, c_x_right, c_y_left, c_y_right, c_left, c_right,
-    normed_grad, out_own, out_x, out_y, out_left, out_right, grad_main, grad_rest,
+    shards, pack, mine, x_left, x_right, x_x, x_y, c_own, c_x_left, c_x_right, c_y_left, c_y_right, c_left, c_right,
+    normed_grad, out_own, out_x, out_y, out_left, out_right, grad_first, grad_second,
     w_in, w_out, xs, cs, hidden, grads, part, from_x, from_y, corner_left, corner_right,
     out_stage, pair_in, pair_out, local_sems, send_sems, recv_sems,
 ):
     wire = Wire(send_sems, recv_sems)
     core = lax.rem(wire.ctx, 2)
     other = 1 - core
-    rows, width = x_own.shape
-    half = width // 2
+    rows, half = x_left.shape
+    width = 2 * half
     units = w_in.shape[2]
     tiles = units // UNIT_TILE
     left, right = pl.ds(0, half), pl.ds(half, half)
@@ -1359,7 +1441,11 @@
     def placed(which, target, one):
         return target.at[which, pl.ds(*one[2]), pl.ds(*one[3])]
 
-    loads = [copy_in(x_own, xs.at[0]), copy_in(c_own, cs.at[0])]
+    loads = [
+        copy_in(x_left, xs.at[0, :, left]),
+        copy_in(x_right, xs.at[0, :, right]),
+        copy_in(c_own, cs.at[0]),
+    ]
     for shard, target, one in spans():
         loads.append(copy_in(packed(shard, one), placed(core, target, one)))
     late = [
@@ -1377,8 +1463,8 @@
     ]
     wire.meet([wire.plane(mask) for mask in PLANE_PEERS])
     x_copies = [
-        wire.send(x_own.at[:, right], xs.at[1, :, right], wire.plane(2)),
-        wire.send(x_own.at[:, left], xs.at[2, :, left], wire.plane(4)),
+        wire.send(x_right, xs.at[1, :, right], wire.plane(2)),
+        wire.send(x_left, xs.at[2, :, left], wire.plane(4)),
     ]
     swaps = [
         wire.send(packed(shard, one), placed(core, target, one), wire.plane(1))
@@ -1495,10 +1581,10 @@
         w_out[1, span, :] = low(value + pair_out[span, :].astype(jnp.float32))
     for shard, source, one in spans():
         start, count = one[0]
-        if start < pack.rows:
-            target = grad_main.at[shard, pl.ds(start, count), pl.ds(*one[1])]
+        if start < pack.main_start:
+            target = grad_first.at[shard, pl.ds(start, count), pl.ds(*one[1])]
         else:
-            target = grad_rest.at[shard, pl.ds(start - pack.rows, count), pl.ds(*one[1])]
+            target = grad_second.at[shard, pl.ds(start - pack.main_start, count), pl.ds(*one[1])]
         final.append(copy_in(placed(1, source, one), target))
     for copy in early + merged:
         copy.wait_recv()
@@ -1512,19 +1598,19 @@
 
 
 def mlp(mine, x, upstream, pack):
-    rows, width = x[0].shape
-    half = width // 2
+    rows, half = x[0].shape
+    width = 2 * half
     units = pack.half + pack.tail
     shards = mine.shape[0]
     low_shape = lambda *shape: jax.ShapeDtypeStruct(shape, jnp.bfloat16)
     low_scratch = lambda *shape: pltpu.VMEM(shape, jnp.bfloat16)
     parts = shards * (1 + pack.rows // pack.split + 2)
     copies = parts + 4 + 2 + 2 + 2 + 2 * (units // UNIT_TILE)
-    locals_ = 2 + parts + 8 + 5 + parts
+    locals_ = 3 + parts + 8 + 5 + parts
     return pl.pallas_call(
         functools.partial(mlp_kernel, shards, pack),
         name="mlp",
-        in_specs=[ANY] * 11,
+        in_specs=[ANY] * 12,
         out_specs=[pl.BlockSpec(memory_space=pltpu.VMEM)] + [ANY] * 7,
         out_shape=[
             jax.ShapeDtypeStruct((rows, width), jnp.float32),
@@ -1533,8 +1619,8 @@
             low_shape(rows, width),
             low_shape(rows, half),
             low_shape(rows, half),
-            low_shape(shards, pack.rows, half),
-            low_shape(shards, pack.total - pack.rows, half),
+            low_shape(shards, pack.main_start, half),
+            low_shape(shards, pack.total - pack.main_start, half),
         ],
         scratch_shapes=[
             low_scratch(2, width, units),
@@ -1734,8 +1820,7 @@
         pieces = lambda w: w.reshape(ctx_size, w.shape[0] // ctx_size, w.shape[1])
         in_line, gains, mine, upstream_x, upstream_y = share_line(
             pieces(w_attn_in),
-            norm_attn[None],
-            norm_mlp[None],
+            jnp.stack([norm_attn, norm_mlp]),
             w_mlp_in,
             w_mlp_out,
             upstream,
@@ -1765,10 +1850,10 @@
         upstream_all = lay.gather_chips(upstream)
 
     where, key_place, bounds, bounds_wide, cosine, sine_part = tables
-    normed_one, queries, key_value = project(x, gains, in_attn, cosine, sine_part)
+    normed_one, queries = project(x, gains, in_attn, cosine, sine_part)
     if lay.plane:
         key_value, out_attn, token = gather_plane(
-            key_value, pieces(w_attn_out), out_line, ctx_size, fsdp_size
+            queries, pieces(w_attn_out), out_line, ctx_size, fsdp_size
         )
         out_attn = out_attn.reshape(-1, width)
         half = width // 2
@@ -1782,22 +1867,21 @@
             lay.xor(after(token, upstream_y), 2),
         )
     else:
-        key_value = lax.all_gather(key_value, "ctx", axis=0)
-    key_value = key_value.reshape(ctx_size * ROUNDS, block, 2 * HD)
+        key_value = lax.all_gather(queries[H:], "ctx", axis=0)
     mixed, log_total = attend(where, queries, key_value, key_place, bounds)
-    middle, normed_two = middle_forward(x, mixed, gains, out_attn)
+    middle, left, right = middle_forward(x, mixed, gains, out_attn)
 
     if lay.plane:
-        grad_normed_two, out_own, *out_parts, grad_main, grad_rest = mlp(
+        grad_normed_two, out_own, *out_parts, grad_first, grad_second = mlp(
             mine,
-            (normed_two, lay.xor(normed_two[:, :half], 2), lay.xor(normed_two[:, half:], 4)),
+            (left, right, lay.xor(left, 2), lay.xor(right, 4)),
             upstream_all,
             pack,
         )
-        grad_main = lax.psum_scatter(grad_main, "fsdp", scatter_dimension=0, tiled=True)[0]
-        grad_rest = lax.psum_scatter(grad_rest, "fsdp", scatter_dimension=0, tiled=True)[0]
+        grad_first = lax.psum_scatter(grad_first, "fsdp", scatter_dimension=0, tiled=True)[0]
+        grad_second = lax.psum_scatter(grad_second, "fsdp", scatter_dimension=0, tiled=True)[0]
     else:
-        normed_all = lay.gather_chips(normed_two)
+        normed_all = lay.gather_chips(jnp.concatenate([left, right], axis=1))
         gate = dot(normed_all, gate_in)
         up = dot(normed_all, up_in)
         hidden, hidden_back = jax.vjp(geglu, gate, up)
@@ -1831,44 +1915,44 @@
     if lay.plane:
         mixed_out = lay.sum_neighbours(out_own, *out_parts)
     result = middle + mixed_out
-    grad_in_queries, grad_normed = project_back_queries(grad_query, normed_one, in_attn)
-    split = lambda grad: grad.reshape(fsdp_size, lay.chips, 2, -1, grad.shape[1])
     if lay.plane:
+        split = lambda grad: grad.reshape(fsdp_size, lay.chips, 2, -1, grad.shape[1])
         grad_kv = grad_kv.reshape(ROUNDS, lay.chips, 2, block, 2 * HD)
-        grad_kv, grad_out_attn, grad_in_queries, grad_main = reduce(
-            "reduce_early",
-            3,
+        *halves, grad_first, grad_inputs, grad_gain_attn = project_back_plane(
+            grad_kv,
+            split(grad_out_attn),
+            grad_first,
+            grad_query,
+            normed_one,
+            x,
+            cosine,
+            sine_part,
+            gains,
+            in_attn,
             ctx_size,
+        )
+        grad_inputs = grad_middle + grad_inputs
+        grad_out_attn, grad_in_queries, grad_in_keys, grad_second, grad_gains = reduce_late(
+            halves, grad_second, grad_gain_attn, grad_gain_mlp, ctx_size
+        )
+        grad_in_mlp, grad_out_mlp, grad_out_attn, grad_in_attn = finish(
+            grad_first,
+            grad_second,
+            grad_out_attn,
+            grad_in_queries,
+            grad_in_keys,
+            pack,
             fsdp_size,
-            planes=[grad_kv],
-            halves=[split(grad_out_attn), split(grad_in_queries)],
-            parts=[grad_main],
         )
-        grad_kv = grad_kv.reshape(own_rows, 2 * HD)
+        grad_gain_attn, grad_gain_mlp = grad_gains[0], grad_gains[1]
     else:
         grad_kv = grad_kv.reshape(ROUNDS, ctx_size, block, 2 * HD)
         grad_kv = lax.psum_scatter(grad_kv, "ctx", scatter_dimension=1, tiled=True)
         grad_kv = grad_kv.reshape(own_rows, 2 * HD).astype(jnp.float32)
-    grad_in_keys, grad_inputs, grad_gain_attn = project_back_keys(
-        grad_kv, cosine, sine_part, normed_one, grad_normed, x, grad_middle, gains, in_attn
-    )
-    if lay.plane:
-        grad_out_attn, grad_in_queries, grad_in_keys, grad_rest, grad_gains = reduce(
-            "reduce_late",
-            4,
-            ctx_size,
-            fsdp_size,
-            lines=[grad_out_attn, grad_in_queries],
-            fulls=[split(grad_in_keys)],
-            parts=[grad_rest],
-            gains=[grad_gain_attn, grad_gain_mlp],
+        grad_in_queries, grad_normed = project_back_queries(grad_query, normed_one, in_attn)
+        grad_in_keys, grad_inputs, grad_gain_attn = project_back_keys(
+            grad_kv, cosine, sine_part, normed_one, grad_normed, x, grad_middle, gains, in_attn
         )
-        whole = lambda grad: grad.reshape(-1, grad.shape[2]).astype(jnp.float32)
-        grad_out_attn = whole(grad_out_attn)
-        grad_in_attn = jnp.concatenate([whole(grad_in_queries), whole(grad_in_keys)], axis=1)
-        grad_in_mlp, grad_out_mlp = finish(grad_main, grad_rest, pack, fsdp_size)
-        grad_gain_attn, grad_gain_mlp = grad_gains[0], grad_gains[1]
-    else:
         grad_in_attn = jnp.concatenate([grad_in_queries, grad_in_keys], axis=1)
         grad_out_attn = lay.reduce_whole(grad_out_attn)
         grad_in_attn = lay.reduce_whole(grad_in_attn)

time: 454 us -> 427 us (0.941)
  Pallas kernels: 385 us -> 362 us
    pallas_call x7 -> x5, Pallas kernels: 178 us -> 153 us  [the longest x1 69 us: project_back_plane(): pl.pallas_call(project_back_plane_kernel, name='project_back_plane', in_s...]
  transfers between devices with their start and end apart: 13 -> 13, of which waited for: 4 -> 6; matrix products, arithmetic and copies ran while one was open for 2% -> 2% of each run, Pallas kernels for 48% -> 44%
where the time goes in v5:
time: 427 us; the launch traced here: 419 us
  Pallas kernels  362 us (85%)
  waiting for transfers between devices  18.4 us (4%)
  between operations  15.5 us (4%)
  starting transfers between devices  10.7 us (3%)
  other arithmetic  6.91 us (2%)
  local copies, waits for them, and re-layouts  5.74 us (1%)
    pallas_call x1, Pallas kernels, mlp(): pl.pallas_call(functools.partial(mlp_kernel, shards, pack), name='mlp', i...  85.4 us
    pallas_call x1, Pallas kernels, project_back_plane(): pl.pallas_call(project_back_plane_kernel, name='project_back_plane', in_s...  69 us
    pallas_call x1, Pallas kernels, reduce_late(): pl.pallas_call(functools.partial(reduce_late_kernel, shards, len(lines)),...  55.1 us
    pallas_call x1, Pallas kernels, gather_plane(): pl.pallas_call(functools.partial(gather_plane_kernel, shards), name='gath...  27.2 us
    pallas_call x1, Pallas kernels, share_plane(): pl.pallas_call(functools.partial(share_plane_kernel, shards, ctx_size), n...  27.1 us
    pallas_call x1, Pallas kernels, attend_back(): pl.pallas_call(functools.partial(attend_back_kernel, window.blocks, block...  22.2 us
    pallas_call x1, Pallas kernels, share_line(): pl.pallas_call(functools.partial(share_line_kernel, shards, pack), name='...  20.9 us
    ppermute x10, waiting for transfers between devices, xor(): return lax.ppermute(values, 'ctx', pairs)  17.7 us
  transfers between devices with their start and end apart: 13, of which 6 were waited for; matrix products, arithmetic and copies ran while one was open for 2% of the time, Pallas kernels for 44%

profile of v5, /device:TPU:0, one launch (start us, length us, event | category | flops | bytes accessed | tf_op | source)
XLA Modules:
  0.0 419.2 jit_solution(16719283007175397180)
XLA Ops:
  9.2 20.9 %share_line.1 = (bf16[4,48,1792]{2,1,0:T(8,128)(2,1)}, f32[4,8,384]{2,1,0:T(8,128)}, bf16[864,768]{1,0:T(8,128)(2,1)}, bf16[384,768]{1,0:T(8,128)(2,1)}, bf16[384,768]{1,0:T(8,128)(2,1)}) custom-call(bf16[8,48,1792]{2,1,0:T(8,128)(2,1)} %bitcast.30, bf16[2,384]{1,0:T(2,128)(2,1)} %pad_maximum_fusion.2.gain_ref, bf16[384,9216]{1,0:T(8,128)(2,1)} %mlp_in.1, ...), custom_call_target="tpu_custom_call" | custom-call | tf_op jit(solution)/shard_map/share_line/pallas_call | solution.py:946
  30.7 27.1 %share_plane.1 = (bf16[4,8,48,1792]{3,2,1,0:T(8,128)(2,1)}, bf16[4,48,1536]{2,1,0:T(8,128)(2,1)}, s32[8,128]{1,0:T(8,128)}, f32[4,1,1152]{2,1,0:T(1,128)}, f32[3...) custom-call(bf16[8,48,1792]{2,1,0:T(8,128)(2,1)} %bitcast.31, ...), custom_call_target="tpu_custom_call" | custom-call | tf_op jit(solution)/shard_map/share_plane/pallas_call | solution.py:975
  57.8 6.6 %project.1 = (bf16[384,1536]{1,0:T(8,128)(2,1)}, bf16[14,384,128]{2,1,0:T(8,128)(2,1)}) custom-call(bf16[384,1536]{1,0:T(8,128)(2,1)} %bitcast.27, f32[4,8,384]{2,1,0:T(8,128)} %get-tuple-element.63.gain_ref, bf16[1536,1792]{1,0:T(8,128)(2,1)} %bitcast.19, f32[384,128]{1,0:T(8,128)} %get-tuple-element.65.cos_ref, f32[384,128]{1,0:T(8,128)} %get-tuple-element.66.sin_ref), custom_call_target="tpu_custom_call" | custom-call | tf_op jit(solution)/shard_map/project/pallas_call | solution.py:96
  64.4 27.2 %gather_plane.1 = (bf16[8,2,384,128]{3,2,1,0:T(8,128)(2,1)}, bf16[4,8,48,1536]{3,2,1,0:T(8,128)(2,1)}, s32[8,128]{1,0:T(8,128)}) custom-call(bf16[14,384,128]{2,1,0:T(8,128)(2,1)} %get-tuple-element.67.heads_ref.q_ref, bf16[8,48,1536]{2,1,0:T(8,128)(2,1)} %bitcast.34, bf16[4,48,1536]{2,1,0:T(8,128)(2,1)} %get-tuple-element.68.out_line), custom_call_target="tpu_custom_call" | custom-call | tf_op jit(solution)/shard_map/gather_plane/pallas_call | solution.py:997
  91.6 1.3 slice.34
  94.7 1.1 collective-permute-start.4
  98.0 14.5 %attend.1 = (bf16[384,1536]{1,0:T(8,128)(2,1)}, f32[4,3,1,384]{3,2,1,0:T(1,128)}) custom-call(s32[8,128]{1,0:T(8,128)} %get-tuple-element.62.where_ref, bf16[14,384,128]{2,1,0:T(8,128)(2,1)} %get-tuple-element.67.heads_ref.q_ref, bf16[8,2,384,128]{3,2,1,0:T(8,128)(2,1)} %get-tuple-element.69.kv_ref, f32[4,1,1152]{2,1,0:T(1,128)} %get-tuple-element.70.key_place_ref, ...), custom_call_target="tpu_custom_call" | custom-call | tf_op jit(solution)/shard_map/attend/pallas_call | solution.py:283
  112.5 6.9 %middle.1 = (f32[384,1536]{1,0:T(8,128)}, bf16[384,768]{1,0:T(8,128)(2,1)}, bf16[384,768]{1,0:T(8,128)(2,1)}) custom-call(bf16[384,1536]{1,0:T(8,128)(2,1)} %bitcast.28, bf16[384,1536]{1,0:T(8,128)(2,1)} %get-tuple-element.72.mixed_ref, f32[4,8,384]{2,1,0:T(8,128)} %get-tuple-element.63.gain_ref, bf16[1536,1536]{1,0:T(8,128)(2,1)} %bitcast.25), custom_call_target="tpu_custom_call" | custom-call | tf_op jit(solution)/shard_map/middle/pallas_call | solution.py:436
  120.4 1.1 collective-permute-start.1
  121.5 1.8 collective-permute-done.3.c_y_left
  123.3 11.5 %collective-permute-done.x_x = bf16[384,768]{1,0:T(8,128)(2,1)} collective-permute-done((bf16[384,768]{1,0:T(8,128)(2,1)}, bf16[384,768]{1,0:T(8,128)(2,1)}, u32[]{:S(2)}, u32[]{:S(2)}) %collective-permute-start) | collective-permute-done | bytes 589856 | tf_op jit(solution)/shard_map/ppermute | solution.py:1667
  135.6 85.4 %mlp.1 = (f32[384,1536]{1,0:T(8,128)}, bf16[384,1536]{1,0:T(8,128)(2,1)}, bf16[384,1536]{1,0:T(8,128)(2,1)}, bf16[384,1536]{1,0:T(8,128)(2,1)}, bf16[384,768]{1,...) custom-call(bf16[4,864,768]{2,1,0:T(8,128)(2,1)} %bitcast.32, ...), custom_call_target="tpu_custom_call" | custom-call | tf_op jit(solution)/shard_map/mlp/pallas_call | solution.py:1610
  222.4 1.7 collective-permute-start.6
  224.3 11.2 %middle_back.1 = (f32[384,1536]{1,0:T(8,128)}, bf16[384,1536]{1,0:T(8,128)(2,1)}, bf16[1536,1536]{1,0:T(8,128)(2,1)}, f32[1,1536]{1,0:T(1,128)}, s32[8,128]{1,0:T(8,128)}) custom-call(f32[384,1536]{1,0:T(8,128)} %get-tuple-element.83.grad_ref, f32[384,1536]{1,0:T(8,128)} %get-tuple-element.74.middle_ref, bf16[384,1536]{1,0:T(8,128)(2,1)} %bitcast.23, ...), custom_call_target="tpu_custom_call" | custom-call | tf_op jit(solution)/shard_map/middle_back/pallas_call | solution.py:477
  235.4 1.2 slice.38
  238.7 1.4 collective-permute-start.7
  240.1 22.2 %attend_back.1 = (bf16[384,1536]{1,0:T(8,128)(2,1)}, bf16[32,96,256]{2,1,0:T(8,128)(2,1)}) custom-call(s32[8,128]{1,0:T(8,128)} %get-tuple-element.62.where_ref, bf16[14,384,128]{2,1,0:T(8,128)(2,1)} %get-tuple-element.67.heads_ref.q_ref, bf16[8,2,384,128]{3,2,1,0:T(8,128)(2,1)} %get-tuple-element.69.kv_ref, bf16[384,1536]{1,0:T(8,128)(2,1)} %get-tuple-element.89.grad_ref, ...), custom_call_target="tpu_custom_call" | custom-call | tf_op jit(solution)/shard_map/attend_back/pallas_call | solution.py:385
  262.4 2.6 collective-permute-done.9
  266.0 1.6 fusion
  267.6 69.0 %project_back_plane.1 = (bf16[4,48,1536]{2,1,0:T(8,128)(2,1)}, bf16[4,48,1536]{2,1,0:T(8,128)(2,1)}, bf16[4,48,256]{2,1,0:T(8,128)(2,1)}, bf16[8,288,768]{2,1,0:...) custom-call(bf16[4,4,2,96,256]{4,3,2,1,0:T(8,128)(2,1)} %bitcast.36, bf16[4,4,2,48,1536]{4,3,2,1,0:T(8,128)(2,1)} %bitcast.35, ...), custom_call_target="tpu_custom_call" | custom-call | tf_op jit(solution)/shard_map/project_back_plane/pallas_call | solution.py:1152
  336.6 3.4 add_bitcast_fusion
  340.1 55.1 %reduce_late.1 = (bf16[8,48,1536]{2,1,0:T(8,128)(2,1)}, bf16[8,48,1536]{2,1,0:T(8,128)(2,1)}, bf16[8,48,256]{2,1,0:T(8,128)(2,1)}, bf16[8,576,768]{2,1,0:T(8,128)(2,1)}, f32[8,384]{1,0:T(8,128)}) custom-call(bf16[4,48,1536]{2,1,0:T(8,128)(2,1)} %get-tuple-element.98.refs_0_, bf16[4,48,1536]{2,1,0:T(8,128)(2,1)} %get-tuple-element.99.refs_1_, ...), custom_call_target="tpu_custom_call" | custom-call | tf_op jit(solution)/shard_map/reduce_late/pallas_call | solution.py:1257
  395.3 1.4 slice_reduce_fusion
  396.6 15.8 %finish.1 = (f32[384,9216]{1,0:T(8,128)}, f32[1152,1536]{1,0:T(8,128)}, f32[384,1536]{1,0:T(8,128)}, f32[384,1792]{1,0:T(8,128)}) custom-call(bf16[8,576,768]{2,1,0:T(8,128)(2,1)} %get-tuple-element.105.main_ref.tail_ref, bf16[8,576,768]{2,1,0:T(8,128)(2,1)} %get-tuple-element.105.main_ref.tail_ref, ...), custom_call_target="tpu_custom_call" | custom-call | tf_op jit(solution)/shard_map/finish/pallas_call | solution.py:1372
  (66 shorter events, 11.6 us)
Async XLA Ops:
  7.2 128.4 %all-gather.3.cloned.1.call-start = ((), (), s32[]{:S(2)}) async-start(), calls=%async_computation.4 | async-start | bytes 6635520 | tf_op jit(solution)/shard_map/all_gather | solution.py:1830
  30.1 237.5 %reduce-scatter.3.cloned.1.call-start = ((), (), s32[]{:S(2)}) async-start(), calls=%async_computation.2 | async-start | bytes 2211840 | tf_op jit(solution)/shard_map/reduce_scatter | solution.py:1881
  64.4 29.2 %copy-start.5 = (bf16[384,768]{1,0:T(8,128)(2,1)S(1)}, bf16[384,768]{1,0:T(8,128)(2,1)}, u32[]{:S(2)}) copy-start(bf16[384,768]{1,0:T(8,128)(2,1)} %get-tuple-element.80.c_y_right) | copy-start | bytes 1769476
  64.4 30.3 %copy-start.4 = (bf16[384,768]{1,0:T(8,128)(2,1)S(1)}, bf16[384,768]{1,0:T(8,128)(2,1)}, u32[]{:S(2)}) copy-start(bf16[384,768]{1,0:T(8,128)(2,1)} %get-tuple-element.78.c_x_left) | copy-start | bytes 1769476
  91.6 4.2 %copy-start = (bf16[1,384,1536]{2,1,0:T(8,128)(2,1)S(1)}, bf16[1,384,1536]{2,1,0:T(8,128)(2,1)}, u32[]{:S(2)}) copy-start(bf16[1,384,1536]{2,1,0:T(8,128)(2,1)} %param.19) | copy-start | bytes 3538948
  93.6 26.8 %collective-permute-start.5 = (bf16[384,768]{1,0:T(8,128)(2,1)S(1)}, bf16[384,768]{1,0:T(8,128)(2,1)}, u32[]{:S(2)}, u32[]{:S(2)}) collective-permute-start(bf16[384,768]{1,0:T(8,128)(2,1)S(1)} %broadcast_select_fusion), channel_id=1, source_target_pairs={{0,8},{4,12},{8,0},{12,4},{16,24},{20,28},{24,16},{28,20},{1,9},{5... | collective-permute-start | bytes 1769480 | tf_op jit(solution)/shard_map/ppermute | solution.py:1667
  94.7 26.8 %collective-permute-start.4 = (bf16[384,768]{1,0:T(8,128)(2,1)S(1)}, bf16[384,768]{1,0:T(8,128)(2,1)S(1)}, u32[]{:S(2)}, u32[]{:S(2)}) collective-permute-start(bf16[384,768]{1,0:T(8,128)(2,1)S(1)} %broadcast_select_fusion.1), channel_id=1, source_target_pairs={{0,16},{4,20},{8,24},{12,28},{16,0},{20,4},{24,8},{28,12},{1,17},{... | collective-permute-start | bytes 1769480 | tf_op jit(solution)/shard_map/ppermute | solution.py:1667
  95.9 27.3 %collective-permute-start.3 = (bf16[384,768]{1,0:T(8,128)(2,1)S(1)}, bf16[384,768]{1,0:T(8,128)(2,1)S(1)}, u32[]{:S(2)}, u32[]{:S(2)}) collective-permute-start(bf16[384,768]{1,0:T(8,128)(2,1)S(1)} %get-tuple-element.116), channel_id=1, source_target_pairs={{0,16},{4,20},{8,24},{12,28},{16,0},{20,4},{24,8},{28,12},{1,17},{... | collective-permute-start | bytes 1769480 | tf_op jit(solution)/shard_map/ppermute | solution.py:1667
  97.0 26.3 %collective-permute-start.2 = (bf16[384,768]{1,0:T(8,128)(2,1)S(1)}, bf16[384,768]{1,0:T(8,128)(2,1)S(1)}, u32[]{:S(2)}, u32[]{:S(2)}) collective-permute-start(bf16[384,768]{1,0:T(8,128)(2,1)S(1)} %get-tuple-element.117), channel_id=1, source_target_pairs={{0,8},{4,12},{8,0},{12,4},{16,24},{20,28},{24,16},{28,20},{1,9},{5... | collective-permute-start | bytes 1769480 | tf_op jit(solution)/shard_map/ppermute | solution.py:1667
  119.4 15.4 %collective-permute-start = (bf16[384,768]{1,0:T(8,128)(2,1)}, bf16[384,768]{1,0:T(8,128)(2,1)}, u32[]{:S(2)}, u32[]{:S(2)}) collective-permute-start(bf16[384,768]{1,0:T(8,128)(2,1)} %get-tuple-element.76.x_left), channel_id=1, source_target_pairs={{0,8},{4,12},{8,0},{12,4},{16,24},{20,28},{24,16},{28,20},{1,9},{5... | collective-permute-start | bytes 1769480 | tf_op jit(solution)/shard_map/ppermute | solution.py:1667
  120.4 15.2 %collective-permute-start.1 = (bf16[384,768]{1,0:T(8,128)(2,1)}, bf16[384,768]{1,0:T(8,128)(2,1)}, u32[]{:S(2)}, u32[]{:S(2)}) collective-permute-start(bf16[384,768]{1,0:T(8,128)(2,1)} %get-tuple-element.77.x_right), channel_id=1, source_target_pairs={{0,16},{4,20},{8,24},{12,28},{16,0},{20,4},{24,8},{28,12},{1,17},{... | collective-permute-start | bytes 1769480 | tf_op jit(solution)/shard_map/ppermute | solution.py:1667
  121.5 14.1 %copy-start.10 = (bf16[384,768]{1,0:T(8,128)(2,1)}, bf16[384,768]{1,0:T(8,128)(2,1)S(1)}, u32[]{:S(2)}) copy-start(bf16[384,768]{1,0:T(8,128)(2,1)S(1)} %collective-permute-done.4.c_left) | copy-start | bytes 1769476
  123.3 12.3 %copy-start.11 = (bf16[384,768]{1,0:T(8,128)(2,1)}, bf16[384,768]{1,0:T(8,128)(2,1)S(1)}, u32[]{:S(2)}) copy-start(bf16[384,768]{1,0:T(8,128)(2,1)S(1)} %collective-permute-done.3.c_y_left) | copy-start | bytes 1769476
  123.3 12.3 %copy-start.12 = (bf16[384,768]{1,0:T(8,128)(2,1)}, bf16[384,768]{1,0:T(8,128)(2,1)S(1)}, u32[]{:S(2)}) copy-start(bf16[384,768]{1,0:T(8,128)(2,1)S(1)} %collective-permute-done.2.c_x_right) | copy-start | bytes 1769476
  221.0 119.1 %reduce-scatter.5.cloned.1.call-start = ((), (), s32[]{:S(2)}) async-start(), calls=%async_computation.3 | async-start | bytes 4423680 | tf_op jit(solution)/shard_map/reduce_scatter | solution.py:1882
  221.1 3.1 copy-start.8
  221.7 2.5 copy-start.9
  222.1 15.3 %collective-permute-start.8 = (bf16[384,768]{1,0:T(8,128)(2,1)S(1)}, bf16[384,768]{1,0:T(8,128)(2,1)S(1)}, u32[]{:S(2)}, u32[]{:S(2)}) collective-permute-start(bf16[384,768]{1,0:T(8,128)(2,1)S(1)} %copy-done.14), channel_id=1, source_target_pairs={{0,16},{4,20},{8,24},{12,28},{16,0},{20,4},{24,8},{28,12},{1,17},{... | collective-permute-start | bytes 1769480 | tf_op jit(solution)/shard_map/ppermute | solution.py:1667
  222.4 16.0 %collective-permute-start.6 = (bf16[384,768]{1,0:T(8,128)(2,1)S(1)}, bf16[384,768]{1,0:T(8,128)(2,1)S(1)}, u32[]{:S(2)}, u32[]{:S(2)}) collective-permute-start(bf16[384,768]{1,0:T(8,128)(2,1)S(1)} %copy-done.13), channel_id=1, source_target_pairs={{0,8},{4,12},{8,0},{12,4},{16,24},{20,28},{24,16},{28,20},{1,9},{5... | collective-permute-start | bytes 1769480 | tf_op jit(solution)/shard_map/ppermute | solution.py:1667
  237.7 27.4 %collective-permute-start.9 = (bf16[384,1536]{1,0:T(8,128)(2,1)S(1)}, bf16[384,1536]{1,0:T(8,128)(2,1)S(1)}, u32[]{:S(2)}, u32[]{:S(2)}) collective-permute-start(bf16[384,1536]{1,0:T(8,128)(2,1)S(1)} %pad_maximum_fusion.1.refs_0_), channel_id=1, source_target_pairs={{0,8},{4,12},{8,0},{12,4},{16,24},{20,28},{24,16},{28,20},{1,9},{5... | collective-permute-start | bytes 3538952 | tf_op jit(solution)/shard_map/ppermute | solution.py:1667
  238.7 27.2 %collective-permute-start.7 = (bf16[384,1536]{1,0:T(8,128)(2,1)S(1)}, bf16[384,1536]{1,0:T(8,128)(2,1)S(1)}, u32[]{:S(2)}, u32[]{:S(2)}) collective-permute-start(bf16[384,1536]{1,0:T(8,128)(2,1)S(1)} %pad_maximum_fusion.refs_1_), channel_id=1, source_target_pairs={{0,16},{4,20},{8,24},{12,28},{16,0},{20,4},{24,8},{28,12},{1,17},{... | collective-permute-start | bytes 3538952 | tf_op jit(solution)/shard_map/ppermute | solution.py:1667
  240.1 25.8 %copy-start.1 = (f32[384,1536]{1,0:T(8,128)S(1)}, f32[384,1536]{1,0:T(8,128)}, u32[]{:S(2)}) copy-start(f32[384,1536]{1,0:T(8,128)} %get-tuple-element.74.middle_ref) | copy-start | bytes 7077892
  240.1 25.8 %copy-start.7 = (bf16[384,1536]{1,0:T(8,128)(2,1)S(1)}, bf16[384,1536]{1,0:T(8,128)(2,1)}, u32[]{:S(2)}) copy-start(bf16[384,1536]{1,0:T(8,128)(2,1)} %get-tuple-element.81) | copy-start | bytes 3538948
  267.6 69.1 %copy-start.6 = (f32[384,1536]{1,0:T(8,128)S(1)}, f32[384,1536]{1,0:T(8,128)}, u32[]{:S(2)}) copy-start(f32[384,1536]{1,0:T(8,128)} %get-tuple-element.88) | copy-start | bytes 7077892
  (4 other events, 4.9 us)
Sparse Core Ops, SparseCore 0:
  30.2 104.6 all-gather.2
  221.1 40.6 reduce-scatter.2
  264.3 65.4 reduce-scatter.4

commit v6 on v5

--- a/solution.py
+++ b/solution.py
@@ -1053,6 +1053,24 @@
         return value
 
 
+def send_lines(wire, source, arrived, shards):
+    return [
+        wire.send(
+            source.at[lax.rem(wire.shard + step, shards)], arrived.at[step - 1], wire.line(step, shards)
+        )
+        for step in range(1, shards)
+    ]
+
+
+def sum_lines(wire, copies, source, arrived):
+    for copy in copies:
+        copy.wait_recv()
+    value = source[wire.shard].astype(jnp.float32)
+    for step in range(len(copies)):
+        value += arrived[step].astype(jnp.float32)
+    return value
+
+
 def project_back_plane_kernel(
     kv_ref, g_out_ref, part_ref, grad_ref, normed_ref, x_ref, cos_ref, sin_ref, gain_ref, w_ref,
     out_half, q_half, k_half, part_all, grad_x_ref, grad_gain_ref,
@@ -1120,24 +1138,30 @@
     queries_sum.step_one()
     pair_sum.step_one()
     gather.forward()
+
+    def store_into(target):
+        def store(part, value):
+            target[part] = low(value)
+
+        return store
+
+    out_sum.result(store_into(out_half))
     change, grad_gain = norm_back(x[...].astype(jnp.float32), gain_row(gains, 0), grad_normed[...])
     grad_x_ref[...] = change
     grad_gain_ref[...] = grad_gain
     queries_sum.step_two()
     pair_sum.step_two()
     gather.corner()
-    for total, target in ((out_sum, out_half), (queries_sum, q_half), (pair_sum, k_half)):
-
-        def store(part, value, target=target):
-            target[part] = low(value)
-
-        total.result(store)
+    queries_sum.result(store_into(q_half))
+    pair_sum.result(store_into(k_half))
     gather.settle()
     relay.settle()
     wire.finish()
 
 
-def project_back_plane(grad_kv, g_out, part, grad_q, normed, x, cosine, sine_part, gains, w, ctx_size):
+def project_back_plane(
+    grad_kv, g_out, part, grad_q, normed, x, cosine, sine_part, gains, w, ctx_size
+):
     rows, width = x.shape
     inner = grad_q.shape[1]
     lead = g_out.shape[:4]
@@ -1186,18 +1210,35 @@
     )(grad_kv, g_out, part, grad_q, normed, x, cosine, sine_part, gains, w)
 
 
-def reduce_late_kernel(shards, line_count, *refs):
+TERMS = 4
+
+
+def reduce_late_kernel(shards, line_count, part_count, *refs):
     line_ins, refs = take(refs, line_count)
-    part_ref, gain_a, gain_b, *refs = refs
+    parts, refs = take(refs, part_count)
+    gain_a, gain_b, *refs = refs
+    terms, refs = take(refs, TERMS)
     line_outs, refs = take(refs, line_count)
-    part_all, gain_out, *refs = refs
+    part_outs, refs = take(refs, part_count)
+    gain_out, total_ref, *refs = refs
     arrived, refs = take(refs, line_count)
     done, refs = take(refs, line_count)
-    stage, gain_now, gain_in, gain_line, done_sems, part_sems, send_sems, recv_sems = refs
+    stages, refs = take(refs, part_count)
+    held, refs = take(refs, TERMS)
+    gain_now, gain_in, gain_line, done_sems, part_sems, term_sems, send_sems, recv_sems = refs
 
     wire = Wire(send_sems, recv_sems)
     ctx, shard = wire.ctx, wire.shard
-    relay = Relay(part_ref, stage, [(stage, part_all.at[ctx])], part_sems)
+    relays = [
+        Relay(source, stage, [(stage, target.at[ctx])], part_sems.at[i])
+        for i, (source, stage, target) in enumerate(zip(parts, stages, part_outs))
+    ]
+    loads = [
+        pltpu.make_async_copy(source, target, term_sems.at[i])
+        for i, (source, target) in enumerate(zip(terms, held))
+    ]
+    for copy in loads:
+        copy.start()
     gain_now[...] = jnp.zeros_like(gain_now)
     columns = gain_now.shape[2]
     for part in range(shards):
@@ -1207,37 +1248,37 @@
         [wire.plane(mask) for mask in PLANE_PEERS] + [wire.line(s, shards) for s in range(1, shards)]
     )
     lines = [
-        [
-            wire.send(
-                source.at[lax.rem(shard + step, shards)], target.at[step - 1], wire.line(step, shards)
-            )
-            for step in range(1, shards)
-        ]
-        for source, target in zip(line_ins, arrived)
+        send_lines(wire, source, target, shards) for source, target in zip(line_ins, arrived)
     ]
-    rows = part_ref.shape[0]
-    gathers = [PlaneGather(wire, part_ref, lambda who: part_all.at[who], rows, rows // 32 * 16)]
+    gathers = []
+    for source, target in zip(parts, part_outs):
+        rows = source.shape[0]
+        place = lambda who, target=target: target.at[who]
+        gathers.append(PlaneGather(wire, source, place, rows, rows // 32 * 16))
     gain = GainSum(wire, gain_now, gain_in, gain_line, shards)
     gain.step()
     gain.step()
     gain.step_line()
-    relay.push()
-    gathers[0].forward()
+    for relay in relays:
+        relay.push()
+    for copy in loads:
+        copy.wait()
+    total = held[0][...]
+    for one in held[1:]:
+        total += one[...].astype(jnp.float32)
+    total_ref[...] = low(total)
+    for gather in gathers:
+        gather.forward()
     locals_ = []
     for i, (source, target) in enumerate(zip(line_ins, line_outs)):
-        for copy in lines[i]:
-            copy.wait_recv()
-        value = source[shard].astype(jnp.float32)
-        for step in range(shards - 1):
-            value += arrived[i][step].astype(jnp.float32)
-        done[i][...] = low(value)
+        done[i][...] = low(sum_lines(wire, lines[i], source, arrived[i]))
         place = lambda who, target=target: target.at[who]
         gathers.append(PlaneGather(wire, done[i], place, target.shape[1], half_rows(target.shape[1], i)))
         copy = pltpu.make_async_copy(done[i], place(ctx), done_sems.at[i])
         copy.start()
         locals_.append(copy)
     gain_out[...] = gain.result()
-    for gather in gathers[1:]:
+    for gather in gathers[part_count:]:
         gather.forward()
     for gather in gathers:
         gather.corner()
@@ -1245,35 +1286,41 @@
         gather.settle()
     for copy in locals_:
         copy.wait()
-    relay.settle()
+    for relay in relays:
+        relay.settle()
     wire.finish()
 
 
-def reduce_late(lines, part, gain_a, gain_b, ctx_size):
+def reduce_late(lines, parts, gain_a, gain_b, terms, ctx_size):
     shards = lines[0].shape[0]
     vmem = pl.BlockSpec(memory_space=pltpu.VMEM)
     gain_shape = (shards, 8, gain_a.shape[1] // shards)
-    copies = (PlaneGather.COPIES + shards - 1) * len(lines) + PlaneGather.COPIES + 3 + shards - 1
+    copies = (PlaneGather.COPIES + shards - 1) * len(lines) + PlaneGather.COPIES * len(parts)
+    copies += 3 + shards - 1
     return pl.pallas_call(
-        functools.partial(reduce_late_kernel, shards, len(lines)),
+        functools.partial(reduce_late_kernel, shards, len(lines), len(parts)),
         name="reduce_late",
-        in_specs=[vmem] * len(lines) + [ANY] + [vmem] * 2,
-        out_specs=[ANY] * (len(lines) + 1) + [vmem],
-        out_shape=[like(array, ctx_size) for array in (*lines, part)]
-        + [jax.ShapeDtypeStruct(gain_shape[1:], jnp.float32)],
+        in_specs=[vmem] * len(lines) + [ANY] * len(parts) + [vmem] * 2 + [ANY] * TERMS,
+        out_specs=[ANY] * (len(lines) + len(parts)) + [vmem] * 2,
+        out_shape=[like(array, ctx_size) for array in (*lines, *parts)]
+        + [
+            jax.ShapeDtypeStruct(gain_shape[1:], jnp.float32),
+            jax.ShapeDtypeStruct(terms[0].shape, jnp.bfloat16),
+        ],
         scratch_shapes=[stage_like(array, shards - 1) for array in lines]
-        + [stage_like(array) for array in (*lines, part)]
+        + [stage_like(array) for array in (*lines, *parts, *terms)]
         + [
             pltpu.VMEM(gain_shape, jnp.float32),
             pltpu.VMEM((3,) + gain_shape, jnp.float32),
             pltpu.VMEM((shards - 1,) + gain_shape[1:], jnp.float32),
             dma_sems(len(lines)),
-            dma_sems(2),
+            pltpu.SemaphoreType.DMA((len(parts), 2)),
+            dma_sems(TERMS),
             dma_sems(copies),
             dma_sems(copies),
         ],
         compiler_params=comm_params(4),
-    )(*lines, part, gain_a, gain_b)
+    )(*lines, *parts, gain_a, gain_b, *terms)
 
 
 class Pack:
@@ -1309,7 +1356,7 @@
 
 def finish_kernel(
     shards, chips, pack, main_ref, tail_ref, out_main_ref, out_rest_ref, attn_out_ref, attn_q_ref, attn_kv_ref,
-    in_ref, out_ref, grad_attn_out_ref, grad_attn_in_ref,
+    x_one_ref, x_two_ref, in_ref, out_ref, grad_attn_out_ref, grad_attn_in_ref, x_ref,
 ):
     step = pl.program_id(0)
     last = pl.num_programs(0) - 1
@@ -1344,6 +1391,7 @@
                 ]
                 in_ref[:, start + chips * main : start + per_shard] = jnp.concatenate(ends, axis=1)
             out_ref[:, core * half : (core + 1) * half] = wide(out_main_ref[core])
+        x_ref[...] = x_one_ref[...] + x_two_ref[...]
         grad_attn_out_ref[...] = wide(attn_out_ref[0])
         inner = attn_q_ref.shape[2]
         grad_attn_in_ref[:, :inner] = wide(attn_q_ref[0])
@@ -1357,7 +1405,7 @@
                 out_ref[chip * rest : (chip + 1) * rest, core * half : (core + 1) * half] = block
 
 
-def finish(first, second, attn_out, attn_q, attn_kv, pack, shards):
+def finish(first, second, attn_out, attn_q, attn_kv, x_one, x_two, pack, shards):
     ctx_size = first.shape[0]
     chips = ctx_size // 2
     steps = ctx_size
@@ -1367,6 +1415,7 @@
     assert out_tile == chips * pack.rest and pack.main % pack.rest == 0
     at = lambda i: jnp.minimum(i, steps - 1)
     rows = attn_out.shape[1]
+    x_rows = x_one.shape[0] // steps
     piece = lambda array: pl.BlockSpec((1,) + array.shape[1:], lambda i: (at(i), 0, 0))
     attn_in = attn_q.shape[2] + attn_kv.shape[2]
     return pl.pallas_call(
@@ -1384,21 +1433,25 @@
             piece(attn_out),
             piece(attn_q),
             piece(attn_kv),
+            pl.BlockSpec((x_rows, x_one.shape[1]), lambda i: (at(i), 0)),
+            pl.BlockSpec((x_rows, x_one.shape[1]), lambda i: (at(i), 0)),
         ],
         out_specs=[
             pl.BlockSpec((tile, 2 * FF), lambda i: (at(i), 0)),
             pl.BlockSpec((out_tile, 2 * pack.half), lambda i: (i, 0)),
             pl.BlockSpec((rows, attn_out.shape[2]), lambda i: (at(i), 0)),
             pl.BlockSpec((rows, attn_in), lambda i: (at(i), 0)),
+            pl.BlockSpec((x_rows, x_one.shape[1]), lambda i: (at(i), 0)),
         ],
         out_shape=[
             jax.ShapeDtypeStruct((pack.rows, 2 * FF), jnp.float32),
             jax.ShapeDtypeStruct((FF // shards, 2 * pack.half), jnp.float32),
             jax.ShapeDtypeStruct((steps * rows, attn_out.shape[2]), jnp.float32),
             jax.ShapeDtypeStruct((steps * rows, attn_in), jnp.float32),
+            jax.ShapeDtypeStruct(x_one.shape, jnp.float32),
         ],
         compiler_params=pltpu.CompilerParams(vmem_limit_bytes=VMEM_LIMIT),
-    )(second, second, first, first, attn_out, attn_q, attn_kv)
+    )(second, second, first, first, attn_out, attn_q, attn_kv, x_one, x_two)
 
 
 TANH_SCALE = 0.7978845608028654
@@ -1496,9 +1549,7 @@
 
         return one_half
 
-    one_half = one_chunk(0)
-    for span in (left, right):
-        normed_grad[:, span] = one_half(span)
+    own_half = one_chunk(0)
     for copy in x_copies:
         copy.wait_recv()
     corners = [
@@ -1523,6 +1574,8 @@
     part[2, :, right] = low(one_half(right))
     corner.append(wire.send(part.at[2, :, right], corner_right, wire.plane(4)))
 
+    for span in (left, right):
+        normed_grad[:, span] = own_half(span)
     out_copies = {}
 
     def out_part(at, targets):
@@ -1547,10 +1600,14 @@
         return columns, tn_dot(everything(xs), picked)
 
     pairs_in = []
-    for tile in range(tiles):
+
+    def send_in_tile(tile):
         columns, value = in_tile(other, tile)
         w_in[0, :, columns] = low(value)
         pairs_in.append(wire.send(w_in.at[0, :, columns], pair_in.at[:, columns], wire.plane(1)))
+
+    for tile in range(tiles):
+        send_in_tile(tile)
     merged = []
     corner[0].wait_recv()
     part[1, :, left] = add_low(part[1, :, left], corner_left[...])
@@ -1676,10 +1733,6 @@
         to_y = jnp.concatenate([add_low(to_y[:, :half], left), to_y[:, half:]], axis=1)
         to_x = jnp.concatenate([to_x[:, :half], add_low(to_x[:, half:], right)], axis=1)
         return to_x, to_y
-
-    def sum_neighbours(self, own, to_x, to_y):
-        wide = lambda part: part.astype(jnp.float32)
-        return wide(own) + wide(self.xor(to_y, 4)) + wide(self.xor(to_x, 2))
 
     def gather_chips(self, values):
         groups = self.same_core_groups()
@@ -1891,7 +1944,7 @@
         grad_gate = low(grad_gate)
         grad_up = low(grad_up)
         grad_normed_two = lay.scatter_chips(dot_nt(grad_gate, gate_in) + dot_nt(grad_up, up_in))
-        mixed_out = lay.scatter_chips(dot(hidden, out_mlp))
+        result = low(middle + lay.scatter_chips(dot(hidden, out_mlp)))
         grad_out_mlp = lay.reduce_mlp_out(dot_tn(hidden, upstream_all))
         grad_in_mlp = lay.reduce_mlp_in(dot_tn(normed_all, grad_gate), dot_tn(normed_all, grad_up))
 
@@ -1913,9 +1966,6 @@
         out_parts,
     )
     if lay.plane:
-        mixed_out = lay.sum_neighbours(out_own, *out_parts)
-    result = middle + mixed_out
-    if lay.plane:
         split = lambda grad: grad.reshape(fsdp_size, lay.chips, 2, -1, grad.shape[1])
         grad_kv = grad_kv.reshape(ROUNDS, lay.chips, 2, block, 2 * HD)
         *halves, grad_first, grad_inputs, grad_gain_attn = project_back_plane(
@@ -1931,16 +1981,19 @@
             in_attn,
             ctx_size,
         )
-        grad_inputs = grad_middle + grad_inputs
-        grad_out_attn, grad_in_queries, grad_in_keys, grad_second, grad_gains = reduce_late(
-            halves, grad_second, grad_gain_attn, grad_gain_mlp, ctx_size
+        to_x, to_y = out_parts
+        terms = (middle, out_own, lay.xor(to_y, 4), lay.xor(to_x, 2))
+        grad_out_attn, grad_in_queries, grad_in_keys, grad_second, grad_gains, result = reduce_late(
+            halves, [grad_second], grad_gain_attn, grad_gain_mlp, terms, ctx_size
         )
-        grad_in_mlp, grad_out_mlp, grad_out_attn, grad_in_attn = finish(
+        grad_in_mlp, grad_out_mlp, grad_out_attn, grad_in_attn, grad_inputs = finish(
             grad_first,
             grad_second,
             grad_out_attn,
             grad_in_queries,
             grad_in_keys,
+            grad_middle,
+            grad_inputs,
             pack,
             fsdp_size,
         )
@@ -1961,7 +2014,7 @@
         grad_gain_attn = lay.reduce_gain(grad_gain_attn[0])
         grad_gain_mlp = lay.reduce_gain(grad_gain_mlp[0])
     return (
-        low(result)[None],
+        result[None],
         grad_inputs[None],
         grad_gain_attn,
         grad_in_attn,

time: 427 us -> 423 us (level)
  other arithmetic: 6.91 us -> 1.85 us
    broadcast_in_dim x2 -> x0, other arithmetic: 5.06 us -> none  [the longest x1 3.45 us: per_device(): grad_inputs[None]]
  transfers between devices with their start and end apart: 13 -> 13, of which waited for: 6 -> 3; matrix products, arithmetic and copies ran while one was open for 2% -> 1% of each run, Pallas kernels for 44% -> 45%
where the time goes in v6:
time: 423 us; the launch traced here: 416 us
  Pallas kernels  365 us (86%)
  between operations  15.6 us (4%)
  waiting for transfers between devices  14.8 us (3%)
  starting transfers between devices  10.7 us (3%)
  local copies, waits for them, and re-layouts  7.68 us (2%)
    pallas_call x1, Pallas kernels, mlp(): pl.pallas_call(functools.partial(mlp_kernel, shards, pack), name='mlp', i...  84.8 us
    pallas_call x1, Pallas kernels, project_back_plane(): pl.pallas_call(project_back_plane_kernel, name='project_back_plane', in_s...  70.5 us
    pallas_call x1, Pallas kernels, reduce_late(): pl.pallas_call(functools.partial(reduce_late_kernel, shards, len(lines),...  56.2 us
    pallas_call x1, Pallas kernels, gather_plane(): pl.pallas_call(functools.partial(gather_plane_kernel, shards), name='gath...  27.2 us
    pallas_call x1, Pallas kernels, share_plane(): pl.pallas_call(functools.partial(share_plane_kernel, shards, ctx_size), n...  27.1 us
    pallas_call x1, Pallas kernels, attend_back(): pl.pallas_call(functools.partial(attend_back_kernel, window.blocks, block...  21.9 us
    pallas_call x1, Pallas kernels, share_line(): pl.pallas_call(functools.partial(share_line_kernel, shards, pack), name='...  20.9 us
    pallas_call x1, Pallas kernels, finish(): pl.pallas_call(functools.partial(finish_kernel, shards, chips, pack), nam...  17.8 us
  transfers between devices with their start and end apart: 13, of which 3 were waited for; matrix products, arithmetic and copies ran while one was open for 1% of the time, Pallas kernels for 45%

profile of v6, /device:TPU:0, one launch (start us, length us, event | category | flops | bytes accessed | tf_op | source)
XLA Modules:
  0.0 416.0 jit_solution(11640502188654624753)
XLA Ops:
  9.2 20.9 %share_line.1 = (bf16[4,48,1792]{2,1,0:T(8,128)(2,1)}, f32[4,8,384]{2,1,0:T(8,128)}, bf16[864,768]{1,0:T(8,128)(2,1)}, bf16[384,768]{1,0:T(8,128)(2,1)}, bf16[384,768]{1,0:T(8,128)(2,1)}) custom-call(bf16[8,48,1792]{2,1,0:T(8,128)(2,1)} %bitcast.28, bf16[2,384]{1,0:T(2,128)(2,1)} %pad_maximum_fusion.2.gain_ref, bf16[384,9216]{1,0:T(8,128)(2,1)} %mlp_in.1, ...), custom_call_target="tpu_custom_call" | custom-call | tf_op jit(solution)/shard_map/share_line/pallas_call | solution.py:946
  30.7 27.1 %share_plane.1 = (bf16[4,8,48,1792]{3,2,1,0:T(8,128)(2,1)}, bf16[4,48,1536]{2,1,0:T(8,128)(2,1)}, s32[8,128]{1,0:T(8,128)}, f32[4,1,1152]{2,1,0:T(1,128)}, f32[3...) custom-call(bf16[8,48,1792]{2,1,0:T(8,128)(2,1)} %bitcast.29, ...), custom_call_target="tpu_custom_call" | custom-call | tf_op jit(solution)/shard_map/share_plane/pallas_call | solution.py:975
  57.8 6.7 %project.1 = (bf16[384,1536]{1,0:T(8,128)(2,1)}, bf16[14,384,128]{2,1,0:T(8,128)(2,1)}) custom-call(bf16[384,1536]{1,0:T(8,128)(2,1)} %bitcast.25, f32[4,8,384]{2,1,0:T(8,128)} %get-tuple-element.65.gain_ref, bf16[1536,1792]{1,0:T(8,128)(2,1)} %bitcast.17, f32[384,128]{1,0:T(8,128)} %get-tuple-element.67.cos_ref, f32[384,128]{1,0:T(8,128)} %get-tuple-element.68.sin_ref), custom_call_target="tpu_custom_call" | custom-call | tf_op jit(solution)/shard_map/project/pallas_call | solution.py:96
  64.5 27.2 %gather_plane.1 = (bf16[8,2,384,128]{3,2,1,0:T(8,128)(2,1)}, bf16[4,8,48,1536]{3,2,1,0:T(8,128)(2,1)}, s32[8,128]{1,0:T(8,128)}) custom-call(bf16[14,384,128]{2,1,0:T(8,128)(2,1)} %get-tuple-element.69.heads_ref.q_ref, bf16[8,48,1536]{2,1,0:T(8,128)(2,1)} %bitcast.32, bf16[4,48,1536]{2,1,0:T(8,128)(2,1)} %get-tuple-element.70.out_line), custom_call_target="tpu_custom_call" | custom-call | tf_op jit(solution)/shard_map/gather_plane/pallas_call | solution.py:997
  91.7 1.3 slice.34
  93.7 1.0 collective-permute-start.5
  94.7 1.1 collective-permute-start.4
  95.9 1.0 collective-permute-start.3
  97.0 1.1 collective-permute-start.2
  98.0 14.5 %attend.1 = (bf16[384,1536]{1,0:T(8,128)(2,1)}, f32[4,3,1,384]{3,2,1,0:T(1,128)}) custom-call(s32[8,128]{1,0:T(8,128)} %get-tuple-element.64.where_ref, bf16[14,384,128]{2,1,0:T(8,128)(2,1)} %get-tuple-element.69.heads_ref.q_ref, bf16[8,2,384,128]{3,2,1,0:T(8,128)(2,1)} %get-tuple-element.71.kv_ref, f32[4,1,1152]{2,1,0:T(1,128)} %get-tuple-element.73.key_place_ref, ...), custom_call_target="tpu_custom_call" | custom-call | tf_op jit(solution)/shard_map/attend/pallas_call | solution.py:283
  112.5 6.9 %middle.1 = (f32[384,1536]{1,0:T(8,128)}, bf16[384,768]{1,0:T(8,128)(2,1)}, bf16[384,768]{1,0:T(8,128)(2,1)}) custom-call(bf16[384,1536]{1,0:T(8,128)(2,1)} %bitcast.26, bf16[384,1536]{1,0:T(8,128)(2,1)} %get-tuple-element.75.mixed_ref, f32[4,8,384]{2,1,0:T(8,128)} %get-tuple-element.65.gain_ref, bf16[1536,1536]{1,0:T(8,128)(2,1)} %bitcast.23), custom_call_target="tpu_custom_call" | custom-call | tf_op jit(solution)/shard_map/middle/pallas_call | solution.py:436
  120.4 1.1 collective-permute-start.1
  121.5 1.8 collective-permute-done.3.c_y_left
  123.3 11.5 %collective-permute-done.x_x = bf16[384,768]{1,0:T(8,128)(2,1)} collective-permute-done((bf16[384,768]{1,0:T(8,128)(2,1)}, bf16[384,768]{1,0:T(8,128)(2,1)}, u32[]{:S(2)}, u32[]{:S(2)}) %collective-permute-start) | collective-permute-done | bytes 589856 | tf_op jit(solution)/shard_map/ppermute | solution.py:1724
  135.6 84.8 %mlp.1 = (f32[384,1536]{1,0:T(8,128)}, bf16[384,1536]{1,0:T(8,128)(2,1)}, bf16[384,1536]{1,0:T(8,128)(2,1)}, bf16[384,1536]{1,0:T(8,128)(2,1)}, bf16[384,768]{1,...) custom-call(bf16[4,864,768]{2,1,0:T(8,128)(2,1)} %bitcast.30, ...), custom_call_target="tpu_custom_call" | custom-call | tf_op jit(solution)/shard_map/mlp/pallas_call | solution.py:1667
  222.2 1.3 collective-permute-start.6
  223.6 11.2 %middle_back.1 = (f32[384,1536]{1,0:T(8,128)}, bf16[384,1536]{1,0:T(8,128)(2,1)}, bf16[1536,1536]{1,0:T(8,128)(2,1)}, f32[1,1536]{1,0:T(1,128)}, s32[8,128]{1,0:T(8,128)}) custom-call(f32[384,1536]{1,0:T(8,128)} %get-tuple-element.82.grad_ref, f32[384,1536]{1,0:T(8,128)} %get-tuple-element.83.middle_ref.refs_6_, bf16[384,1536]{1,0:T(8,128)(2,1)} %bitcast.21, ...), custom_call_target="tpu_custom_call" | custom-call | tf_op jit(solution)/shard_map/middle_back/pallas_call | solution.py:477
  234.8 1.2 slice.39
  238.0 1.4 collective-permute-start.9
  239.4 21.9 %attend_back.1 = (bf16[384,1536]{1,0:T(8,128)(2,1)}, bf16[32,96,256]{2,1,0:T(8,128)(2,1)}) custom-call(s32[8,128]{1,0:T(8,128)} %get-tuple-element.64.where_ref, bf16[14,384,128]{2,1,0:T(8,128)(2,1)} %get-tuple-element.69.heads_ref.q_ref, bf16[8,2,384,128]{3,2,1,0:T(8,128)(2,1)} %get-tuple-element.71.kv_ref, bf16[384,1536]{1,0:T(8,128)(2,1)} %get-tuple-element.84.grad_ref, ...), custom_call_target="tpu_custom_call" | custom-call | tf_op jit(solution)/shard_map/attend_back/pallas_call | solution.py:385
  261.4 70.5 %project_back_plane.1 = (bf16[4,48,1536]{2,1,0:T(8,128)(2,1)}, bf16[4,48,1536]{2,1,0:T(8,128)(2,1)}, bf16[4,48,256]{2,1,0:T(8,128)(2,1)}, bf16[8,288,768]{2,1,0:...) custom-call(bf16[4,4,2,96,256]{4,3,2,1,0:T(8,128)(2,1)} %bitcast.34, bf16[4,4,2,48,1536]{4,3,2,1,0:T(8,128)(2,1)} %bitcast.33, ...), custom_call_target="tpu_custom_call" | custom-call | tf_op jit(solution)/shard_map/project_back_plane/pallas_call | solution.py:1176
  332.8 56.2 %reduce_late.1 = (bf16[8,48,1536]{2,1,0:T(8,128)(2,1)}, bf16[8,48,1536]{2,1,0:T(8,128)(2,1)}, bf16[8,48,256]{2,1,0:T(8,128)(2,1)}, bf16[8,576,768]{2,1,0:T(8,128...) custom-call(bf16[4,48,1536]{2,1,0:T(8,128)(2,1)} %get-tuple-element.97.refs_0_, ...), custom_call_target="tpu_custom_call" | custom-call | tf_op jit(solution)/shard_map/reduce_late/pallas_call | solution.py:1300
  389.0 1.4 slice_reduce_fusion
  390.4 17.8 %finish.1 = (f32[384,9216]{1,0:T(8,128)}, f32[1152,1536]{1,0:T(8,128)}, f32[384,1536]{1,0:T(8,128)}, f32[384,1792]{1,0:T(8,128)}, f32[384,1536]{1,0:T(8,128)}) custom-call(bf16[8,576,768]{2,1,0:T(8,128)(2,1)} %get-tuple-element.105.main_ref.tail_ref, bf16[8,576,768]{2,1,0:T(8,128)(2,1)} %get-tuple-element.105.main_ref.tail_ref, ...), custom_call_target="tpu_custom_call" | custom-call | tf_op jit(solution)/shard_map/finish/pallas_call | solution.py:1421
  (61 shorter events, 9.9 us)
Async XLA Ops:
  7.2 128.4 %all-gather.3.cloned.1.call-start = ((), (), s32[]{:S(2)}) async-start(), calls=%async_computation.4 | async-start | bytes 6635520 | tf_op jit(solution)/shard_map/all_gather | solution.py:1883
  30.1 231.3 %reduce-scatter.3.cloned.1.call-start = ((), (), s32[]{:S(2)}) async-start(), calls=%async_computation.2 | async-start | bytes 2211840 | tf_op jit(solution)/shard_map/reduce_scatter | solution.py:1934
  64.5 29.1 %copy-start.4 = (bf16[384,768]{1,0:T(8,128)(2,1)S(1)}, bf16[384,768]{1,0:T(8,128)(2,1)}, u32[]{:S(2)}) copy-start(bf16[384,768]{1,0:T(8,128)(2,1)} %get-tuple-element.81.c_y_right) | copy-start | bytes 1769476
  91.7 3.0 copy-start.3
  93.6 2.3 copy-start
  93.7 26.8 %collective-permute-start.5 = (bf16[384,768]{1,0:T(8,128)(2,1)S(1)}, bf16[384,768]{1,0:T(8,128)(2,1)}, u32[]{:S(2)}, u32[]{:S(2)}) collective-permute-start(bf16[384,768]{1,0:T(8,128)(2,1)S(1)} %broadcast_select_fusion), channel_id=1, source_target_pairs={{0,8},{4,12},{8,0},{12,4},{16,24},{20,28},{24,16},{28,20},{1,9},{5... | collective-permute-start | bytes 1769480 | tf_op jit(solution)/shard_map/ppermute | solution.py:1724
  94.7 26.8 %collective-permute-start.4 = (bf16[384,768]{1,0:T(8,128)(2,1)S(1)}, bf16[384,768]{1,0:T(8,128)(2,1)S(1)}, u32[]{:S(2)}, u32[]{:S(2)}) collective-permute-start(bf16[384,768]{1,0:T(8,128)(2,1)S(1)} %broadcast_select_fusion.1), channel_id=1, source_target_pairs={{0,16},{4,20},{8,24},{12,28},{16,0},{20,4},{24,8},{28,12},{1,17},{... | collective-permute-start | bytes 1769480 | tf_op jit(solution)/shard_map/ppermute | solution.py:1724
  95.9 27.4 %collective-permute-start.3 = (bf16[384,768]{1,0:T(8,128)(2,1)S(1)}, bf16[384,768]{1,0:T(8,128)(2,1)S(1)}, u32[]{:S(2)}, u32[]{:S(2)}) collective-permute-start(bf16[384,768]{1,0:T(8,128)(2,1)S(1)} %get-tuple-element.120), channel_id=1, source_target_pairs={{0,16},{4,20},{8,24},{12,28},{16,0},{20,4},{24,8},{28,12},{1,17},{... | collective-permute-start | bytes 1769480 | tf_op jit(solution)/shard_map/ppermute | solution.py:1724
  97.0 26.3 %collective-permute-start.2 = (bf16[384,768]{1,0:T(8,128)(2,1)S(1)}, bf16[384,768]{1,0:T(8,128)(2,1)S(1)}, u32[]{:S(2)}, u32[]{:S(2)}) collective-permute-start(bf16[384,768]{1,0:T(8,128)(2,1)S(1)} %get-tuple-element.121), channel_id=1, source_target_pairs={{0,8},{4,12},{8,0},{12,4},{16,24},{20,28},{24,16},{28,20},{1,9},{5... | collective-permute-start | bytes 1769480 | tf_op jit(solution)/shard_map/ppermute | solution.py:1724
  119.4 15.4 %collective-permute-start = (bf16[384,768]{1,0:T(8,128)(2,1)}, bf16[384,768]{1,0:T(8,128)(2,1)}, u32[]{:S(2)}, u32[]{:S(2)}) collective-permute-start(bf16[384,768]{1,0:T(8,128)(2,1)} %get-tuple-element.77.x_left), channel_id=1, source_target_pairs={{0,8},{4,12},{8,0},{12,4},{16,24},{20,28},{24,16},{28,20},{1,9},{5... | collective-permute-start | bytes 1769480 | tf_op jit(solution)/shard_map/ppermute | solution.py:1724
  120.4 15.2 %collective-permute-start.1 = (bf16[384,768]{1,0:T(8,128)(2,1)}, bf16[384,768]{1,0:T(8,128)(2,1)}, u32[]{:S(2)}, u32[]{:S(2)}) collective-permute-start(bf16[384,768]{1,0:T(8,128)(2,1)} %get-tuple-element.78.x_right), channel_id=1, source_target_pairs={{0,16},{4,20},{8,24},{12,28},{16,0},{20,4},{24,8},{28,12},{1,17},{... | collective-permute-start | bytes 1769480 | tf_op jit(solution)/shard_map/ppermute | solution.py:1724
  121.5 14.1 %copy-start.9 = (bf16[384,768]{1,0:T(8,128)(2,1)}, bf16[384,768]{1,0:T(8,128)(2,1)S(1)}, u32[]{:S(2)}) copy-start(bf16[384,768]{1,0:T(8,128)(2,1)S(1)} %collective-permute-done.4.c_left) | copy-start | bytes 1769476
  123.3 12.3 %copy-start.10 = (bf16[384,768]{1,0:T(8,128)(2,1)}, bf16[384,768]{1,0:T(8,128)(2,1)S(1)}, u32[]{:S(2)}) copy-start(bf16[384,768]{1,0:T(8,128)(2,1)S(1)} %collective-permute-done.3.c_y_left) | copy-start | bytes 1769476
  123.3 12.3 %copy-start.11 = (bf16[384,768]{1,0:T(8,128)(2,1)}, bf16[384,768]{1,0:T(8,128)(2,1)S(1)}, u32[]{:S(2)}) copy-start(bf16[384,768]{1,0:T(8,128)(2,1)S(1)} %collective-permute-done.2.c_x_right) | copy-start | bytes 1769476
  220.4 111.5 %reduce-scatter.5.cloned.1.call-start = ((), (), s32[]{:S(2)}) async-start(), calls=%async_computation.3 | async-start | bytes 4423680 | tf_op jit(solution)/shard_map/reduce_scatter | solution.py:1935
  220.4 3.1 copy-start.6
  221.1 2.5 copy-start.7
  221.5 15.1 %collective-permute-start.7 = (bf16[384,768]{1,0:T(8,128)(2,1)S(1)}, bf16[384,768]{1,0:T(8,128)(2,1)S(1)}, u32[]{:S(2)}, u32[]{:S(2)}) collective-permute-start(bf16[384,768]{1,0:T(8,128)(2,1)S(1)} %copy-done.12), channel_id=1, source_target_pairs={{0,8},{4,12},{8,0},{12,4},{16,24},{20,28},{24,16},{28,20},{1,9},{5... | collective-permute-start | bytes 1769480 | tf_op jit(solution)/shard_map/ppermute | solution.py:1724
  222.2 15.5 %collective-permute-start.6 = (bf16[384,768]{1,0:T(8,128)(2,1)}, bf16[384,768]{1,0:T(8,128)(2,1)S(1)}, u32[]{:S(2)}, u32[]{:S(2)}) collective-permute-start(bf16[384,768]{1,0:T(8,128)(2,1)} %get-tuple-element.89), channel_id=1, source_target_pairs={{0,16},{4,20},{8,24},{12,28},{16,0},{20,4},{24,8},{28,12},{1,17},{... | collective-permute-start | bytes 1769480 | tf_op jit(solution)/shard_map/ppermute | solution.py:1724
  236.9 1.1 copy-start.1
  236.9 94.9 %collective-permute-start.8 = (bf16[384,1536]{1,0:T(8,128)(2,1)S(1)}, bf16[384,1536]{1,0:T(8,128)(2,1)S(1)}, u32[]{:S(2)}, u32[]{:S(2)}) collective-permute-start(bf16[384,1536]{1,0:T(8,128)(2,1)S(1)} %pad_maximum_fusion.1.refs_1_), channel_id=1, source_target_pairs={{0,16},{4,20},{8,24},{12,28},{16,0},{20,4},{24,8},{28,12},{1,17},{... | collective-permute-start | bytes 3538952 | tf_op jit(solution)/shard_map/ppermute | solution.py:1724
  238.0 1.4 copy-start.2
  238.0 93.8 %collective-permute-start.9 = (bf16[384,1536]{1,0:T(8,128)(2,1)S(1)}, bf16[384,1536]{1,0:T(8,128)(2,1)}, u32[]{:S(2)}, u32[]{:S(2)}) collective-permute-start(bf16[384,1536]{1,0:T(8,128)(2,1)S(1)} %pad_maximum_fusion.refs_0_), channel_id=1, source_target_pairs={{0,8},{4,12},{8,0},{12,4},{16,24},{20,28},{24,16},{28,20},{1,9},{5... | collective-permute-start | bytes 3538952 | tf_op jit(solution)/shard_map/ppermute | solution.py:1724
  390.4 17.8 %copy-start.5 = (bf16[384,1536]{1,0:T(8,128)(2,1)S(1)}, bf16[384,1536]{1,0:T(8,128)(2,1)}, u32[]{:S(2)}) copy-start(bf16[384,1536]{1,0:T(8,128)(2,1)} %get-tuple-element.104) | copy-start | bytes 3538948
  (2 other events, 2.1 us)
Sparse Core Ops, SparseCore 0:
  30.2 104.6 all-gather.2
  220.5 40.7 reduce-scatter.2
  263.8 65.4 reduce-scatter.4

commit v7 on v6

--- a/solution.py
+++ b/solution.py
@@ -1485,6 +1485,7 @@
         for shard in range(shards):
             for one in pack.in_spans(shard):
                 yield shard, w_in, one
+        for shard in range(shards):
             for one in pack.out_spans(shard, shards):
                 yield shard, w_out, one
 
@@ -1497,10 +1498,10 @@
     loads = [
         copy_in(x_left, xs.at[0, :, left]),
         copy_in(x_right, xs.at[0, :, right]),
-        copy_in(c_own, cs.at[0]),
     ]
     for shard, target, one in spans():
         loads.append(copy_in(packed(shard, one), placed(core, target, one)))
+    loads.append(copy_in(c_own, cs.at[0]))
     late = [
         copy_in(source, target)
         for source, target in (
@@ -1523,14 +1524,23 @@
         wire.send(packed(shard, one), placed(core, target, one), wire.plane(1))
         for shard, target, one in spans()
     ]
-    for copy in loads:
+    first = sum(len(list(pack.in_spans(shard))) for shard in range(shards))
+    for copy in loads[: 2 + first]:
         copy.wait()
-    for copy in swaps:
+    for copy in swaps[:first]:
         copy.wait_recv()
 
-    def one_chunk(at):
+    def wait_rest():
+        for copy in loads[2 + first :]:
+            copy.wait()
+        for copy in swaps[first:]:
+            copy.wait_recv()
+
+    def one_chunk(at, ready=None):
         gate = dot(xs[at], w_in[0])
         up = dot(xs[at], w_in[1])
+        if ready is not None:
+            ready()
         grad = nt_dot(cs[at, :, left], w_out[0]) + nt_dot(cs[at, :, right], w_out[1])
         square = gate * gate
         bend = jnp.tanh(TANH_SCALE * gate * (1.0 + TANH_CUBE * square))
@@ -1549,7 +1559,7 @@
 
         return one_half
 
-    own_half = one_chunk(0)
+    own_half = one_chunk(0, wait_rest)
     for copy in x_copies:
         copy.wait_recv()
     corners = [

time: 423 us -> 423 us (level)
  no operation moved by 1% of the time
where the time goes in v7:
time: 423 us; the launch traced here: 416 us
  Pallas kernels  365 us (86%)
  between operations  15.6 us (4%)
  waiting for transfers between devices  14.8 us (3%)
  starting transfers between devices  10.7 us (3%)
  local copies, waits for them, and re-layouts  7.68 us (2%)
    pallas_call x1, Pallas kernels, mlp(): pl.pallas_call(functools.partial(mlp_kernel, shards, pack), name='mlp', i...  84 us
    pallas_call x1, Pallas kernels, project_back_plane(): pl.pallas_call(project_back_plane_kernel, name='project_back_plane', in_s...  70.5 us
    pallas_call x1, Pallas kernels, reduce_late(): pl.pallas_call(functools.partial(reduce_late_kernel, shards, len(lines),...  56.6 us
    pallas_call x1, Pallas kernels, gather_plane(): pl.pallas_call(functools.partial(gather_plane_kernel, shards), name='gath...  27.2 us
    pallas_call x1, Pallas kernels, share_plane(): pl.pallas_call(functools.partial(share_plane_kernel, shards, ctx_size), n...  27.1 us
    pallas_call x1, Pallas kernels, attend_back(): pl.pallas_call(functools.partial(attend_back_kernel, window.blocks, block...  21.9 us
    pallas_call x1, Pallas kernels, share_line(): pl.pallas_call(functools.partial(share_line_kernel, shards, pack), name='...  20.9 us
    pallas_call x1, Pallas kernels, finish(): pl.pallas_call(functools.partial(finish_kernel, shards, chips, pack), nam...  17.8 us
  transfers between devices with their start and end apart: 13, of which 3 were waited for; matrix products, arithmetic and copies ran while one was open for 1% of the time, Pallas kernels for 45%

profile of v7, /device:TPU:0, one launch (start us, length us, event | category | flops | bytes accessed | tf_op | source)
XLA Modules:
  0.0 415.6 jit_solution(9616456659092581366)
XLA Ops:
  9.2 20.9 %share_line.1 = (bf16[4,48,1792]{2,1,0:T(8,128)(2,1)}, f32[4,8,384]{2,1,0:T(8,128)}, bf16[864,768]{1,0:T(8,128)(2,1)}, bf16[384,768]{1,0:T(8,128)(2,1)}, bf16[384,768]{1,0:T(8,128)(2,1)}) custom-call(bf16[8,48,1792]{2,1,0:T(8,128)(2,1)} %bitcast.28, bf16[2,384]{1,0:T(2,128)(2,1)} %pad_maximum_fusion.2.gain_ref, bf16[384,9216]{1,0:T(8,128)(2,1)} %mlp_in.1, ...), custom_call_target="tpu_custom_call" | custom-call | tf_op jit(solution)/shard_map/share_line/pallas_call | solution.py:946
  30.7 27.1 %share_plane.1 = (bf16[4,8,48,1792]{3,2,1,0:T(8,128)(2,1)}, bf16[4,48,1536]{2,1,0:T(8,128)(2,1)}, s32[8,128]{1,0:T(8,128)}, f32[4,1,1152]{2,1,0:T(1,128)}, f32[3...) custom-call(bf16[8,48,1792]{2,1,0:T(8,128)(2,1)} %bitcast.29, ...), custom_call_target="tpu_custom_call" | custom-call | tf_op jit(solution)/shard_map/share_plane/pallas_call | solution.py:975
  57.8 6.7 %project.1 = (bf16[384,1536]{1,0:T(8,128)(2,1)}, bf16[14,384,128]{2,1,0:T(8,128)(2,1)}) custom-call(bf16[384,1536]{1,0:T(8,128)(2,1)} %bitcast.25, f32[4,8,384]{2,1,0:T(8,128)} %get-tuple-element.65.gain_ref, bf16[1536,1792]{1,0:T(8,128)(2,1)} %bitcast.17, f32[384,128]{1,0:T(8,128)} %get-tuple-element.67.cos_ref, f32[384,128]{1,0:T(8,128)} %get-tuple-element.68.sin_ref), custom_call_target="tpu_custom_call" | custom-call | tf_op jit(solution)/shard_map/project/pallas_call | solution.py:96
  64.5 27.2 %gather_plane.1 = (bf16[8,2,384,128]{3,2,1,0:T(8,128)(2,1)}, bf16[4,8,48,1536]{3,2,1,0:T(8,128)(2,1)}, s32[8,128]{1,0:T(8,128)}) custom-call(bf16[14,384,128]{2,1,0:T(8,128)(2,1)} %get-tuple-element.69.heads_ref.q_ref, bf16[8,48,1536]{2,1,0:T(8,128)(2,1)} %bitcast.32, bf16[4,48,1536]{2,1,0:T(8,128)(2,1)} %get-tuple-element.70.out_line), custom_call_target="tpu_custom_call" | custom-call | tf_op jit(solution)/shard_map/gather_plane/pallas_call | solution.py:997
  91.7 1.3 slice.34
  94.7 1.1 collective-permute-start.4
  95.9 1.0 collective-permute-start.3
  97.0 1.1 collective-permute-start.2
  98.0 14.5 %attend.1 = (bf16[384,1536]{1,0:T(8,128)(2,1)}, f32[4,3,1,384]{3,2,1,0:T(1,128)}) custom-call(s32[8,128]{1,0:T(8,128)} %get-tuple-element.64.where_ref, bf16[14,384,128]{2,1,0:T(8,128)(2,1)} %get-tuple-element.69.heads_ref.q_ref, bf16[8,2,384,128]{3,2,1,0:T(8,128)(2,1)} %get-tuple-element.71.kv_ref, f32[4,1,1152]{2,1,0:T(1,128)} %get-tuple-element.73.key_place_ref, ...), custom_call_target="tpu_custom_call" | custom-call | tf_op jit(solution)/shard_map/attend/pallas_call | solution.py:283
  112.5 6.9 %middle.1 = (f32[384,1536]{1,0:T(8,128)}, bf16[384,768]{1,0:T(8,128)(2,1)}, bf16[384,768]{1,0:T(8,128)(2,1)}) custom-call(bf16[384,1536]{1,0:T(8,128)(2,1)} %bitcast.26, bf16[384,1536]{1,0:T(8,128)(2,1)} %get-tuple-element.75.mixed_ref, f32[4,8,384]{2,1,0:T(8,128)} %get-tuple-element.65.gain_ref, bf16[1536,1536]{1,0:T(8,128)(2,1)} %bitcast.23), custom_call_target="tpu_custom_call" | custom-call | tf_op jit(solution)/shard_map/middle/pallas_call | solution.py:436
  119.4 1.0 collective-permute-start
  120.4 1.1 collective-permute-start.1
  121.5 1.8 collective-permute-done.3.c_y_left
  123.3 11.5 %collective-permute-done.x_x = bf16[384,768]{1,0:T(8,128)(2,1)} collective-permute-done((bf16[384,768]{1,0:T(8,128)(2,1)}, bf16[384,768]{1,0:T(8,128)(2,1)}, u32[]{:S(2)}, u32[]{:S(2)}) %collective-permute-start) | collective-permute-done | bytes 589856 | tf_op jit(solution)/shard_map/ppermute | solution.py:1734
  135.6 84.0 %mlp.1 = (f32[384,1536]{1,0:T(8,128)}, bf16[384,1536]{1,0:T(8,128)(2,1)}, bf16[384,1536]{1,0:T(8,128)(2,1)}, bf16[384,1536]{1,0:T(8,128)(2,1)}, bf16[384,768]{1,...) custom-call(bf16[4,864,768]{2,1,0:T(8,128)(2,1)} %bitcast.30, ...), custom_call_target="tpu_custom_call" | custom-call | tf_op jit(solution)/shard_map/mlp/pallas_call | solution.py:1677
  221.4 1.3 collective-permute-start.6
  222.8 11.2 %middle_back.1 = (f32[384,1536]{1,0:T(8,128)}, bf16[384,1536]{1,0:T(8,128)(2,1)}, bf16[1536,1536]{1,0:T(8,128)(2,1)}, f32[1,1536]{1,0:T(1,128)}, s32[8,128]{1,0:T(8,128)}) custom-call(f32[384,1536]{1,0:T(8,128)} %get-tuple-element.82.grad_ref, f32[384,1536]{1,0:T(8,128)} %get-tuple-element.83.middle_ref.refs_6_, bf16[384,1536]{1,0:T(8,128)(2,1)} %bitcast.21, ...), custom_call_target="tpu_custom_call" | custom-call | tf_op jit(solution)/shard_map/middle_back/pallas_call | solution.py:477
  234.0 1.2 slice.39
  237.2 1.4 collective-permute-start.9
  238.6 21.9 %attend_back.1 = (bf16[384,1536]{1,0:T(8,128)(2,1)}, bf16[32,96,256]{2,1,0:T(8,128)(2,1)}) custom-call(s32[8,128]{1,0:T(8,128)} %get-tuple-element.64.where_ref, bf16[14,384,128]{2,1,0:T(8,128)(2,1)} %get-tuple-element.69.heads_ref.q_ref, bf16[8,2,384,128]{3,2,1,0:T(8,128)(2,1)} %get-tuple-element.71.kv_ref, bf16[384,1536]{1,0:T(8,128)(2,1)} %get-tuple-element.84.grad_ref, ...), custom_call_target="tpu_custom_call" | custom-call | tf_op jit(solution)/shard_map/attend_back/pallas_call | solution.py:385
  260.5 70.5 %project_back_plane.1 = (bf16[4,48,1536]{2,1,0:T(8,128)(2,1)}, bf16[4,48,1536]{2,1,0:T(8,128)(2,1)}, bf16[4,48,256]{2,1,0:T(8,128)(2,1)}, bf16[8,288,768]{2,1,0:...) custom-call(bf16[4,4,2,96,256]{4,3,2,1,0:T(8,128)(2,1)} %bitcast.34, bf16[4,4,2,48,1536]{4,3,2,1,0:T(8,128)(2,1)} %bitcast.33, ...), custom_call_target="tpu_custom_call" | custom-call | tf_op jit(solution)/shard_map/project_back_plane/pallas_call | solution.py:1176
  332.1 56.6 %reduce_late.1 = (bf16[8,48,1536]{2,1,0:T(8,128)(2,1)}, bf16[8,48,1536]{2,1,0:T(8,128)(2,1)}, bf16[8,48,256]{2,1,0:T(8,128)(2,1)}, bf16[8,576,768]{2,1,0:T(8,128...) custom-call(bf16[4,48,1536]{2,1,0:T(8,128)(2,1)} %get-tuple-element.97.refs_0_, ...), custom_call_target="tpu_custom_call" | custom-call | tf_op jit(solution)/shard_map/reduce_late/pallas_call | solution.py:1300
  388.7 1.4 slice_reduce_fusion
  390.1 17.8 %finish.1 = (f32[384,9216]{1,0:T(8,128)}, f32[1152,1536]{1,0:T(8,128)}, f32[384,1536]{1,0:T(8,128)}, f32[384,1792]{1,0:T(8,128)}, f32[384,1536]{1,0:T(8,128)}) custom-call(bf16[8,576,768]{2,1,0:T(8,128)(2,1)} %get-tuple-element.105.main_ref.tail_ref, bf16[8,576,768]{2,1,0:T(8,128)(2,1)} %get-tuple-element.105.main_ref.tail_ref, ...), custom_call_target="tpu_custom_call" | custom-call | tf_op jit(solution)/shard_map/finish/pallas_call | solution.py:1421
  (61 shorter events, 9.9 us)
Async XLA Ops:
  7.2 128.4 %all-gather.3.cloned.1.call-start = ((), (), s32[]{:S(2)}) async-start(), calls=%async_computation.4 | async-start | bytes 6635520 | tf_op jit(solution)/shard_map/all_gather | solution.py:1893
  30.1 230.4 %reduce-scatter.3.cloned.1.call-start = ((), (), s32[]{:S(2)}) async-start(), calls=%async_computation.2 | async-start | bytes 2211840 | tf_op jit(solution)/shard_map/reduce_scatter | solution.py:1944
  64.5 29.1 %copy-start.4 = (bf16[384,768]{1,0:T(8,128)(2,1)S(1)}, bf16[384,768]{1,0:T(8,128)(2,1)}, u32[]{:S(2)}) copy-start(bf16[384,768]{1,0:T(8,128)(2,1)} %get-tuple-element.81.c_y_right) | copy-start | bytes 1769476
  91.7 3.0 copy-start.3
  93.6 2.3 copy-start
  93.7 26.8 %collective-permute-start.5 = (bf16[384,768]{1,0:T(8,128)(2,1)S(1)}, bf16[384,768]{1,0:T(8,128)(2,1)}, u32[]{:S(2)}, u32[]{:S(2)}) collective-permute-start(bf16[384,768]{1,0:T(8,128)(2,1)S(1)} %broadcast_select_fusion), channel_id=1, source_target_pairs={{0,8},{4,12},{8,0},{12,4},{16,24},{20,28},{24,16},{28,20},{1,9},{5... | collective-permute-start | bytes 1769480 | tf_op jit(solution)/shard_map/ppermute | solution.py:1734
  94.7 26.8 %collective-permute-start.4 = (bf16[384,768]{1,0:T(8,128)(2,1)S(1)}, bf16[384,768]{1,0:T(8,128)(2,1)S(1)}, u32[]{:S(2)}, u32[]{:S(2)}) collective-permute-start(bf16[384,768]{1,0:T(8,128)(2,1)S(1)} %broadcast_select_fusion.1), channel_id=1, source_target_pairs={{0,16},{4,20},{8,24},{12,28},{16,0},{20,4},{24,8},{28,12},{1,17},{... | collective-permute-start | bytes 1769480 | tf_op jit(solution)/shard_map/ppermute | solution.py:1734
  95.9 27.4 %collective-permute-start.3 = (bf16[384,768]{1,0:T(8,128)(2,1)S(1)}, bf16[384,768]{1,0:T(8,128)(2,1)S(1)}, u32[]{:S(2)}, u32[]{:S(2)}) collective-permute-start(bf16[384,768]{1,0:T(8,128)(2,1)S(1)} %get-tuple-element.120), channel_id=1, source_target_pairs={{0,16},{4,20},{8,24},{12,28},{16,0},{20,4},{24,8},{28,12},{1,17},{... | collective-permute-start | bytes 1769480 | tf_op jit(solution)/shard_map/ppermute | solution.py:1734
  97.0 26.3 %collective-permute-start.2 = (bf16[384,768]{1,0:T(8,128)(2,1)S(1)}, bf16[384,768]{1,0:T(8,128)(2,1)S(1)}, u32[]{:S(2)}, u32[]{:S(2)}) collective-permute-start(bf16[384,768]{1,0:T(8,128)(2,1)S(1)} %get-tuple-element.121), channel_id=1, source_target_pairs={{0,8},{4,12},{8,0},{12,4},{16,24},{20,28},{24,16},{28,20},{1,9},{5... | collective-permute-start | bytes 1769480 | tf_op jit(solution)/shard_map/ppermute | solution.py:1734
  119.4 15.4 %collective-permute-start = (bf16[384,768]{1,0:T(8,128)(2,1)}, bf16[384,768]{1,0:T(8,128)(2,1)}, u32[]{:S(2)}, u32[]{:S(2)}) collective-permute-start(bf16[384,768]{1,0:T(8,128)(2,1)} %get-tuple-element.77.x_left), channel_id=1, source_target_pairs={{0,8},{4,12},{8,0},{12,4},{16,24},{20,28},{24,16},{28,20},{1,9},{5... | collective-permute-start | bytes 1769480 | tf_op jit(solution)/shard_map/ppermute | solution.py:1734
  120.4 15.2 %collective-permute-start.1 = (bf16[384,768]{1,0:T(8,128)(2,1)}, bf16[384,768]{1,0:T(8,128)(2,1)}, u32[]{:S(2)}, u32[]{:S(2)}) collective-permute-start(bf16[384,768]{1,0:T(8,128)(2,1)} %get-tuple-element.78.x_right), channel_id=1, source_target_pairs={{0,16},{4,20},{8,24},{12,28},{16,0},{20,4},{24,8},{28,12},{1,17},{... | collective-permute-start | bytes 1769480 | tf_op jit(solution)/shard_map/ppermute | solution.py:1734
  121.5 14.1 %copy-start.9 = (bf16[384,768]{1,0:T(8,128)(2,1)}, bf16[384,768]{1,0:T(8,128)(2,1)S(1)}, u32[]{:S(2)}) copy-start(bf16[384,768]{1,0:T(8,128)(2,1)S(1)} %collective-permute-done.4.c_left) | copy-start | bytes 1769476
  123.3 12.3 %copy-start.10 = (bf16[384,768]{1,0:T(8,128)(2,1)}, bf16[384,768]{1,0:T(8,128)(2,1)S(1)}, u32[]{:S(2)}) copy-start(bf16[384,768]{1,0:T(8,128)(2,1)S(1)} %collective-permute-done.3.c_y_left) | copy-start | bytes 1769476
  123.3 12.3 %copy-start.11 = (bf16[384,768]{1,0:T(8,128)(2,1)}, bf16[384,768]{1,0:T(8,128)(2,1)S(1)}, u32[]{:S(2)}) copy-start(bf16[384,768]{1,0:T(8,128)(2,1)S(1)} %collective-permute-done.2.c_x_right) | copy-start | bytes 1769476
  219.6 111.5 %reduce-scatter.5.cloned.1.call-start = ((), (), s32[]{:S(2)}) async-start(), calls=%async_computation.3 | async-start | bytes 4423680 | tf_op jit(solution)/shard_map/reduce_scatter | solution.py:1945
  219.6 3.1 copy-start.6
  220.3 2.5 copy-start.7
  220.7 15.2 %collective-permute-start.7 = (bf16[384,768]{1,0:T(8,128)(2,1)S(1)}, bf16[384,768]{1,0:T(8,128)(2,1)S(1)}, u32[]{:S(2)}, u32[]{:S(2)}) collective-permute-start(bf16[384,768]{1,0:T(8,128)(2,1)S(1)} %copy-done.12), channel_id=1, source_target_pairs={{0,8},{4,12},{8,0},{12,4},{16,24},{20,28},{24,16},{28,20},{1,9},{5... | collective-permute-start | bytes 1769480 | tf_op jit(solution)/shard_map/ppermute | solution.py:1734
  221.4 15.5 %collective-permute-start.6 = (bf16[384,768]{1,0:T(8,128)(2,1)}, bf16[384,768]{1,0:T(8,128)(2,1)S(1)}, u32[]{:S(2)}, u32[]{:S(2)}) collective-permute-start(bf16[384,768]{1,0:T(8,128)(2,1)} %get-tuple-element.89), channel_id=1, source_target_pairs={{0,16},{4,20},{8,24},{12,28},{16,0},{20,4},{24,8},{28,12},{1,17},{... | collective-permute-start | bytes 1769480 | tf_op jit(solution)/shard_map/ppermute | solution.py:1734
  236.1 1.1 copy-start.1
  236.1 94.9 %collective-permute-start.8 = (bf16[384,1536]{1,0:T(8,128)(2,1)S(1)}, bf16[384,1536]{1,0:T(8,128)(2,1)S(1)}, u32[]{:S(2)}, u32[]{:S(2)}) collective-permute-start(bf16[384,1536]{1,0:T(8,128)(2,1)S(1)} %pad_maximum_fusion.1.refs_1_), channel_id=1, source_target_pairs={{0,16},{4,20},{8,24},{12,28},{16,0},{20,4},{24,8},{28,12},{1,17},{... | collective-permute-start | bytes 3538952 | tf_op jit(solution)/shard_map/ppermute | solution.py:1734
  237.2 1.4 copy-start.2
  237.2 93.9 %collective-permute-start.9 = (bf16[384,1536]{1,0:T(8,128)(2,1)S(1)}, bf16[384,1536]{1,0:T(8,128)(2,1)}, u32[]{:S(2)}, u32[]{:S(2)}) collective-permute-start(bf16[384,1536]{1,0:T(8,128)(2,1)S(1)} %pad_maximum_fusion.refs_0_), channel_id=1, source_target_pairs={{0,8},{4,12},{8,0},{12,4},{16,24},{20,28},{24,16},{28,20},{1,9},{5... | collective-permute-start | bytes 3538952 | tf_op jit(solution)/shard_map/ppermute | solution.py:1734
  390.1 17.8 %copy-start.5 = (bf16[384,1536]{1,0:T(8,128)(2,1)S(1)}, bf16[384,1536]{1,0:T(8,128)(2,1)}, u32[]{:S(2)}) copy-start(bf16[384,1536]{1,0:T(8,128)(2,1)} %get-tuple-element.104) | copy-start | bytes 3538948
  (2 other events, 2.1 us)
Sparse Core Ops, SparseCore 0:
  30.2 104.6 all-gather.2
  219.7 40.7 reduce-scatter.2
  263.0 65.4 reduce-scatter.4
